TPU v7x, 512 devices: a whole 4x8x8 slice. The times are simulated.
512 devices in a mesh: seq: 128 (over z_lo, y, x, core), pair: 4 (over z_hi).
Axes of the slice: x: 4, y: 8, z: 8 (z_hi: 4, z_lo: 2; z = z_hi * 2 + z_lo), core: 2. Of those that a mesh axis runs over, the one named last changes fastest.
Arguments:
- tokens: int32 [262144], P('seq'), may hold values from 0 to 3
- w_stem: bfloat16 [60, 768], replicated, may hold values from -1.5 to 1.5
- w_conv: bfloat16 [3840, 1536], P('seq', 'pair'), may hold values from -0.09375 to 0.09375
- w_query: bfloat16 [1536, 512], P(None, 'pair')
- w_key: bfloat16 [1536, 512], P(None, 'pair'), may hold values from -0.15625 to 0.15625
- w_value: bfloat16 [1536, 768], P(None, 'pair'), may hold values from -0.15625 to 0.15625
- w_out: bfloat16 [768, 1536], P('pair'), may hold values from -0.21875 to 0.21875
- w_pair: bfloat16 [2, 1536, 128], P(None, None, 'pair'), may hold values from -0.15625 to 0.15625
- pair_bias: bfloat16 [18, 128], P(None, 'pair'), may hold values from -6 to 6
- pair_in: bfloat16 [128, 128, 128], P('seq', None, 'pair'), may hold values from -6 to 6
Outputs:
- seq_out: bfloat16 [2048, 1536], P('seq', 'pair')
- pair_out: bfloat16 [128, 128, 128], P('seq', None, 'pair')
All inputs are finite; a program needn't handle non-finite values.
Results may differ from a plain program's by a relative error of at most 0.02.
Values may be sent and summed in bfloat16 or wider, within the bound.
No kernel may reach another device: no remote copies, remote signals or barrier semaphores. Data moves between devices by JAX's collectives and lax.ppermute only.
A program may use at most 64 MiB of HBM per device.

v0:
```python
import math

import jax
import jax.numpy as jnp
from jax import lax
from jax.sharding import PartitionSpec as P

HQK = 128
HV = 192
KS_CONV = 5
STEM_POOL = 64
CONV_POOL = 2
PAIR_POOL = 16


EDGES = (1, 2, 3, 4, 6, 8, 12, 16, 24, 32, 48, 64, 96, 128, 192, 256, 384)


def padded_2(cells, sides, width):
    for axis, dim in sides:
        count = lax.axis_size(axis)
        ends = count - 1
        head = lax.slice_in_dim(cells, 0, width, axis=dim)
        tail = lax.slice_in_dim(cells, cells.shape[dim] - width, cells.shape[dim], axis=dim)
        cells = jnp.concatenate(
            [
                lax.ppermute(tail, axis, [(i, (i + 1) % count) for i in range(ends)]),
                cells,
                lax.ppermute(head, axis, [((i + 1) % count, i) for i in range(ends)]),
            ],
            axis=dim,
        )
    return cells


def distance_bias(rows_index, cols_index, pair_bias):
    delta = jnp.abs(rows_index[:, None] - cols_index[None, :])
    bins = jnp.zeros(delta.shape, jnp.int32)
    for edge in EDGES:
        bins = bins + (delta >= edge).astype(jnp.int32)
    labels = jnp.arange(pair_bias.shape[0], dtype=jnp.int32)
    onehot = (bins[:, :, None] == labels[None, None, :]).astype(jnp.bfloat16)
    return jnp.einsum("ijn,nc->ijc", onehot, pair_bias, preferred_element_type=jnp.float32)


def stem_rows(onehot, stem_weight, block):

    def stem_block(rows):
        hidden = jax.nn.gelu(jnp.dot(rows, stem_weight, preferred_element_type=jnp.float32))
        return jnp.max(hidden.reshape(block // STEM_POOL, STEM_POOL, hidden.shape[1]), axis=1)

    bases = onehot.shape[0]
    section = lax.map(stem_block, onehot.reshape(bases // block, block, onehot.shape[1]))
    return section.reshape(bases // STEM_POOL, -1).astype(jnp.bfloat16)


def on_device(tokens, w_stem, w_conv, w_query, w_key, w_value, w_out, w_pair, pair_bias, pair_in):
    bases = tokens.shape[0]
    stem_taps = w_stem.shape[0] // 4
    half_stem = stem_taps // 2
    codes = padded_2(tokens + 1, (("seq", 0),), half_stem)
    levels = jnp.arange(1, 5, dtype=jnp.int32)
    onehot = jnp.concatenate(
        [codes[k : k + bases, None] == levels[None, :] for k in range(stem_taps)], axis=1
    ).astype(jnp.bfloat16)
    block = min(1024, bases)
    section = stem_rows(onehot, w_stem, block)
    section_rows = section.shape[0]
    half_conv = KS_CONV // 2
    padded = padded_2(section, (("seq", 0),), half_conv)
    unfold = jnp.concatenate([padded[k : k + section_rows] for k in range(KS_CONV)], axis=1)
    conv = jnp.dot(
        unfold,
        lax.all_gather(w_conv, "seq", axis=0, tiled=True),
        preferred_element_type=jnp.float32,
    )
    active = jax.nn.gelu(conv)
    trunk_part = jnp.max(
        active.reshape(section_rows // CONV_POOL, CONV_POOL, active.shape[1]), axis=1
    ).astype(jnp.bfloat16)
    trunk_full = lax.all_gather(trunk_part, "pair", axis=1, tiled=True)
    count = trunk_full.shape[0]
    heads = w_query.shape[1] // HQK
    queries = (
        jnp.dot(trunk_full, w_query, preferred_element_type=jnp.float32)
        .astype(jnp.bfloat16)
        .reshape(count, heads, HQK)
    )
    keys = jnp.dot(trunk_full, w_key, preferred_element_type=jnp.float32).astype(jnp.bfloat16)
    values = jnp.dot(trunk_full, w_value, preferred_element_type=jnp.float32).astype(jnp.bfloat16)
    scale = 1.0 / math.sqrt(HQK)
    top = jnp.full((heads, count), -1e30, jnp.float32)
    key_rows = lax.all_gather(keys, "seq", axis=0, tiled=True).reshape(-1, heads, HQK)
    value_rows = lax.all_gather(values, "seq", axis=0, tiled=True).reshape(-1, heads, HV)
    scores = (
        jnp.einsum("qhd,khd->hqk", queries, key_rows, preferred_element_type=jnp.float32) * scale
    )
    new_top = jnp.maximum(top, jnp.max(scores, axis=2))
    expo = jnp.exp(scores - new_top[:, :, None])
    total = jnp.sum(expo, axis=2)
    accum = jnp.einsum(
        "hqk,khd->hqd", expo.astype(jnp.bfloat16), value_rows, preferred_element_type=jnp.float32
    )
    top, total, accum = (new_top, total, accum)
    mixed = (accum / total[:, :, None]).astype(jnp.bfloat16)
    mixed = jnp.transpose(mixed, (1, 0, 2)).reshape(count, heads * HV)
    partial_out = jnp.dot(mixed, w_out, preferred_element_type=jnp.float32)
    attended = lax.psum(partial_out.astype(jnp.bfloat16), "pair").astype(jnp.float32)
    summed = trunk_full.astype(jnp.float32) + attended
    width = trunk_part.shape[1]
    seq_out = lax.dynamic_slice_in_dim(summed, lax.axis_index("pair") * width, width, 1).astype(
        jnp.bfloat16
    )
    pooled = jnp.mean(
        summed.reshape(count // PAIR_POOL, PAIR_POOL, summed.shape[1]), axis=1
    ).astype(jnp.bfloat16)
    row_a = jnp.dot(pooled, w_pair[0], preferred_element_type=jnp.float32)
    row_b = jnp.dot(pooled, w_pair[1], preferred_element_type=jnp.float32)
    pair_rows = pooled.shape[0]
    rows_index = lax.axis_index("seq") * pair_rows + jnp.arange(pair_rows, dtype=jnp.int32)
    cols_index = jnp.arange(pair_in.shape[1], dtype=jnp.int32)
    bias = distance_bias(rows_index, cols_index, pair_bias)
    all_b = lax.all_gather(row_b, "seq", axis=0, tiled=True)
    direct = pair_in.astype(jnp.float32) + row_a[:, None, :] * all_b[None, :, :] + bias
    mirrored = jnp.transpose(
        lax.all_to_all(direct, "seq", split_axis=1, concat_axis=0, tiled=True), (1, 0, 2)
    )
    pair_out = (0.5 * (direct + mirrored)).astype(jnp.bfloat16)
    return (seq_out, pair_out)


def solution(mesh):
    placed = (
        P("seq"),
        P(),
        P("seq", "pair"),
        P(None, "pair"),
        P(None, "pair"),
        P(None, "pair"),
        P("pair", None),
        P(None, None, "pair"),
        P(None, "pair"),
        P("seq", None, "pair"),
    )
    return jax.shard_map(
        on_device,
        mesh=mesh,
        in_specs=placed,
        out_specs=(P("seq", "pair"), P("seq", None, "pair")),
        check_vma=False,
    )
```

profile of v0, /device:TPU:1, one launch (start us, length us, event | category | flops | bytes accessed | tf_op | source)
XLA Modules:
  0.0 1163.6 jit_solution(13315235590700607711)
XLA Ops:
  7.2 0.0 copy-start
  7.2 0.0 all-gather.4.cloned.1.call-start
  7.2 0.7 all-gather.4.cloned.1.call-update
  7.9 0.7 broadcast_add_fusion
  8.6 0.1 fusion.67
  8.7 4.5 collective-permute-start
  13.2 5.6 collective-permute-start.1
  18.8 0.5 iota_add_fusion
  19.3 0.1 pad_add_fusion.1
  19.5 0.6 eq.266
  20.1 0.6 eq.269
  20.7 0.6 eq.272
  21.3 0.6 eq.275
  21.9 0.1 pad_add_fusion
  22.0 0.6 eq.281
  22.6 0.6 eq.284
  23.2 0.6 eq.287
  23.8 0.6 eq.290
  24.4 0.6 eq.293
  25.0 0.6 eq.296
  25.6 0.6 eq.299
  26.2 6.8 broadcast_compare_fusion
  33.0 6.9 concatenate.37
  39.8 1.1 convert_element_type.214
  40.9 4.4 while.10
  40.9 2.1 bitcast_reduce_fusion.2
  43.1 2.1 bitcast_reduce_fusion.2
  45.3 1.9 collective-permute-start.2
  47.2 1.3 dynamic-slice
  49.2 2.4 collective-permute-start.3
  51.6 0.6 fusion.25
  52.2 0.6 fusion.34
  52.8 0.6 constant_dynamic-update-slice_fusion
  53.5 0.6 collective-permute-done.3
  54.1 0.6 fusion.23
  54.7 0.6 fusion.33
  55.3 176.5 %all-gather.4.cloned.1.call-done = bf16[128,30,384]{2,1,0:T(8,128)(2,1)} async-done(((bf16[1,30,384]{2,1,0:T(8,128)(2,1)}), bf16[128,30,384]{2,1,0:T(8,128)(2,1)}) %all-gather.4.cloned.1.call-update) | async-done | bytes 2949136 | tf_op jit(solution)/shard_map/all_gather | solution.py:74
  231.9 3.8 reshape.361
  235.7 2.1 fusion.32
  237.8 0.8 reshape.355
  238.6 0.1 reduce_max.27
  238.7 13.3 %all_gather.16 = bf16[16,1536]{1,0:T(8,128)(2,1)S(1)} all-gather(bf16[16,384]{1,0:T(8,128)(2,1)S(1)} %reduce_max.27), channel_id=1, replica_groups=mesh['seq'=128,'pair'=4] {'pair'}, dimensions={1}, use_global_device_ids=true | all-gather | bytes 61440 | tf_op jit(solution)/shard_map/all_gather | solution.py:81
  252.0 1.2 convolution_convert_fusion.2
  253.1 0.0 copy-start.3
  253.1 160.4 %all_gather.17 = bf16[2048,128]{1,0:T(8,128)(2,1)S(1)} all-gather(bf16[16,128]{1,0:T(8,128)(2,1)S(1)} %convolution_convert_fusion.2), channel_id=1, replica_groups=mesh['seq'=128,'pair'=4] {'seq'}, dimensions={0}, use_global_device_ids=true | all-gather | bytes 528384 | tf_op jit(solution)/shard_map/all_gather | solution.py:93
  413.6 1.5 fusion.68
  415.1 1.3 convolution_convert_fusion.1
  416.4 153.9 %all_gather.18 = bf16[2048,192]{1,0:T(8,128)(2,1)S(1)} all-gather(bf16[16,192]{1,0:T(8,128)(2,1)S(1)} %convolution_convert_fusion.1), channel_id=1, replica_groups=mesh['seq'=128,'pair'=4] {'seq'}, dimensions={0}, use_global_device_ids=true | all-gather | bytes 792576 | tf_op jit(solution)/shard_map/all_gather | solution.py:94
  570.2 0.2 fusion.12
  570.5 0.6 convolution_convert_fusion
  571.0 14.8 %psum.7 = bf16[16,1536]{1,0:T(8,128)(2,1)S(1)} all-reduce(bf16[16,1536]{1,0:T(8,128)(2,1)S(1)} %convolution_convert_fusion), channel_id=1, replica_groups=mesh['seq'=128,'pair'=4] {'pair'}, use_global_device_ids=true, to_apply=%region_6.7 | all-reduce | flops 24576 | bytes 98304 | tf_op jit(solution)/shard_map/psum | solution.py:108
  585.9 0.1 convolution_bitcast_fusion.1
  586.1 0.1 convolution_bitcast_fusion.2
  586.2 0.3 dynamic-update-slice
  586.5 545.8 %all-reduce = f32[4096]{0:T(1024)S(1)} all-reduce(f32[4096]{0:T(1024)S(1)} %dynamic-update-slice), channel_id=2, replica_groups=mesh['seq'=128,'pair'=4] {'seq'}, use_global_device_ids=true, to_apply=%add | all-reduce | flops 4096 | bytes 32768
  1132.3 0.1 reshape.356
  1132.4 0.1 copy.13
  1132.4 0.2 fusion.10
  1132.7 0.7 copy.14
  1133.4 11.7 %all-to-all-start = ((f32[1,128,32]{2,0,1:T(1,128)}), f32[1,128,32]{2,0,1:T(1,128)S(1)}, u32[]{:S(2)}, u32[]{:S(2)}) async-start(f32[1,128,32]{2,0,1:T(1,128)} %copy.14), calls=%async_computation | async-start | bytes 131072 | tf_op jit(solution)/shard_map/all_to_all | solution.py:126
  1145.1 0.6 dynamic-slice_convert_fusion
  1145.7 10.3 all-to-all-done
  1156.1 0.1 copy.15
  1156.1 0.6 multiply_convert_fusion
  (24 shorter events, 0.2 us)
Async XLA Ops:
  7.2 563.3 %copy-start = (bf16[192,1536]{1,0:T(8,128)(2,1)S(1)}, bf16[192,1536]{1,0:T(8,128)(2,1)}, u32[]{:S(2)}) copy-start(bf16[192,1536]{1,0:T(8,128)(2,1)} %param.18) | copy-start | bytes 1769476
  7.2 224.7 %all-gather.4.cloned.1.call-start = ((), (), s32[]{:S(2)}) async-start(), calls=%async_computation.1 | async-start | bytes 3170304 | tf_op jit(solution)/shard_map/all_gather | solution.py:74
  8.7 10.6 collective-permute-start
  13.2 8.7 collective-permute-start.1
  45.3 6.3 collective-permute-start.2
  49.2 4.9 collective-permute-start.3
  237.8 348.1 %copy-start.1 = (bf16[2,1536,32]{1,2,0:T(8,128)(2,1)S(1)}, bf16[2,1536,32]{1,2,0:T(8,128)(2,1)}, u32[]{:S(2)}) copy-start(bf16[2,1536,32]{1,2,0:T(8,128)(2,1)} %param.19) | copy-start | bytes 589828
  253.1 879.3 %copy-start.2 = (bf16[1,128,32]{1,2,0:T(8,128)(2,1)S(1)}, bf16[1,128,32]{1,2,0:T(8,128)(2,1)}, u32[]{:S(2)}) copy-start(bf16[1,128,32]{1,2,0:T(8,128)(2,1)} %param.21) | copy-start | bytes 24580
  253.1 879.3 %copy-start.3 = (bf16[18,32]{1,0:T(8,128)(2,1)S(1)}, bf16[18,32]{1,0:T(8,128)(2,1)}, u32[]{:S(2)}) copy-start(bf16[18,32]{1,0:T(8,128)(2,1)} %param.20) | copy-start | bytes 3460
  1133.4 22.7 %all-to-all-start = ((f32[1,128,32]{2,0,1:T(1,128)}), f32[1,128,32]{2,0,1:T(1,128)S(1)}, u32[]{:S(2)}, u32[]{:S(2)}) async-start(f32[1,128,32]{2,0,1:T(1,128)} %copy.14), calls=%async_computation | async-start | bytes 131072 | tf_op jit(solution)/shard_map/all_to_all | solution.py:126
Sparse Core Ops, SparseCore 0:
  10.2 221.6 all-gather.3
where the time goes:
time: 1170 us; the launch traced here: 1160 us
  blocking collectives  888 us (76%)
  waiting for transfers between devices  188 us (16%)
  starting transfers between devices  26.1 us (2%)
  local copies, waits for them, and re-layouts  21.9 us (2%)
  between operations  14.9 us (1%)
  other arithmetic  12.8 us (1%)
    unnamed x1, blocking collectives  546 us
    all_gather x1, waiting for transfers between devices, on_device(): lax.all_gather(w_conv, 'seq', axis=0, tiled=True)  177 us
    all_gather x1, blocking collectives, on_device(): lax.all_gather(keys, 'seq', axis=0, tiled=True).reshape(-1, heads, HQK)  160 us
    all_gather x1, blocking collectives, on_device(): lax.all_gather(values, 'seq', axis=0, tiled=True).reshape(-1, heads, HV)  154 us
  transfers between devices with their start and end apart: 6, of which 3 were waited for; matrix products, arithmetic and copies ran while one was open for 3% of the time, Pallas kernels for 0%

commit v1 on v0

v1 whole, which is shorter than its diff:
```python
import math

import jax
import jax.numpy as jnp
from jax import lax
from jax.experimental import pallas as pl
from jax.experimental.pallas import tpu as pltpu
from jax.sharding import Mesh
from jax.sharding import PartitionSpec as P

HQK = 128
HV = 192
KS_STEM = 15
KS_CONV = 5
STEM_POOL = 64
PAIR_POOL = 16
EDGES = (1, 2, 3, 4, 6, 8, 12, 16, 24, 32, 48, 64, 96, 128, 192, 256, 384)

SEQ = ("zl", "y", "x", "core")
SHARE = ("zl", "core")
SIZES = {"zl": 2, "y": 8, "x": 4, "core": 2, "pair": 4}
N_SEQ = 128
N_SHARE = 4
N_PAIR = 4

SIDE = 256
ROWS = 32
EXT = ROWS + 4
EXT_PAD = 40
VMEM = 48 * 1024 * 1024


def params(**kw):
    return pltpu.CompilerParams(vmem_limit_bytes=VMEM, **kw)


def whole(count):
    return [pl.BlockSpec(memory_space=pltpu.VMEM) for _ in range(count)]


def gelu(x):
    return 0.5 * x * (1.0 + jnp.tanh(math.sqrt(2.0 / math.pi) * (x + 0.044715 * (x * x * x))))


def stem_kernel(place_ref, codes_ref, weight_ref, out_ref):
    length = codes_ref.shape[1]
    codes = jnp.broadcast_to(codes_ref[...], (16, length))
    first = SIDE - 2 * STEM_POOL + KS_STEM // 2
    shifted = pltpu.roll(codes, length - first, 1, stride=1, stride_axis=0)
    shifted = shifted[:, : EXT * STEM_POOL]
    onehot = jnp.concatenate(
        [(shifted == base + 1).astype(jnp.float32) for base in range(4)], axis=0
    ).astype(jnp.bfloat16)
    weight = weight_ref[...]
    step = 6
    for at in range(0, EXT, step):
        part = onehot[:, at * STEM_POOL : (at + step) * STEM_POOL]
        hidden = lax.dot_general(
            part, weight, (((0,), (0,)), ((), ())), preferred_element_type=jnp.float32
        ).reshape(step, STEM_POOL, weight.shape[1])
        high = gelu(jnp.max(hidden, axis=1))
        low = gelu(jnp.min(hidden, axis=1))
        rows = jnp.maximum(high, low)
        index = place_ref[0] * ROWS - 2 + at + lax.broadcasted_iota(jnp.int32, rows.shape, 0)
        inside = (index >= 0) & (index < N_SEQ * ROWS)
        out_ref[at : at + step, :] = jnp.where(inside, rows, 0.0)
    out_ref[EXT:EXT_PAD, :] = jnp.zeros((EXT_PAD - EXT, weight.shape[1]), jnp.float32)


def stem(place, codes, weight):
    return pl.pallas_call(
        stem_kernel,
        out_shape=jax.ShapeDtypeStruct((EXT_PAD, weight.shape[1]), jnp.float32),
        in_specs=[pl.BlockSpec(memory_space=pltpu.SMEM)] + whole(2),
        out_specs=whole(1)[0],
        compiler_params=params(),
        cost_estimate=pl.CostEstimate(flops=2 * 2304 * 64 * 768, bytes_accessed=200000, transcendentals=0),
    )(place, codes, weight)


def conv_kernel(section_ref, weight_ref, out_ref, wide, act):
    windows, _, channels = section_ref.shape
    wide[...] = section_ref[...].astype(jnp.float32)
    total = None
    for tap in range(KS_CONV):
        rows = wide[:, tap : tap + ROWS, :].astype(jnp.bfloat16).reshape(windows * ROWS, channels)
        term = jnp.dot(
            rows,
            weight_ref[tap * channels : (tap + 1) * channels, :],
            preferred_element_type=jnp.float32,
        )
        total = term if total is None else total + term
    act[...] = gelu(total)
    half = windows * ROWS // 2
    best = jnp.maximum(act[pl.ds(0, half, stride=2), :], act[pl.ds(1, half, stride=2), :])
    out_ref[...] = best.astype(jnp.bfloat16).reshape(out_ref.shape)


def conv(section, weight):
    windows, _, channels = section.shape
    columns = weight.shape[1]
    return pl.pallas_call(
        conv_kernel,
        out_shape=jax.ShapeDtypeStruct((windows, ROWS // 2, columns), jnp.bfloat16),
        in_specs=whole(2),
        out_specs=whole(1)[0],
        scratch_shapes=[
            pltpu.VMEM((windows, EXT_PAD, channels), jnp.float32),
            pltpu.VMEM((windows * ROWS, columns), jnp.float32),
        ],
        compiler_params=params(),
    )(section, weight)


def attention_kernel(query_ref, kv_ref, w_out_ref, out_ref):
    scale = 1.0 / math.sqrt(HQK)
    scores = (
        lax.dot_general(
            query_ref[...],
            kv_ref[:, :HQK],
            (((1,), (1,)), ((), ())),
            preferred_element_type=jnp.float32,
        )
        * scale
    )
    top = jnp.max(scores, axis=1, keepdims=True)
    expo = jnp.exp(scores - top)
    total = jnp.sum(expo, axis=1, keepdims=True)
    mixed = jnp.dot(
        expo.astype(jnp.bfloat16), kv_ref[:, HQK : HQK + HV], preferred_element_type=jnp.float32
    )
    mixed = (mixed / total).astype(jnp.bfloat16)
    term = jnp.dot(mixed, w_out_ref[...], preferred_element_type=jnp.float32)
    mean = jnp.sum(term, axis=0, keepdims=True) * (1.0 / PAIR_POOL)
    width = term.shape[1] // N_PAIR
    count = term.shape[0]
    tail = jnp.concatenate(
        [mean[:, c * width : (c + 1) * width] for c in range(N_PAIR)]
        + [jnp.zeros((4, width), jnp.float32)],
        axis=0,
    )
    for c in range(N_PAIR):
        out_ref[c, :count, :] = term[:, c * width : (c + 1) * width]
        out_ref[c, count : count + 8, :] = tail


def attention(query, kv, w_out):
    count = query.shape[0]
    width = w_out.shape[1] // N_PAIR
    return pl.pallas_call(
        attention_kernel,
        out_shape=jax.ShapeDtypeStruct((N_PAIR, count + 8, width), jnp.float32),
        in_specs=whole(3),
        out_specs=whole(1)[0],
        compiler_params=params(),
    )(query, kv, w_out)


def close_kernel(terms_ref, own_ref, trunk_ref, w_pair_ref, seq_ref, rows_ref):
    count, width = own_ref.shape
    total = terms_ref[0] + terms_ref[1] + terms_ref[2] + terms_ref[3]
    seq_ref[...] = (own_ref[...].astype(jnp.float32) + total[:count, :]).astype(jnp.bfloat16)
    trunk_mean = jnp.sum(trunk_ref[...].astype(jnp.float32), axis=0, keepdims=True) * (1.0 / PAIR_POOL)
    rows = None
    for c in range(N_PAIR):
        pooled = trunk_mean[:, c * width : (c + 1) * width] + total[count + c : count + c + 1, :]
        term = jnp.dot(
            jnp.broadcast_to(pooled, (8, width)).astype(jnp.bfloat16),
            w_pair_ref[c * width : (c + 1) * width, :],
            preferred_element_type=jnp.float32,
        )
        rows = term if rows is None else rows + term
    rows_ref[...] = rows


def close(terms, own, trunk, w_pair):
    return pl.pallas_call(
        close_kernel,
        out_shape=(
            jax.ShapeDtypeStruct(own.shape, jnp.bfloat16),
            jax.ShapeDtypeStruct((8, w_pair.shape[1]), jnp.float32),
        ),
        in_specs=whole(4),
        out_specs=tuple(whole(2)),
        compiler_params=params(),
    )(terms, own, trunk, w_pair)


def distance_bias(row, cols, pair_bias):
    delta = jnp.abs(row - cols)
    bins = jnp.zeros(delta.shape, jnp.int32)
    for edge in EDGES:
        bins = bins + (delta >= edge).astype(jnp.int32)
    labels = jnp.arange(pair_bias.shape[0], dtype=jnp.int32)
    onehot = (bins[:, None] == labels[None, :]).astype(jnp.bfloat16)
    return jnp.dot(onehot, pair_bias, preferred_element_type=jnp.float32)


def on_device(tokens, w_stem, w_conv, w_query, w_key, w_value, w_out, w_pair, pair_bias, pair_in):
    place = lax.axis_index(SEQ)
    pair_place = lax.axis_index("pair")

    taps, width = w_conv.shape
    share = width // N_SHARE
    blocks = w_conv.reshape(taps, N_SHARE, share).transpose(1, 0, 2)
    blocks = blocks.reshape(2, 1, 1, 2, taps, share)
    blocks = jnp.broadcast_to(blocks, (2, 8, 4, 2, taps, share)).reshape(N_SEQ, taps, share)
    channels = pair_in.shape[2]
    mirror = jnp.pad(pair_in.reshape(N_SEQ, 1, channels), ((0, 0), (0, 0), (0, share - channels)))
    sent = jnp.concatenate([blocks, mirror], axis=1)
    held = lax.all_to_all(sent, SEQ, split_axis=0, concat_axis=0, tiled=True)
    conv_weight = held[:, :taps, :].reshape(N_SEQ * taps, share)
    mirror = held[:, taps, :channels]

    codes = tokens + 1
    ends = N_SEQ - 1
    left = lax.ppermute(codes[-SIDE:], SEQ, [(i, i + 1) for i in range(ends)])
    right = lax.ppermute(codes[:SIDE], SEQ, [(i + 1, i) for i in range(ends)])
    codes = jnp.concatenate([left, codes, right])[None, :]
    stem_weight = w_stem.reshape(KS_STEM, 4, -1)[::-1].transpose(1, 0, 2)
    stem_weight = jnp.pad(stem_weight, ((0, 0), (0, 1), (0, 0))).reshape(64, -1)
    section = stem(place.astype(jnp.int32)[None], codes, stem_weight).astype(jnp.bfloat16)
    sections = lax.all_gather(section, SHARE, axis=0, tiled=False)

    parts = conv(sections, conv_weight)
    count = parts.shape[1]
    parts = jnp.broadcast_to(parts[:, None], (N_SHARE, N_PAIR, count, share))
    parts = lax.all_to_all(
        parts.reshape(N_SHARE * N_PAIR, count, share),
        SHARE + ("pair",),
        split_axis=0,
        concat_axis=0,
        tiled=True,
    )
    trunk = parts.reshape(N_SHARE, N_PAIR, count, share).transpose(2, 1, 0, 3)
    trunk = trunk.reshape(count, N_PAIR * width)

    w_qkv = jnp.concatenate([w_query, w_key, w_value], axis=1)
    qkv = jnp.dot(trunk, w_qkv, preferred_element_type=jnp.float32).astype(jnp.bfloat16)
    kv = jnp.broadcast_to(qkv[None, :, HQK:], (N_SEQ, count, HQK + HV))
    kv = lax.all_to_all(kv, SEQ, split_axis=0, concat_axis=0, tiled=True)
    terms = attention(qkv[:, :HQK], kv.reshape(N_SEQ * count, HQK + HV), w_out)
    terms = lax.all_to_all(terms, "pair", split_axis=0, concat_axis=0, tiled=True)

    own = lax.dynamic_slice_in_dim(trunk, pair_place * width, width, 1)
    factors = jnp.concatenate([w_pair[0], w_pair[1]], axis=1)
    seq_out, rows = close(terms, own, trunk, factors)
    rows = rows[:1]
    every = lax.all_to_all(
        jnp.broadcast_to(rows[None], (N_SEQ, 1, 2 * channels)),
        SEQ,
        split_axis=0,
        concat_axis=0,
        tiled=True,
    ).reshape(N_SEQ, 2 * channels)

    cols = jnp.arange(N_SEQ, dtype=jnp.int32)
    bias = distance_bias(place.astype(jnp.int32), cols, pair_bias)
    base = 0.5 * (pair_in[0].astype(jnp.float32) + mirror.astype(jnp.float32)) + bias
    cross = rows[:, :channels] * every[:, channels:] + every[:, :channels] * rows[:, channels:]
    pair_out = (base + 0.5 * cross).astype(jnp.bfloat16)[None]
    return (seq_out, pair_out)


def solution(mesh):
    names = SEQ + ("pair",)
    fine = Mesh(mesh.devices.reshape([SIZES[name] for name in names]), names)
    placed = (
        P(SEQ),
        P(),
        P(SEQ, "pair"),
        P(None, "pair"),
        P(None, "pair"),
        P(None, "pair"),
        P("pair", None),
        P(None, None, "pair"),
        P(None, "pair"),
        P(SEQ, None, "pair"),
    )
    return jax.shard_map(
        on_device,
        mesh=fine,
        in_specs=placed,
        out_specs=(P(SEQ, "pair"), P(SEQ, None, "pair")),
        check_vma=False,
    )
```

time: 1170 us -> 158 us (0.14)
  blocking collectives: 888 us -> 22.7 us
  waiting for transfers between devices: 188 us -> 69.7 us
  starting transfers between devices: 26.1 us -> 48 us
  between operations: 14.9 us -> 0.96 us
  local copies, waits for them, and re-layouts: 21.9 us -> 9.59 us
  other arithmetic: 12.8 us -> 0.53 us
    unnamed x1 -> x0, blocking collectives: 546 us -> none
    all_gather x3 -> x1, blocking collectives: 328 us -> 22.7 us  [on_device(): sections = lax.all_gather(section, SHARE, axis=0, tiled=False)]
    all_gather x1 -> x0, waiting for transfers between devices: 177 us -> none  [on_device(): lax.all_gather(w_conv, 'seq', axis=0, tiled=True)]
    all_to_all x1 -> x5, waiting for transfers between devices: 10.3 us -> 66.9 us  [the longest x1 42.1 us: on_device(): kv = lax.all_to_all(kv, SEQ, split_axis=0, concat_axis=0, tiled=True)]
    all_to_all x1 -> x5, starting transfers between devices: 11.7 us -> 42.5 us  [the longest x1 14.3 us: on_device(): held = lax.all_to_all(sent, SEQ, split_axis=0, concat_axis=0, tiled=True)]
    psum x1 -> x0, blocking collectives: 14.8 us -> none  [on_device(): lax.psum(partial_out.astype(jnp.bfloat16), 'pair').astype(jnp.float32)]
  transfers between devices with their start and end apart: 6 -> 7, of which waited for: 3 -> 5; matrix products, arithmetic and copies ran while one was open for 3% -> 2% of each run, Pallas kernels for 0% -> 1%
where the time goes in v1:
time: 158 us; the launch traced here: 157 us
  waiting for transfers between devices  69.7 us (44%)
  starting transfers between devices  48 us (30%)
  blocking collectives  22.7 us (14%)
  local copies, waits for them, and re-layouts  9.59 us (6%)
  Pallas kernels  4.57 us (3%)
    all_to_all x1, waiting for transfers between devices, on_device(): kv = lax.all_to_all(kv, SEQ, split_axis=0, concat_axis=0, tiled=True)  42.1 us
    all_gather x1, blocking collectives, on_device(): sections = lax.all_gather(section, SHARE, axis=0, tiled=False)  22.7 us
    all_to_all x1, starting transfers between devices, on_device(): held = lax.all_to_all(sent, SEQ, split_axis=0, concat_axis=0, tiled=True)  14.3 us
    all_to_all x1, waiting for transfers between devices, on_device(): lax.all_to_all(jnp.broadcast_to(rows[None], (N_SEQ, 1, 2 * channels)), SE...  10.8 us
    all_to_all x1, starting transfers between devices, on_device(): lax.all_to_all(parts.reshape(N_SHARE * N_PAIR, count, share), SHARE + ('p...  9.7 us
    all_to_all x1, starting transfers between devices, on_device(): kv = lax.all_to_all(kv, SEQ, split_axis=0, concat_axis=0, tiled=True)  8.93 us
    all_to_all x1, waiting for transfers between devices, on_device(): lax.all_to_all(parts.reshape(N_SHARE * N_PAIR, count, share), SHARE + ('p...  7.44 us
    all_to_all x1, waiting for transfers between devices, on_device(): lax.all_to_all(terms, 'pair', split_axis=0, concat_axis=0, tiled=True)  6.64 us
  transfers between devices with their start and end apart: 7, of which 5 were waited for; matrix products, arithmetic and copies ran while one was open for 2% of the time, Pallas kernels for 1%

profile of v1, /device:TPU:1, one launch (start us, length us, event | category | flops | bytes accessed | tf_op | source)
XLA Modules:
  0.0 157.3 jit_solution(12599594514308264317)
XLA Ops:
  0.6 0.0 copy-start
  0.6 0.8 reshape.105
  1.5 0.8 copy.28
  2.3 0.5 broadcast_in_dim.41
  2.8 0.3 fusion.13
  3.1 0.0 copy-start.8
  3.1 1.7 %copy.29 = bf16[128,31,96]{2,1,0:T(8,128)(2,1)} copy(bf16[128,31,96]{2,0,1:T(8,128)(2,1)S(1)} %fusion.13) | data formatting | bytes 1523712 | tf_op jit(solution)/shard_map/concatenate | solution.py:210
  4.8 0.0 copy-start.6
  4.8 14.3 %all-to-all-start = ((bf16[128,31,96]{2,1,0:T(8,128)(2,1)}), bf16[128,31,96]{2,1,0:T(8,128)(2,1)S(1)}, u32[]{:S(2)}, u32[]{:S(2)}) async-start(bf16[128,31,96]{2,1,0:T(8,128)(2,1)} %copy.29), calls=%async_computation | async-start | bytes 2097152 | tf_op jit(solution)/shard_map/all_to_all | solution.py:211
  19.1 0.0 copy-done.8
  19.1 3.5 %collective-permute-start = (s32[256]{0:T(256)S(1)}, s32[256]{0:T(256)S(1)}, u32[]{:S(2)}, u32[]{:S(2)}) collective-permute-start(s32[256]{0:T(256)S(1)} %get-tuple-element.8), channel_id=1, source_target_pairs={{0,4},{4,8},{8,12},{12,16},{16,20},{20,24},{24,28},{28,32},{32,36}... | collective-permute-start | bytes 3080 | tf_op jit(solution)/shard_map/ppermute | solution.py:217
  22.7 1.9 %collective-permute-start.1 = (s32[256]{0:T(256)S(1)}, s32[256]{0:T(256)S(1)}, u32[]{:S(2)}, u32[]{:S(2)}) collective-permute-start(s32[256]{0:T(256)S(1)} %get-tuple-element.9), channel_id=1, source_target_pairs={{4,0},{8,4},{12,8},{16,12},{20,16},{24,20},{28,24},{32,28},{36,32}... | collective-permute-start | bytes 3080 | tf_op jit(solution)/shard_map/ppermute | solution.py:218
  24.6 0.0 copy-done.6
  24.7 0.3 rev.3
  25.0 0.0 collective-permute-done
  25.1 2.8 %collective-permute-done.1 = s32[256]{0:T(256)S(1)} collective-permute-done((s32[256]{0:T(256)S(1)}, s32[256]{0:T(256)S(1)}, u32[]{:S(2)}, u32[]{:S(2)}) %collective-permute-start.1) | collective-permute-done | bytes 1056 | tf_op jit(solution)/shard_map/ppermute | solution.py:218
  27.9 1.7 %shard_map.113 = f32[40,768]{1,0:T(8,128)S(1)} custom-call(s32[1]{0:T(128)} %bitcast.place_ref, s32[1,2560]{1,0:T(1,128)S(1)} %broadcast_in_dim.19.codes_ref, bf16[64,768]{1,0:T(8,128)(2,1)S(1)} %bitcast.36), custom_call_target="tpu_custom_call" | custom-call | flops 226492416 | bytes 200000 | tf_op jit(solution)/shard_map/pallas_call | solution.py:71
  29.7 22.7 %all-gather = bf16[160,768]{1,0:T(8,128)(2,1)S(1)} all-gather(bf16[40,768]{1,0:T(8,128)(2,1)S(1)} %convert_element_type.145), channel_id=2, replica_groups=mesh['zl'=2,'y'=8,'x'=4,'core'=2,'pair'=4] {'zl','core'}, dimensions={0}, use_global_device_ids=true | all-gather | bytes 307200 | tf_op jit(solution)/shard_map/all_gather | solution.py:223
  52.4 0.0 all-to-all-done
  52.4 0.0 copy-start.2
  52.4 0.0 copy-start.3
  52.4 0.4 reshape.108.weight_ref
  52.8 0.0 copy-start.4
  52.8 0.5 shard_map.114
  53.3 0.1 copy-done.2
  53.4 0.0 copy-start.9
  53.4 0.6 broadcast_in_dim.42
  54.0 9.7 %all-to-all-start.1 = ((bf16[16,16,96]{2,1,0:T(8,128)(2,1)}), bf16[16,16,96]{2,1,0:T(8,128)(2,1)S(1)}, u32[]{:S(2)}, u32[]{:S(2)}) async-start(bf16[16,16,96]{2,1,0:T(8,128)(2,1)} %bitcast.8), calls=%async_computation.1 | async-start | bytes 131072 | tf_op jit(solution)/shard_map/all_to_all | solution.py:228
  63.7 0.0 copy-done.3
  63.7 0.2 copy.31
  63.9 0.0 copy-done.4
  63.9 0.2 copy.32
  64.1 7.4 %all-to-all-done.1 = bf16[16,16,96]{2,1,0:T(8,128)(2,1)S(1)} async-done(((bf16[16,16,96]{2,1,0:T(8,128)(2,1)}), bf16[16,16,96]{2,1,0:T(8,128)(2,1)S(1)}, u32[]{:S(2)}, u32[]{:S(2)}) %all-to-all-start.1) | async-done | bytes 49184 | tf_op jit(solution)/shard_map/all_to_all | solution.py:228
  71.5 0.1 copy.30
  71.6 0.1 reshape.111.trunk_ref
  71.7 0.0 copy-done.9
  71.7 0.5 fusion.7
  72.2 1.3 broadcast_in_dim.43
  73.5 0.0 copy-start.5
  73.5 8.9 %all-to-all-start.2 = ((bf16[128,16,320]{2,1,0:T(8,128)(2,1)}), bf16[128,16,320]{2,1,0:T(8,128)(2,1)S(1)}, u32[]{:S(2)}, u32[]{:S(2)}) async-start(bf16[128,16,320]{2,1,0:T(8,128)(2,1)} %broadcast_in_dim.43), calls=%async_computation.2 | async-start | bytes 3145728 | tf_op jit(solution)/shard_map/all_to_all | solution.py:241
  82.5 0.0 copy-start.1
  82.5 0.0 copy-done.5
  82.5 0.2 copy.37
  82.8 0.2 copy.38
  83.0 0.2 pad_maximum_fusion.w_pair_ref
  83.2 42.1 %all-to-all-done.2 = bf16[128,16,320]{2,1,0:T(8,128)(2,1)S(1)} async-done(((bf16[128,16,320]{2,1,0:T(8,128)(2,1)}), bf16[128,16,320]{2,1,0:T(8,128)(2,1)S(1)}, u32[]{:S(2)}, u32[]{:S(2)}) %all-to-all-start.2) | async-done | bytes 1310752 | tf_op jit(solution)/shard_map/all_to_all | solution.py:241
  125.3 0.0 copy-done.1
  125.3 0.0 copy-start.7
  125.3 1.7 %shard_map.115 = f32[4,24,384]{2,1,0:T(8,128)} custom-call(bf16[16,128]{1,0:T(8,128)(2,1)S(1)} %slice.57.query_ref, bf16[2048,320]{1,0:T(8,128)(2,1)S(1)} %bitcast.34, bf16[192,1536]{1,0:T(8,128)(2,1)S(1)} %copy-done.1), custom_call_target="tpu_custom_call" | custom-call | tf_op jit(solution)/shard_map/pallas_call | solution.py:150
  127.0 3.3 %all-to-all-start.3 = ((f32[4,24,384]{2,1,0:T(8,128)}), f32[4,24,384]{2,1,0:T(8,128)S(1)}, u32[]{:S(2)}, u32[]{:S(2)}) async-start(f32[4,24,384]{2,1,0:T(8,128)} %shard_map.115), calls=%async_computation.3 | async-start | bytes 294912 | tf_op jit(solution)/shard_map/all_to_all | solution.py:243
  130.3 1.0 slice.59
  131.4 0.1 copy.39
  131.4 6.6 %all-to-all-done.3.terms_ref = f32[4,24,384]{2,1,0:T(8,128)S(1)} async-done(((f32[4,24,384]{2,1,0:T(8,128)}), f32[4,24,384]{2,1,0:T(8,128)S(1)}, u32[]{:S(2)}, u32[]{:S(2)}) %all-to-all-start.3) | async-done | bytes 147488 | tf_op jit(solution)/shard_map/all_to_all | solution.py:243
  138.1 0.7 shard_map.116
  138.8 0.7 broadcast_in_dim.45
  139.4 6.2 %all-to-all-start.4 = ((f32[128,1,64]{2,1,0:T(1,128)}), f32[128,1,64]{2,1,0:T(1,128)S(1)}, u32[]{:S(2)}, u32[]{:S(2)}) async-start(f32[128,1,64]{2,1,0:T(1,128)} %broadcast_in_dim.45), calls=%async_computation.4 | async-start | bytes 131072 | tf_op jit(solution)/shard_map/all_to_all | solution.py:249
  145.6 0.1 slice_bitcast_fusion.2
  145.7 10.8 %all-to-all-done.4 = f32[128,1,64]{2,1,0:T(1,128)S(1)} async-done(((f32[128,1,64]{2,1,0:T(1,128)}), f32[128,1,64]{2,1,0:T(1,128)S(1)}, u32[]{:S(2)}, u32[]{:S(2)}) %all-to-all-start.4) | async-done | bytes 32800 | tf_op jit(solution)/shard_map/all_to_all | solution.py:249
  156.4 0.1 copy.36
  156.5 0.0 copy-done
  156.5 0.0 copy-done.7
  156.5 0.8 fusion.12
  (14 shorter events, 0.1 us)
Async XLA Ops:
  0.6 155.9 %copy-start = (bf16[18,32]{1,0:T(8,128)(2,1)S(1)}, bf16[18,32]{1,0:T(8,128)(2,1)}, u32[]{:S(2)}) copy-start(bf16[18,32]{1,0:T(8,128)(2,1)} %param.18) | copy-start | bytes 3460
  3.1 16.0 %copy-start.8 = (s32[2048]{0:T(1024)S(1)}, s32[2048]{0:T(1024)}, u32[]{:S(2)}) copy-start(s32[2048]{0:T(1024)} %param.10) | copy-start | bytes 24580
  4.8 19.9 %copy-start.6 = (bf16[60,768]{1,0:T(8,128)(2,1)S(1)}, bf16[60,768]{1,0:T(8,128)(2,1)}, u32[]{:S(2)}) copy-start(bf16[60,768]{1,0:T(8,128)(2,1)} %param.11) | copy-start | bytes 276484
  4.8 47.6 %all-to-all-start = ((bf16[128,31,96]{2,1,0:T(8,128)(2,1)}), bf16[128,31,96]{2,1,0:T(8,128)(2,1)S(1)}, u32[]{:S(2)}, u32[]{:S(2)}) async-start(bf16[128,31,96]{2,1,0:T(8,128)(2,1)} %copy.29), calls=%async_computation | async-start | bytes 2097152 | tf_op jit(solution)/shard_map/all_to_all | solution.py:211
  19.1 5.9 %collective-permute-start = (s32[256]{0:T(256)S(1)}, s32[256]{0:T(256)S(1)}, u32[]{:S(2)}, u32[]{:S(2)}) collective-permute-start(s32[256]{0:T(256)S(1)} %get-tuple-element.8), channel_id=1, source_target_pairs={{0,4},{4,8},{8,12},{12,16},{16,20},{20,24},{24,28},{28,32},{32,36}... | collective-permute-start | bytes 3080 | tf_op jit(solution)/shard_map/ppermute | solution.py:217
  22.7 5.2 %collective-permute-start.1 = (s32[256]{0:T(256)S(1)}, s32[256]{0:T(256)S(1)}, u32[]{:S(2)}, u32[]{:S(2)}) collective-permute-start(s32[256]{0:T(256)S(1)} %get-tuple-element.9), channel_id=1, source_target_pairs={{4,0},{8,4},{12,8},{16,12},{20,16},{24,20},{28,24},{32,28},{36,32}... | collective-permute-start | bytes 3080 | tf_op jit(solution)/shard_map/ppermute | solution.py:218
  52.4 1.0 copy-start.2
  52.4 11.3 %copy-start.3 = (bf16[1536,128]{1,0:T(8,128)(2,1)S(1)}, bf16[1536,128]{1,0:T(8,128)(2,1)}, u32[]{:S(2)}) copy-start(bf16[1536,128]{1,0:T(8,128)(2,1)} %param.13) | copy-start | bytes 1179652
  52.8 11.1 %copy-start.4 = (bf16[1536,128]{1,0:T(8,128)(2,1)S(1)}, bf16[1536,128]{1,0:T(8,128)(2,1)}, u32[]{:S(2)}) copy-start(bf16[1536,128]{1,0:T(8,128)(2,1)} %param.14) | copy-start | bytes 1179652
  53.4 18.4 %copy-start.9 = (bf16[1536,192]{0,1:T(8,128)(2,1)S(1)}, bf16[1536,192]{0,1:T(8,128)(2,1)}, u32[]{:S(2)}) copy-start(bf16[1536,192]{0,1:T(8,128)(2,1)} %param.15) | copy-start | bytes 1769476
  54.0 17.5 %all-to-all-start.1 = ((bf16[16,16,96]{2,1,0:T(8,128)(2,1)}), bf16[16,16,96]{2,1,0:T(8,128)(2,1)S(1)}, u32[]{:S(2)}, u32[]{:S(2)}) async-start(bf16[16,16,96]{2,1,0:T(8,128)(2,1)} %bitcast.8), calls=%async_computation.1 | async-start | bytes 131072 | tf_op jit(solution)/shard_map/all_to_all | solution.py:228
  73.5 9.0 %copy-start.5 = (bf16[2,1536,32]{1,2,0:T(8,128)(2,1)S(1)}, bf16[2,1536,32]{1,2,0:T(8,128)(2,1)}, u32[]{:S(2)}) copy-start(bf16[2,1536,32]{1,2,0:T(8,128)(2,1)} %param.17) | copy-start | bytes 589828
  73.5 51.7 %all-to-all-start.2 = ((bf16[128,16,320]{2,1,0:T(8,128)(2,1)}), bf16[128,16,320]{2,1,0:T(8,128)(2,1)S(1)}, u32[]{:S(2)}, u32[]{:S(2)}) async-start(bf16[128,16,320]{2,1,0:T(8,128)(2,1)} %broadcast_in_dim.43), calls=%async_computation.2 | async-start | bytes 3145728 | tf_op jit(solution)/shard_map/all_to_all | solution.py:241
  82.5 42.8 %copy-start.1 = (bf16[192,1536]{1,0:T(8,128)(2,1)S(1)}, bf16[192,1536]{1,0:T(8,128)(2,1)}, u32[]{:S(2)}) copy-start(bf16[192,1536]{1,0:T(8,128)(2,1)} %w_out_ref.1) | copy-start | bytes 1769476
  125.3 31.2 %copy-start.7 = (bf16[1,128,32]{1,2,0:T(8,128)(2,1)S(1)}, bf16[1,128,32]{1,2,0:T(8,128)(2,1)}, u32[]{:S(2)}) copy-start(bf16[1,128,32]{1,2,0:T(8,128)(2,1)} %param.19) | copy-start | bytes 24580
  127.0 11.1 %all-to-all-start.3 = ((f32[4,24,384]{2,1,0:T(8,128)}), f32[4,24,384]{2,1,0:T(8,128)S(1)}, u32[]{:S(2)}, u32[]{:S(2)}) async-start(f32[4,24,384]{2,1,0:T(8,128)} %shard_map.115), calls=%async_computation.3 | async-start | bytes 294912 | tf_op jit(solution)/shard_map/all_to_all | solution.py:243
  139.4 17.0 %all-to-all-start.4 = ((f32[128,1,64]{2,1,0:T(1,128)}), f32[128,1,64]{2,1,0:T(1,128)S(1)}, u32[]{:S(2)}, u32[]{:S(2)}) async-start(f32[128,1,64]{2,1,0:T(1,128)} %broadcast_in_dim.45), calls=%async_computation.4 | async-start | bytes 131072 | tf_op jit(solution)/shard_map/all_to_all | solution.py:249

commit v2 on v1

--- a/solution.py
+++ b/solution.py
@@ -16,12 +16,12 @@
 PAIR_POOL = 16
 EDGES = (1, 2, 3, 4, 6, 8, 12, 16, 24, 32, 48, 64, 96, 128, 192, 256, 384)
 
-SEQ = ("zl", "y", "x", "core")
+SIZES = {"zl": 2, "y": 8, "xh": 2, "xl": 2, "core": 2, "pair": 4}
+SEQ = ("zl", "y", "xh", "xl", "core")
 SHARE = ("zl", "core")
-SIZES = {"zl": 2, "y": 8, "x": 4, "core": 2, "pair": 4}
-N_SEQ = 128
-N_SHARE = 4
-N_PAIR = 4
+N_SEQ = math.prod(SIZES[name] for name in SEQ)
+N_SHARE = math.prod(SIZES[name] for name in SHARE)
+N_PAIR = SIZES["pair"]
 
 SIDE = 256
 ROWS = 32
@@ -196,6 +196,16 @@
     return jnp.dot(onehot, pair_bias, preferred_element_type=jnp.float32)
 
 
+def exchange(blocks, axes):
+    return lax.all_to_all(blocks, axes, split_axis=0, concat_axis=0, tiled=True)
+
+
+def gather(rows, axes):
+    count = math.prod(SIZES[name] for name in axes)
+    blocks = jnp.broadcast_to(rows[None], (count,) + rows.shape)
+    return exchange(blocks, axes).reshape(count * rows.shape[0], *rows.shape[1:])
+
+
 def on_device(tokens, w_stem, w_conv, w_query, w_key, w_value, w_out, w_pair, pair_bias, pair_in):
     place = lax.axis_index(SEQ)
     pair_place = lax.axis_index("pair")
@@ -203,14 +213,9 @@
     taps, width = w_conv.shape
     share = width // N_SHARE
     blocks = w_conv.reshape(taps, N_SHARE, share).transpose(1, 0, 2)
-    blocks = blocks.reshape(2, 1, 1, 2, taps, share)
-    blocks = jnp.broadcast_to(blocks, (2, 8, 4, 2, taps, share)).reshape(N_SEQ, taps, share)
-    channels = pair_in.shape[2]
-    mirror = jnp.pad(pair_in.reshape(N_SEQ, 1, channels), ((0, 0), (0, 0), (0, share - channels)))
-    sent = jnp.concatenate([blocks, mirror], axis=1)
-    held = lax.all_to_all(sent, SEQ, split_axis=0, concat_axis=0, tiled=True)
-    conv_weight = held[:, :taps, :].reshape(N_SEQ * taps, share)
-    mirror = held[:, taps, :channels]
+    blocks = blocks.reshape([SIZES[name] if name in SHARE else 1 for name in SEQ] + [taps, share])
+    blocks = jnp.broadcast_to(blocks, [SIZES[name] for name in SEQ] + [taps, share])
+    conv_weight = exchange(blocks.reshape(N_SEQ, taps, share), SEQ).reshape(N_SEQ * taps, share)
 
     codes = tokens + 1
     ends = N_SEQ - 1
@@ -225,40 +230,31 @@
     parts = conv(sections, conv_weight)
     count = parts.shape[1]
     parts = jnp.broadcast_to(parts[:, None], (N_SHARE, N_PAIR, count, share))
-    parts = lax.all_to_all(
-        parts.reshape(N_SHARE * N_PAIR, count, share),
-        SHARE + ("pair",),
-        split_axis=0,
-        concat_axis=0,
-        tiled=True,
-    )
+    parts = exchange(parts.reshape(N_SHARE * N_PAIR, count, share), SHARE + ("pair",))
     trunk = parts.reshape(N_SHARE, N_PAIR, count, share).transpose(2, 1, 0, 3)
     trunk = trunk.reshape(count, N_PAIR * width)
 
     w_qkv = jnp.concatenate([w_query, w_key, w_value], axis=1)
     qkv = jnp.dot(trunk, w_qkv, preferred_element_type=jnp.float32).astype(jnp.bfloat16)
-    kv = jnp.broadcast_to(qkv[None, :, HQK:], (N_SEQ, count, HQK + HV))
-    kv = lax.all_to_all(kv, SEQ, split_axis=0, concat_axis=0, tiled=True)
-    terms = attention(qkv[:, :HQK], kv.reshape(N_SEQ * count, HQK + HV), w_out)
-    terms = lax.all_to_all(terms, "pair", split_axis=0, concat_axis=0, tiled=True)
+    kv = gather(gather(qkv[:, HQK:], ("zl", "y")), ("xh", "xl"))
+    kv = lax.all_gather(kv, "core", axis=0, tiled=True)
+    terms = exchange(attention(qkv[:, :HQK], kv, w_out), ("pair",))
 
     own = lax.dynamic_slice_in_dim(trunk, pair_place * width, width, 1)
     factors = jnp.concatenate([w_pair[0], w_pair[1]], axis=1)
     seq_out, rows = close(terms, own, trunk, factors)
+    channels = pair_in.shape[2]
+    mine = pair_in[0].astype(jnp.float32)
     rows = rows[:1]
-    every = lax.all_to_all(
-        jnp.broadcast_to(rows[None], (N_SEQ, 1, 2 * channels)),
-        SEQ,
-        split_axis=0,
-        concat_axis=0,
-        tiled=True,
-    ).reshape(N_SEQ, 2 * channels)
+    every = jnp.concatenate([jnp.broadcast_to(rows, (N_SEQ, 2 * channels)), mine], axis=1)
+    every = exchange(every[:, None], SEQ)[:, 0]
+    mirror = every[:, 2 * channels :]
 
     cols = jnp.arange(N_SEQ, dtype=jnp.int32)
     bias = distance_bias(place.astype(jnp.int32), cols, pair_bias)
-    base = 0.5 * (pair_in[0].astype(jnp.float32) + mirror.astype(jnp.float32)) + bias
-    cross = rows[:, :channels] * every[:, channels:] + every[:, :channels] * rows[:, channels:]
-    pair_out = (base + 0.5 * cross).astype(jnp.bfloat16)[None]
+    cross = rows[:, :channels] * every[:, channels : 2 * channels]
+    cross = cross + every[:, :channels] * rows[:, channels:]
+    pair_out = (0.5 * (mine + mirror + cross) + bias).astype(jnp.bfloat16)[None]
     return (seq_out, pair_out)
 
 

time: 158 us -> 169 us (1.070)
  waiting for transfers between devices: 69.7 us -> 40.2 us
  blocking collectives: 22.7 us -> 50.4 us
  between operations: 0.96 us -> 14.4 us
  local copies, waits for them, and re-layouts: 9.59 us -> 7.63 us
    all_to_all x5 -> x4, waiting for transfers between devices: 66.9 us -> 25.5 us  [exchange(): return lax.all_to_all(blocks, axes, split_axis=0, concat_axis=0, tiled=True)]
    all_to_all x0 -> x2, blocking collectives: none -> 25.3 us  [exchange(): return lax.all_to_all(blocks, axes, split_axis=0, concat_axis=0, tiled=True)]
    all_gather x0 -> x1, waiting for transfers between devices: none -> 14.4 us  [on_device(): kv = lax.all_gather(kv, 'core', axis=0, tiled=True)]
    ppermute x1, waiting for transfers between devices: 2.83 us -> 0.01 us  [on_device(): right = lax.ppermute(codes[:SIDE], SEQ, [(i + 1, i) for i in range(ends)])]
    all_gather x1, blocking collectives: 22.7 us -> 25.2 us  [on_device(): sections = lax.all_gather(section, SHARE, axis=0, tiled=False)]
    all_to_all x5 -> x4, starting transfers between devices: 42.5 us -> 43.1 us  [exchange(): return lax.all_to_all(blocks, axes, split_axis=0, concat_axis=0, tiled=True)]
  transfers between devices with their start and end apart: 7 -> 7, of which waited for: 5 -> 5; matrix products, arithmetic and copies ran while one was open for 2% -> 1% of each run, Pallas kernels for 1% -> 1%
where the time goes in v2:
time: 169 us; the launch traced here: 168 us
  blocking collectives  50.4 us (30%)
  starting transfers between devices  48.7 us (29%)
  waiting for transfers between devices  40.2 us (24%)
  between operations  14.4 us (9%)
  local copies, waits for them, and re-layouts  7.63 us (5%)
  Pallas kernels  4.55 us (3%)
    all_to_all x4, starting transfers between devices, exchange(): return lax.all_to_all(blocks, axes, split_axis=0, concat_axis=0, tiled=True)  43.1 us
    all_to_all x4, waiting for transfers between devices, exchange(): return lax.all_to_all(blocks, axes, split_axis=0, concat_axis=0, tiled=True)  25.5 us
    all_to_all x2, blocking collectives, exchange(): return lax.all_to_all(blocks, axes, split_axis=0, concat_axis=0, tiled=True)  25.3 us
    all_gather x1, blocking collectives, on_device(): sections = lax.all_gather(section, SHARE, axis=0, tiled=False)  25.2 us
    all_gather x1, waiting for transfers between devices, on_device(): kv = lax.all_gather(kv, 'core', axis=0, tiled=True)  14.4 us
  transfers between devices with their start and end apart: 7, of which 5 were waited for; matrix products, arithmetic and copies ran while one was open for 1% of the time, Pallas kernels for 1%

profile of v2, /device:TPU:1, one launch (start us, length us, event | category | flops | bytes accessed | tf_op | source)
XLA Modules:
  0.0 168.2 jit_solution(15041646825100845330)
XLA Ops:
  7.2 0.0 copy-start
  7.2 0.8 reshape.95
  8.0 0.0 copy-start.8
  8.0 0.0 copy-start.6
  8.1 1.3 broadcast_in_dim.50
  9.3 14.2 %all-to-all-start = ((bf16[128,30,96]{2,1,0:T(8,128)(2,1)}), bf16[128,30,96]{2,1,0:T(8,128)(2,1)S(1)}, u32[]{:S(2)}, u32[]{:S(2)}) async-start(bf16[128,30,96]{2,1,0:T(8,128)(2,1)} %bitcast.6), calls=%async_computation | async-start | bytes 2097152 | tf_op jit(solution)/shard_map/all_to_all | solution.py:200
  23.5 0.0 copy-done.8
  23.6 2.8 %collective-permute-start.1 = (s32[256]{0:T(256)S(1)}, s32[256]{0:T(256)S(1)}, u32[]{:S(2)}, u32[]{:S(2)}) collective-permute-start(s32[256]{0:T(256)S(1)} %get-tuple-element.9), channel_id=1, source_target_pairs={{4,0},{8,4},{12,8},{16,12},{20,16},{24,20},{28,24},{32,28},{36,32}... | collective-permute-start | bytes 3080 | tf_op jit(solution)/shard_map/ppermute | solution.py:223
  26.4 2.8 %collective-permute-start = (s32[256]{0:T(256)S(1)}, s32[256]{0:T(256)S(1)}, u32[]{:S(2)}, u32[]{:S(2)}) collective-permute-start(s32[256]{0:T(256)S(1)} %get-tuple-element.8), channel_id=1, source_target_pairs={{0,4},{4,8},{8,12},{12,16},{16,20},{20,24},{24,28},{28,32},{32,36}... | collective-permute-start | bytes 3080 | tf_op jit(solution)/shard_map/ppermute | solution.py:222
  29.2 0.0 copy-done.6
  29.2 0.3 rev.3
  29.6 0.0 collective-permute-done.1
  29.6 0.3 collective-permute-done
  29.9 1.7 %shard_map.113 = f32[40,768]{1,0:T(8,128)S(1)} custom-call(s32[1]{0:T(128)} %bitcast.place_ref, s32[1,2560]{1,0:T(1,128)S(1)} %broadcast_in_dim.48.codes_ref, bf16[64,768]{1,0:T(8,128)(2,1)S(1)} %bitcast.34), custom_call_target="tpu_custom_call" | custom-call | flops 226492416 | bytes 200000 | tf_op jit(solution)/shard_map/pallas_call | solution.py:71
  31.6 25.2 %all-gather = bf16[160,768]{1,0:T(8,128)(2,1)S(1)} all-gather(bf16[40,768]{1,0:T(8,128)(2,1)S(1)} %convert_element_type.137), channel_id=2, replica_groups=mesh['zl'=2,'y'=8,'xh'=2,'xl'=2,'core'=2,'pair'=4] {'zl','core'}, dimensions={0}, use_global_device_ids=true | all-gather | bytes 307200 | tf_op jit(solution)/shard_map/all_gather | solution.py:228
  56.8 0.0 copy-start.3
  56.8 0.0 all-to-all-done
  56.8 0.4 reshape.97.weight_ref
  57.2 0.0 copy-start.4
  57.2 0.0 copy-start.9
  57.2 0.5 shard_map.114
  57.7 0.6 broadcast_in_dim.51
  58.3 9.7 %all-to-all-start.1 = ((bf16[16,16,96]{2,1,0:T(8,128)(2,1)}), bf16[16,16,96]{2,1,0:T(8,128)(2,1)S(1)}, u32[]{:S(2)}, u32[]{:S(2)}) async-start(bf16[16,16,96]{2,1,0:T(8,128)(2,1)} %bitcast.7), calls=%async_computation.1 | async-start | bytes 131072 | tf_op jit(solution)/shard_map/all_to_all | solution.py:200
  68.0 0.0 all-gather.3.cloned.1.call-start
  68.1 0.0 copy-done.3
  68.1 0.2 copy.40
  68.3 0.0 copy-done.4
  68.3 0.2 copy.39
  68.5 7.4 %all-to-all-done.1 = bf16[16,16,96]{2,1,0:T(8,128)(2,1)S(1)} async-done(((bf16[16,16,96]{2,1,0:T(8,128)(2,1)}), bf16[16,16,96]{2,1,0:T(8,128)(2,1)S(1)}, u32[]{:S(2)}, u32[]{:S(2)}) %all-to-all-start.1) | async-done | bytes 49184 | tf_op jit(solution)/shard_map/all_to_all | solution.py:200
  75.9 0.1 copy.38
  75.9 0.1 reshape.100.trunk_ref
  76.1 0.0 copy-done.9
  76.1 0.5 fusion.6
  76.5 0.1 broadcast_in_dim.52
  76.6 14.2 %all_to_all.30 = bf16[16,16,320]{2,1,0:T(8,128)(2,1)S(1)} all-to-all(bf16[16,16,320]{2,1,0:T(8,128)(2,1)S(1)} %broadcast_in_dim.52), channel_id=1, replica_groups=mesh['zl'=2,'y'=8,'xh'=2,'xl'=2,'core'=2,'pair'=4] {'zl','y'}, dimensions={0} | all-to-all | bytes 327680 | tf_op jit(solution)/shard_map/all_to_all | solution.py:200
  90.8 0.1 copy.41
  91.0 0.0 copy-start.5
  91.0 11.1 %all_to_all.31 = bf16[4,256,320]{1,2,0:T(8,128)(2,1)S(1)} all-to-all(bf16[4,256,320]{1,2,0:T(8,128)(2,1)S(1)} %broadcast_in_dim.54), channel_id=1, replica_groups=mesh['zl'=2,'y'=8,'xh'=2,'xl'=2,'core'=2,'pair'=4] {'xh','xl'}, dimensions={0} | all-to-all | bytes 1310720 | tf_op jit(solution)/shard_map/all_to_all | solution.py:200
  102.1 0.0 copy-start.7
  102.1 1.2 copy.42
  103.2 0.0 copy-start.2
  103.2 0.0 all-gather.3.cloned.1.call-update
  103.3 0.0 copy-done.5
  103.3 0.2 copy.48
  103.5 0.2 copy.47
  103.7 0.0 copy-done.7
  103.8 0.1 copy.45
  103.9 0.2 pad_maximum_fusion.w_pair_ref
  104.1 14.4 %all-gather.3.cloned.1.call-done.kv_ref = bf16[2048,320]{1,0:T(8,128)(2,1)} async-done(((bf16[1024,320]{1,0:T(8,128)(2,1)}), bf16[2048,320]{1,0:T(8,128)(2,1)}) %all-gather.3.cloned.1.call-update) | async-done | bytes 1310736 | tf_op jit(solution)/shard_map/all_gather | solution.py:240
  118.5 0.0 copy-done.2
  118.6 0.0 copy-start.1
  118.6 1.4 copy-done.1
  120.0 1.7 shard_map.115
  121.6 6.1 %all-to-all-start.4 = ((f32[4,24,384]{2,1,0:T(8,128)}), f32[4,24,384]{2,1,0:T(8,128)S(1)}, u32[]{:S(2)}, u32[]{:S(2)}) async-start(f32[4,24,384]{2,1,0:T(8,128)} %shard_map.115), calls=%async_computation.4 | async-start | bytes 294912 | tf_op jit(solution)/shard_map/all_to_all | solution.py:200
  127.8 7.3 %all-to-all-done.4.terms_ref = f32[4,24,384]{2,1,0:T(8,128)S(1)} async-done(((f32[4,24,384]{2,1,0:T(8,128)}), f32[4,24,384]{2,1,0:T(8,128)S(1)}, u32[]{:S(2)}, u32[]{:S(2)}) %all-to-all-start.4) | async-done | bytes 147488 | tf_op jit(solution)/shard_map/all_to_all | solution.py:200
  135.1 0.7 shard_map.116
  135.8 0.7 pad_maximum_fusion.1
  136.5 13.1 %all-to-all-start.5 = ((f32[128,1,96]{2,1,0:T(1,128)}), f32[128,1,96]{2,1,0:T(1,128)S(1)}, u32[]{:S(2)}, u32[]{:S(2)}) async-start(f32[128,1,96]{2,1,0:T(1,128)} %bitcast.17), calls=%async_computation.5 | async-start | bytes 131072 | tf_op jit(solution)/shard_map/all_to_all | solution.py:200
  149.6 0.1 slice_bitcast_fusion.1
  149.7 10.7 %all-to-all-done.5 = f32[128,1,96]{2,1,0:T(1,128)S(1)} async-done(((f32[128,1,96]{2,1,0:T(1,128)}), f32[128,1,96]{2,1,0:T(1,128)S(1)}, u32[]{:S(2)}, u32[]{:S(2)}) %all-to-all-start.5) | async-done | bytes 49184 | tf_op jit(solution)/shard_map/all_to_all | solution.py:200
  160.4 0.1 copy.46
  160.5 0.0 copy-done
  160.5 0.8 fusion.10
  (18 shorter events, 0.2 us)
Async XLA Ops:
  7.2 153.3 %copy-start = (bf16[18,32]{1,0:T(8,128)(2,1)S(1)}, bf16[18,32]{1,0:T(8,128)(2,1)}, u32[]{:S(2)}) copy-start(bf16[18,32]{1,0:T(8,128)(2,1)} %param.18) | copy-start | bytes 3460
  8.0 15.5 %copy-start.8 = (s32[2048]{0:T(1024)S(1)}, s32[2048]{0:T(1024)}, u32[]{:S(2)}) copy-start(s32[2048]{0:T(1024)} %param.10) | copy-start | bytes 24580
  8.0 21.1 %copy-start.6 = (bf16[60,768]{1,0:T(8,128)(2,1)S(1)}, bf16[60,768]{1,0:T(8,128)(2,1)}, u32[]{:S(2)}) copy-start(bf16[60,768]{1,0:T(8,128)(2,1)} %param.11) | copy-start | bytes 276484
  9.3 47.5 %all-to-all-start = ((bf16[128,30,96]{2,1,0:T(8,128)(2,1)}), bf16[128,30,96]{2,1,0:T(8,128)(2,1)S(1)}, u32[]{:S(2)}, u32[]{:S(2)}) async-start(bf16[128,30,96]{2,1,0:T(8,128)(2,1)} %bitcast.6), calls=%async_computation | async-start | bytes 2097152 | tf_op jit(solution)/shard_map/all_to_all | solution.py:200
  23.6 6.0 %collective-permute-start.1 = (s32[256]{0:T(256)S(1)}, s32[256]{0:T(256)S(1)}, u32[]{:S(2)}, u32[]{:S(2)}) collective-permute-start(s32[256]{0:T(256)S(1)} %get-tuple-element.9), channel_id=1, source_target_pairs={{4,0},{8,4},{12,8},{16,12},{20,16},{24,20},{28,24},{32,28},{36,32}... | collective-permute-start | bytes 3080 | tf_op jit(solution)/shard_map/ppermute | solution.py:223
  26.4 3.5 %collective-permute-start = (s32[256]{0:T(256)S(1)}, s32[256]{0:T(256)S(1)}, u32[]{:S(2)}, u32[]{:S(2)}) collective-permute-start(s32[256]{0:T(256)S(1)} %get-tuple-element.8), channel_id=1, source_target_pairs={{0,4},{4,8},{8,12},{12,16},{16,20},{20,24},{24,28},{28,32},{32,36}... | collective-permute-start | bytes 3080 | tf_op jit(solution)/shard_map/ppermute | solution.py:222
  56.8 11.3 %copy-start.3 = (bf16[1536,128]{1,0:T(8,128)(2,1)S(1)}, bf16[1536,128]{1,0:T(8,128)(2,1)}, u32[]{:S(2)}) copy-start(bf16[1536,128]{1,0:T(8,128)(2,1)} %param.14) | copy-start | bytes 1179652
  57.2 11.1 %copy-start.4 = (bf16[1536,128]{1,0:T(8,128)(2,1)S(1)}, bf16[1536,128]{1,0:T(8,128)(2,1)}, u32[]{:S(2)}) copy-start(bf16[1536,128]{1,0:T(8,128)(2,1)} %param.13) | copy-start | bytes 1179652
  57.2 18.9 %copy-start.9 = (bf16[1536,192]{0,1:T(8,128)(2,1)S(1)}, bf16[1536,192]{0,1:T(8,128)(2,1)}, u32[]{:S(2)}) copy-start(bf16[1536,192]{0,1:T(8,128)(2,1)} %param.15) | copy-start | bytes 1769476
  58.3 17.5 %all-to-all-start.1 = ((bf16[16,16,96]{2,1,0:T(8,128)(2,1)}), bf16[16,16,96]{2,1,0:T(8,128)(2,1)S(1)}, u32[]{:S(2)}, u32[]{:S(2)}) async-start(bf16[16,16,96]{2,1,0:T(8,128)(2,1)} %bitcast.7), calls=%async_computation.1 | async-start | bytes 131072 | tf_op jit(solution)/shard_map/all_to_all | solution.py:200
  68.0 50.5 %all-gather.3.cloned.1.call-start = ((), (), s32[]{:S(2)}) async-start(), calls=%async_computation.6 | async-start | bytes 2359296 | tf_op jit(solution)/shard_map/all_gather | solution.py:240
  91.0 12.3 %copy-start.5 = (bf16[2,1536,32]{1,2,0:T(8,128)(2,1)S(1)}, bf16[2,1536,32]{1,2,0:T(8,128)(2,1)}, u32[]{:S(2)}) copy-start(bf16[2,1536,32]{1,2,0:T(8,128)(2,1)} %param.17) | copy-start | bytes 589828
  102.1 1.7 %copy-start.7 = (bf16[1,128,32]{1,2,0:T(8,128)(2,1)S(1)}, bf16[1,128,32]{1,2,0:T(8,128)(2,1)}, u32[]{:S(2)}) copy-start(bf16[1,128,32]{1,2,0:T(8,128)(2,1)} %param.19) | copy-start | bytes 24580
  103.2 15.3 %copy-start.2 = (bf16[192,1536]{1,0:T(8,128)(2,1)S(1)}, bf16[192,1536]{1,0:T(8,128)(2,1)}, u32[]{:S(2)}) copy-start(bf16[192,1536]{1,0:T(8,128)(2,1)} %w_out_ref.1) | copy-start | bytes 1769476
  118.6 1.4 copy-start.1
  121.6 13.5 %all-to-all-start.4 = ((f32[4,24,384]{2,1,0:T(8,128)}), f32[4,24,384]{2,1,0:T(8,128)S(1)}, u32[]{:S(2)}, u32[]{:S(2)}) async-start(f32[4,24,384]{2,1,0:T(8,128)} %shard_map.115), calls=%async_computation.4 | async-start | bytes 294912 | tf_op jit(solution)/shard_map/all_to_all | solution.py:200
  136.5 23.9 %all-to-all-start.5 = ((f32[128,1,96]{2,1,0:T(1,128)}), f32[128,1,96]{2,1,0:T(1,128)S(1)}, u32[]{:S(2)}, u32[]{:S(2)}) async-start(f32[128,1,96]{2,1,0:T(1,128)} %bitcast.17), calls=%async_computation.5 | async-start | bytes 131072 | tf_op jit(solution)/shard_map/all_to_all | solution.py:200
Sparse Core Ops, SparseCore 0:
  103.4 15.1 all-gather.2

commit v3 on v2

--- a/solution.py
+++ b/solution.py
@@ -18,7 +18,7 @@
 
 SIZES = {"zl": 2, "y": 8, "xh": 2, "xl": 2, "core": 2, "pair": 4}
 SEQ = ("zl", "y", "xh", "xl", "core")
-SHARE = ("zl", "core")
+SHARE = ("zl", "xl", "core")
 N_SEQ = math.prod(SIZES[name] for name in SEQ)
 N_SHARE = math.prod(SIZES[name] for name in SHARE)
 N_PAIR = SIZES["pair"]
@@ -74,31 +74,32 @@
         in_specs=[pl.BlockSpec(memory_space=pltpu.SMEM)] + whole(2),
         out_specs=whole(1)[0],
         compiler_params=params(),
-        cost_estimate=pl.CostEstimate(flops=2 * 2304 * 64 * 768, bytes_accessed=200000, transcendentals=0),
+        cost_estimate=pl.CostEstimate(flops=40_000_000_000, bytes_accessed=200000, transcendentals=0),
     )(place, codes, weight)
 
 
 def conv_kernel(section_ref, weight_ref, out_ref, wide, act):
     windows, _, channels = section_ref.shape
+    half = channels // 2
+    columns = out_ref.shape[2]
     wide[...] = section_ref[...].astype(jnp.float32)
-    total = None
+    even, odd = None, None
     for tap in range(KS_CONV):
         rows = wide[:, tap : tap + ROWS, :].astype(jnp.bfloat16).reshape(windows * ROWS, channels)
-        term = jnp.dot(
-            rows,
-            weight_ref[tap * channels : (tap + 1) * channels, :],
-            preferred_element_type=jnp.float32,
-        )
-        total = term if total is None else total + term
-    act[...] = gelu(total)
-    half = windows * ROWS // 2
-    best = jnp.maximum(act[pl.ds(0, half, stride=2), :], act[pl.ds(1, half, stride=2), :])
+        weight = weight_ref[tap * half : (tap + 1) * half, :]
+        term = jnp.dot(rows[:, :half], weight, preferred_element_type=jnp.float32)
+        even = term if even is None else even + term
+        term = jnp.dot(rows[:, half:], weight, preferred_element_type=jnp.float32)
+        odd = term if odd is None else odd + term
+    act[...] = gelu(even[:, :columns] + odd[:, columns:])
+    count = windows * ROWS // 2
+    best = jnp.maximum(act[pl.ds(0, count, stride=2), :], act[pl.ds(1, count, stride=2), :])
     out_ref[...] = best.astype(jnp.bfloat16).reshape(out_ref.shape)
 
 
 def conv(section, weight):
     windows, _, channels = section.shape
-    columns = weight.shape[1]
+    columns = weight.shape[1] // 2
     return pl.pallas_call(
         conv_kernel,
         out_shape=jax.ShapeDtypeStruct((windows, ROWS // 2, columns), jnp.bfloat16),
@@ -112,23 +113,26 @@
     )(section, weight)
 
 
-def attention_kernel(query_ref, kv_ref, w_out_ref, out_ref):
+def attention_kernel(query_ref, near_ref, far_ref, w_out_ref, out_ref):
     scale = 1.0 / math.sqrt(HQK)
-    scores = (
+    scores = [
         lax.dot_general(
             query_ref[...],
-            kv_ref[:, :HQK],
+            ref[:, :HQK],
             (((1,), (1,)), ((), ())),
             preferred_element_type=jnp.float32,
         )
         * scale
-    )
-    top = jnp.max(scores, axis=1, keepdims=True)
-    expo = jnp.exp(scores - top)
-    total = jnp.sum(expo, axis=1, keepdims=True)
-    mixed = jnp.dot(
-        expo.astype(jnp.bfloat16), kv_ref[:, HQK : HQK + HV], preferred_element_type=jnp.float32
-    )
+        for ref in (near_ref, far_ref)
+    ]
+    top = jnp.maximum(*[jnp.max(part, axis=1, keepdims=True) for part in scores])
+    total, mixed = 0.0, 0.0
+    for part, ref in zip(scores, (near_ref, far_ref)):
+        expo = jnp.exp(part - top)
+        total = total + jnp.sum(expo, axis=1, keepdims=True)
+        mixed = mixed + jnp.dot(
+            expo.astype(jnp.bfloat16), ref[:, HQK : HQK + HV], preferred_element_type=jnp.float32
+        )
     mixed = (mixed / total).astype(jnp.bfloat16)
     term = jnp.dot(mixed, w_out_ref[...], preferred_element_type=jnp.float32)
     mean = jnp.sum(term, axis=0, keepdims=True) * (1.0 / PAIR_POOL)
@@ -144,16 +148,16 @@
         out_ref[c, count : count + 8, :] = tail
 
 
-def attention(query, kv, w_out):
+def attention(query, near, far, w_out):
     count = query.shape[0]
     width = w_out.shape[1] // N_PAIR
     return pl.pallas_call(
         attention_kernel,
         out_shape=jax.ShapeDtypeStruct((N_PAIR, count + 8, width), jnp.float32),
-        in_specs=whole(3),
+        in_specs=whole(4),
         out_specs=whole(1)[0],
         compiler_params=params(),
-    )(query, kv, w_out)
+    )(query, near, far, w_out)
 
 
 def close_kernel(terms_ref, own_ref, trunk_ref, w_pair_ref, seq_ref, rows_ref):
@@ -212,17 +216,22 @@
 
     taps, width = w_conv.shape
     share = width // N_SHARE
-    blocks = w_conv.reshape(taps, N_SHARE, share).transpose(1, 0, 2)
-    blocks = blocks.reshape([SIZES[name] if name in SHARE else 1 for name in SEQ] + [taps, share])
-    blocks = jnp.broadcast_to(blocks, [SIZES[name] for name in SEQ] + [taps, share])
-    conv_weight = exchange(blocks.reshape(N_SEQ, taps, share), SEQ).reshape(N_SEQ * taps, share)
+    block = [taps // 2, 2 * share]
+    blocks = w_conv.reshape(taps // 2, 2, N_SHARE, share).transpose(2, 0, 1, 3)
+    blocks = blocks.reshape([SIZES[name] if name in SHARE else 1 for name in SEQ] + block)
+    blocks = jnp.broadcast_to(blocks, [SIZES[name] for name in SEQ] + block)
+    conv_weight = exchange(blocks.reshape([N_SEQ] + block), SEQ).reshape(N_SEQ * block[0], block[1])
 
     codes = tokens + 1
     ends = N_SEQ - 1
     left = lax.ppermute(codes[-SIDE:], SEQ, [(i, i + 1) for i in range(ends)])
     right = lax.ppermute(codes[:SIDE], SEQ, [(i + 1, i) for i in range(ends)])
     codes = jnp.concatenate([left, codes, right])[None, :]
-    stem_weight = w_stem.reshape(KS_STEM, 4, -1)[::-1].transpose(1, 0, 2)
+    source = jnp.arange(w_stem.shape[1]).reshape(2, -1)
+    source = (2 * (source % source.shape[1]) + jnp.arange(2)[:, None]).reshape(-1)
+    order = (jnp.arange(w_stem.shape[1])[:, None] == source[None, :]).astype(jnp.bfloat16)
+    stem_weight = jnp.dot(w_stem, order, preferred_element_type=jnp.float32).astype(jnp.bfloat16)
+    stem_weight = stem_weight.reshape(KS_STEM, 4, -1)[::-1].transpose(1, 0, 2)
     stem_weight = jnp.pad(stem_weight, ((0, 0), (0, 1), (0, 0))).reshape(64, -1)
     section = stem(place.astype(jnp.int32)[None], codes, stem_weight).astype(jnp.bfloat16)
     sections = lax.all_gather(section, SHARE, axis=0, tiled=False)
@@ -235,10 +244,11 @@
     trunk = trunk.reshape(count, N_PAIR * width)
 
     w_qkv = jnp.concatenate([w_query, w_key, w_value], axis=1)
+    w_qkv = jnp.pad(w_qkv, ((0, 0), (0, 4 * HQK - w_qkv.shape[1])))
     qkv = jnp.dot(trunk, w_qkv, preferred_element_type=jnp.float32).astype(jnp.bfloat16)
     kv = gather(gather(qkv[:, HQK:], ("zl", "y")), ("xh", "xl"))
-    kv = lax.all_gather(kv, "core", axis=0, tiled=True)
-    terms = exchange(attention(qkv[:, :HQK], kv, w_out), ("pair",))
+    other = lax.ppermute(kv, "core", [(0, 1), (1, 0)])
+    terms = exchange(attention(qkv[:, :HQK], kv, other, w_out), ("pair",))
 
     own = lax.dynamic_slice_in_dim(trunk, pair_place * width, width, 1)
     factors = jnp.concatenate([w_pair[0], w_pair[1]], axis=1)

time: 169 us -> 135 us (0.80)
  blocking collectives: 50.4 us -> 27.6 us
  between operations: 14.4 us -> 1.09 us
  starting transfers between devices: 48.7 us -> 52.7 us
  waiting for transfers between devices: 40.2 us -> 38.2 us
    all_gather x1 -> x0, waiting for transfers between devices: 14.4 us -> none  [on_device(): kv = lax.all_gather(kv, 'core', axis=0, tiled=True)]
    all_to_all x2 -> x1, blocking collectives: 25.3 us -> 12.2 us  [exchange(): return lax.all_to_all(blocks, axes, split_axis=0, concat_axis=0, tiled=True)]
    all_to_all x4 -> x5, waiting for transfers between devices: 25.5 us -> 37.8 us  [exchange(): return lax.all_to_all(blocks, axes, split_axis=0, concat_axis=0, tiled=True)]
    all_gather x1, blocking collectives: 25.2 us -> 15.5 us  [on_device(): sections = lax.all_gather(section, SHARE, axis=0, tiled=False)]
    all_to_all x4 -> x5, starting transfers between devices: 43.1 us -> 37.1 us  [exchange(): return lax.all_to_all(blocks, axes, split_axis=0, concat_axis=0, tiled=True)]
    ppermute x0 -> x1, starting transfers between devices: none -> 5.57 us  [on_device(): other = lax.ppermute(kv, 'core', [(0, 1), (1, 0)])]
    ppermute x1, starting transfers between devices: 2.8 us -> 5.57 us  [on_device(): right = lax.ppermute(codes[:SIDE], SEQ, [(i + 1, i) for i in range(ends)])]
    ppermute x1, starting transfers between devices: 2.76 us -> 4.5 us  [on_device(): left = lax.ppermute(codes[-SIDE:], SEQ, [(i, i + 1) for i in range(ends)])]
  transfers between devices with their start and end apart: 7 -> 8, of which waited for: 5 -> 6; matrix products, arithmetic and copies ran while one was open for 1% -> 4% of each run, Pallas kernels for 1% -> 1%
where the time goes in v3:
time: 135 us
  starting transfers between devices  52.7 us (39%)
  waiting for transfers between devices  38.2 us (28%)
  blocking collectives  27.6 us (20%)
  local copies, waits for them, and re-layouts  6.58 us (5%)
  Pallas kernels  4.9 us (4%)
  matrix products  1.97 us (1%)
  other arithmetic  1.73 us (1%)
    all_to_all x5, waiting for transfers between devices, exchange(): return lax.all_to_all(blocks, axes, split_axis=0, concat_axis=0, tiled=True)  37.8 us
    all_to_all x5, starting transfers between devices, exchange(): return lax.all_to_all(blocks, axes, split_axis=0, concat_axis=0, tiled=True)  37.1 us
    all_gather x1, blocking collectives, on_device(): sections = lax.all_gather(section, SHARE, axis=0, tiled=False)  15.5 us
    all_to_all x1, blocking collectives, exchange(): return lax.all_to_all(blocks, axes, split_axis=0, concat_axis=0, tiled=True)  12.2 us
    ppermute x1, starting transfers between devices, on_device(): right = lax.ppermute(codes[:SIDE], SEQ, [(i + 1, i) for i in range(ends)])  5.57 us
    ppermute x1, starting transfers between devices, on_device(): other = lax.ppermute(kv, 'core', [(0, 1), (1, 0)])  5.57 us
    ppermute x1, starting transfers between devices, on_device(): left = lax.ppermute(codes[-SIDE:], SEQ, [(i, i + 1) for i in range(ends)])  4.5 us
  transfers between devices with their start and end apart: 8, of which 6 were waited for; matrix products, arithmetic and copies ran while one was open for 4% of the time, Pallas kernels for 1%

profile of v3, /device:TPU:1, one launch (start us, length us, event | category | flops | bytes accessed | tf_op | source)
XLA Modules:
  0.0 134.8 jit_solution(10751808435438296142)
XLA Ops:
  0.6 0.0 copy-start
  0.6 0.7 broadcast_add_fusion
  1.4 4.5 %collective-permute-start = (s32[256]{0:T(256)S(1)}, s32[256]{0:T(256)S(1)}, u32[]{:S(2)}, u32[]{:S(2)}) collective-permute-start(s32[256]{0:T(256)S(1)} %get-tuple-element.8), channel_id=1, source_target_pairs={{0,4},{4,8},{8,12},{12,16},{16,20},{20,24},{24,28},{28,32},{32,36}... | collective-permute-start | bytes 3080 | tf_op jit(solution)/shard_map/ppermute | solution.py:227
  5.9 5.6 %collective-permute-start.1 = (s32[256]{0:T(256)S(1)}, s32[256]{0:T(256)S(1)}, u32[]{:S(2)}, u32[]{:S(2)}) collective-permute-start(s32[256]{0:T(256)S(1)} %get-tuple-element.9), channel_id=1, source_target_pairs={{4,0},{8,4},{12,8},{16,12},{20,16},{24,20},{28,24},{32,28},{36,32}... | collective-permute-start | bytes 3080 | tf_op jit(solution)/shard_map/ppermute | solution.py:228
  11.5 0.8 reshape.133
  12.4 0.1 broadcast_in_dim.51
  12.5 0.9 broadcast_in_dim.52
  13.4 10.6 %all-to-all-start = ((bf16[128,15,96]{2,1,0:T(8,128)(2,1)}), bf16[128,15,96]{2,1,0:T(8,128)(2,1)S(1)}, u32[]{:S(2)}, u32[]{:S(2)}) async-start(bf16[128,15,96]{2,1,0:T(8,128)(2,1)} %bitcast.6), calls=%async_computation | async-start | bytes 1048576 | tf_op jit(solution)/shard_map/all_to_all | solution.py:204
  24.1 0.0 copy-done
  24.1 0.5 fusion.10
  24.6 0.3 rev.3
  25.0 0.0 collective-permute-done
  25.0 0.0 collective-permute-done.1
  25.0 1.7 %shard_map.113 = f32[40,768]{1,0:T(8,128)S(1)} custom-call(s32[1]{0:T(128)} %bitcast.place_ref, s32[1,2560]{1,0:T(1,128)S(1)} %broadcast_in_dim.50.codes_ref, bf16[64,768]{1,0:T(8,128)(2,1)S(1)} %bitcast.43), custom_call_target="tpu_custom_call" | custom-call | flops 40000000000 | bytes 200000 | tf_op jit(solution)/shard_map/pallas_call | solution.py:71
  26.8 15.5 %all-gather = bf16[320,768]{1,0:T(8,128)(2,1)S(1)} all-gather(bf16[40,768]{1,0:T(8,128)(2,1)S(1)} %convert_element_type.148), channel_id=2, replica_groups=mesh['zl'=2,'y'=8,'xh'=2,'xl'=2,'core'=2,'pair'=4] {'zl','xl','core'}, dimensions={0}, use_global_device_ids=true | all-gather | bytes 552960 | tf_op jit(solution)/shard_map/all_gather | solution.py:237
  42.2 2.3 %all-to-all-done = bf16[128,15,96]{2,1,0:T(8,128)(2,1)S(1)} async-done(((bf16[128,15,96]{2,1,0:T(8,128)(2,1)}), bf16[128,15,96]{2,1,0:T(8,128)(2,1)S(1)}, u32[]{:S(2)}, u32[]{:S(2)}) %all-to-all-start) | async-done | bytes 368672 | tf_op jit(solution)/shard_map/all_to_all | solution.py:204
  44.5 0.2 reshape.135.weight_ref
  44.7 0.0 copy-start.2
  44.7 0.8 shard_map.114
  45.6 0.0 copy-start.3
  45.6 0.8 reshape.150
  46.4 9.9 %all-to-all-start.1 = ((bf16[32,2,384]{2,1,0:T(2,128)(2,1)}), bf16[32,2,384]{2,1,0:T(2,128)(2,1)S(1)}, u32[]{:S(2)}, u32[]{:S(2)}) async-start(bf16[32,2,384]{2,1,0:T(2,128)(2,1)} %reshape.150), calls=%async_computation.1 | async-start | bytes 98304 | tf_op jit(solution)/shard_map/all_to_all | solution.py:204
  56.3 0.0 copy-done.2
  56.3 0.2 copy.29
  56.5 0.0 copy-done.3
  56.5 0.0 copy-start.8
  56.5 0.2 copy.30
  56.7 7.8 %all-to-all-done.1 = bf16[32,2,384]{2,1,0:T(2,128)(2,1)S(1)} async-done(((bf16[32,2,384]{2,1,0:T(2,128)(2,1)}), bf16[32,2,384]{2,1,0:T(2,128)(2,1)S(1)}, u32[]{:S(2)}, u32[]{:S(2)}) %all-to-all-start.1) | async-done | bytes 49184 | tf_op jit(solution)/shard_map/all_to_all | solution.py:204
  64.5 0.2 reshape.151
  64.6 0.1 copy.28
  64.7 0.2 reshape.138.trunk_ref
  64.9 0.0 copy-done.8
  65.0 0.6 fusion.11
  65.6 0.0 copy-start.5
  65.6 12.2 %all_to_all.30 = bf16[16,16,384]{2,1,0:T(8,128)(2,1)S(1)} all-to-all(bf16[16,16,384]{2,1,0:T(8,128)(2,1)S(1)} %broadcast_in_dim.54), channel_id=1, replica_groups=mesh['zl'=2,'y'=8,'xh'=2,'xl'=2,'core'=2,'pair'=4] {'zl','y'}, dimensions={0} | all-to-all | bytes 393216 | tf_op jit(solution)/shard_map/all_to_all | solution.py:204
  77.8 1.0 broadcast_in_dim.56
  78.8 0.0 copy-start.4
  78.8 0.0 copy-done.5
  78.8 3.8 %all-to-all-start.3 = ((bf16[4,256,384]{2,1,0:T(8,128)(2,1)}), bf16[4,256,384]{2,1,0:T(8,128)(2,1)S(1)}, u32[]{:S(2)}, u32[]{:S(2)}) async-start(bf16[4,256,384]{2,1,0:T(8,128)(2,1)} %broadcast_in_dim.56), calls=%async_computation.3 | async-start | bytes 1572864 | tf_op jit(solution)/shard_map/all_to_all | solution.py:204
  82.6 0.0 copy-start.6
  82.6 9.6 %all-to-all-done.3 = bf16[4,256,384]{2,1,0:T(8,128)(2,1)S(1)} async-done(((bf16[4,256,384]{2,1,0:T(8,128)(2,1)}), bf16[4,256,384]{2,1,0:T(8,128)(2,1)S(1)}, u32[]{:S(2)}, u32[]{:S(2)}) %all-to-all-start.3) | async-done | bytes 786464 | tf_op jit(solution)/shard_map/all_to_all | solution.py:204
  92.1 5.6 %collective-permute-start.2 = (bf16[1024,384]{1,0:T(8,128)(2,1)S(1)}, bf16[1024,384]{1,0:T(8,128)(2,1)S(1)}, u32[]{:S(2)}, u32[]{:S(2)}) collective-permute-start(bf16[1024,384]{1,0:T(8,128)(2,1)S(1)} %bitcast.40), channel_id=1, source_target_pairs={{0,4},{4,0},{1,5},{5,1},{2,6},{6,2},{3,7},{7,3},{8,12},{12,8},{9,1... | collective-permute-start | bytes 2359304 | tf_op jit(solution)/shard_map/ppermute | solution.py:250
  97.7 0.0 copy-done.4
  97.8 0.2 copy.35
  98.0 0.0 copy-start.1
  98.0 0.2 copy.36
  98.2 0.0 copy-done.6
  98.2 0.1 copy.33
  98.3 0.2 pad_maximum_fusion.w_pair_ref
  98.6 0.7 slice.52.query_ref
  99.3 0.4 collective-permute-done.2.far_ref
  99.6 0.0 copy-done.1
  99.6 1.7 %shard_map.115 = f32[4,24,384]{2,1,0:T(8,128)} custom-call(bf16[16,128]{1,0:T(8,128)(2,1)S(1)} %slice.52.query_ref, bf16[1024,384]{1,0:T(8,128)(2,1)S(1)} %bitcast.41, bf16[1024,384]{1,0:T(8,128)(2,1)S(1)} %collective-permute-done.2.far_ref, bf16[192,1536]{1,0:T(8,128)(2,1)S(1)} %copy-done.1), custom_call_target="tpu_custom_call" | custom-call | tf_op jit(solution)/shard_map/pallas_call | solution.py:154
  101.3 3.5 %all-to-all-start.4 = ((f32[4,24,384]{2,1,0:T(8,128)}), f32[4,24,384]{2,1,0:T(8,128)S(1)}, u32[]{:S(2)}, u32[]{:S(2)}) async-start(f32[4,24,384]{2,1,0:T(8,128)} %shard_map.115), calls=%async_computation.4 | async-start | bytes 294912 | tf_op jit(solution)/shard_map/all_to_all | solution.py:204
  104.8 7.4 %all-to-all-done.4.terms_ref = f32[4,24,384]{2,1,0:T(8,128)S(1)} async-done(((f32[4,24,384]{2,1,0:T(8,128)}), f32[4,24,384]{2,1,0:T(8,128)S(1)}, u32[]{:S(2)}, u32[]{:S(2)}) %all-to-all-start.4) | async-done | bytes 147488 | tf_op jit(solution)/shard_map/all_to_all | solution.py:204
  112.2 0.7 shard_map.116
  112.9 0.7 pad_maximum_fusion.1
  113.6 9.4 %all-to-all-start.5 = ((f32[128,1,96]{2,1,0:T(1,128)}), f32[128,1,96]{2,1,0:T(1,128)S(1)}, u32[]{:S(2)}, u32[]{:S(2)}) async-start(f32[128,1,96]{2,1,0:T(1,128)} %bitcast.17), calls=%async_computation.5 | async-start | bytes 131072 | tf_op jit(solution)/shard_map/all_to_all | solution.py:204
  123.1 0.1 slice_bitcast_fusion.1
  123.1 10.7 %all-to-all-done.5 = f32[128,1,96]{2,1,0:T(1,128)S(1)} async-done(((f32[128,1,96]{2,1,0:T(1,128)}), f32[128,1,96]{2,1,0:T(1,128)S(1)}, u32[]{:S(2)}, u32[]{:S(2)}) %all-to-all-start.5) | async-done | bytes 49184 | tf_op jit(solution)/shard_map/all_to_all | solution.py:204
  133.9 0.1 copy.34
  134.0 0.0 copy-done.7
  134.0 0.0 copy-done.9
  134.0 0.8 fusion.15
  (25 shorter events, 0.3 us)
Async XLA Ops:
  0.6 23.4 %copy-start = (bf16[60,768]{1,0:T(8,128)(2,1)S(1)}, bf16[60,768]{1,0:T(8,128)(2,1)}, u32[]{:S(2)}) copy-start(bf16[60,768]{1,0:T(8,128)(2,1)} %param.11) | copy-start | bytes 276484
  1.4 23.6 %collective-permute-start = (s32[256]{0:T(256)S(1)}, s32[256]{0:T(256)S(1)}, u32[]{:S(2)}, u32[]{:S(2)}) collective-permute-start(s32[256]{0:T(256)S(1)} %get-tuple-element.8), channel_id=1, source_target_pairs={{0,4},{4,8},{8,12},{12,16},{16,20},{20,24},{24,28},{28,32},{32,36}... | collective-permute-start | bytes 3080 | tf_op jit(solution)/shard_map/ppermute | solution.py:227
  5.9 19.1 %collective-permute-start.1 = (s32[256]{0:T(256)S(1)}, s32[256]{0:T(256)S(1)}, u32[]{:S(2)}, u32[]{:S(2)}) collective-permute-start(s32[256]{0:T(256)S(1)} %get-tuple-element.9), channel_id=1, source_target_pairs={{4,0},{8,4},{12,8},{16,12},{20,16},{24,20},{28,24},{32,28},{36,32}... | collective-permute-start | bytes 3080 | tf_op jit(solution)/shard_map/ppermute | solution.py:228
  13.4 31.1 %all-to-all-start = ((bf16[128,15,96]{2,1,0:T(8,128)(2,1)}), bf16[128,15,96]{2,1,0:T(8,128)(2,1)S(1)}, u32[]{:S(2)}, u32[]{:S(2)}) async-start(bf16[128,15,96]{2,1,0:T(8,128)(2,1)} %bitcast.6), calls=%async_computation | async-start | bytes 1048576 | tf_op jit(solution)/shard_map/all_to_all | solution.py:204
  44.7 11.6 %copy-start.2 = (bf16[1536,128]{1,0:T(8,128)(2,1)S(1)}, bf16[1536,128]{1,0:T(8,128)(2,1)}, u32[]{:S(2)}) copy-start(bf16[1536,128]{1,0:T(8,128)(2,1)} %param.13) | copy-start | bytes 1179652
  45.6 10.9 %copy-start.3 = (bf16[1536,128]{1,0:T(8,128)(2,1)S(1)}, bf16[1536,128]{1,0:T(8,128)(2,1)}, u32[]{:S(2)}) copy-start(bf16[1536,128]{1,0:T(8,128)(2,1)} %param.14) | copy-start | bytes 1179652
  46.4 18.1 %all-to-all-start.1 = ((bf16[32,2,384]{2,1,0:T(2,128)(2,1)}), bf16[32,2,384]{2,1,0:T(2,128)(2,1)S(1)}, u32[]{:S(2)}, u32[]{:S(2)}) async-start(bf16[32,2,384]{2,1,0:T(2,128)(2,1)} %reshape.150), calls=%async_computation.1 | async-start | bytes 98304 | tf_op jit(solution)/shard_map/all_to_all | solution.py:204
  56.5 8.5 %copy-start.8 = (bf16[1536,192]{0,1:T(8,128)(2,1)S(1)}, bf16[1536,192]{0,1:T(8,128)(2,1)}, u32[]{:S(2)}) copy-start(bf16[1536,192]{0,1:T(8,128)(2,1)} %param.15) | copy-start | bytes 1769476
  65.6 13.2 %copy-start.5 = (bf16[16,512]{1,0:T(8,128)(2,1)}, bf16[16,512]{1,0:T(8,128)(2,1)S(1)}, u32[]{:S(2)}) copy-start(bf16[16,512]{1,0:T(8,128)(2,1)S(1)} %fusion.11) | copy-start | bytes 49156
  78.8 18.9 %copy-start.4 = (bf16[2,1536,32]{1,2,0:T(8,128)(2,1)S(1)}, bf16[2,1536,32]{1,2,0:T(8,128)(2,1)}, u32[]{:S(2)}) copy-start(bf16[2,1536,32]{1,2,0:T(8,128)(2,1)} %param.17) | copy-start | bytes 589828
  78.8 13.3 %all-to-all-start.3 = ((bf16[4,256,384]{2,1,0:T(8,128)(2,1)}), bf16[4,256,384]{2,1,0:T(8,128)(2,1)S(1)}, u32[]{:S(2)}, u32[]{:S(2)}) async-start(bf16[4,256,384]{2,1,0:T(8,128)(2,1)} %broadcast_in_dim.56), calls=%async_computation.3 | async-start | bytes 1572864 | tf_op jit(solution)/shard_map/all_to_all | solution.py:204
  82.6 15.6 %copy-start.6 = (bf16[1,128,32]{1,2,0:T(8,128)(2,1)S(1)}, bf16[1,128,32]{1,2,0:T(8,128)(2,1)}, u32[]{:S(2)}) copy-start(bf16[1,128,32]{1,2,0:T(8,128)(2,1)} %param.19) | copy-start | bytes 24580
  92.1 7.5 %collective-permute-start.2 = (bf16[1024,384]{1,0:T(8,128)(2,1)S(1)}, bf16[1024,384]{1,0:T(8,128)(2,1)S(1)}, u32[]{:S(2)}, u32[]{:S(2)}) collective-permute-start(bf16[1024,384]{1,0:T(8,128)(2,1)S(1)} %bitcast.40), channel_id=1, source_target_pairs={{0,4},{4,0},{1,5},{5,1},{2,6},{6,2},{3,7},{7,3},{8,12},{12,8},{9,1... | collective-permute-start | bytes 2359304 | tf_op jit(solution)/shard_map/ppermute | solution.py:250
  98.0 1.6 %copy-start.1 = (bf16[192,1536]{1,0:T(8,128)(2,1)S(1)}, bf16[192,1536]{1,0:T(8,128)(2,1)}, u32[]{:S(2)}) copy-start(bf16[192,1536]{1,0:T(8,128)(2,1)} %w_out_ref.1) | copy-start | bytes 1769476
  101.3 32.7 %copy-start.7 = (bf16[1,128,32]{1,2,0:T(8,128)(2,1)S(1)}, bf16[1,128,32]{1,2,0:T(8,128)(2,1)}, u32[]{:S(2)}) copy-start(bf16[1,128,32]{1,2,0:T(8,128)(2,1)} %param.19) | copy-start | bytes 24580
  101.3 32.7 %copy-start.9 = (bf16[18,32]{1,0:T(8,128)(2,1)S(1)}, bf16[18,32]{1,0:T(8,128)(2,1)}, u32[]{:S(2)}) copy-start(bf16[18,32]{1,0:T(8,128)(2,1)} %param.18) | copy-start | bytes 3460
  101.3 10.9 %all-to-all-start.4 = ((f32[4,24,384]{2,1,0:T(8,128)}), f32[4,24,384]{2,1,0:T(8,128)S(1)}, u32[]{:S(2)}, u32[]{:S(2)}) async-start(f32[4,24,384]{2,1,0:T(8,128)} %shard_map.115), calls=%async_computation.4 | async-start | bytes 294912 | tf_op jit(solution)/shard_map/all_to_all | solution.py:204
  113.6 20.3 %all-to-all-start.5 = ((f32[128,1,96]{2,1,0:T(1,128)}), f32[128,1,96]{2,1,0:T(1,128)S(1)}, u32[]{:S(2)}, u32[]{:S(2)}) async-start(f32[128,1,96]{2,1,0:T(1,128)} %bitcast.17), calls=%async_computation.5 | async-start | bytes 131072 | tf_op jit(solution)/shard_map/all_to_all | solution.py:204

commit v4 on v3

--- a/solution.py
+++ b/solution.py
@@ -19,6 +19,8 @@
 SIZES = {"zl": 2, "y": 8, "xh": 2, "xl": 2, "core": 2, "pair": 4}
 SEQ = ("zl", "y", "xh", "xl", "core")
 SHARE = ("zl", "xl", "core")
+SPREAD = ("xh", "xl", "core")
+LINE = ("zl", "y")
 N_SEQ = math.prod(SIZES[name] for name in SEQ)
 N_SHARE = math.prod(SIZES[name] for name in SHARE)
 N_PAIR = SIZES["pair"]
@@ -78,6 +80,46 @@
     )(place, codes, weight)
 
 
+def pack_kernel(weight_ref, out_ref, wide):
+    taps, width = weight_ref.shape
+    share = width // N_SHARE
+    half = taps // 2
+    even, odd = [], []
+    for part in range(wide.shape[0]):
+        lanes = weight_ref[:, part * HQK : (part + 1) * HQK]
+        wide[part, :taps, :] = lanes.astype(jnp.float32)
+        wide[part, taps:, :] = jnp.zeros((wide.shape[1] - taps, HQK), jnp.float32)
+        even.append(wide[part, pl.ds(0, half + 1, stride=2), :])
+        odd.append(wide[part, pl.ds(1, half + 1, stride=2), :])
+    even, odd = jnp.concatenate(even, axis=1), jnp.concatenate(odd, axis=1)
+    lane = lax.broadcasted_iota(jnp.int32, (half + 1, HQK), 1)
+    blocks = []
+    for index in range(N_SHARE):
+        low = pltpu.roll(even, (width - index * share) % width, 1)[:, :HQK]
+        high = pltpu.roll(odd, (width - index * share + share) % width, 1)[:, :HQK]
+        block = jnp.where(lane < share, low, high).astype(jnp.bfloat16)
+        blocks.append(block[:half, : 2 * share])
+    for place in range(N_SEQ):
+        at, index, base = place, 0, 1
+        for name in reversed(SEQ):
+            if name in SHARE:
+                index, base = index + base * (at % SIZES[name]), base * SIZES[name]
+            at = at // SIZES[name]
+        out_ref[place] = blocks[index]
+
+
+def pack(weight):
+    taps, width = weight.shape
+    return pl.pallas_call(
+        pack_kernel,
+        out_shape=jax.ShapeDtypeStruct((N_SEQ, taps // 2, 2 * width // N_SHARE), jnp.bfloat16),
+        in_specs=whole(1),
+        out_specs=whole(1)[0],
+        scratch_shapes=[pltpu.VMEM((width // HQK, taps + 2, HQK), jnp.float32)],
+        compiler_params=params(),
+    )(weight)
+
+
 def conv_kernel(section_ref, weight_ref, out_ref, wide, act):
     windows, _, channels = section_ref.shape
     half = channels // 2
@@ -113,27 +155,43 @@
     )(section, weight)
 
 
-def attention_kernel(query_ref, near_ref, far_ref, w_out_ref, out_ref):
+def attention_kernel(query_ref, kv_ref, out_ref):
     scale = 1.0 / math.sqrt(HQK)
-    scores = [
+    scores = (
         lax.dot_general(
             query_ref[...],
-            ref[:, :HQK],
+            kv_ref[:, :HQK],
             (((1,), (1,)), ((), ())),
             preferred_element_type=jnp.float32,
         )
         * scale
-        for ref in (near_ref, far_ref)
-    ]
-    top = jnp.maximum(*[jnp.max(part, axis=1, keepdims=True) for part in scores])
-    total, mixed = 0.0, 0.0
-    for part, ref in zip(scores, (near_ref, far_ref)):
-        expo = jnp.exp(part - top)
-        total = total + jnp.sum(expo, axis=1, keepdims=True)
-        mixed = mixed + jnp.dot(
-            expo.astype(jnp.bfloat16), ref[:, HQK : HQK + HV], preferred_element_type=jnp.float32
-        )
-    mixed = (mixed / total).astype(jnp.bfloat16)
+    )
+    top = jnp.max(scores, axis=1, keepdims=True)
+    expo = jnp.exp(scores - top)
+    total = jnp.sum(expo, axis=1, keepdims=True)
+    mixed = jnp.dot(expo.astype(jnp.bfloat16), kv_ref[:, HQK:], preferred_element_type=jnp.float32)
+    lane = lax.broadcasted_iota(jnp.int32, mixed.shape, 1)
+    mixed = jnp.where(lane == HV, top, jnp.where(lane == HV + 1, total, mixed))
+    out_ref[...] = mixed.reshape(out_ref.shape)
+
+
+def attention(query, kv, groups):
+    count, width = query.shape[0] // groups, kv.shape[1] - HQK
+    return pl.pallas_call(
+        attention_kernel,
+        out_shape=jax.ShapeDtypeStruct((groups, count, width), jnp.float32),
+        in_specs=whole(2),
+        out_specs=whole(1)[0],
+        compiler_params=params(),
+    )(query, kv)
+
+
+def combine_kernel(parts_ref, w_out_ref, out_ref):
+    parts = parts_ref[...]
+    top = parts[:, :, HV : HV + 1]
+    gain = jnp.exp(top - jnp.max(top, axis=0, keepdims=True))
+    total = jnp.sum(gain * parts[:, :, HV + 1 : HV + 2], axis=0)
+    mixed = (jnp.sum(gain * parts, axis=0) / total)[:, :HV].astype(jnp.bfloat16)
     term = jnp.dot(mixed, w_out_ref[...], preferred_element_type=jnp.float32)
     mean = jnp.sum(term, axis=0, keepdims=True) * (1.0 / PAIR_POOL)
     width = term.shape[1] // N_PAIR
@@ -148,19 +206,19 @@
         out_ref[c, count : count + 8, :] = tail
 
 
-def attention(query, near, far, w_out):
-    count = query.shape[0]
+def combine(parts, w_out):
+    count = parts.shape[1]
     width = w_out.shape[1] // N_PAIR
     return pl.pallas_call(
-        attention_kernel,
+        combine_kernel,
         out_shape=jax.ShapeDtypeStruct((N_PAIR, count + 8, width), jnp.float32),
-        in_specs=whole(4),
-        out_specs=whole(1)[0],
-        compiler_params=params(),
-    )(query, near, far, w_out)
-
-
-def close_kernel(terms_ref, own_ref, trunk_ref, w_pair_ref, seq_ref, rows_ref):
+        in_specs=whole(2),
+        out_specs=whole(1)[0],
+        compiler_params=params(),
+    )(parts, w_out)
+
+
+def close_kernel(terms_ref, own_ref, trunk_ref, w_pair_ref, pair_ref, seq_ref, rows_ref, every_ref):
     count, width = own_ref.shape
     total = terms_ref[0] + terms_ref[1] + terms_ref[2] + terms_ref[3]
     seq_ref[...] = (own_ref[...].astype(jnp.float32) + total[:count, :]).astype(jnp.bfloat16)
@@ -175,19 +233,23 @@
         )
         rows = term if rows is None else rows + term
     rows_ref[...] = rows
-
-
-def close(terms, own, trunk, w_pair):
+    mine = pair_ref[0].astype(jnp.float32)
+    factors = jnp.broadcast_to(rows[:1], (mine.shape[0], rows.shape[1]))
+    every_ref[...] = jnp.concatenate([factors, mine], axis=1)
+
+
+def close(terms, own, trunk, w_pair, pair_in):
     return pl.pallas_call(
         close_kernel,
         out_shape=(
             jax.ShapeDtypeStruct(own.shape, jnp.bfloat16),
             jax.ShapeDtypeStruct((8, w_pair.shape[1]), jnp.float32),
+            jax.ShapeDtypeStruct((pair_in.shape[1], w_pair.shape[1] + pair_in.shape[2]), jnp.float32),
         ),
-        in_specs=whole(4),
-        out_specs=tuple(whole(2)),
-        compiler_params=params(),
-    )(terms, own, trunk, w_pair)
+        in_specs=whole(5),
+        out_specs=tuple(whole(3)),
+        compiler_params=params(),
+    )(terms, own, trunk, w_pair, pair_in)
 
 
 def distance_bias(row, cols, pair_bias):
@@ -216,11 +278,8 @@
 
     taps, width = w_conv.shape
     share = width // N_SHARE
-    block = [taps // 2, 2 * share]
-    blocks = w_conv.reshape(taps // 2, 2, N_SHARE, share).transpose(2, 0, 1, 3)
-    blocks = blocks.reshape([SIZES[name] if name in SHARE else 1 for name in SEQ] + block)
-    blocks = jnp.broadcast_to(blocks, [SIZES[name] for name in SEQ] + block)
-    conv_weight = exchange(blocks.reshape([N_SEQ] + block), SEQ).reshape(N_SEQ * block[0], block[1])
+    blocks = exchange(pack(w_conv), SEQ)
+    conv_weight = blocks.reshape(N_SEQ * blocks.shape[1], blocks.shape[2])
 
     codes = tokens + 1
     ends = N_SEQ - 1
@@ -246,17 +305,17 @@
     w_qkv = jnp.concatenate([w_query, w_key, w_value], axis=1)
     w_qkv = jnp.pad(w_qkv, ((0, 0), (0, 4 * HQK - w_qkv.shape[1])))
     qkv = jnp.dot(trunk, w_qkv, preferred_element_type=jnp.float32).astype(jnp.bfloat16)
-    kv = gather(gather(qkv[:, HQK:], ("zl", "y")), ("xh", "xl"))
-    other = lax.ppermute(kv, "core", [(0, 1), (1, 0)])
-    terms = exchange(attention(qkv[:, :HQK], kv, other, w_out), ("pair",))
+    query = gather(qkv[:, :HQK], SPREAD)
+    kv = gather(qkv[:, HQK:], LINE)
+    parts = exchange(attention(query, kv, query.shape[0] // count), SPREAD)
+    terms = exchange(combine(parts, w_out), ("pair",))
 
     own = lax.dynamic_slice_in_dim(trunk, pair_place * width, width, 1)
     factors = jnp.concatenate([w_pair[0], w_pair[1]], axis=1)
-    seq_out, rows = close(terms, own, trunk, factors)
+    seq_out, rows, every = close(terms, own, trunk, factors, pair_in)
     channels = pair_in.shape[2]
     mine = pair_in[0].astype(jnp.float32)
     rows = rows[:1]
-    every = jnp.concatenate([jnp.broadcast_to(rows, (N_SEQ, 2 * channels)), mine], axis=1)
     every = exchange(every[:, None], SEQ)[:, 0]
     mirror = every[:, 2 * channels :]
 

time: 135 us -> 134 us (level)
  blocking collectives: 27.6 us -> 15.4 us
  waiting for transfers between devices: 38.2 us -> 44.6 us
  starting transfers between devices: 52.7 us -> 57.7 us
  Pallas kernels: 4.9 us -> 6.39 us
    all_to_all x1 -> x0, blocking collectives: 12.2 us -> none  [exchange(): return lax.all_to_all(blocks, axes, split_axis=0, concat_axis=0, tiled=True)]
    all_to_all x5 -> x7, starting transfers between devices: 37.1 us -> 47.6 us  [exchange(): return lax.all_to_all(blocks, axes, split_axis=0, concat_axis=0, tiled=True)]
    all_to_all x5 -> x7, waiting for transfers between devices: 37.8 us -> 44.6 us  [exchange(): return lax.all_to_all(blocks, axes, split_axis=0, concat_axis=0, tiled=True)]
    ppermute x1 -> x0, starting transfers between devices: 5.57 us -> none  [on_device(): other = lax.ppermute(kv, 'core', [(0, 1), (1, 0)])]
    pallas_call x1 -> x3, Pallas kernels: 1.67 us -> 3.05 us  [the longest x1 1.05 us: attention(): pl.pallas_call(attention_kernel, out_shape=jax.ShapeDtypeStruct((groups,...]
    unnamed x26 -> x25, local copies, waits for them, and re-layouts: 1.82 us -> 3.13 us
  transfers between devices with their start and end apart: 8 -> 9, of which waited for: 6 -> 7; matrix products, arithmetic and copies ran while one was open for 4% -> 2% of each run, Pallas kernels for 1% -> 2%
where the time goes in v4:
time: 134 us
  starting transfers between devices  57.7 us (43%)
  waiting for transfers between devices  44.6 us (33%)
  blocking collectives  15.4 us (11%)
  Pallas kernels  6.39 us (5%)
  local copies, waits for them, and re-layouts  5.53 us (4%)
  matrix products  1.97 us (1%)
    all_to_all x7, starting transfers between devices, exchange(): return lax.all_to_all(blocks, axes, split_axis=0, concat_axis=0, tiled=True)  47.6 us
    all_to_all x7, waiting for transfers between devices, exchange(): return lax.all_to_all(blocks, axes, split_axis=0, concat_axis=0, tiled=True)  44.6 us
    all_gather x1, blocking collectives, on_device(): sections = lax.all_gather(section, SHARE, axis=0, tiled=False)  15.4 us
    ppermute x1, starting transfers between devices, on_device(): right = lax.ppermute(codes[:SIDE], SEQ, [(i + 1, i) for i in range(ends)])  5.57 us
    ppermute x1, starting transfers between devices, on_device(): left = lax.ppermute(codes[-SIDE:], SEQ, [(i, i + 1) for i in range(ends)])  4.5 us
    unnamed x25, local copies, waits for them, and re-layouts  3.13 us
  transfers between devices with their start and end apart: 9, of which 7 were waited for; matrix products, arithmetic and copies ran while one was open for 2% of the time, Pallas kernels for 2%

profile of v4, /device:TPU:1, one launch (start us, length us, event | category | flops | bytes accessed | tf_op | source)
XLA Modules:
  0.0 133.6 jit_solution(16090086378798233237)
XLA Ops:
  0.6 0.0 copy-start
  0.6 0.7 broadcast_add_fusion
  1.4 4.5 %collective-permute-start = (s32[256]{0:T(256)S(1)}, s32[256]{0:T(256)S(1)}, u32[]{:S(2)}, u32[]{:S(2)}) collective-permute-start(s32[256]{0:T(256)S(1)} %get-tuple-element.14), channel_id=1, source_target_pairs={{0,4},{4,8},{8,12},{12,16},{16,20},{20,24},{24,28},{28,32},{32,36}... | collective-permute-start | bytes 3080 | tf_op jit(solution)/shard_map/ppermute | solution.py:286
  5.9 5.6 %collective-permute-start.1 = (s32[256]{0:T(256)S(1)}, s32[256]{0:T(256)S(1)}, u32[]{:S(2)}, u32[]{:S(2)}) collective-permute-start(s32[256]{0:T(256)S(1)} %get-tuple-element.15), channel_id=1, source_target_pairs={{4,0},{8,4},{12,8},{16,12},{20,16},{24,20},{28,24},{32,28},{36,32}... | collective-permute-start | bytes 3080 | tf_op jit(solution)/shard_map/ppermute | solution.py:287
  11.5 0.0 copy-start.2
  11.5 0.7 copy-done.2
  12.2 1.0 shard_map.114
  13.2 10.6 %all-to-all-start = ((bf16[128,15,96]{2,1,0:T(8,128)(2,1)}), bf16[128,15,96]{2,1,0:T(8,128)(2,1)S(1)}, u32[]{:S(2)}, u32[]{:S(2)}) async-start(bf16[128,15,96]{2,1,0:T(8,128)(2,1)} %shard_map.114), calls=%async_computation | async-start | bytes 1048576 | tf_op jit(solution)/shard_map/all_to_all | solution.py:266
  23.8 0.0 copy-done
  23.9 0.5 fusion.10
  24.4 0.3 rev.3
  24.8 0.0 collective-permute-done
  24.8 0.0 collective-permute-done.1
  24.8 1.7 %shard_map.113 = f32[40,768]{1,0:T(8,128)S(1)} custom-call(s32[1]{0:T(128)} %bitcast.place_ref, s32[1,2560]{1,0:T(1,128)S(1)} %broadcast_in_dim.15.codes_ref, bf16[64,768]{1,0:T(8,128)(2,1)S(1)} %bitcast.35), custom_call_target="tpu_custom_call" | custom-call | flops 40000000000 | bytes 200000 | tf_op jit(solution)/shard_map/pallas_call | solution.py:73
  26.6 15.4 %all-gather = bf16[320,768]{1,0:T(8,128)(2,1)S(1)} all-gather(bf16[40,768]{1,0:T(8,128)(2,1)S(1)} %convert_element_type.148), channel_id=2, replica_groups=mesh['zl'=2,'y'=8,'xh'=2,'xl'=2,'core'=2,'pair'=4] {'zl','xl','core'}, dimensions={0}, use_global_device_ids=true | all-gather | bytes 552960 | tf_op jit(solution)/shard_map/all_gather | solution.py:296
  41.9 2.4 %all-to-all-done = bf16[128,15,96]{2,1,0:T(8,128)(2,1)S(1)} async-done(((bf16[128,15,96]{2,1,0:T(8,128)(2,1)}), bf16[128,15,96]{2,1,0:T(8,128)(2,1)S(1)}, u32[]{:S(2)}, u32[]{:S(2)}) %all-to-all-start) | async-done | bytes 368672 | tf_op jit(solution)/shard_map/all_to_all | solution.py:266
  44.3 0.2 reshape.128.weight_ref
  44.5 0.0 copy-start.3
  44.5 0.8 shard_map.115
  45.3 0.0 copy-start.4
  45.4 0.8 reshape.143
  46.2 9.9 %all-to-all-start.1 = ((bf16[32,2,384]{2,1,0:T(2,128)(2,1)}), bf16[32,2,384]{2,1,0:T(2,128)(2,1)S(1)}, u32[]{:S(2)}, u32[]{:S(2)}) async-start(bf16[32,2,384]{2,1,0:T(2,128)(2,1)} %reshape.143), calls=%async_computation.1 | async-start | bytes 98304 | tf_op jit(solution)/shard_map/all_to_all | solution.py:266
  56.0 0.0 copy-done.3
  56.0 0.2 copy.33
  56.2 0.0 copy-done.4
  56.2 0.0 copy-start.7
  56.3 0.2 copy.34
  56.4 7.8 %all-to-all-done.1 = bf16[32,2,384]{2,1,0:T(2,128)(2,1)S(1)} async-done(((bf16[32,2,384]{2,1,0:T(2,128)(2,1)}), bf16[32,2,384]{2,1,0:T(2,128)(2,1)S(1)}, u32[]{:S(2)}, u32[]{:S(2)}) %all-to-all-start.1) | async-done | bytes 49184 | tf_op jit(solution)/shard_map/all_to_all | solution.py:266
  64.2 0.2 reshape.144
  64.4 0.1 copy.32
  64.5 0.2 reshape.131.trunk_ref
  64.7 0.0 copy-done.7
  64.7 0.6 fusion.11
  65.4 0.0 copy-start.5
  65.4 0.6 broadcast_in_dim.17
  66.0 3.6 %all-to-all-start.2 = ((bf16[8,16,128]{2,1,0:T(8,128)(2,1)}), bf16[8,16,128]{2,1,0:T(8,128)(2,1)S(1)}, u32[]{:S(2)}, u32[]{:S(2)}) async-start(bf16[8,16,128]{2,1,0:T(8,128)(2,1)} %broadcast_in_dim.17), calls=%async_computation.2 | async-start | bytes 65536 | tf_op jit(solution)/shard_map/all_to_all | solution.py:266
  69.6 4.7 %all-to-all-done.2 = bf16[8,16,128]{2,1,0:T(8,128)(2,1)S(1)} async-done(((bf16[8,16,128]{2,1,0:T(8,128)(2,1)}), bf16[8,16,128]{2,1,0:T(8,128)(2,1)S(1)}, u32[]{:S(2)}, u32[]{:S(2)}) %all-to-all-start.2) | async-done | bytes 32800 | tf_op jit(solution)/shard_map/all_to_all | solution.py:266
  74.4 0.7 broadcast_in_dim.18
  75.1 5.5 %all-to-all-start.3 = ((bf16[16,16,384]{2,1,0:T(8,128)(2,1)}), bf16[16,16,384]{2,1,0:T(8,128)(2,1)S(1)}, u32[]{:S(2)}, u32[]{:S(2)}) async-start(bf16[16,16,384]{2,1,0:T(8,128)(2,1)} %broadcast_in_dim.18), calls=%async_computation.3 | async-start | bytes 393216 | tf_op jit(solution)/shard_map/all_to_all | solution.py:266
  80.6 0.0 copy-done.5
  80.6 0.2 copy.40
  80.9 0.2 copy.41
  81.1 7.1 %all-to-all-done.3 = bf16[16,16,384]{2,1,0:T(8,128)(2,1)S(1)} async-done(((bf16[16,16,384]{2,1,0:T(8,128)(2,1)}), bf16[16,16,384]{2,1,0:T(8,128)(2,1)S(1)}, u32[]{:S(2)}, u32[]{:S(2)}) %all-to-all-start.3) | async-done | bytes 196640 | tf_op jit(solution)/shard_map/all_to_all | solution.py:266
  88.2 1.1 shard_map.116
  89.2 5.7 %all-to-all-start.4 = ((f32[8,16,256]{2,1,0:T(8,128)}), f32[8,16,256]{2,1,0:T(8,128)S(1)}, u32[]{:S(2)}, u32[]{:S(2)}) async-start(f32[8,16,256]{2,1,0:T(8,128)} %shard_map.116), calls=%async_computation.4 | async-start | bytes 262144 | tf_op jit(solution)/shard_map/all_to_all | solution.py:266
  94.9 0.0 copy-start.6
  94.9 0.0 copy-start.1
  95.0 0.2 pad_maximum_fusion.w_pair_ref
  95.2 0.5 copy-done.6
  95.6 0.1 copy.37.pair_ref
  95.8 4.5 %all-to-all-done.4.parts_ref = f32[8,16,256]{2,1,0:T(8,128)S(1)} async-done(((f32[8,16,256]{2,1,0:T(8,128)}), f32[8,16,256]{2,1,0:T(8,128)S(1)}, u32[]{:S(2)}, u32[]{:S(2)}) %all-to-all-start.4) | async-done | bytes 131104 | tf_op jit(solution)/shard_map/all_to_all | solution.py:266
  100.2 0.0 copy-done.1
  100.2 1.0 shard_map.117
  101.2 0.0 copy-start.8
  101.3 3.5 %all-to-all-start.5 = ((f32[4,24,384]{2,1,0:T(8,128)}), f32[4,24,384]{2,1,0:T(8,128)S(1)}, u32[]{:S(2)}, u32[]{:S(2)}) async-start(f32[4,24,384]{2,1,0:T(8,128)} %shard_map.117), calls=%async_computation.5 | async-start | bytes 294912 | tf_op jit(solution)/shard_map/all_to_all | solution.py:266
  104.8 7.4 %all-to-all-done.5.terms_ref = f32[4,24,384]{2,1,0:T(8,128)S(1)} async-done(((f32[4,24,384]{2,1,0:T(8,128)}), f32[4,24,384]{2,1,0:T(8,128)S(1)}, u32[]{:S(2)}, u32[]{:S(2)}) %all-to-all-start.5) | async-done | bytes 147488 | tf_op jit(solution)/shard_map/all_to_all | solution.py:266
  112.1 0.8 shard_map.118
  112.9 8.9 %all-to-all-start.6 = ((f32[128,1,96]{2,1,0:T(1,128)}), f32[128,1,96]{2,1,0:T(1,128)S(1)}, u32[]{:S(2)}, u32[]{:S(2)}) async-start(f32[128,1,96]{2,1,0:T(1,128)} %bitcast.14), calls=%async_computation.6 | async-start | bytes 131072 | tf_op jit(solution)/shard_map/all_to_all | solution.py:266
  121.8 0.1 slice_bitcast_fusion.1
  121.9 10.8 %all-to-all-done.6 = f32[128,1,96]{2,1,0:T(1,128)S(1)} async-done(((f32[128,1,96]{2,1,0:T(1,128)}), f32[128,1,96]{2,1,0:T(1,128)S(1)}, u32[]{:S(2)}, u32[]{:S(2)}) %all-to-all-start.6) | async-done | bytes 49184 | tf_op jit(solution)/shard_map/all_to_all | solution.py:266
  132.7 0.1 copy.39
  132.8 0.0 copy-done.8
  132.8 0.8 fusion.15
  (18 shorter events, 0.2 us)
Async XLA Ops:
  0.6 23.2 %copy-start = (bf16[60,768]{1,0:T(8,128)(2,1)S(1)}, bf16[60,768]{1,0:T(8,128)(2,1)}, u32[]{:S(2)}) copy-start(bf16[60,768]{1,0:T(8,128)(2,1)} %param.11) | copy-start | bytes 276484
  1.4 23.4 %collective-permute-start = (s32[256]{0:T(256)S(1)}, s32[256]{0:T(256)S(1)}, u32[]{:S(2)}, u32[]{:S(2)}) collective-permute-start(s32[256]{0:T(256)S(1)} %get-tuple-element.14), channel_id=1, source_target_pairs={{0,4},{4,8},{8,12},{12,16},{16,20},{20,24},{24,28},{28,32},{32,36}... | collective-permute-start | bytes 3080 | tf_op jit(solution)/shard_map/ppermute | solution.py:286
  5.9 18.9 %collective-permute-start.1 = (s32[256]{0:T(256)S(1)}, s32[256]{0:T(256)S(1)}, u32[]{:S(2)}, u32[]{:S(2)}) collective-permute-start(s32[256]{0:T(256)S(1)} %get-tuple-element.15), channel_id=1, source_target_pairs={{4,0},{8,4},{12,8},{16,12},{20,16},{24,20},{28,24},{32,28},{36,32}... | collective-permute-start | bytes 3080 | tf_op jit(solution)/shard_map/ppermute | solution.py:287
  11.5 0.7 copy-start.2
  13.2 31.1 %all-to-all-start = ((bf16[128,15,96]{2,1,0:T(8,128)(2,1)}), bf16[128,15,96]{2,1,0:T(8,128)(2,1)S(1)}, u32[]{:S(2)}, u32[]{:S(2)}) async-start(bf16[128,15,96]{2,1,0:T(8,128)(2,1)} %shard_map.114), calls=%async_computation | async-start | bytes 1048576 | tf_op jit(solution)/shard_map/all_to_all | solution.py:266
  44.5 11.5 %copy-start.3 = (bf16[1536,128]{1,0:T(8,128)(2,1)S(1)}, bf16[1536,128]{1,0:T(8,128)(2,1)}, u32[]{:S(2)}) copy-start(bf16[1536,128]{1,0:T(8,128)(2,1)} %param.13) | copy-start | bytes 1179652
  45.3 10.9 %copy-start.4 = (bf16[1536,128]{1,0:T(8,128)(2,1)S(1)}, bf16[1536,128]{1,0:T(8,128)(2,1)}, u32[]{:S(2)}) copy-start(bf16[1536,128]{1,0:T(8,128)(2,1)} %param.14) | copy-start | bytes 1179652
  46.2 18.1 %all-to-all-start.1 = ((bf16[32,2,384]{2,1,0:T(2,128)(2,1)}), bf16[32,2,384]{2,1,0:T(2,128)(2,1)S(1)}, u32[]{:S(2)}, u32[]{:S(2)}) async-start(bf16[32,2,384]{2,1,0:T(2,128)(2,1)} %reshape.143), calls=%async_computation.1 | async-start | bytes 98304 | tf_op jit(solution)/shard_map/all_to_all | solution.py:266
  56.2 8.5 %copy-start.7 = (bf16[1536,192]{0,1:T(8,128)(2,1)S(1)}, bf16[1536,192]{0,1:T(8,128)(2,1)}, u32[]{:S(2)}) copy-start(bf16[1536,192]{0,1:T(8,128)(2,1)} %param.15) | copy-start | bytes 1769476
  65.4 15.3 %copy-start.5 = (bf16[2,1536,32]{1,2,0:T(8,128)(2,1)S(1)}, bf16[2,1536,32]{1,2,0:T(8,128)(2,1)}, u32[]{:S(2)}) copy-start(bf16[2,1536,32]{1,2,0:T(8,128)(2,1)} %param.17) | copy-start | bytes 589828
  66.0 8.4 %all-to-all-start.2 = ((bf16[8,16,128]{2,1,0:T(8,128)(2,1)}), bf16[8,16,128]{2,1,0:T(8,128)(2,1)S(1)}, u32[]{:S(2)}, u32[]{:S(2)}) async-start(bf16[8,16,128]{2,1,0:T(8,128)(2,1)} %broadcast_in_dim.17), calls=%async_computation.2 | async-start | bytes 65536 | tf_op jit(solution)/shard_map/all_to_all | solution.py:266
  75.1 13.1 %all-to-all-start.3 = ((bf16[16,16,384]{2,1,0:T(8,128)(2,1)}), bf16[16,16,384]{2,1,0:T(8,128)(2,1)S(1)}, u32[]{:S(2)}, u32[]{:S(2)}) async-start(bf16[16,16,384]{2,1,0:T(8,128)(2,1)} %broadcast_in_dim.18), calls=%async_computation.3 | async-start | bytes 393216 | tf_op jit(solution)/shard_map/all_to_all | solution.py:266
  89.2 11.0 %all-to-all-start.4 = ((f32[8,16,256]{2,1,0:T(8,128)}), f32[8,16,256]{2,1,0:T(8,128)S(1)}, u32[]{:S(2)}, u32[]{:S(2)}) async-start(f32[8,16,256]{2,1,0:T(8,128)} %shard_map.116), calls=%async_computation.4 | async-start | bytes 262144 | tf_op jit(solution)/shard_map/all_to_all | solution.py:266
  94.9 0.7 copy-start.6
  94.9 5.3 %copy-start.1 = (bf16[192,1536]{1,0:T(8,128)(2,1)S(1)}, bf16[192,1536]{1,0:T(8,128)(2,1)}, u32[]{:S(2)}) copy-start(bf16[192,1536]{1,0:T(8,128)(2,1)} %w_out_ref.1) | copy-start | bytes 1769476
  101.2 31.5 %copy-start.8 = (bf16[18,32]{1,0:T(8,128)(2,1)S(1)}, bf16[18,32]{1,0:T(8,128)(2,1)}, u32[]{:S(2)}) copy-start(bf16[18,32]{1,0:T(8,128)(2,1)} %param.18) | copy-start | bytes 3460
  101.3 10.9 %all-to-all-start.5 = ((f32[4,24,384]{2,1,0:T(8,128)}), f32[4,24,384]{2,1,0:T(8,128)S(1)}, u32[]{:S(2)}, u32[]{:S(2)}) async-start(f32[4,24,384]{2,1,0:T(8,128)} %shard_map.117), calls=%async_computation.5 | async-start | bytes 294912 | tf_op jit(solution)/shard_map/all_to_all | solution.py:266
  112.9 19.7 %all-to-all-start.6 = ((f32[128,1,96]{2,1,0:T(1,128)}), f32[128,1,96]{2,1,0:T(1,128)S(1)}, u32[]{:S(2)}, u32[]{:S(2)}) async-start(f32[128,1,96]{2,1,0:T(1,128)} %bitcast.14), calls=%async_computation.6 | async-start | bytes 131072 | tf_op jit(solution)/shard_map/all_to_all | solution.py:266

commit v5 on v4

--- a/solution.py
+++ b/solution.py
@@ -19,11 +19,13 @@
 SIZES = {"zl": 2, "y": 8, "xh": 2, "xl": 2, "core": 2, "pair": 4}
 SEQ = ("zl", "y", "xh", "xl", "core")
 SHARE = ("zl", "xl", "core")
-SPREAD = ("xh", "xl", "core")
-LINE = ("zl", "y")
+SPREAD = ("zl", "xl", "core")
+LINE = ("y", "xh")
 N_SEQ = math.prod(SIZES[name] for name in SEQ)
 N_SHARE = math.prod(SIZES[name] for name in SHARE)
 N_PAIR = SIZES["pair"]
+N_SPREAD = math.prod(SIZES[name] for name in SPREAD)
+N_LINE = math.prod(SIZES[name] for name in LINE)
 
 SIDE = 256
 ROWS = 32
@@ -120,10 +122,10 @@
     )(weight)
 
 
-def conv_kernel(section_ref, weight_ref, out_ref, wide, act):
+def conv_kernel(section_ref, weight_ref, out_ref, wide, act, best):
     windows, _, channels = section_ref.shape
     half = channels // 2
-    columns = out_ref.shape[2]
+    columns = out_ref.shape[2] // 8
     wide[...] = section_ref[...].astype(jnp.float32)
     even, odd = None, None
     for tap in range(KS_CONV):
@@ -133,10 +135,20 @@
         even = term if even is None else even + term
         term = jnp.dot(rows[:, half:], weight, preferred_element_type=jnp.float32)
         odd = term if odd is None else odd + term
-    act[...] = gelu(even[:, :columns] + odd[:, columns:])
+    act[...] = jnp.zeros(act.shape, jnp.float32)
+    act[:, :columns] = gelu(even[:, :columns] + odd[:, columns:])
     count = windows * ROWS // 2
-    best = jnp.maximum(act[pl.ds(0, count, stride=2), :], act[pl.ds(1, count, stride=2), :])
-    out_ref[...] = best.astype(jnp.bfloat16).reshape(out_ref.shape)
+    best[...] = jnp.maximum(act[pl.ds(0, count, stride=2), :], act[pl.ds(1, count, stride=2), :])
+    flat = None
+    for index in range(8):
+        part = best[pl.ds(index, count // 8, stride=8), :]
+        part = jnp.pad(part, ((0, 0), (0, 8 * columns - part.shape[1])))
+        part = pltpu.roll(part, index * columns, 1)
+        flat = part if flat is None else flat + part
+    for window in range(windows):
+        block = flat[2 * window : 2 * window + 2, :].astype(jnp.bfloat16)
+        for index in range(N_PAIR):
+            out_ref[window * N_PAIR + index] = block
 
 
 def conv(section, weight):
@@ -144,15 +156,45 @@
     columns = weight.shape[1] // 2
     return pl.pallas_call(
         conv_kernel,
-        out_shape=jax.ShapeDtypeStruct((windows, ROWS // 2, columns), jnp.bfloat16),
+        out_shape=jax.ShapeDtypeStruct((windows * N_PAIR, 2, 8 * columns), jnp.bfloat16),
         in_specs=whole(2),
         out_specs=whole(1)[0],
         scratch_shapes=[
             pltpu.VMEM((windows, EXT_PAD, channels), jnp.float32),
-            pltpu.VMEM((windows * ROWS, columns), jnp.float32),
+            pltpu.VMEM((windows * ROWS, HQK), jnp.float32),
+            pltpu.VMEM((windows * ROWS // 2, HQK), jnp.float32),
         ],
         compiler_params=params(),
     )(section, weight)
+
+
+def project_kernel(trunk_ref, w_query_ref, w_key_ref, w_value_ref, query_ref, kv_ref):
+    trunk = trunk_ref[...]
+    query, key, value = [
+        jnp.dot(trunk, ref[...], preferred_element_type=jnp.float32).astype(jnp.bfloat16)
+        for ref in (w_query_ref, w_key_ref, w_value_ref)
+    ]
+    for index in range(N_SPREAD):
+        query_ref[index] = query
+    rest = jnp.zeros((trunk.shape[0], kv_ref.shape[2] - HQK - HV), jnp.bfloat16)
+    for index in range(N_LINE):
+        kv_ref[index, :, :HQK] = key
+        kv_ref[index, :, HQK : HQK + HV] = value
+        kv_ref[index, :, HQK + HV :] = rest
+
+
+def project(trunk, w_query, w_key, w_value):
+    count = trunk.shape[0]
+    return pl.pallas_call(
+        project_kernel,
+        out_shape=(
+            jax.ShapeDtypeStruct((N_SPREAD, count, HQK), jnp.bfloat16),
+            jax.ShapeDtypeStruct((N_LINE, count, 3 * HQK), jnp.bfloat16),
+        ),
+        in_specs=whole(4),
+        out_specs=tuple(whole(2)),
+        compiler_params=params(),
+    )(trunk, w_query, w_key, w_value)
 
 
 def attention_kernel(query_ref, kv_ref, out_ref):
@@ -198,12 +240,12 @@
     count = term.shape[0]
     tail = jnp.concatenate(
         [mean[:, c * width : (c + 1) * width] for c in range(N_PAIR)]
-        + [jnp.zeros((4, width), jnp.float32)],
+        + [jnp.zeros((count - N_PAIR, width), jnp.float32)],
         axis=0,
-    )
+    ).astype(jnp.bfloat16)
     for c in range(N_PAIR):
-        out_ref[c, :count, :] = term[:, c * width : (c + 1) * width]
-        out_ref[c, count : count + 8, :] = tail
+        out_ref[c, :count, :] = term[:, c * width : (c + 1) * width].astype(jnp.bfloat16)
+        out_ref[c, count:, :] = tail
 
 
 def combine(parts, w_out):
@@ -211,7 +253,7 @@
     width = w_out.shape[1] // N_PAIR
     return pl.pallas_call(
         combine_kernel,
-        out_shape=jax.ShapeDtypeStruct((N_PAIR, count + 8, width), jnp.float32),
+        out_shape=jax.ShapeDtypeStruct((N_PAIR, 2 * count, width), jnp.bfloat16),
         in_specs=whole(2),
         out_specs=whole(1)[0],
         compiler_params=params(),
@@ -220,7 +262,7 @@
 
 def close_kernel(terms_ref, own_ref, trunk_ref, w_pair_ref, pair_ref, seq_ref, rows_ref, every_ref):
     count, width = own_ref.shape
-    total = terms_ref[0] + terms_ref[1] + terms_ref[2] + terms_ref[3]
+    total = jnp.sum(terms_ref[...].astype(jnp.float32), axis=0)
     seq_ref[...] = (own_ref[...].astype(jnp.float32) + total[:count, :]).astype(jnp.bfloat16)
     trunk_mean = jnp.sum(trunk_ref[...].astype(jnp.float32), axis=0, keepdims=True) * (1.0 / PAIR_POOL)
     rows = None
@@ -266,12 +308,6 @@
     return lax.all_to_all(blocks, axes, split_axis=0, concat_axis=0, tiled=True)
 
 
-def gather(rows, axes):
-    count = math.prod(SIZES[name] for name in axes)
-    blocks = jnp.broadcast_to(rows[None], (count,) + rows.shape)
-    return exchange(blocks, axes).reshape(count * rows.shape[0], *rows.shape[1:])
-
-
 def on_device(tokens, w_stem, w_conv, w_query, w_key, w_value, w_out, w_pair, pair_bias, pair_in):
     place = lax.axis_index(SEQ)
     pair_place = lax.axis_index("pair")
@@ -295,19 +331,15 @@
     section = stem(place.astype(jnp.int32)[None], codes, stem_weight).astype(jnp.bfloat16)
     sections = lax.all_gather(section, SHARE, axis=0, tiled=False)
 
-    parts = conv(sections, conv_weight)
-    count = parts.shape[1]
-    parts = jnp.broadcast_to(parts[:, None], (N_SHARE, N_PAIR, count, share))
-    parts = exchange(parts.reshape(N_SHARE * N_PAIR, count, share), SHARE + ("pair",))
+    parts = exchange(conv(sections, conv_weight), SHARE + ("pair",))
+    count = ROWS // 2
     trunk = parts.reshape(N_SHARE, N_PAIR, count, share).transpose(2, 1, 0, 3)
     trunk = trunk.reshape(count, N_PAIR * width)
 
-    w_qkv = jnp.concatenate([w_query, w_key, w_value], axis=1)
-    w_qkv = jnp.pad(w_qkv, ((0, 0), (0, 4 * HQK - w_qkv.shape[1])))
-    qkv = jnp.dot(trunk, w_qkv, preferred_element_type=jnp.float32).astype(jnp.bfloat16)
-    query = gather(qkv[:, :HQK], SPREAD)
-    kv = gather(qkv[:, HQK:], LINE)
-    parts = exchange(attention(query, kv, query.shape[0] // count), SPREAD)
+    query, kv = project(trunk, w_query, w_key, w_value)
+    query = exchange(query, SPREAD).reshape(N_SPREAD * count, HQK)
+    kv = exchange(kv, LINE).reshape(N_LINE * count, kv.shape[2])
+    parts = exchange(attention(query, kv, N_SPREAD), SPREAD)
     terms = exchange(combine(parts, w_out), ("pair",))
 
     own = lax.dynamic_slice_in_dim(trunk, pair_place * width, width, 1)

time: 134 us -> 134 us (level)
  blocking collectives: 15.4 us -> 22.3 us
  starting transfers between devices: 57.7 us -> 54.4 us
  local copies, waits for them, and re-layouts: 5.53 us -> 2.81 us
  waiting for transfers between devices: 44.6 us -> 42.1 us
  Pallas kernels: 6.39 us -> 8.05 us
    all_to_all x0 -> x1, blocking collectives: none -> 6.78 us  [exchange(): return lax.all_to_all(blocks, axes, split_axis=0, concat_axis=0, tiled=True)]
    all_to_all x7 -> x6, starting transfers between devices: 47.6 us -> 44.3 us  [exchange(): return lax.all_to_all(blocks, axes, split_axis=0, concat_axis=0, tiled=True)]
    all_to_all x7 -> x6, waiting for transfers between devices: 44.6 us -> 42.1 us  [exchange(): return lax.all_to_all(blocks, axes, split_axis=0, concat_axis=0, tiled=True)]
    pallas_call x2 -> x3, Pallas kernels: 1.81 us -> 3.49 us  [the longest x1 1.5 us: conv(): pl.pallas_call(conv_kernel, out_shape=jax.ShapeDtypeStruct((windows * N_P...]
    unnamed x25 -> x22, local copies, waits for them, and re-layouts: 3.13 us -> 1.62 us
    broadcast_in_dim x3 -> x0, local copies, waits for them, and re-layouts: 1.35 us -> none  [the longest x2 1.33 us: gather(): blocks = jnp.broadcast_to(rows[None], (count,) + rows.shape)]
  transfers between devices with their start and end apart: 9 -> 8, of which waited for: 7 -> 6; matrix products, arithmetic and copies ran while one was open for 2% -> 2% of each run, Pallas kernels for 2% -> 2%
where the time goes in v5:
time: 134 us; the launch traced here: 133 us
  starting transfers between devices  54.4 us (41%)
  waiting for transfers between devices  42.1 us (31%)
  blocking collectives  22.3 us (17%)
  Pallas kernels  8.05 us (6%)
  local copies, waits for them, and re-layouts  2.81 us (2%)
    all_to_all x6, starting transfers between devices, exchange(): return lax.all_to_all(blocks, axes, split_axis=0, concat_axis=0, tiled=True)  44.3 us
    all_to_all x6, waiting for transfers between devices, exchange(): return lax.all_to_all(blocks, axes, split_axis=0, concat_axis=0, tiled=True)  42.1 us
    all_gather x1, blocking collectives, on_device(): sections = lax.all_gather(section, SHARE, axis=0, tiled=False)  15.5 us
    all_to_all x1, blocking collectives, exchange(): return lax.all_to_all(blocks, axes, split_axis=0, concat_axis=0, tiled=True)  6.78 us
    ppermute x1, starting transfers between devices, on_device(): right = lax.ppermute(codes[:SIDE], SEQ, [(i + 1, i) for i in range(ends)])  5.57 us
    ppermute x1, starting transfers between devices, on_device(): left = lax.ppermute(codes[-SIDE:], SEQ, [(i, i + 1) for i in range(ends)])  4.5 us
  transfers between devices with their start and end apart: 8, of which 6 were waited for; matrix products, arithmetic and copies ran while one was open for 2% of the time, Pallas kernels for 2%

profile of v5, /device:TPU:1, one launch (start us, length us, event | category | flops | bytes accessed | tf_op | source)
XLA Modules:
  0.0 133.0 jit_solution(16966323353020210072)
XLA Ops:
  0.6 0.0 copy-start
  0.6 0.7 broadcast_add_fusion
  1.4 4.5 %collective-permute-start = (s32[256]{0:T(256)S(1)}, s32[256]{0:T(256)S(1)}, u32[]{:S(2)}, u32[]{:S(2)}) collective-permute-start(s32[256]{0:T(256)S(1)} %get-tuple-element.18), channel_id=1, source_target_pairs={{0,4},{4,8},{8,12},{12,16},{16,20},{20,24},{24,28},{28,32},{32,36}... | collective-permute-start | bytes 3080 | tf_op jit(solution)/shard_map/ppermute | solution.py:322
  5.9 5.6 %collective-permute-start.1 = (s32[256]{0:T(256)S(1)}, s32[256]{0:T(256)S(1)}, u32[]{:S(2)}, u32[]{:S(2)}) collective-permute-start(s32[256]{0:T(256)S(1)} %get-tuple-element.19), channel_id=1, source_target_pairs={{4,0},{8,4},{12,8},{16,12},{20,16},{24,20},{28,24},{32,28},{36,32}... | collective-permute-start | bytes 3080 | tf_op jit(solution)/shard_map/ppermute | solution.py:323
  11.5 0.0 copy-start.4
  11.5 0.7 copy-done.4
  12.2 1.0 shard_map.114
  13.2 10.6 %all-to-all-start = ((bf16[128,15,96]{2,1,0:T(8,128)(2,1)}), bf16[128,15,96]{2,1,0:T(8,128)(2,1)S(1)}, u32[]{:S(2)}, u32[]{:S(2)}) async-start(bf16[128,15,96]{2,1,0:T(8,128)(2,1)} %shard_map.114), calls=%async_computation | async-start | bytes 1048576 | tf_op jit(solution)/shard_map/all_to_all | solution.py:308
  23.8 0.0 copy-done
  23.9 0.5 fusion.3
  24.4 0.3 rev.3
  24.8 0.0 collective-permute-done
  24.8 0.0 collective-permute-done.1
  24.8 1.7 %shard_map.113 = f32[40,768]{1,0:T(8,128)S(1)} custom-call(s32[1]{0:T(128)} %bitcast.place_ref, s32[1,2560]{1,0:T(1,128)S(1)} %broadcast_in_dim.17.codes_ref, bf16[64,768]{1,0:T(8,128)(2,1)S(1)} %bitcast.33), custom_call_target="tpu_custom_call" | custom-call | flops 40000000000 | bytes 200000 | tf_op jit(solution)/shard_map/pallas_call | solution.py:75
  26.6 15.5 %all-gather = bf16[320,768]{1,0:T(8,128)(2,1)S(1)} all-gather(bf16[40,768]{1,0:T(8,128)(2,1)S(1)} %convert_element_type.143), channel_id=2, replica_groups=mesh['zl'=2,'y'=8,'xh'=2,'xl'=2,'core'=2,'pair'=4] {'zl','xl','core'}, dimensions={0}, use_global_device_ids=true | all-gather | bytes 552960 | tf_op jit(solution)/shard_map/all_gather | solution.py:332
  42.1 2.2 %all-to-all-done = bf16[128,15,96]{2,1,0:T(8,128)(2,1)S(1)} async-done(((bf16[128,15,96]{2,1,0:T(8,128)(2,1)}), bf16[128,15,96]{2,1,0:T(8,128)(2,1)S(1)}, u32[]{:S(2)}, u32[]{:S(2)}) %all-to-all-start) | async-done | bytes 368672 | tf_op jit(solution)/shard_map/all_to_all | solution.py:308
  44.3 0.2 reshape.122.weight_ref
  44.5 0.0 copy-start.5
  44.5 1.5 %shard_map.115 = bf16[32,2,384]{2,1,0:T(2,128)(2,1)} custom-call(bf16[8,40,768]{2,1,0:T(8,128)(2,1)S(1)} %bitcast.30, bf16[1920,96]{1,0:T(8,128)(2,1)S(1)} %reshape.122.weight_ref), custom_call_target="tpu_custom_call" | custom-call | tf_op jit(solution)/shard_map/pallas_call | solution.py:157
  46.0 9.9 %all-to-all-start.1 = ((bf16[32,2,384]{2,1,0:T(2,128)(2,1)}), bf16[32,2,384]{2,1,0:T(2,128)(2,1)S(1)}, u32[]{:S(2)}, u32[]{:S(2)}) async-start(bf16[32,2,384]{2,1,0:T(2,128)(2,1)} %shard_map.115), calls=%async_computation.1 | async-start | bytes 98304 | tf_op jit(solution)/shard_map/all_to_all | solution.py:308
  55.9 0.0 copy-done.5
  55.9 0.0 copy-start.2
  55.9 0.0 copy-start.3
  55.9 0.3 copy.32.w_value_ref
  56.2 7.9 %all-to-all-done.1 = bf16[32,2,384]{2,1,0:T(2,128)(2,1)S(1)} async-done(((bf16[32,2,384]{2,1,0:T(2,128)(2,1)}), bf16[32,2,384]{2,1,0:T(2,128)(2,1)S(1)}, u32[]{:S(2)}, u32[]{:S(2)}) %all-to-all-start.1) | async-done | bytes 49184 | tf_op jit(solution)/shard_map/all_to_all | solution.py:308
  64.1 0.2 reshape.123
  64.3 0.1 copy.41
  64.4 0.2 reshape.124.trunk_ref
  64.5 0.0 copy-done.2
  64.6 0.0 copy-done.3
  64.6 0.0 copy-start.6
  64.6 1.0 shard_map.116
  65.6 6.8 %all_to_all.35 = bf16[8,16,128]{2,1,0:T(8,128)(2,1)S(1)} all-to-all(bf16[8,16,128]{2,1,0:T(8,128)(2,1)S(1)} %get-tuple-element.7), channel_id=1, replica_groups=mesh['zl'=2,'y'=8,'xh'=2,'xl'=2,'core'=2,'pair'=4] {'zl','xl','core'}, dimensions={0} | all-to-all | bytes 65536 | tf_op jit(solution)/shard_map/all_to_all | solution.py:308
  72.4 6.9 %all-to-all-start.3 = ((bf16[16,16,384]{2,1,0:T(8,128)(2,1)}), bf16[16,16,384]{2,1,0:T(8,128)(2,1)S(1)}, u32[]{:S(2)}, u32[]{:S(2)}) async-start(bf16[16,16,384]{2,1,0:T(8,128)(2,1)} %get-tuple-element.8), calls=%async_computation.3 | async-start | bytes 393216 | tf_op jit(solution)/shard_map/all_to_all | solution.py:308
  79.3 0.0 copy-done.6
  79.3 0.2 copy.38
  79.5 0.2 copy.39
  79.8 10.2 %all-to-all-done.3 = bf16[16,16,384]{2,1,0:T(8,128)(2,1)S(1)} async-done(((bf16[16,16,384]{2,1,0:T(8,128)(2,1)}), bf16[16,16,384]{2,1,0:T(8,128)(2,1)S(1)}, u32[]{:S(2)}, u32[]{:S(2)}) %all-to-all-start.3) | async-done | bytes 196640 | tf_op jit(solution)/shard_map/all_to_all | solution.py:308
  90.0 1.0 shard_map.117
  91.0 0.0 copy-start.1
  91.0 6.0 %all-to-all-start.4 = ((f32[8,16,256]{2,1,0:T(8,128)}), f32[8,16,256]{2,1,0:T(8,128)S(1)}, u32[]{:S(2)}, u32[]{:S(2)}) async-start(f32[8,16,256]{2,1,0:T(8,128)} %shard_map.117), calls=%async_computation.4 | async-start | bytes 262144 | tf_op jit(solution)/shard_map/all_to_all | solution.py:308
  97.1 0.2 pad_maximum_fusion.w_pair_ref
  97.3 0.0 copy-start.7
  97.3 0.0 copy-start.8
  97.3 4.0 %all-to-all-done.4.parts_ref = f32[8,16,256]{2,1,0:T(8,128)S(1)} async-done(((f32[8,16,256]{2,1,0:T(8,128)}), f32[8,16,256]{2,1,0:T(8,128)S(1)}, u32[]{:S(2)}, u32[]{:S(2)}) %all-to-all-start.4) | async-done | bytes 131104 | tf_op jit(solution)/shard_map/all_to_all | solution.py:308
  101.4 0.0 copy-done.1
  101.4 1.0 shard_map.118
  102.3 3.3 %all-to-all-start.5 = ((bf16[4,32,384]{2,1,0:T(8,128)(2,1)}), bf16[4,32,384]{2,1,0:T(8,128)(2,1)S(1)}, u32[]{:S(2)}, u32[]{:S(2)}) async-start(bf16[4,32,384]{2,1,0:T(8,128)(2,1)} %shard_map.118), calls=%async_computation.5 | async-start | bytes 196608 | tf_op jit(solution)/shard_map/all_to_all | solution.py:308
  105.7 0.0 copy-done.7
  105.7 0.1 copy.35.pair_ref
  105.8 6.8 %all-to-all-done.5.terms_ref = bf16[4,32,384]{2,1,0:T(8,128)(2,1)S(1)} async-done(((bf16[4,32,384]{2,1,0:T(8,128)(2,1)}), bf16[4,32,384]{2,1,0:T(8,128)(2,1)S(1)}, u32[]{:S(2)}, u32[]{:S(2)}) %all-to-all-start.5) | async-done | bytes 98336 | tf_op jit(solution)/shard_map/all_to_all | solution.py:308
  112.7 0.8 shard_map.119
  113.5 7.7 %all-to-all-start.6 = ((f32[128,1,96]{2,1,0:T(1,128)}), f32[128,1,96]{2,1,0:T(1,128)S(1)}, u32[]{:S(2)}, u32[]{:S(2)}) async-start(f32[128,1,96]{2,1,0:T(1,128)} %bitcast.12), calls=%async_computation.6 | async-start | bytes 131072 | tf_op jit(solution)/shard_map/all_to_all | solution.py:308
  121.2 0.1 slice_bitcast_fusion.1
  121.2 10.9 %all-to-all-done.6 = f32[128,1,96]{2,1,0:T(1,128)S(1)} async-done(((f32[128,1,96]{2,1,0:T(1,128)}), f32[128,1,96]{2,1,0:T(1,128)S(1)}, u32[]{:S(2)}, u32[]{:S(2)}) %all-to-all-start.6) | async-done | bytes 49184 | tf_op jit(solution)/shard_map/all_to_all | solution.py:308
  132.1 0.1 copy.37
  132.2 0.0 copy-done.8
  132.2 0.8 fusion.5
  (15 shorter events, 0.2 us)
Async XLA Ops:
  0.6 23.2 %copy-start = (bf16[60,768]{1,0:T(8,128)(2,1)S(1)}, bf16[60,768]{1,0:T(8,128)(2,1)}, u32[]{:S(2)}) copy-start(bf16[60,768]{1,0:T(8,128)(2,1)} %param.11) | copy-start | bytes 276484
  1.4 23.4 %collective-permute-start = (s32[256]{0:T(256)S(1)}, s32[256]{0:T(256)S(1)}, u32[]{:S(2)}, u32[]{:S(2)}) collective-permute-start(s32[256]{0:T(256)S(1)} %get-tuple-element.18), channel_id=1, source_target_pairs={{0,4},{4,8},{8,12},{12,16},{16,20},{20,24},{24,28},{28,32},{32,36}... | collective-permute-start | bytes 3080 | tf_op jit(solution)/shard_map/ppermute | solution.py:322
  5.9 18.9 %collective-permute-start.1 = (s32[256]{0:T(256)S(1)}, s32[256]{0:T(256)S(1)}, u32[]{:S(2)}, u32[]{:S(2)}) collective-permute-start(s32[256]{0:T(256)S(1)} %get-tuple-element.19), channel_id=1, source_target_pairs={{4,0},{8,4},{12,8},{16,12},{20,16},{24,20},{28,24},{32,28},{36,32}... | collective-permute-start | bytes 3080 | tf_op jit(solution)/shard_map/ppermute | solution.py:323
  11.5 0.7 copy-start.4
  13.2 31.1 %all-to-all-start = ((bf16[128,15,96]{2,1,0:T(8,128)(2,1)}), bf16[128,15,96]{2,1,0:T(8,128)(2,1)S(1)}, u32[]{:S(2)}, u32[]{:S(2)}) async-start(bf16[128,15,96]{2,1,0:T(8,128)(2,1)} %shard_map.114), calls=%async_computation | async-start | bytes 1048576 | tf_op jit(solution)/shard_map/all_to_all | solution.py:308
  44.5 11.4 %copy-start.5 = (bf16[1536,192]{0,1:T(8,128)(2,1)S(1)}, bf16[1536,192]{0,1:T(8,128)(2,1)}, u32[]{:S(2)}) copy-start(bf16[1536,192]{0,1:T(8,128)(2,1)} %param.15) | copy-start | bytes 1769476
  46.0 18.1 %all-to-all-start.1 = ((bf16[32,2,384]{2,1,0:T(2,128)(2,1)}), bf16[32,2,384]{2,1,0:T(2,128)(2,1)S(1)}, u32[]{:S(2)}, u32[]{:S(2)}) async-start(bf16[32,2,384]{2,1,0:T(2,128)(2,1)} %shard_map.115), calls=%async_computation.1 | async-start | bytes 98304 | tf_op jit(solution)/shard_map/all_to_all | solution.py:308
  55.9 8.6 %copy-start.2 = (bf16[1536,128]{1,0:T(8,128)(2,1)S(1)}, bf16[1536,128]{1,0:T(8,128)(2,1)}, u32[]{:S(2)}) copy-start(bf16[1536,128]{1,0:T(8,128)(2,1)} %w_query_ref.1) | copy-start | bytes 1179652
  55.9 8.6 %copy-start.3 = (bf16[1536,128]{1,0:T(8,128)(2,1)S(1)}, bf16[1536,128]{1,0:T(8,128)(2,1)}, u32[]{:S(2)}) copy-start(bf16[1536,128]{1,0:T(8,128)(2,1)} %w_key_ref.1) | copy-start | bytes 1179652
  64.6 14.7 %copy-start.6 = (bf16[2,1536,32]{1,2,0:T(8,128)(2,1)S(1)}, bf16[2,1536,32]{1,2,0:T(8,128)(2,1)}, u32[]{:S(2)}) copy-start(bf16[2,1536,32]{1,2,0:T(8,128)(2,1)} %param.17) | copy-start | bytes 589828
  72.4 17.6 %all-to-all-start.3 = ((bf16[16,16,384]{2,1,0:T(8,128)(2,1)}), bf16[16,16,384]{2,1,0:T(8,128)(2,1)S(1)}, u32[]{:S(2)}, u32[]{:S(2)}) async-start(bf16[16,16,384]{2,1,0:T(8,128)(2,1)} %get-tuple-element.8), calls=%async_computation.3 | async-start | bytes 393216 | tf_op jit(solution)/shard_map/all_to_all | solution.py:308
  91.0 10.3 %copy-start.1 = (bf16[192,1536]{1,0:T(8,128)(2,1)S(1)}, bf16[192,1536]{1,0:T(8,128)(2,1)}, u32[]{:S(2)}) copy-start(bf16[192,1536]{1,0:T(8,128)(2,1)} %w_out_ref.1) | copy-start | bytes 1769476
  91.0 10.3 %all-to-all-start.4 = ((f32[8,16,256]{2,1,0:T(8,128)}), f32[8,16,256]{2,1,0:T(8,128)S(1)}, u32[]{:S(2)}, u32[]{:S(2)}) async-start(f32[8,16,256]{2,1,0:T(8,128)} %shard_map.117), calls=%async_computation.4 | async-start | bytes 262144 | tf_op jit(solution)/shard_map/all_to_all | solution.py:308
  97.3 8.4 %copy-start.7 = (bf16[1,128,32]{1,2,0:T(8,128)(2,1)S(1)}, bf16[1,128,32]{1,2,0:T(8,128)(2,1)}, u32[]{:S(2)}) copy-start(bf16[1,128,32]{1,2,0:T(8,128)(2,1)} %param.19) | copy-start | bytes 24580
  97.3 34.9 %copy-start.8 = (bf16[18,32]{1,0:T(8,128)(2,1)S(1)}, bf16[18,32]{1,0:T(8,128)(2,1)}, u32[]{:S(2)}) copy-start(bf16[18,32]{1,0:T(8,128)(2,1)} %param.18) | copy-start | bytes 3460
  102.3 10.3 %all-to-all-start.5 = ((bf16[4,32,384]{2,1,0:T(8,128)(2,1)}), bf16[4,32,384]{2,1,0:T(8,128)(2,1)S(1)}, u32[]{:S(2)}, u32[]{:S(2)}) async-start(bf16[4,32,384]{2,1,0:T(8,128)(2,1)} %shard_map.118), calls=%async_computation.5 | async-start | bytes 196608 | tf_op jit(solution)/shard_map/all_to_all | solution.py:308
  113.5 18.6 %all-to-all-start.6 = ((f32[128,1,96]{2,1,0:T(1,128)}), f32[128,1,96]{2,1,0:T(1,128)S(1)}, u32[]{:S(2)}, u32[]{:S(2)}) async-start(f32[128,1,96]{2,1,0:T(1,128)} %bitcast.12), calls=%async_computation.6 | async-start | bytes 131072 | tf_op jit(solution)/shard_map/all_to_all | solution.py:308

commit v6 on v5

--- a/solution.py
+++ b/solution.py
@@ -2,6 +2,7 @@
 
 import jax
 import jax.numpy as jnp
+import numpy as np
 from jax import lax
 from jax.experimental import pallas as pl
 from jax.experimental.pallas import tpu as pltpu
@@ -19,8 +20,8 @@
 SIZES = {"zl": 2, "y": 8, "xh": 2, "xl": 2, "core": 2, "pair": 4}
 SEQ = ("zl", "y", "xh", "xl", "core")
 SHARE = ("zl", "xl", "core")
-SPREAD = ("zl", "xl", "core")
-LINE = ("y", "xh")
+SPREAD = ("xh", "xl", "core")
+LINE = ("zl", "y")
 N_SEQ = math.prod(SIZES[name] for name in SEQ)
 N_SHARE = math.prod(SIZES[name] for name in SHARE)
 N_PAIR = SIZES["pair"]
@@ -46,7 +47,7 @@
     return 0.5 * x * (1.0 + jnp.tanh(math.sqrt(2.0 / math.pi) * (x + 0.044715 * (x * x * x))))
 
 
-def stem_kernel(place_ref, codes_ref, weight_ref, out_ref):
+def stem_kernel(place_ref, codes_ref, weight_ref, order_ref, out_ref):
     length = codes_ref.shape[1]
     codes = jnp.broadcast_to(codes_ref[...], (16, length))
     first = SIDE - 2 * STEM_POOL + KS_STEM // 2
@@ -55,7 +56,14 @@
     onehot = jnp.concatenate(
         [(shifted == base + 1).astype(jnp.float32) for base in range(4)], axis=0
     ).astype(jnp.bfloat16)
-    weight = weight_ref[...]
+    taps = weight_ref.shape[0]
+    row = lax.broadcasted_iota(jnp.int32, (64, taps), 0)
+    column = lax.broadcasted_iota(jnp.int32, (64, taps), 1)
+    picked = (column == (KS_STEM - 1 - row % 16) * 4 + row // 16) & (row % 16 < KS_STEM)
+    picked = picked.astype(jnp.float32).astype(jnp.bfloat16)
+    weight = jnp.dot(picked, weight_ref[...], preferred_element_type=jnp.float32)
+    weight = jnp.dot(weight.astype(jnp.bfloat16), order_ref[...], preferred_element_type=jnp.float32)
+    weight = weight.astype(jnp.bfloat16)
     step = 6
     for at in range(0, EXT, step):
         part = onehot[:, at * STEM_POOL : (at + step) * STEM_POOL]
@@ -71,18 +79,22 @@
     out_ref[EXT:EXT_PAD, :] = jnp.zeros((EXT_PAD - EXT, weight.shape[1]), jnp.float32)
 
 
-def stem(place, codes, weight):
+def stem(place, codes, weight, order):
     return pl.pallas_call(
         stem_kernel,
         out_shape=jax.ShapeDtypeStruct((EXT_PAD, weight.shape[1]), jnp.float32),
-        in_specs=[pl.BlockSpec(memory_space=pltpu.SMEM)] + whole(2),
+        in_specs=[pl.BlockSpec(memory_space=pltpu.SMEM)] + whole(3),
         out_specs=whole(1)[0],
         compiler_params=params(),
         cost_estimate=pl.CostEstimate(flops=40_000_000_000, bytes_accessed=200000, transcendentals=0),
-    )(place, codes, weight)
-
-
-def pack_kernel(weight_ref, out_ref, wide):
+    )(place, codes, weight, order)
+
+
+def start_kernel(weight_ref, tokens_ref, out_ref, codes_ref, head_ref, tail_ref, wide):
+    codes = tokens_ref[...] + 1
+    codes_ref[...] = codes
+    head_ref[...] = codes[: head_ref.shape[0]]
+    tail_ref[...] = codes[codes.shape[0] - tail_ref.shape[0] :]
     taps, width = weight_ref.shape
     share = width // N_SHARE
     half = taps // 2
@@ -110,16 +122,22 @@
         out_ref[place] = blocks[index]
 
 
-def pack(weight):
+def start(weight, tokens):
     taps, width = weight.shape
-    return pl.pallas_call(
-        pack_kernel,
-        out_shape=jax.ShapeDtypeStruct((N_SEQ, taps // 2, 2 * width // N_SHARE), jnp.bfloat16),
-        in_specs=whole(1),
-        out_specs=whole(1)[0],
+    ends = jax.ShapeDtypeStruct((SIDE // HQK, HQK), jnp.int32)
+    return pl.pallas_call(
+        start_kernel,
+        out_shape=(
+            jax.ShapeDtypeStruct((N_SEQ, taps // 2, 2 * width // N_SHARE), jnp.bfloat16),
+            jax.ShapeDtypeStruct(tokens.shape, jnp.int32),
+            ends,
+            ends,
+        ),
+        in_specs=whole(2),
+        out_specs=tuple(whole(4)),
         scratch_shapes=[pltpu.VMEM((width // HQK, taps + 2, HQK), jnp.float32)],
         compiler_params=params(),
-    )(weight)
+    )(weight, tokens)
 
 
 def conv_kernel(section_ref, weight_ref, out_ref, wide, act, best):
@@ -174,8 +192,7 @@
         jnp.dot(trunk, ref[...], preferred_element_type=jnp.float32).astype(jnp.bfloat16)
         for ref in (w_query_ref, w_key_ref, w_value_ref)
     ]
-    for index in range(N_SPREAD):
-        query_ref[index] = query
+    query_ref[...] = query
     rest = jnp.zeros((trunk.shape[0], kv_ref.shape[2] - HQK - HV), jnp.bfloat16)
     for index in range(N_LINE):
         kv_ref[index, :, :HQK] = key
@@ -188,7 +205,7 @@
     return pl.pallas_call(
         project_kernel,
         out_shape=(
-            jax.ShapeDtypeStruct((N_SPREAD, count, HQK), jnp.bfloat16),
+            jax.ShapeDtypeStruct((count, HQK), jnp.bfloat16),
             jax.ShapeDtypeStruct((N_LINE, count, 3 * HQK), jnp.bfloat16),
         ),
         in_specs=whole(4),
@@ -197,7 +214,7 @@
     )(trunk, w_query, w_key, w_value)
 
 
-def attention_kernel(query_ref, kv_ref, out_ref):
+def attention_kernel(place_ref, query_ref, kv_ref, out_ref):
     scale = 1.0 / math.sqrt(HQK)
     scores = (
         lax.dot_general(
@@ -214,18 +231,21 @@
     mixed = jnp.dot(expo.astype(jnp.bfloat16), kv_ref[:, HQK:], preferred_element_type=jnp.float32)
     lane = lax.broadcasted_iota(jnp.int32, mixed.shape, 1)
     mixed = jnp.where(lane == HV, top, jnp.where(lane == HV + 1, total, mixed))
-    out_ref[...] = mixed.reshape(out_ref.shape)
-
-
-def attention(query, kv, groups):
+    groups, count, _ = out_ref.shape
+    for index in range(groups):
+        out_ref[place_ref[0] ^ index] = mixed[index * count : (index + 1) * count, :]
+
+
+def attention(place, query, kv):
+    groups = N_SPREAD
     count, width = query.shape[0] // groups, kv.shape[1] - HQK
     return pl.pallas_call(
         attention_kernel,
         out_shape=jax.ShapeDtypeStruct((groups, count, width), jnp.float32),
-        in_specs=whole(2),
+        in_specs=[pl.BlockSpec(memory_space=pltpu.SMEM)] + whole(2),
         out_specs=whole(1)[0],
         compiler_params=params(),
-    )(query, kv)
+    )(place, query, kv)
 
 
 def combine_kernel(parts_ref, w_out_ref, out_ref):
@@ -240,11 +260,11 @@
     count = term.shape[0]
     tail = jnp.concatenate(
         [mean[:, c * width : (c + 1) * width] for c in range(N_PAIR)]
-        + [jnp.zeros((count - N_PAIR, width), jnp.float32)],
+        + [jnp.zeros((8 - N_PAIR, width), jnp.float32)],
         axis=0,
-    ).astype(jnp.bfloat16)
+    )
     for c in range(N_PAIR):
-        out_ref[c, :count, :] = term[:, c * width : (c + 1) * width].astype(jnp.bfloat16)
+        out_ref[c, :count, :] = term[:, c * width : (c + 1) * width]
         out_ref[c, count:, :] = tail
 
 
@@ -253,7 +273,7 @@
     width = w_out.shape[1] // N_PAIR
     return pl.pallas_call(
         combine_kernel,
-        out_shape=jax.ShapeDtypeStruct((N_PAIR, 2 * count, width), jnp.bfloat16),
+        out_shape=jax.ShapeDtypeStruct((N_PAIR, count + 8, width), jnp.float32),
         in_specs=whole(2),
         out_specs=whole(1)[0],
         compiler_params=params(),
@@ -262,7 +282,7 @@
 
 def close_kernel(terms_ref, own_ref, trunk_ref, w_pair_ref, pair_ref, seq_ref, rows_ref, every_ref):
     count, width = own_ref.shape
-    total = jnp.sum(terms_ref[...].astype(jnp.float32), axis=0)
+    total = jnp.sum(terms_ref[...], axis=0)
     seq_ref[...] = (own_ref[...].astype(jnp.float32) + total[:count, :]).astype(jnp.bfloat16)
     trunk_mean = jnp.sum(trunk_ref[...].astype(jnp.float32), axis=0, keepdims=True) * (1.0 / PAIR_POOL)
     rows = None
@@ -314,21 +334,20 @@
 
     taps, width = w_conv.shape
     share = width // N_SHARE
-    blocks = exchange(pack(w_conv), SEQ)
+    blocks, codes, head, tail = start(w_conv, tokens.reshape(-1, HQK))
+    blocks = exchange(blocks, SEQ)
     conv_weight = blocks.reshape(N_SEQ * blocks.shape[1], blocks.shape[2])
 
-    codes = tokens + 1
     ends = N_SEQ - 1
-    left = lax.ppermute(codes[-SIDE:], SEQ, [(i, i + 1) for i in range(ends)])
-    right = lax.ppermute(codes[:SIDE], SEQ, [(i + 1, i) for i in range(ends)])
-    codes = jnp.concatenate([left, codes, right])[None, :]
-    source = jnp.arange(w_stem.shape[1]).reshape(2, -1)
-    source = (2 * (source % source.shape[1]) + jnp.arange(2)[:, None]).reshape(-1)
-    order = (jnp.arange(w_stem.shape[1])[:, None] == source[None, :]).astype(jnp.bfloat16)
-    stem_weight = jnp.dot(w_stem, order, preferred_element_type=jnp.float32).astype(jnp.bfloat16)
-    stem_weight = stem_weight.reshape(KS_STEM, 4, -1)[::-1].transpose(1, 0, 2)
-    stem_weight = jnp.pad(stem_weight, ((0, 0), (0, 1), (0, 0))).reshape(64, -1)
-    section = stem(place.astype(jnp.int32)[None], codes, stem_weight).astype(jnp.bfloat16)
+    left = lax.ppermute(tail, SEQ, [(i, i + 1) for i in range(ends)])
+    right = lax.ppermute(head, SEQ, [(i + 1, i) for i in range(ends)])
+    codes = jnp.concatenate([left, codes, right]).reshape(1, -1)
+    half = w_stem.shape[1] // 2
+    order = np.zeros((2 * half, 2 * half), np.float32)
+    order[2 * np.arange(half), np.arange(half)] = 1
+    order[2 * np.arange(half) + 1, half + np.arange(half)] = 1
+    order = jnp.asarray(order, jnp.bfloat16)
+    section = stem(place.astype(jnp.int32)[None], codes, w_stem, order).astype(jnp.bfloat16)
     sections = lax.all_gather(section, SHARE, axis=0, tiled=False)
 
     parts = exchange(conv(sections, conv_weight), SHARE + ("pair",))
@@ -337,9 +356,12 @@
     trunk = trunk.reshape(count, N_PAIR * width)
 
     query, kv = project(trunk, w_query, w_key, w_value)
-    query = exchange(query, SPREAD).reshape(N_SPREAD * count, HQK)
+    for name in reversed(SPREAD):
+        other = lax.ppermute(query, name, [(0, 1), (1, 0)])
+        query = jnp.concatenate([query, other], axis=0)
     kv = exchange(kv, LINE).reshape(N_LINE * count, kv.shape[2])
-    parts = exchange(attention(query, kv, N_SPREAD), SPREAD)
+    spread = lax.axis_index(SPREAD).astype(jnp.int32)[None]
+    parts = exchange(attention(spread, query, kv), SPREAD)
     terms = exchange(combine(parts, w_out), ("pair",))
 
     own = lax.dynamic_slice_in_dim(trunk, pair_place * width, width, 1)

time: 134 us -> 137 us (1.022)
  starting transfers between devices: 54.4 us -> 62 us
  blocking collectives: 22.3 us -> 18.9 us
  waiting for transfers between devices: 42.1 us -> 40.1 us
  local copies, waits for them, and re-layouts: 2.81 us -> 4.39 us
    all_to_all x6, waiting for transfers between devices: 42.1 us -> 32.3 us  [exchange(): return lax.all_to_all(blocks, axes, split_axis=0, concat_axis=0, tiled=True)]
    ppermute x2 -> x5, waiting for transfers between devices: 0.01 us -> 7.82 us  [the longest x3 4.49 us: on_device(): other = lax.ppermute(query, name, [(0, 1), (1, 0)])]
    all_to_all x1 -> x0, blocking collectives: 6.78 us -> none  [exchange(): return lax.all_to_all(blocks, axes, split_axis=0, concat_axis=0, tiled=True)]
    all_to_all x6, starting transfers between devices: 44.3 us -> 50.1 us  [exchange(): return lax.all_to_all(blocks, axes, split_axis=0, concat_axis=0, tiled=True)]
    all_gather x1, blocking collectives: 15.5 us -> 18.9 us  [on_device(): sections = lax.all_gather(section, SHARE, axis=0, tiled=False)]
    unnamed x22 -> x27, local copies, waits for them, and re-layouts: 1.62 us -> 3.59 us
    ppermute x2 -> x5, starting transfers between devices: 10.1 us -> 11.9 us  [the longest x3 6.42 us: on_device(): other = lax.ppermute(query, name, [(0, 1), (1, 0)])]
  transfers between devices with their start and end apart: 8 -> 11, of which waited for: 6 -> 8; matrix products, arithmetic and copies ran while one was open for 2% -> 1% of each run, Pallas kernels for 2% -> 1%
where the time goes in v6:
time: 137 us; the launch traced here: 136 us
  starting transfers between devices  62 us (45%)
  waiting for transfers between devices  40.1 us (29%)
  blocking collectives  18.9 us (14%)
  Pallas kernels  8.39 us (6%)
  local copies, waits for them, and re-layouts  4.39 us (3%)
    all_to_all x6, starting transfers between devices, exchange(): return lax.all_to_all(blocks, axes, split_axis=0, concat_axis=0, tiled=True)  50.1 us
    all_to_all x6, waiting for transfers between devices, exchange(): return lax.all_to_all(blocks, axes, split_axis=0, concat_axis=0, tiled=True)  32.3 us
    all_gather x1, blocking collectives, on_device(): sections = lax.all_gather(section, SHARE, axis=0, tiled=False)  18.9 us
    ppermute x3, starting transfers between devices, on_device(): other = lax.ppermute(query, name, [(0, 1), (1, 0)])  6.42 us
    ppermute x3, waiting for transfers between devices, on_device(): other = lax.ppermute(query, name, [(0, 1), (1, 0)])  4.49 us
    unnamed x27, local copies, waits for them, and re-layouts  3.59 us
    ppermute x1, starting transfers between devices, on_device(): left = lax.ppermute(tail, SEQ, [(i, i + 1) for i in range(ends)])  3.54 us
    ppermute x1, waiting for transfers between devices, on_device(): right = lax.ppermute(head, SEQ, [(i + 1, i) for i in range(ends)])  3.33 us
  transfers between devices with their start and end apart: 11, of which 8 were waited for; matrix products, arithmetic and copies ran while one was open for 1% of the time, Pallas kernels for 1%

profile of v6, /device:TPU:1, one launch (start us, length us, event | category | flops | bytes accessed | tf_op | source)
XLA Modules:
  0.0 135.8 jit_solution(12355828701568898127)
XLA Ops:
  0.6 0.0 copy-start
  0.6 0.0 copy-start.4
  0.7 0.7 copy-done.4
  1.4 0.0 copy-start.5
  1.4 0.7 copy-done.5
  2.1 0.0 copy-start.6
  2.1 1.0 shard_map.122
  3.1 14.2 %all-to-all-start = ((bf16[128,15,96]{2,1,0:T(8,128)(2,1)}), bf16[128,15,96]{2,1,0:T(8,128)(2,1)S(1)}, u32[]{:S(2)}, u32[]{:S(2)}) async-start(bf16[128,15,96]{2,1,0:T(8,128)(2,1)} %get-tuple-element.14), calls=%async_computation | async-start | bytes 1048576 | tf_op jit(solution)/shard_map/all_to_all | solution.py:328
  17.3 3.5 %collective-permute-start = (s32[2,128]{1,0:T(2,128)S(1)}, s32[2,128]{1,0:T(2,128)S(1)}, u32[]{:S(2)}, u32[]{:S(2)}) collective-permute-start(s32[2,128]{1,0:T(2,128)S(1)} %get-tuple-element.11), channel_id=1, source_target_pairs={{0,4},{4,8},{8,12},{12,16},{16,20},{20,24},{24,28},{28,32},{32,36}... | collective-permute-start | bytes 3080 | tf_op jit(solution)/shard_map/ppermute | solution.py:342
  20.9 1.9 %collective-permute-start.1 = (s32[2,128]{1,0:T(2,128)S(1)}, s32[2,128]{1,0:T(2,128)S(1)}, u32[]{:S(2)}, u32[]{:S(2)}) collective-permute-start(s32[2,128]{1,0:T(2,128)S(1)} %get-tuple-element.13), channel_id=1, source_target_pairs={{4,0},{8,4},{12,8},{16,12},{20,16},{24,20},{28,24},{32,28},{36,32}... | collective-permute-start | bytes 3080 | tf_op jit(solution)/shard_map/ppermute | solution.py:343
  22.8 0.0 collective-permute-done
  22.8 3.3 %collective-permute-done.1 = s32[2,128]{1,0:T(2,128)S(1)} collective-permute-done((s32[2,128]{1,0:T(2,128)S(1)}, s32[2,128]{1,0:T(2,128)S(1)}, u32[]{:S(2)}, u32[]{:S(2)}) %collective-permute-start.1) | collective-permute-done | bytes 1056 | tf_op jit(solution)/shard_map/ppermute | solution.py:343
  26.2 0.0 copy-done.6
  26.2 0.0 copy-start.7
  26.2 1.3 copy-done.7
  27.4 2.0 %shard_map.123 = f32[40,768]{1,0:T(8,128)S(1)} custom-call(s32[1]{0:T(128)} %bitcast.1.place_ref, s32[1,2560]{1,0:T(1,128)S(1)} %bitcast.34, bf16[60,768]{1,0:T(8,128)(2,1)S(1)} %copy-done.6, bf16[768,768]{1,0:T(8,128)(2,1)S(1)} %copy-done.7), custom_call_target="tpu_custom_call" | custom-call | flops 40000000000 | bytes 200000 | tf_op jit(solution)/shard_map/pallas_call | solution.py:83
  29.4 18.9 %all-gather = bf16[320,768]{1,0:T(8,128)(2,1)S(1)} all-gather(bf16[40,768]{1,0:T(8,128)(2,1)S(1)} %convert_element_type.132), channel_id=2, replica_groups=mesh['zl'=2,'y'=8,'xh'=2,'xl'=2,'core'=2,'pair'=4] {'zl','xl','core'}, dimensions={0}, use_global_device_ids=true | all-gather | bytes 552960 | tf_op jit(solution)/shard_map/all_gather | solution.py:351
  48.3 0.0 copy-start.8
  48.4 0.0 all-to-all-done
  48.4 0.2 reshape.81.weight_ref
  48.5 1.5 %shard_map.124 = bf16[32,2,384]{2,1,0:T(2,128)(2,1)} custom-call(bf16[8,40,768]{2,1,0:T(8,128)(2,1)S(1)} %bitcast.32, bf16[1920,96]{1,0:T(8,128)(2,1)S(1)} %reshape.81.weight_ref), custom_call_target="tpu_custom_call" | custom-call | tf_op jit(solution)/shard_map/pallas_call | solution.py:175
  50.1 0.0 copy-start.2
  50.1 0.0 copy-start.3
  50.1 9.9 %all-to-all-start.1 = ((bf16[32,2,384]{2,1,0:T(2,128)(2,1)}), bf16[32,2,384]{2,1,0:T(2,128)(2,1)S(1)}, u32[]{:S(2)}, u32[]{:S(2)}) async-start(bf16[32,2,384]{2,1,0:T(2,128)(2,1)} %shard_map.124), calls=%async_computation.1 | async-start | bytes 98304 | tf_op jit(solution)/shard_map/all_to_all | solution.py:328
  60.0 0.0 copy-done.8
  60.0 0.3 copy.30.w_value_ref
  60.2 7.9 %all-to-all-done.1 = bf16[32,2,384]{2,1,0:T(2,128)(2,1)S(1)} async-done(((bf16[32,2,384]{2,1,0:T(2,128)(2,1)}), bf16[32,2,384]{2,1,0:T(2,128)(2,1)S(1)}, u32[]{:S(2)}, u32[]{:S(2)}) %all-to-all-start.1) | async-done | bytes 49184 | tf_op jit(solution)/shard_map/all_to_all | solution.py:328
  68.2 0.2 reshape.82
  68.3 0.1 copy.41
  68.4 0.0 copy-start.9
  68.4 0.2 reshape.83.trunk_ref
  68.6 0.0 copy-done.2
  68.6 0.0 copy-done.3
  68.7 1.0 shard_map.125
  69.7 2.3 %collective-permute-start.2 = (bf16[16,128]{1,0:T(8,128)(2,1)S(1)}, bf16[16,128]{1,0:T(8,128)(2,1)S(1)}, u32[]{:S(2)}, u32[]{:S(2)}) collective-permute-start(bf16[16,128]{1,0:T(8,128)(2,1)S(1)} %get-tuple-element.15), channel_id=1, source_target_pairs={{0,4},{4,0},{1,5},{5,1},{2,6},{6,2},{3,7},{7,3},{8,12},{12,8},{9,1... | collective-permute-start | bytes 12296 | tf_op jit(solution)/shard_map/ppermute | solution.py:360
  72.0 0.8 collective-permute-done.2
  72.8 2.2 %collective-permute-start.3 = (bf16[32,128]{1,0:T(8,128)(2,1)S(1)}, bf16[32,128]{1,0:T(8,128)(2,1)S(1)}, u32[]{:S(2)}, u32[]{:S(2)}) collective-permute-start(bf16[32,128]{1,0:T(8,128)(2,1)S(1)} %pad_maximum_fusion.3), channel_id=1, source_target_pairs={{0,8},{8,0},{1,9},{9,1},{2,10},{10,2},{3,11},{11,3},{4,12},{12,4},... | collective-permute-start | bytes 24584 | tf_op jit(solution)/shard_map/ppermute | solution.py:360
  75.0 6.5 %all-to-all-start.2 = ((bf16[16,16,384]{2,1,0:T(8,128)(2,1)}), bf16[16,16,384]{2,1,0:T(8,128)(2,1)S(1)}, u32[]{:S(2)}, u32[]{:S(2)}) async-start(bf16[16,16,384]{2,1,0:T(8,128)(2,1)} %get-tuple-element.16), calls=%async_computation.2 | async-start | bytes 393216 | tf_op jit(solution)/shard_map/all_to_all | solution.py:328
  81.5 0.0 collective-permute-done.3
  81.5 1.9 %collective-permute-start.4 = (bf16[64,128]{1,0:T(8,128)(2,1)S(1)}, bf16[64,128]{1,0:T(8,128)(2,1)S(1)}, u32[]{:S(2)}, u32[]{:S(2)}) collective-permute-start(bf16[64,128]{1,0:T(8,128)(2,1)S(1)} %pad_maximum_fusion.2), channel_id=1, source_target_pairs={{0,16},{16,0},{1,17},{17,1},{2,18},{18,2},{3,19},{19,3},{4,20},{20... | collective-permute-start | bytes 49160 | tf_op jit(solution)/shard_map/ppermute | solution.py:360
  83.4 0.0 copy-done.9
  83.4 0.2 copy.36
  83.7 0.0 copy-start.10
  83.7 0.0 copy-start.1
  83.7 0.2 copy.37
  83.9 3.7 %collective-permute-done.4 = bf16[64,128]{1,0:T(8,128)(2,1)S(1)} collective-permute-done((bf16[64,128]{1,0:T(8,128)(2,1)S(1)}, bf16[64,128]{1,0:T(8,128)(2,1)S(1)}, u32[]{:S(2)}, u32[]{:S(2)}) %collective-permute-start.4) | collective-permute-done | bytes 16416 | tf_op jit(solution)/shard_map/ppermute | solution.py:360
  87.6 1.3 all-to-all-done.2
  89.0 1.0 shard_map.126
  90.0 5.8 %all-to-all-start.3 = ((f32[8,16,256]{2,1,0:T(8,128)}), f32[8,16,256]{2,1,0:T(8,128)S(1)}, u32[]{:S(2)}, u32[]{:S(2)}) async-start(f32[8,16,256]{2,1,0:T(8,128)} %shard_map.126), calls=%async_computation.3 | async-start | bytes 262144 | tf_op jit(solution)/shard_map/all_to_all | solution.py:328
  95.8 0.2 pad_maximum_fusion.w_pair_ref
  96.0 0.0 copy-done.10
  96.0 0.1 copy.33.pair_ref
  96.1 4.9 %all-to-all-done.3.parts_ref = f32[8,16,256]{2,1,0:T(8,128)S(1)} async-done(((f32[8,16,256]{2,1,0:T(8,128)}), f32[8,16,256]{2,1,0:T(8,128)S(1)}, u32[]{:S(2)}, u32[]{:S(2)}) %all-to-all-start.3) | async-done | bytes 131104 | tf_op jit(solution)/shard_map/all_to_all | solution.py:328
  101.1 0.0 copy-done.1
  101.1 1.0 shard_map.127
  102.1 3.3 %all-to-all-start.4 = ((f32[4,24,384]{2,1,0:T(8,128)}), f32[4,24,384]{2,1,0:T(8,128)S(1)}, u32[]{:S(2)}, u32[]{:S(2)}) async-start(f32[4,24,384]{2,1,0:T(8,128)} %shard_map.127), calls=%async_computation.4 | async-start | bytes 294912 | tf_op jit(solution)/shard_map/all_to_all | solution.py:328
  105.5 7.4 %all-to-all-done.4.terms_ref = f32[4,24,384]{2,1,0:T(8,128)S(1)} async-done(((f32[4,24,384]{2,1,0:T(8,128)}), f32[4,24,384]{2,1,0:T(8,128)S(1)}, u32[]{:S(2)}, u32[]{:S(2)}) %all-to-all-start.4) | async-done | bytes 147488 | tf_op jit(solution)/shard_map/all_to_all | solution.py:328
  112.8 0.8 shard_map.128
  113.7 10.4 %all-to-all-start.5 = ((f32[128,1,96]{2,1,0:T(1,128)}), f32[128,1,96]{2,1,0:T(1,128)S(1)}, u32[]{:S(2)}, u32[]{:S(2)}) async-start(f32[128,1,96]{2,1,0:T(1,128)} %bitcast.10), calls=%async_computation.5 | async-start | bytes 131072 | tf_op jit(solution)/shard_map/all_to_all | solution.py:328
  124.1 0.1 slice_bitcast_fusion.1
  124.2 10.7 %all-to-all-done.5 = f32[128,1,96]{2,1,0:T(1,128)S(1)} async-done(((f32[128,1,96]{2,1,0:T(1,128)}), f32[128,1,96]{2,1,0:T(1,128)S(1)}, u32[]{:S(2)}, u32[]{:S(2)}) %all-to-all-start.5) | async-done | bytes 49184 | tf_op jit(solution)/shard_map/all_to_all | solution.py:328
  134.9 0.1 copy.35
  135.0 0.0 copy-done
  135.0 0.8 fusion.1
  (9 shorter events, 0.1 us)
Async XLA Ops:
  0.6 134.4 %copy-start = (bf16[18,32]{1,0:T(8,128)(2,1)S(1)}, bf16[18,32]{1,0:T(8,128)(2,1)}, u32[]{:S(2)}) copy-start(bf16[18,32]{1,0:T(8,128)(2,1)} %param.19) | copy-start | bytes 3460
  0.6 0.7 copy-start.4
  1.4 0.7 copy-start.5
  2.1 24.1 %copy-start.6 = (bf16[60,768]{1,0:T(8,128)(2,1)S(1)}, bf16[60,768]{1,0:T(8,128)(2,1)}, u32[]{:S(2)}) copy-start(bf16[60,768]{1,0:T(8,128)(2,1)} %weight_ref.3) | copy-start | bytes 276484
  3.1 45.3 %all-to-all-start = ((bf16[128,15,96]{2,1,0:T(8,128)(2,1)}), bf16[128,15,96]{2,1,0:T(8,128)(2,1)S(1)}, u32[]{:S(2)}, u32[]{:S(2)}) async-start(bf16[128,15,96]{2,1,0:T(8,128)(2,1)} %get-tuple-element.14), calls=%async_computation | async-start | bytes 1048576 | tf_op jit(solution)/shard_map/all_to_all | solution.py:328
  17.3 5.5 %collective-permute-start = (s32[2,128]{1,0:T(2,128)S(1)}, s32[2,128]{1,0:T(2,128)S(1)}, u32[]{:S(2)}, u32[]{:S(2)}) collective-permute-start(s32[2,128]{1,0:T(2,128)S(1)} %get-tuple-element.11), channel_id=1, source_target_pairs={{0,4},{4,8},{8,12},{12,16},{16,20},{20,24},{24,28},{28,32},{32,36}... | collective-permute-start | bytes 3080 | tf_op jit(solution)/shard_map/ppermute | solution.py:342
  20.9 5.3 %collective-permute-start.1 = (s32[2,128]{1,0:T(2,128)S(1)}, s32[2,128]{1,0:T(2,128)S(1)}, u32[]{:S(2)}, u32[]{:S(2)}) collective-permute-start(s32[2,128]{1,0:T(2,128)S(1)} %get-tuple-element.13), channel_id=1, source_target_pairs={{4,0},{8,4},{12,8},{16,12},{20,16},{24,20},{28,24},{32,28},{36,32}... | collective-permute-start | bytes 3080 | tf_op jit(solution)/shard_map/ppermute | solution.py:343
  26.2 1.3 copy-start.7
  48.3 11.6 %copy-start.8 = (bf16[1536,192]{0,1:T(8,128)(2,1)S(1)}, bf16[1536,192]{0,1:T(8,128)(2,1)}, u32[]{:S(2)}) copy-start(bf16[1536,192]{0,1:T(8,128)(2,1)} %param.16) | copy-start | bytes 1769476
  50.1 18.5 %copy-start.2 = (bf16[1536,128]{1,0:T(8,128)(2,1)S(1)}, bf16[1536,128]{1,0:T(8,128)(2,1)}, u32[]{:S(2)}) copy-start(bf16[1536,128]{1,0:T(8,128)(2,1)} %w_query_ref.1) | copy-start | bytes 1179652
  50.1 18.6 %copy-start.3 = (bf16[1536,128]{1,0:T(8,128)(2,1)S(1)}, bf16[1536,128]{1,0:T(8,128)(2,1)}, u32[]{:S(2)}) copy-start(bf16[1536,128]{1,0:T(8,128)(2,1)} %w_key_ref.1) | copy-start | bytes 1179652
  50.1 18.1 %all-to-all-start.1 = ((bf16[32,2,384]{2,1,0:T(2,128)(2,1)}), bf16[32,2,384]{2,1,0:T(2,128)(2,1)S(1)}, u32[]{:S(2)}, u32[]{:S(2)}) async-start(bf16[32,2,384]{2,1,0:T(2,128)(2,1)} %shard_map.124), calls=%async_computation.1 | async-start | bytes 98304 | tf_op jit(solution)/shard_map/all_to_all | solution.py:328
  68.4 15.0 %copy-start.9 = (bf16[2,1536,32]{1,2,0:T(8,128)(2,1)S(1)}, bf16[2,1536,32]{1,2,0:T(8,128)(2,1)}, u32[]{:S(2)}) copy-start(bf16[2,1536,32]{1,2,0:T(8,128)(2,1)} %param.18) | copy-start | bytes 589828
  69.7 3.1 %collective-permute-start.2 = (bf16[16,128]{1,0:T(8,128)(2,1)S(1)}, bf16[16,128]{1,0:T(8,128)(2,1)S(1)}, u32[]{:S(2)}, u32[]{:S(2)}) collective-permute-start(bf16[16,128]{1,0:T(8,128)(2,1)S(1)} %get-tuple-element.15), channel_id=1, source_target_pairs={{0,4},{4,0},{1,5},{5,1},{2,6},{6,2},{3,7},{7,3},{8,12},{12,8},{9,1... | collective-permute-start | bytes 12296 | tf_op jit(solution)/shard_map/ppermute | solution.py:360
  72.8 8.7 %collective-permute-start.3 = (bf16[32,128]{1,0:T(8,128)(2,1)S(1)}, bf16[32,128]{1,0:T(8,128)(2,1)S(1)}, u32[]{:S(2)}, u32[]{:S(2)}) collective-permute-start(bf16[32,128]{1,0:T(8,128)(2,1)S(1)} %pad_maximum_fusion.3), channel_id=1, source_target_pairs={{0,8},{8,0},{1,9},{9,1},{2,10},{10,2},{3,11},{11,3},{4,12},{12,4},... | collective-permute-start | bytes 24584 | tf_op jit(solution)/shard_map/ppermute | solution.py:360
  75.0 14.0 %all-to-all-start.2 = ((bf16[16,16,384]{2,1,0:T(8,128)(2,1)}), bf16[16,16,384]{2,1,0:T(8,128)(2,1)S(1)}, u32[]{:S(2)}, u32[]{:S(2)}) async-start(bf16[16,16,384]{2,1,0:T(8,128)(2,1)} %get-tuple-element.16), calls=%async_computation.2 | async-start | bytes 393216 | tf_op jit(solution)/shard_map/all_to_all | solution.py:328
  81.5 6.1 %collective-permute-start.4 = (bf16[64,128]{1,0:T(8,128)(2,1)S(1)}, bf16[64,128]{1,0:T(8,128)(2,1)S(1)}, u32[]{:S(2)}, u32[]{:S(2)}) collective-permute-start(bf16[64,128]{1,0:T(8,128)(2,1)S(1)} %pad_maximum_fusion.2), channel_id=1, source_target_pairs={{0,16},{16,0},{1,17},{17,1},{2,18},{18,2},{3,19},{19,3},{4,20},{20... | collective-permute-start | bytes 49160 | tf_op jit(solution)/shard_map/ppermute | solution.py:360
  83.7 12.3 %copy-start.10 = (bf16[1,128,32]{1,2,0:T(8,128)(2,1)S(1)}, bf16[1,128,32]{1,2,0:T(8,128)(2,1)}, u32[]{:S(2)}) copy-start(bf16[1,128,32]{1,2,0:T(8,128)(2,1)} %param.20) | copy-start | bytes 24580
  83.7 17.4 %copy-start.1 = (bf16[192,1536]{1,0:T(8,128)(2,1)S(1)}, bf16[192,1536]{1,0:T(8,128)(2,1)}, u32[]{:S(2)}) copy-start(bf16[192,1536]{1,0:T(8,128)(2,1)} %w_out_ref.1) | copy-start | bytes 1769476
  90.0 11.1 %all-to-all-start.3 = ((f32[8,16,256]{2,1,0:T(8,128)}), f32[8,16,256]{2,1,0:T(8,128)S(1)}, u32[]{:S(2)}, u32[]{:S(2)}) async-start(f32[8,16,256]{2,1,0:T(8,128)} %shard_map.126), calls=%async_computation.3 | async-start | bytes 262144 | tf_op jit(solution)/shard_map/all_to_all | solution.py:328
  102.1 10.7 %all-to-all-start.4 = ((f32[4,24,384]{2,1,0:T(8,128)}), f32[4,24,384]{2,1,0:T(8,128)S(1)}, u32[]{:S(2)}, u32[]{:S(2)}) async-start(f32[4,24,384]{2,1,0:T(8,128)} %shard_map.127), calls=%async_computation.4 | async-start | bytes 294912 | tf_op jit(solution)/shard_map/all_to_all | solution.py:328
  113.7 21.2 %all-to-all-start.5 = ((f32[128,1,96]{2,1,0:T(1,128)}), f32[128,1,96]{2,1,0:T(1,128)S(1)}, u32[]{:S(2)}, u32[]{:S(2)}) async-start(f32[128,1,96]{2,1,0:T(1,128)} %bitcast.10), calls=%async_computation.5 | async-start | bytes 131072 | tf_op jit(solution)/shard_map/all_to_all | solution.py:328

commit v7 on v5

--- a/solution.py
+++ b/solution.py
@@ -19,8 +19,8 @@
 SIZES = {"zl": 2, "y": 8, "xh": 2, "xl": 2, "core": 2, "pair": 4}
 SEQ = ("zl", "y", "xh", "xl", "core")
 SHARE = ("zl", "xl", "core")
-SPREAD = ("zl", "xl", "core")
-LINE = ("y", "xh")
+SPREAD = ("xh", "xl", "core")
+LINE = ("zl", "y")
 N_SEQ = math.prod(SIZES[name] for name in SEQ)
 N_SHARE = math.prod(SIZES[name] for name in SHARE)
 N_PAIR = SIZES["pair"]
@@ -174,8 +174,7 @@
         jnp.dot(trunk, ref[...], preferred_element_type=jnp.float32).astype(jnp.bfloat16)
         for ref in (w_query_ref, w_key_ref, w_value_ref)
     ]
-    for index in range(N_SPREAD):
-        query_ref[index] = query
+    query_ref[...] = query
     rest = jnp.zeros((trunk.shape[0], kv_ref.shape[2] - HQK - HV), jnp.bfloat16)
     for index in range(N_LINE):
         kv_ref[index, :, :HQK] = key
@@ -188,7 +187,7 @@
     return pl.pallas_call(
         project_kernel,
         out_shape=(
-            jax.ShapeDtypeStruct((N_SPREAD, count, HQK), jnp.bfloat16),
+            jax.ShapeDtypeStruct((count, HQK), jnp.bfloat16),
             jax.ShapeDtypeStruct((N_LINE, count, 3 * HQK), jnp.bfloat16),
         ),
         in_specs=whole(4),
@@ -197,7 +196,7 @@
     )(trunk, w_query, w_key, w_value)
 
 
-def attention_kernel(query_ref, kv_ref, out_ref):
+def attention_kernel(place_ref, query_ref, kv_ref, out_ref):
     scale = 1.0 / math.sqrt(HQK)
     scores = (
         lax.dot_general(
@@ -214,18 +213,21 @@
     mixed = jnp.dot(expo.astype(jnp.bfloat16), kv_ref[:, HQK:], preferred_element_type=jnp.float32)
     lane = lax.broadcasted_iota(jnp.int32, mixed.shape, 1)
     mixed = jnp.where(lane == HV, top, jnp.where(lane == HV + 1, total, mixed))
-    out_ref[...] = mixed.reshape(out_ref.shape)
-
-
-def attention(query, kv, groups):
+    groups, count, _ = out_ref.shape
+    for index in range(groups):
+        out_ref[place_ref[0] ^ index] = mixed[index * count : (index + 1) * count, :]
+
+
+def attention(place, query, kv):
+    groups = N_SPREAD
     count, width = query.shape[0] // groups, kv.shape[1] - HQK
     return pl.pallas_call(
         attention_kernel,
         out_shape=jax.ShapeDtypeStruct((groups, count, width), jnp.float32),
-        in_specs=whole(2),
-        out_specs=whole(1)[0],
-        compiler_params=params(),
-    )(query, kv)
+        in_specs=[pl.BlockSpec(memory_space=pltpu.SMEM)] + whole(2),
+        out_specs=whole(1)[0],
+        compiler_params=params(),
+    )(place, query, kv)
 
 
 def combine_kernel(parts_ref, w_out_ref, out_ref):
@@ -240,11 +242,11 @@
     count = term.shape[0]
     tail = jnp.concatenate(
         [mean[:, c * width : (c + 1) * width] for c in range(N_PAIR)]
-        + [jnp.zeros((count - N_PAIR, width), jnp.float32)],
+        + [jnp.zeros((8 - N_PAIR, width), jnp.float32)],
         axis=0,
-    ).astype(jnp.bfloat16)
+    )
     for c in range(N_PAIR):
-        out_ref[c, :count, :] = term[:, c * width : (c + 1) * width].astype(jnp.bfloat16)
+        out_ref[c, :count, :] = term[:, c * width : (c + 1) * width]
         out_ref[c, count:, :] = tail
 
 
@@ -253,7 +255,7 @@
     width = w_out.shape[1] // N_PAIR
     return pl.pallas_call(
         combine_kernel,
-        out_shape=jax.ShapeDtypeStruct((N_PAIR, 2 * count, width), jnp.bfloat16),
+        out_shape=jax.ShapeDtypeStruct((N_PAIR, count + 8, width), jnp.float32),
         in_specs=whole(2),
         out_specs=whole(1)[0],
         compiler_params=params(),
@@ -262,7 +264,7 @@
 
 def close_kernel(terms_ref, own_ref, trunk_ref, w_pair_ref, pair_ref, seq_ref, rows_ref, every_ref):
     count, width = own_ref.shape
-    total = jnp.sum(terms_ref[...].astype(jnp.float32), axis=0)
+    total = jnp.sum(terms_ref[...], axis=0)
     seq_ref[...] = (own_ref[...].astype(jnp.float32) + total[:count, :]).astype(jnp.bfloat16)
     trunk_mean = jnp.sum(trunk_ref[...].astype(jnp.float32), axis=0, keepdims=True) * (1.0 / PAIR_POOL)
     rows = None
@@ -337,9 +339,12 @@
     trunk = trunk.reshape(count, N_PAIR * width)
 
     query, kv = project(trunk, w_query, w_key, w_value)
-    query = exchange(query, SPREAD).reshape(N_SPREAD * count, HQK)
+    for name in reversed(SPREAD):
+        other = lax.ppermute(query, name, [(0, 1), (1, 0)])
+        query = jnp.concatenate([query, other], axis=0)
     kv = exchange(kv, LINE).reshape(N_LINE * count, kv.shape[2])
-    parts = exchange(attention(query, kv, N_SPREAD), SPREAD)
+    spread = lax.axis_index(SPREAD).astype(jnp.int32)[None]
+    parts = exchange(attention(spread, query, kv), SPREAD)
     terms = exchange(combine(parts, w_out), ("pair",))
 
     own = lax.dynamic_slice_in_dim(trunk, pair_place * width, width, 1)

time: 134 us -> 132 us (0.985)
  starting transfers between devices: 54.4 us -> 64.4 us
  blocking collectives: 22.3 us -> 15.3 us
  waiting for transfers between devices: 42.1 us -> 36.8 us
    ppermute x0 -> x3, starting transfers between devices: none -> 8.78 us  [on_device(): other = lax.ppermute(query, name, [(0, 1), (1, 0)])]
    all_to_all x6, waiting for transfers between devices: 42.1 us -> 34.7 us  [exchange(): return lax.all_to_all(blocks, axes, split_axis=0, concat_axis=0, tiled=True)]
    all_to_all x1 -> x0, blocking collectives: 6.78 us -> none  [exchange(): return lax.all_to_all(blocks, axes, split_axis=0, concat_axis=0, tiled=True)]
    ppermute x0 -> x3, waiting for transfers between devices: none -> 2.15 us  [on_device(): other = lax.ppermute(query, name, [(0, 1), (1, 0)])]
  transfers between devices with their start and end apart: 8 -> 11, of which waited for: 6 -> 8; matrix products, arithmetic and copies ran while one was open for 2% -> 2% of each run, Pallas kernels for 2% -> 2%
where the time goes in v7:
time: 132 us; the launch traced here: 131 us
  starting transfers between devices  64.4 us (49%)
  waiting for transfers between devices  36.8 us (28%)
  blocking collectives  15.3 us (12%)
  Pallas kernels  8.1 us (6%)
  local copies, waits for them, and re-layouts  2.81 us (2%)
  matrix products  1.33 us (1%)
    all_to_all x6, starting transfers between devices, exchange(): return lax.all_to_all(blocks, axes, split_axis=0, concat_axis=0, tiled=True)  45.5 us
    all_to_all x6, waiting for transfers between devices, exchange(): return lax.all_to_all(blocks, axes, split_axis=0, concat_axis=0, tiled=True)  34.7 us
    all_gather x1, blocking collectives, on_device(): sections = lax.all_gather(section, SHARE, axis=0, tiled=False)  15.3 us
    ppermute x3, starting transfers between devices, on_device(): other = lax.ppermute(query, name, [(0, 1), (1, 0)])  8.78 us
    ppermute x1, starting transfers between devices, on_device(): right = lax.ppermute(codes[:SIDE], SEQ, [(i + 1, i) for i in range(ends)])  5.57 us
    ppermute x1, starting transfers between devices, on_device(): left = lax.ppermute(codes[-SIDE:], SEQ, [(i, i + 1) for i in range(ends)])  4.5 us
  transfers between devices with their start and end apart: 11, of which 8 were waited for; matrix products, arithmetic and copies ran while one was open for 2% of the time, Pallas kernels for 2%

profile of v7, /device:TPU:1, one launch (start us, length us, event | category | flops | bytes accessed | tf_op | source)
XLA Modules:
  0.0 130.8 jit_solution(2417979181781334530)
XLA Ops:
  0.6 0.0 copy-start
  0.6 0.7 broadcast_add_fusion
  1.4 4.5 %collective-permute-start = (s32[256]{0:T(256)S(1)}, s32[256]{0:T(256)S(1)}, u32[]{:S(2)}, u32[]{:S(2)}) collective-permute-start(s32[256]{0:T(256)S(1)} %get-tuple-element.18), channel_id=1, source_target_pairs={{0,4},{4,8},{8,12},{12,16},{16,20},{20,24},{24,28},{28,32},{32,36}... | collective-permute-start | bytes 3080 | tf_op jit(solution)/shard_map/ppermute | solution.py:324
  5.9 5.6 %collective-permute-start.1 = (s32[256]{0:T(256)S(1)}, s32[256]{0:T(256)S(1)}, u32[]{:S(2)}, u32[]{:S(2)}) collective-permute-start(s32[256]{0:T(256)S(1)} %get-tuple-element.19), channel_id=1, source_target_pairs={{4,0},{8,4},{12,8},{16,12},{20,16},{24,20},{28,24},{32,28},{36,32}... | collective-permute-start | bytes 3080 | tf_op jit(solution)/shard_map/ppermute | solution.py:325
  11.5 0.0 copy-start.4
  11.5 0.7 copy-done.4
  12.2 1.0 shard_map.114
  13.2 10.6 %all-to-all-start = ((bf16[128,15,96]{2,1,0:T(8,128)(2,1)}), bf16[128,15,96]{2,1,0:T(8,128)(2,1)S(1)}, u32[]{:S(2)}, u32[]{:S(2)}) async-start(bf16[128,15,96]{2,1,0:T(8,128)(2,1)} %shard_map.114), calls=%async_computation | async-start | bytes 1048576 | tf_op jit(solution)/shard_map/all_to_all | solution.py:310
  23.9 0.0 copy-done
  23.9 0.5 fusion.3
  24.4 0.3 rev.3
  24.8 0.0 collective-permute-done
  24.8 0.0 collective-permute-done.1
  24.8 1.7 %shard_map.113 = f32[40,768]{1,0:T(8,128)S(1)} custom-call(s32[1]{0:T(128)} %bitcast.1.place_ref, s32[1,2560]{1,0:T(1,128)S(1)} %broadcast_in_dim.21.codes_ref, bf16[64,768]{1,0:T(8,128)(2,1)S(1)} %bitcast.32), custom_call_target="tpu_custom_call" | custom-call | flops 40000000000 | bytes 200000 | tf_op jit(solution)/shard_map/pallas_call | solution.py:75
  26.6 15.3 %all-gather = bf16[320,768]{1,0:T(8,128)(2,1)S(1)} all-gather(bf16[40,768]{1,0:T(8,128)(2,1)S(1)} %convert_element_type.143), channel_id=2, replica_groups=mesh['zl'=2,'y'=8,'xh'=2,'xl'=2,'core'=2,'pair'=4] {'zl','xl','core'}, dimensions={0}, use_global_device_ids=true | all-gather | bytes 552960 | tf_op jit(solution)/shard_map/all_gather | solution.py:334
  41.9 2.4 %all-to-all-done = bf16[128,15,96]{2,1,0:T(8,128)(2,1)S(1)} async-done(((bf16[128,15,96]{2,1,0:T(8,128)(2,1)}), bf16[128,15,96]{2,1,0:T(8,128)(2,1)S(1)}, u32[]{:S(2)}, u32[]{:S(2)}) %all-to-all-start) | async-done | bytes 368672 | tf_op jit(solution)/shard_map/all_to_all | solution.py:310
  44.3 0.2 reshape.119.weight_ref
  44.5 0.0 copy-start.5
  44.5 1.5 %shard_map.115 = bf16[32,2,384]{2,1,0:T(2,128)(2,1)} custom-call(bf16[8,40,768]{2,1,0:T(8,128)(2,1)S(1)} %bitcast.30, bf16[1920,96]{1,0:T(8,128)(2,1)S(1)} %reshape.119.weight_ref), custom_call_target="tpu_custom_call" | custom-call | tf_op jit(solution)/shard_map/pallas_call | solution.py:157
  46.0 9.9 %all-to-all-start.1 = ((bf16[32,2,384]{2,1,0:T(2,128)(2,1)}), bf16[32,2,384]{2,1,0:T(2,128)(2,1)S(1)}, u32[]{:S(2)}, u32[]{:S(2)}) async-start(bf16[32,2,384]{2,1,0:T(2,128)(2,1)} %shard_map.115), calls=%async_computation.1 | async-start | bytes 98304 | tf_op jit(solution)/shard_map/all_to_all | solution.py:310
  55.9 0.0 copy-done.5
  55.9 0.0 copy-start.2
  55.9 0.0 copy-start.3
  55.9 0.3 copy.32.w_value_ref
  56.2 7.9 %all-to-all-done.1 = bf16[32,2,384]{2,1,0:T(2,128)(2,1)S(1)} async-done(((bf16[32,2,384]{2,1,0:T(2,128)(2,1)}), bf16[32,2,384]{2,1,0:T(2,128)(2,1)S(1)}, u32[]{:S(2)}, u32[]{:S(2)}) %all-to-all-start.1) | async-done | bytes 49184 | tf_op jit(solution)/shard_map/all_to_all | solution.py:310
  64.1 0.2 reshape.120
  64.3 0.1 copy.41
  64.4 0.2 reshape.121.trunk_ref
  64.6 0.0 copy-done.2
  64.6 0.0 copy-done.3
  64.6 0.0 copy-start.6
  64.6 1.0 shard_map.116
  65.6 2.3 %collective-permute-start.2 = (bf16[16,128]{1,0:T(8,128)(2,1)S(1)}, bf16[16,128]{1,0:T(8,128)(2,1)S(1)}, u32[]{:S(2)}, u32[]{:S(2)}) collective-permute-start(bf16[16,128]{1,0:T(8,128)(2,1)S(1)} %get-tuple-element.7), channel_id=1, source_target_pairs={{0,4},{4,0},{1,5},{5,1},{2,6},{6,2},{3,7},{7,3},{8,12},{12,8},{9,1... | collective-permute-start | bytes 12296 | tf_op jit(solution)/shard_map/ppermute | solution.py:343
  67.9 0.8 collective-permute-done.2
  68.7 2.2 %collective-permute-start.3 = (bf16[32,128]{1,0:T(8,128)(2,1)S(1)}, bf16[32,128]{1,0:T(8,128)(2,1)S(1)}, u32[]{:S(2)}, u32[]{:S(2)}) collective-permute-start(bf16[32,128]{1,0:T(8,128)(2,1)S(1)} %pad_maximum_fusion.3), channel_id=1, source_target_pairs={{0,8},{8,0},{1,9},{9,1},{2,10},{10,2},{3,11},{11,3},{4,12},{12,4},... | collective-permute-start | bytes 24584 | tf_op jit(solution)/shard_map/ppermute | solution.py:343
  70.9 4.9 %all-to-all-start.2 = ((bf16[16,16,384]{2,1,0:T(8,128)(2,1)}), bf16[16,16,384]{2,1,0:T(8,128)(2,1)S(1)}, u32[]{:S(2)}, u32[]{:S(2)}) async-start(bf16[16,16,384]{2,1,0:T(8,128)(2,1)} %get-tuple-element.8), calls=%async_computation.2 | async-start | bytes 393216 | tf_op jit(solution)/shard_map/all_to_all | solution.py:310
  75.8 0.0 collective-permute-done.3
  75.8 4.3 %collective-permute-start.4 = (bf16[64,128]{1,0:T(8,128)(2,1)S(1)}, bf16[64,128]{1,0:T(8,128)(2,1)S(1)}, u32[]{:S(2)}, u32[]{:S(2)}) collective-permute-start(bf16[64,128]{1,0:T(8,128)(2,1)S(1)} %pad_maximum_fusion.2), channel_id=1, source_target_pairs={{0,16},{16,0},{1,17},{17,1},{2,18},{18,2},{3,19},{19,3},{4,20},{20... | collective-permute-start | bytes 49160 | tf_op jit(solution)/shard_map/ppermute | solution.py:343
  80.1 0.0 copy-done.6
  80.2 0.2 copy.38
  80.4 0.2 copy.39
  80.6 1.3 %collective-permute-done.4 = bf16[64,128]{1,0:T(8,128)(2,1)S(1)} collective-permute-done((bf16[64,128]{1,0:T(8,128)(2,1)S(1)}, bf16[64,128]{1,0:T(8,128)(2,1)S(1)}, u32[]{:S(2)}, u32[]{:S(2)}) %collective-permute-start.4) | collective-permute-done | bytes 16416 | tf_op jit(solution)/shard_map/ppermute | solution.py:343
  82.0 1.3 %all-to-all-done.2 = bf16[16,16,384]{2,1,0:T(8,128)(2,1)S(1)} async-done(((bf16[16,16,384]{2,1,0:T(8,128)(2,1)}), bf16[16,16,384]{2,1,0:T(8,128)(2,1)S(1)}, u32[]{:S(2)}, u32[]{:S(2)}) %all-to-all-start.2) | async-done | bytes 196640 | tf_op jit(solution)/shard_map/all_to_all | solution.py:310
  83.3 1.0 shard_map.117
  84.4 0.0 copy-start.7
  84.4 0.0 copy-start.1
  84.4 6.6 %all-to-all-start.3 = ((f32[8,16,256]{2,1,0:T(8,128)}), f32[8,16,256]{2,1,0:T(8,128)S(1)}, u32[]{:S(2)}, u32[]{:S(2)}) async-start(f32[8,16,256]{2,1,0:T(8,128)} %shard_map.117), calls=%async_computation.3 | async-start | bytes 262144 | tf_op jit(solution)/shard_map/all_to_all | solution.py:310
  90.9 0.2 pad_maximum_fusion.w_pair_ref
  91.2 0.0 copy-done.7
  91.2 0.1 copy.35.pair_ref
  91.3 4.9 %all-to-all-done.3.parts_ref = f32[8,16,256]{2,1,0:T(8,128)S(1)} async-done(((f32[8,16,256]{2,1,0:T(8,128)}), f32[8,16,256]{2,1,0:T(8,128)S(1)}, u32[]{:S(2)}, u32[]{:S(2)}) %all-to-all-start.3) | async-done | bytes 131104 | tf_op jit(solution)/shard_map/all_to_all | solution.py:310
  96.2 0.0 copy-done.1
  96.2 1.0 shard_map.118
  97.2 0.0 copy-start.8
  97.2 3.5 %all-to-all-start.4 = ((f32[4,24,384]{2,1,0:T(8,128)}), f32[4,24,384]{2,1,0:T(8,128)S(1)}, u32[]{:S(2)}, u32[]{:S(2)}) async-start(f32[4,24,384]{2,1,0:T(8,128)} %shard_map.118), calls=%async_computation.4 | async-start | bytes 294912 | tf_op jit(solution)/shard_map/all_to_all | solution.py:310
  100.7 7.4 %all-to-all-done.4.terms_ref = f32[4,24,384]{2,1,0:T(8,128)S(1)} async-done(((f32[4,24,384]{2,1,0:T(8,128)}), f32[4,24,384]{2,1,0:T(8,128)S(1)}, u32[]{:S(2)}, u32[]{:S(2)}) %all-to-all-start.4) | async-done | bytes 147488 | tf_op jit(solution)/shard_map/all_to_all | solution.py:310
  108.1 0.8 shard_map.119
  108.9 10.2 %all-to-all-start.5 = ((f32[128,1,96]{2,1,0:T(1,128)}), f32[128,1,96]{2,1,0:T(1,128)S(1)}, u32[]{:S(2)}, u32[]{:S(2)}) async-start(f32[128,1,96]{2,1,0:T(1,128)} %bitcast.12), calls=%async_computation.5 | async-start | bytes 131072 | tf_op jit(solution)/shard_map/all_to_all | solution.py:310
  119.1 0.1 slice_bitcast_fusion.1
  119.2 10.7 %all-to-all-done.5 = f32[128,1,96]{2,1,0:T(1,128)S(1)} async-done(((f32[128,1,96]{2,1,0:T(1,128)}), f32[128,1,96]{2,1,0:T(1,128)S(1)}, u32[]{:S(2)}, u32[]{:S(2)}) %all-to-all-start.5) | async-done | bytes 49184 | tf_op jit(solution)/shard_map/all_to_all | solution.py:310
  129.9 0.1 copy.37
  130.0 0.0 copy-done.8
  130.0 0.8 fusion.5
  (18 shorter events, 0.2 us)
Async XLA Ops:
  0.6 23.2 %copy-start = (bf16[60,768]{1,0:T(8,128)(2,1)S(1)}, bf16[60,768]{1,0:T(8,128)(2,1)}, u32[]{:S(2)}) copy-start(bf16[60,768]{1,0:T(8,128)(2,1)} %param.11) | copy-start | bytes 276484
  1.4 23.4 %collective-permute-start = (s32[256]{0:T(256)S(1)}, s32[256]{0:T(256)S(1)}, u32[]{:S(2)}, u32[]{:S(2)}) collective-permute-start(s32[256]{0:T(256)S(1)} %get-tuple-element.18), channel_id=1, source_target_pairs={{0,4},{4,8},{8,12},{12,16},{16,20},{20,24},{24,28},{28,32},{32,36}... | collective-permute-start | bytes 3080 | tf_op jit(solution)/shard_map/ppermute | solution.py:324
  5.9 18.9 %collective-permute-start.1 = (s32[256]{0:T(256)S(1)}, s32[256]{0:T(256)S(1)}, u32[]{:S(2)}, u32[]{:S(2)}) collective-permute-start(s32[256]{0:T(256)S(1)} %get-tuple-element.19), channel_id=1, source_target_pairs={{4,0},{8,4},{12,8},{16,12},{20,16},{24,20},{28,24},{32,28},{36,32}... | collective-permute-start | bytes 3080 | tf_op jit(solution)/shard_map/ppermute | solution.py:325
  11.5 0.7 copy-start.4
  13.2 31.1 %all-to-all-start = ((bf16[128,15,96]{2,1,0:T(8,128)(2,1)}), bf16[128,15,96]{2,1,0:T(8,128)(2,1)S(1)}, u32[]{:S(2)}, u32[]{:S(2)}) async-start(bf16[128,15,96]{2,1,0:T(8,128)(2,1)} %shard_map.114), calls=%async_computation | async-start | bytes 1048576 | tf_op jit(solution)/shard_map/all_to_all | solution.py:310
  44.5 11.4 %copy-start.5 = (bf16[1536,192]{0,1:T(8,128)(2,1)S(1)}, bf16[1536,192]{0,1:T(8,128)(2,1)}, u32[]{:S(2)}) copy-start(bf16[1536,192]{0,1:T(8,128)(2,1)} %param.15) | copy-start | bytes 1769476
  46.0 18.1 %all-to-all-start.1 = ((bf16[32,2,384]{2,1,0:T(2,128)(2,1)}), bf16[32,2,384]{2,1,0:T(2,128)(2,1)S(1)}, u32[]{:S(2)}, u32[]{:S(2)}) async-start(bf16[32,2,384]{2,1,0:T(2,128)(2,1)} %shard_map.115), calls=%async_computation.1 | async-start | bytes 98304 | tf_op jit(solution)/shard_map/all_to_all | solution.py:310
  55.9 8.6 %copy-start.2 = (bf16[1536,128]{1,0:T(8,128)(2,1)S(1)}, bf16[1536,128]{1,0:T(8,128)(2,1)}, u32[]{:S(2)}) copy-start(bf16[1536,128]{1,0:T(8,128)(2,1)} %w_query_ref.1) | copy-start | bytes 1179652
  55.9 8.6 %copy-start.3 = (bf16[1536,128]{1,0:T(8,128)(2,1)S(1)}, bf16[1536,128]{1,0:T(8,128)(2,1)}, u32[]{:S(2)}) copy-start(bf16[1536,128]{1,0:T(8,128)(2,1)} %w_key_ref.1) | copy-start | bytes 1179652
  64.6 15.6 %copy-start.6 = (bf16[2,1536,32]{1,2,0:T(8,128)(2,1)S(1)}, bf16[2,1536,32]{1,2,0:T(8,128)(2,1)}, u32[]{:S(2)}) copy-start(bf16[2,1536,32]{1,2,0:T(8,128)(2,1)} %param.17) | copy-start | bytes 589828
  65.6 3.1 %collective-permute-start.2 = (bf16[16,128]{1,0:T(8,128)(2,1)S(1)}, bf16[16,128]{1,0:T(8,128)(2,1)S(1)}, u32[]{:S(2)}, u32[]{:S(2)}) collective-permute-start(bf16[16,128]{1,0:T(8,128)(2,1)S(1)} %get-tuple-element.7), channel_id=1, source_target_pairs={{0,4},{4,0},{1,5},{5,1},{2,6},{6,2},{3,7},{7,3},{8,12},{12,8},{9,1... | collective-permute-start | bytes 12296 | tf_op jit(solution)/shard_map/ppermute | solution.py:343
  68.7 7.1 %collective-permute-start.3 = (bf16[32,128]{1,0:T(8,128)(2,1)S(1)}, bf16[32,128]{1,0:T(8,128)(2,1)S(1)}, u32[]{:S(2)}, u32[]{:S(2)}) collective-permute-start(bf16[32,128]{1,0:T(8,128)(2,1)S(1)} %pad_maximum_fusion.3), channel_id=1, source_target_pairs={{0,8},{8,0},{1,9},{9,1},{2,10},{10,2},{3,11},{11,3},{4,12},{12,4},... | collective-permute-start | bytes 24584 | tf_op jit(solution)/shard_map/ppermute | solution.py:343
  70.9 12.4 %all-to-all-start.2 = ((bf16[16,16,384]{2,1,0:T(8,128)(2,1)}), bf16[16,16,384]{2,1,0:T(8,128)(2,1)S(1)}, u32[]{:S(2)}, u32[]{:S(2)}) async-start(bf16[16,16,384]{2,1,0:T(8,128)(2,1)} %get-tuple-element.8), calls=%async_computation.2 | async-start | bytes 393216 | tf_op jit(solution)/shard_map/all_to_all | solution.py:310
  75.8 6.1 %collective-permute-start.4 = (bf16[64,128]{1,0:T(8,128)(2,1)S(1)}, bf16[64,128]{1,0:T(8,128)(2,1)S(1)}, u32[]{:S(2)}, u32[]{:S(2)}) collective-permute-start(bf16[64,128]{1,0:T(8,128)(2,1)S(1)} %pad_maximum_fusion.2), channel_id=1, source_target_pairs={{0,16},{16,0},{1,17},{17,1},{2,18},{18,2},{3,19},{19,3},{4,20},{20... | collective-permute-start | bytes 49160 | tf_op jit(solution)/shard_map/ppermute | solution.py:343
  84.4 6.8 %copy-start.7 = (bf16[1,128,32]{1,2,0:T(8,128)(2,1)S(1)}, bf16[1,128,32]{1,2,0:T(8,128)(2,1)}, u32[]{:S(2)}) copy-start(bf16[1,128,32]{1,2,0:T(8,128)(2,1)} %param.19) | copy-start | bytes 24580
  84.4 11.8 %copy-start.1 = (bf16[192,1536]{1,0:T(8,128)(2,1)S(1)}, bf16[192,1536]{1,0:T(8,128)(2,1)}, u32[]{:S(2)}) copy-start(bf16[192,1536]{1,0:T(8,128)(2,1)} %w_out_ref.1) | copy-start | bytes 1769476
  84.4 11.8 %all-to-all-start.3 = ((f32[8,16,256]{2,1,0:T(8,128)}), f32[8,16,256]{2,1,0:T(8,128)S(1)}, u32[]{:S(2)}, u32[]{:S(2)}) async-start(f32[8,16,256]{2,1,0:T(8,128)} %shard_map.117), calls=%async_computation.3 | async-start | bytes 262144 | tf_op jit(solution)/shard_map/all_to_all | solution.py:310
  97.2 32.8 %copy-start.8 = (bf16[18,32]{1,0:T(8,128)(2,1)S(1)}, bf16[18,32]{1,0:T(8,128)(2,1)}, u32[]{:S(2)}) copy-start(bf16[18,32]{1,0:T(8,128)(2,1)} %param.18) | copy-start | bytes 3460
  97.2 10.9 %all-to-all-start.4 = ((f32[4,24,384]{2,1,0:T(8,128)}), f32[4,24,384]{2,1,0:T(8,128)S(1)}, u32[]{:S(2)}, u32[]{:S(2)}) async-start(f32[4,24,384]{2,1,0:T(8,128)} %shard_map.118), calls=%async_computation.4 | async-start | bytes 294912 | tf_op jit(solution)/shard_map/all_to_all | solution.py:310
  108.9 21.0 %all-to-all-start.5 = ((f32[128,1,96]{2,1,0:T(1,128)}), f32[128,1,96]{2,1,0:T(1,128)S(1)}, u32[]{:S(2)}, u32[]{:S(2)}) async-start(f32[128,1,96]{2,1,0:T(1,128)} %bitcast.12), calls=%async_computation.5 | async-start | bytes 131072 | tf_op jit(solution)/shard_map/all_to_all | solution.py:310

commit v8 on v7

--- a/solution.py
+++ b/solution.py
@@ -122,11 +122,12 @@
     )(weight)
 
 
-def conv_kernel(section_ref, weight_ref, out_ref, wide, act, best):
-    windows, _, channels = section_ref.shape
+def conv_kernel(core_ref, near_ref, far_ref, weight_ref, out_ref, wide, act, best):
+    windows, _, channels = wide.shape
     half = channels // 2
     columns = out_ref.shape[2] // 8
-    wide[...] = section_ref[...].astype(jnp.float32)
+    wide[: windows // 2] = near_ref[...].astype(jnp.float32)
+    wide[windows // 2 :] = far_ref[...].astype(jnp.float32)
     even, odd = None, None
     for tap in range(KS_CONV):
         rows = wide[:, tap : tap + ROWS, :].astype(jnp.bfloat16).reshape(windows * ROWS, channels)
@@ -147,17 +148,20 @@
         flat = part if flat is None else flat + part
     for window in range(windows):
         block = flat[2 * window : 2 * window + 2, :].astype(jnp.bfloat16)
+        far = window * 2 // windows
+        place = window % (windows // 2) * 2 + (core_ref[0] ^ far)
         for index in range(N_PAIR):
-            out_ref[window * N_PAIR + index] = block
-
-
-def conv(section, weight):
-    windows, _, channels = section.shape
+            out_ref[place * N_PAIR + index] = block
+
+
+def conv(core, near, far, weight):
+    windows, _, channels = near.shape
+    windows = 2 * windows
     columns = weight.shape[1] // 2
     return pl.pallas_call(
         conv_kernel,
         out_shape=jax.ShapeDtypeStruct((windows * N_PAIR, 2, 8 * columns), jnp.bfloat16),
-        in_specs=whole(2),
+        in_specs=[pl.BlockSpec(memory_space=pltpu.SMEM)] + whole(3),
         out_specs=whole(1)[0],
         scratch_shapes=[
             pltpu.VMEM((windows, EXT_PAD, channels), jnp.float32),
@@ -165,7 +169,7 @@
             pltpu.VMEM((windows * ROWS // 2, HQK), jnp.float32),
         ],
         compiler_params=params(),
-    )(section, weight)
+    )(core, near, far, weight)
 
 
 def project_kernel(trunk_ref, w_query_ref, w_key_ref, w_value_ref, query_ref, kv_ref):
@@ -230,7 +234,8 @@
     )(place, query, kv)
 
 
-def combine_kernel(parts_ref, w_out_ref, out_ref):
+def combine_kernel(place_ref, parts_ref, w_out_ref, means_ref, *refs):
+    terms_refs, blocks = refs[:-1], refs[-1]
     parts = parts_ref[...]
     top = parts[:, :, HV : HV + 1]
     gain = jnp.exp(top - jnp.max(top, axis=0, keepdims=True))
@@ -239,37 +244,40 @@
     term = jnp.dot(mixed, w_out_ref[...], preferred_element_type=jnp.float32)
     mean = jnp.sum(term, axis=0, keepdims=True) * (1.0 / PAIR_POOL)
     width = term.shape[1] // N_PAIR
-    count = term.shape[0]
     tail = jnp.concatenate(
         [mean[:, c * width : (c + 1) * width] for c in range(N_PAIR)]
         + [jnp.zeros((8 - N_PAIR, width), jnp.float32)],
         axis=0,
     )
     for c in range(N_PAIR):
-        out_ref[c, :count, :] = term[:, c * width : (c + 1) * width]
-        out_ref[c, count:, :] = tail
-
-
-def combine(parts, w_out):
+        means_ref[c] = tail
+        blocks[c] = term[:, c * width : (c + 1) * width]
+    for shift, ref in enumerate(terms_refs):
+        ref[...] = blocks[(place_ref[0] + shift) % N_PAIR]
+
+
+def combine(place, parts, w_out):
     count = parts.shape[1]
     width = w_out.shape[1] // N_PAIR
+    block = jax.ShapeDtypeStruct((count, width), jnp.float32)
     return pl.pallas_call(
         combine_kernel,
-        out_shape=jax.ShapeDtypeStruct((N_PAIR, count + 8, width), jnp.float32),
-        in_specs=whole(2),
-        out_specs=whole(1)[0],
-        compiler_params=params(),
-    )(parts, w_out)
-
-
-def close_kernel(terms_ref, own_ref, trunk_ref, w_pair_ref, pair_ref, seq_ref, rows_ref, every_ref):
-    count, width = own_ref.shape
-    total = jnp.sum(terms_ref[...], axis=0)
-    seq_ref[...] = (own_ref[...].astype(jnp.float32) + total[:count, :]).astype(jnp.bfloat16)
+        out_shape=(jax.ShapeDtypeStruct((N_PAIR, 8, width), jnp.float32),) + (block,) * N_PAIR,
+        in_specs=[pl.BlockSpec(memory_space=pltpu.SMEM)] + whole(2),
+        out_specs=tuple(whole(1 + N_PAIR)),
+        scratch_shapes=[pltpu.VMEM((N_PAIR, count, width), jnp.float32)],
+        compiler_params=params(),
+    )(place, parts, w_out)
+
+
+def close_kernel(means_ref, trunk_ref, w_pair_ref, pair_ref, *refs):
+    terms_refs, (rows_ref, every_ref), sent_refs = refs[:3], refs[3:5], refs[5:]
+    total = jnp.sum(means_ref[...], axis=0)
+    width = total.shape[1]
     trunk_mean = jnp.sum(trunk_ref[...].astype(jnp.float32), axis=0, keepdims=True) * (1.0 / PAIR_POOL)
     rows = None
     for c in range(N_PAIR):
-        pooled = trunk_mean[:, c * width : (c + 1) * width] + total[count + c : count + c + 1, :]
+        pooled = trunk_mean[:, c * width : (c + 1) * width] + total[c : c + 1, :]
         term = jnp.dot(
             jnp.broadcast_to(pooled, (8, width)).astype(jnp.bfloat16),
             w_pair_ref[c * width : (c + 1) * width, :],
@@ -280,20 +288,23 @@
     mine = pair_ref[0].astype(jnp.float32)
     factors = jnp.broadcast_to(rows[:1], (mine.shape[0], rows.shape[1]))
     every_ref[...] = jnp.concatenate([factors, mine], axis=1)
-
-
-def close(terms, own, trunk, w_pair, pair_in):
+    for term_ref, sent_ref in zip(terms_refs, sent_refs):
+        sent_ref[...] = term_ref[...]
+
+
+def close(means, trunk, w_pair, pair_in, terms):
+    factors = w_pair.shape[1]
     return pl.pallas_call(
         close_kernel,
         out_shape=(
-            jax.ShapeDtypeStruct(own.shape, jnp.bfloat16),
-            jax.ShapeDtypeStruct((8, w_pair.shape[1]), jnp.float32),
-            jax.ShapeDtypeStruct((pair_in.shape[1], w_pair.shape[1] + pair_in.shape[2]), jnp.float32),
-        ),
-        in_specs=whole(5),
-        out_specs=tuple(whole(3)),
-        compiler_params=params(),
-    )(terms, own, trunk, w_pair, pair_in)
+            jax.ShapeDtypeStruct((8, factors), jnp.float32),
+            jax.ShapeDtypeStruct((pair_in.shape[1], factors + pair_in.shape[2]), jnp.float32),
+        )
+        + tuple(jax.ShapeDtypeStruct(term.shape, jnp.float32) for term in terms),
+        in_specs=whole(4 + len(terms)),
+        out_specs=tuple(whole(2 + len(terms))),
+        compiler_params=params(),
+    )(means, trunk, w_pair, pair_in, *terms)
 
 
 def distance_bias(row, cols, pair_bias):
@@ -313,6 +324,7 @@
 def on_device(tokens, w_stem, w_conv, w_query, w_key, w_value, w_out, w_pair, pair_bias, pair_in):
     place = lax.axis_index(SEQ)
     pair_place = lax.axis_index("pair")
+    core = lax.axis_index("core").astype(jnp.int32)[None]
 
     taps, width = w_conv.shape
     share = width // N_SHARE
@@ -331,9 +343,10 @@
     stem_weight = stem_weight.reshape(KS_STEM, 4, -1)[::-1].transpose(1, 0, 2)
     stem_weight = jnp.pad(stem_weight, ((0, 0), (0, 1), (0, 0))).reshape(64, -1)
     section = stem(place.astype(jnp.int32)[None], codes, stem_weight).astype(jnp.bfloat16)
-    sections = lax.all_gather(section, SHARE, axis=0, tiled=False)
-
-    parts = exchange(conv(sections, conv_weight), SHARE + ("pair",))
+    near = lax.all_gather(section, SHARE[:-1], axis=0, tiled=False)
+    far = lax.ppermute(near, "core", [(0, 1), (1, 0)])
+
+    parts = exchange(conv(core, near, far, conv_weight), SHARE + ("pair",))
     count = ROWS // 2
     trunk = parts.reshape(N_SHARE, N_PAIR, count, share).transpose(2, 1, 0, 3)
     trunk = trunk.reshape(count, N_PAIR * width)
@@ -345,16 +358,20 @@
     kv = exchange(kv, LINE).reshape(N_LINE * count, kv.shape[2])
     spread = lax.axis_index(SPREAD).astype(jnp.int32)[None]
     parts = exchange(attention(spread, query, kv), SPREAD)
-    terms = exchange(combine(parts, w_out), ("pair",))
-
-    own = lax.dynamic_slice_in_dim(trunk, pair_place * width, width, 1)
+    means, term, *terms = combine(pair_place.astype(jnp.int32)[None], parts, w_out)
+    means = exchange(means, ("pair",))
+
     factors = jnp.concatenate([w_pair[0], w_pair[1]], axis=1)
-    seq_out, rows, every = close(terms, own, trunk, factors, pair_in)
+    rows, every, *terms = close(means, trunk, factors, pair_in, terms)
     channels = pair_in.shape[2]
     mine = pair_in[0].astype(jnp.float32)
     rows = rows[:1]
     every = exchange(every[:, None], SEQ)[:, 0]
     mirror = every[:, 2 * channels :]
+    summed = lax.dynamic_slice_in_dim(trunk, pair_place * width, width, 1).astype(jnp.float32) + term
+    for shift, block in enumerate(terms, 1):
+        summed = summed + lax.ppermute(block, "pair", [(i, (i + shift) % N_PAIR) for i in range(N_PAIR)])
+    seq_out = summed.astype(jnp.bfloat16)
 
     cols = jnp.arange(N_SEQ, dtype=jnp.int32)
     bias = distance_bias(place.astype(jnp.int32), cols, pair_bias)

time: 132 us -> 136 us (1.030)
  starting transfers between devices: 64.4 us -> 80.3 us
  waiting for transfers between devices: 36.8 us -> 27.2 us
  blocking collectives: 15.3 us -> 12.4 us
    ppermute x0 -> x4, starting transfers between devices: none -> 13.9 us  [the longest x3 9.68 us: on_device(): lax.ppermute(block, 'pair', [(i, (i + shift) % N_PAIR) for i in range(N_P...]
    all_to_all x6, waiting for transfers between devices: 34.7 us -> 22.2 us  [exchange(): return lax.all_to_all(blocks, axes, split_axis=0, concat_axis=0, tiled=True)]
    all_gather x1, blocking collectives: 15.3 us -> 12.4 us  [on_device(): near = lax.all_gather(section, SHARE[:-1], axis=0, tiled=False)]
    ppermute x0 -> x4, waiting for transfers between devices: none -> 2.94 us  [the longest x3 2.93 us: on_device(): lax.ppermute(block, 'pair', [(i, (i + shift) % N_PAIR) for i in range(N_P...]
    all_to_all x6, starting transfers between devices: 45.5 us -> 47.5 us  [exchange(): return lax.all_to_all(blocks, axes, split_axis=0, concat_axis=0, tiled=True)]
  transfers between devices with their start and end apart: 11 -> 15, of which waited for: 8 -> 9; matrix products, arithmetic and copies ran while one was open for 2% -> 2% of each run, Pallas kernels for 2% -> 2%
where the time goes in v8:
time: 136 us; the launch traced here: 135 us
  starting transfers between devices  80.3 us (59%)
  waiting for transfers between devices  27.2 us (20%)
  blocking collectives  12.4 us (9%)
  Pallas kernels  8.01 us (6%)
  local copies, waits for them, and re-layouts  2.8 us (2%)
  other arithmetic  1.63 us (1%)
    all_to_all x6, starting transfers between devices, exchange(): return lax.all_to_all(blocks, axes, split_axis=0, concat_axis=0, tiled=True)  47.5 us
    all_to_all x6, waiting for transfers between devices, exchange(): return lax.all_to_all(blocks, axes, split_axis=0, concat_axis=0, tiled=True)  22.2 us
    all_gather x1, blocking collectives, on_device(): near = lax.all_gather(section, SHARE[:-1], axis=0, tiled=False)  12.4 us
    ppermute x3, starting transfers between devices, on_device(): lax.ppermute(block, 'pair', [(i, (i + shift) % N_PAIR) for i in range(N_P...  9.68 us
    ppermute x3, starting transfers between devices, on_device(): other = lax.ppermute(query, name, [(0, 1), (1, 0)])  8.83 us
    ppermute x1, starting transfers between devices, on_device(): right = lax.ppermute(codes[:SIDE], SEQ, [(i + 1, i) for i in range(ends)])  5.57 us
    ppermute x1, starting transfers between devices, on_device(): left = lax.ppermute(codes[-SIDE:], SEQ, [(i, i + 1) for i in range(ends)])  4.5 us
    ppermute x1, starting transfers between devices, on_device(): far = lax.ppermute(near, 'core', [(0, 1), (1, 0)])  4.2 us
  transfers between devices with their start and end apart: 15, of which 9 were waited for; matrix products, arithmetic and copies ran while one was open for 2% of the time, Pallas kernels for 2%

profile of v8, /device:TPU:1, one launch (start us, length us, event | category | flops | bytes accessed | tf_op | source)
XLA Modules:
  0.0 134.8 jit_solution(6665841742861889593)
XLA Ops:
  0.6 0.0 copy-start
  0.6 0.7 broadcast_add_fusion
  1.4 4.5 %collective-permute-start = (s32[256]{0:T(256)S(1)}, s32[256]{0:T(256)S(1)}, u32[]{:S(2)}, u32[]{:S(2)}) collective-permute-start(s32[256]{0:T(256)S(1)} %get-tuple-element.32), channel_id=1, source_target_pairs={{0,4},{4,8},{8,12},{12,16},{16,20},{20,24},{24,28},{28,32},{32,36}... | collective-permute-start | bytes 3080 | tf_op jit(solution)/shard_map/ppermute | solution.py:336
  5.9 5.6 %collective-permute-start.1 = (s32[256]{0:T(256)S(1)}, s32[256]{0:T(256)S(1)}, u32[]{:S(2)}, u32[]{:S(2)}) collective-permute-start(s32[256]{0:T(256)S(1)} %get-tuple-element.33), channel_id=1, source_target_pairs={{4,0},{8,4},{12,8},{16,12},{20,16},{24,20},{28,24},{32,28},{36,32}... | collective-permute-start | bytes 3080 | tf_op jit(solution)/shard_map/ppermute | solution.py:337
  11.5 0.0 copy-start.4
  11.5 0.7 copy-done.4
  12.2 1.0 shard_map.114
  13.2 10.6 %all-to-all-start = ((bf16[128,15,96]{2,1,0:T(8,128)(2,1)}), bf16[128,15,96]{2,1,0:T(8,128)(2,1)S(1)}, u32[]{:S(2)}, u32[]{:S(2)}) async-start(bf16[128,15,96]{2,1,0:T(8,128)(2,1)} %shard_map.114), calls=%async_computation | async-start | bytes 1048576 | tf_op jit(solution)/shard_map/all_to_all | solution.py:321
  23.8 0.0 copy-done
  23.8 0.5 fusion.3
  24.4 0.3 rev.3
  24.7 0.0 collective-permute-done
  24.8 0.0 collective-permute-done.1
  24.8 1.7 %shard_map.113 = f32[40,768]{1,0:T(8,128)S(1)} custom-call(s32[1]{0:T(128)} %bitcast.1.place_ref, s32[1,2560]{1,0:T(1,128)S(1)} %broadcast_in_dim.27.codes_ref, bf16[64,768]{1,0:T(8,128)(2,1)S(1)} %bitcast.35), custom_call_target="tpu_custom_call" | custom-call | flops 40000000000 | bytes 200000 | tf_op jit(solution)/shard_map/pallas_call | solution.py:75
  26.5 12.4 %all-gather = bf16[160,768]{1,0:T(8,128)(2,1)S(1)} all-gather(bf16[40,768]{1,0:T(8,128)(2,1)S(1)} %convert_element_type.149), channel_id=2, replica_groups=mesh['zl'=2,'y'=8,'xh'=2,'xl'=2,'core'=2,'pair'=4] {'zl','xl'}, dimensions={0}, use_global_device_ids=true | all-gather | bytes 307200 | tf_op jit(solution)/shard_map/all_gather | solution.py:346
  38.9 4.2 %collective-permute-start.2 = (bf16[4,40,768]{2,1,0:T(8,128)(2,1)S(1)}, bf16[4,40,768]{2,1,0:T(8,128)(2,1)S(1)}, u32[]{:S(2)}, u32[]{:S(2)}) collective-permute-start(bf16[4,40,768]{2,1,0:T(8,128)(2,1)S(1)} %bitcast.32), channel_id=1, source_target_pairs={{0,4},{4,0},{1,5},{5,1},{2,6},{6,2},{3,7},{7,3},{8,12},{12,8},{9,1... | collective-permute-start | bytes 737288 | tf_op jit(solution)/shard_map/ppermute | solution.py:347
  43.1 1.2 all-to-all-done
  44.3 0.2 reshape.119.weight_ref
  44.5 0.0 copy-start.5
  44.5 0.0 collective-permute-done.2.far_ref
  44.5 1.5 %shard_map.115 = bf16[32,2,384]{2,1,0:T(2,128)(2,1)} custom-call(s32[1]{0:T(128)} %bitcast.core_ref, bf16[4,40,768]{2,1,0:T(8,128)(2,1)S(1)} %bitcast.33, bf16[4,40,768]{2,1,0:T(8,128)(2,1)S(1)} %collective-permute-done.2.far_ref, bf16[1920,96]{1,0:T(8,128)(2,1)S(1)} %reshape.119.weight_ref), custom_call_target="tpu_custom_call" | custom-call | tf_op jit(solution)/shard_map/pallas_call | solution.py:161
  46.0 10.9 %all-to-all-start.1 = ((bf16[32,2,384]{2,1,0:T(2,128)(2,1)}), bf16[32,2,384]{2,1,0:T(2,128)(2,1)S(1)}, u32[]{:S(2)}, u32[]{:S(2)}) async-start(bf16[32,2,384]{2,1,0:T(2,128)(2,1)} %shard_map.115), calls=%async_computation.1 | async-start | bytes 98304 | tf_op jit(solution)/shard_map/all_to_all | solution.py:321
  57.0 0.0 copy-start.2
  57.0 0.0 copy-start.3
  57.0 0.3 copy.32.w_value_ref
  57.3 7.9 %all-to-all-done.1 = bf16[32,2,384]{2,1,0:T(2,128)(2,1)S(1)} async-done(((bf16[32,2,384]{2,1,0:T(2,128)(2,1)}), bf16[32,2,384]{2,1,0:T(2,128)(2,1)S(1)}, u32[]{:S(2)}, u32[]{:S(2)}) %all-to-all-start.1) | async-done | bytes 49184 | tf_op jit(solution)/shard_map/all_to_all | solution.py:321
  65.2 0.2 reshape.120
  65.3 0.1 copy.41
  65.4 0.2 reshape.121.trunk_ref
  65.6 0.0 copy-start.6
  65.6 1.0 shard_map.116
  66.7 2.3 %collective-permute-start.3 = (bf16[16,128]{1,0:T(8,128)(2,1)S(1)}, bf16[16,128]{1,0:T(8,128)(2,1)S(1)}, u32[]{:S(2)}, u32[]{:S(2)}) collective-permute-start(bf16[16,128]{1,0:T(8,128)(2,1)S(1)} %get-tuple-element.14), channel_id=1, source_target_pairs={{0,4},{4,0},{1,5},{5,1},{2,6},{6,2},{3,7},{7,3},{8,12},{12,8},{9,1... | collective-permute-start | bytes 12296 | tf_op jit(solution)/shard_map/ppermute | solution.py:356
  69.0 0.8 collective-permute-done.3
  69.8 2.2 %collective-permute-start.4 = (bf16[32,128]{1,0:T(8,128)(2,1)S(1)}, bf16[32,128]{1,0:T(8,128)(2,1)S(1)}, u32[]{:S(2)}, u32[]{:S(2)}) collective-permute-start(bf16[32,128]{1,0:T(8,128)(2,1)S(1)} %pad_maximum_fusion.3), channel_id=1, source_target_pairs={{0,8},{8,0},{1,9},{9,1},{2,10},{10,2},{3,11},{11,3},{4,12},{12,4},... | collective-permute-start | bytes 24584 | tf_op jit(solution)/shard_map/ppermute | solution.py:356
  72.0 6.1 %all-to-all-start.2 = ((bf16[16,16,384]{2,1,0:T(8,128)(2,1)}), bf16[16,16,384]{2,1,0:T(8,128)(2,1)S(1)}, u32[]{:S(2)}, u32[]{:S(2)}) async-start(bf16[16,16,384]{2,1,0:T(8,128)(2,1)} %get-tuple-element.15), calls=%async_computation.2 | async-start | bytes 393216 | tf_op jit(solution)/shard_map/all_to_all | solution.py:321
  78.1 0.0 collective-permute-done.4
  78.1 4.3 %collective-permute-start.5 = (bf16[64,128]{1,0:T(8,128)(2,1)S(1)}, bf16[64,128]{1,0:T(8,128)(2,1)S(1)}, u32[]{:S(2)}, u32[]{:S(2)}) collective-permute-start(bf16[64,128]{1,0:T(8,128)(2,1)S(1)} %pad_maximum_fusion.2), channel_id=1, source_target_pairs={{0,16},{16,0},{1,17},{17,1},{2,18},{18,2},{3,19},{19,3},{4,20},{20... | collective-permute-start | bytes 49160 | tf_op jit(solution)/shard_map/ppermute | solution.py:356
  82.5 0.2 copy.38
  82.7 0.2 copy.39
  83.0 1.3 collective-permute-done.5
  84.3 1.3 %all-to-all-done.2 = bf16[16,16,384]{2,1,0:T(8,128)(2,1)S(1)} async-done(((bf16[16,16,384]{2,1,0:T(8,128)(2,1)}), bf16[16,16,384]{2,1,0:T(8,128)(2,1)S(1)}, u32[]{:S(2)}, u32[]{:S(2)}) %all-to-all-start.2) | async-done | bytes 196640 | tf_op jit(solution)/shard_map/all_to_all | solution.py:321
  85.6 1.0 shard_map.117
  86.6 6.6 %all-to-all-start.3 = ((f32[8,16,256]{2,1,0:T(8,128)}), f32[8,16,256]{2,1,0:T(8,128)S(1)}, u32[]{:S(2)}, u32[]{:S(2)}) async-start(f32[8,16,256]{2,1,0:T(8,128)} %shard_map.117), calls=%async_computation.3 | async-start | bytes 262144 | tf_op jit(solution)/shard_map/all_to_all | solution.py:321
  93.3 0.2 pad_maximum_fusion.w_pair_ref
  93.5 0.0 copy-done.7
  93.5 0.1 copy.35.pair_ref
  93.6 4.9 %all-to-all-done.3.parts_ref = f32[8,16,256]{2,1,0:T(8,128)S(1)} async-done(((f32[8,16,256]{2,1,0:T(8,128)}), f32[8,16,256]{2,1,0:T(8,128)S(1)}, u32[]{:S(2)}, u32[]{:S(2)}) %all-to-all-start.3) | async-done | bytes 131104 | tf_op jit(solution)/shard_map/all_to_all | solution.py:321
  98.5 1.0 shard_map.118
  99.5 3.3 %all-to-all-start.4 = ((f32[4,8,384]{2,1,0:T(8,128)}), f32[4,8,384]{2,1,0:T(8,128)S(1)}, u32[]{:S(2)}, u32[]{:S(2)}) async-start(f32[4,8,384]{2,1,0:T(8,128)} %get-tuple-element.17), calls=%async_computation.4 | async-start | bytes 98304 | tf_op jit(solution)/shard_map/all_to_all | solution.py:321
  102.8 6.8 %all-to-all-done.4.means_ref = f32[4,8,384]{2,1,0:T(8,128)S(1)} async-done(((f32[4,8,384]{2,1,0:T(8,128)}), f32[4,8,384]{2,1,0:T(8,128)S(1)}, u32[]{:S(2)}, u32[]{:S(2)}) %all-to-all-start.4) | async-done | bytes 49184 | tf_op jit(solution)/shard_map/all_to_all | solution.py:321
  109.6 0.8 shard_map.119
  110.5 10.0 %all-to-all-start.5 = ((f32[128,1,96]{2,1,0:T(1,128)}), f32[128,1,96]{2,1,0:T(1,128)S(1)}, u32[]{:S(2)}, u32[]{:S(2)}) async-start(f32[128,1,96]{2,1,0:T(1,128)} %bitcast.14), calls=%async_computation.5 | async-start | bytes 131072 | tf_op jit(solution)/shard_map/all_to_all | solution.py:321
  120.5 2.2 %collective-permute-start.6 = (f32[16,384]{1,0:T(8,128)S(1)}, f32[16,384]{1,0:T(8,128)S(1)}, u32[]{:S(2)}, u32[]{:S(2)}) collective-permute-start(f32[16,384]{1,0:T(8,128)S(1)} %get-tuple-element.21), channel_id=1, source_target_pairs={{0,1},{1,2},{2,3},{3,0},{4,5},{5,6},{6,7},{7,4},{8,9},{9,10},{10,1... | collective-permute-start | bytes 73736 | tf_op jit(solution)/shard_map/ppermute | solution.py:373
  122.7 4.1 %collective-permute-start.7 = (f32[16,384]{1,0:T(8,128)S(1)}, f32[16,384]{1,0:T(8,128)S(1)}, u32[]{:S(2)}, u32[]{:S(2)}) collective-permute-start(f32[16,384]{1,0:T(8,128)S(1)} %get-tuple-element.22), channel_id=1, source_target_pairs={{0,2},{1,3},{2,0},{3,1},{4,6},{5,7},{6,4},{7,5},{8,10},{9,11},{10,... | collective-permute-start | bytes 73736 | tf_op jit(solution)/shard_map/ppermute | solution.py:373
  126.8 3.4 %collective-permute-start.8 = (f32[16,384]{1,0:T(8,128)S(1)}, f32[16,384]{1,0:T(8,128)S(1)}, u32[]{:S(2)}, u32[]{:S(2)}) collective-permute-start(f32[16,384]{1,0:T(8,128)S(1)} %get-tuple-element.23), channel_id=1, source_target_pairs={{0,3},{1,0},{2,1},{3,2},{4,7},{5,4},{6,5},{7,6},{8,11},{9,8},{10,9... | collective-permute-start | bytes 73736 | tf_op jit(solution)/shard_map/ppermute | solution.py:373
  130.2 0.1 slice_bitcast_fusion.1
  130.3 0.0 collective-permute-done.6
  130.3 1.2 collective-permute-done.7
  131.5 1.8 %collective-permute-done.8 = f32[16,384]{1,0:T(8,128)S(1)} collective-permute-done((f32[16,384]{1,0:T(8,128)S(1)}, f32[16,384]{1,0:T(8,128)S(1)}, u32[]{:S(2)}, u32[]{:S(2)}) %collective-permute-start.8) | collective-permute-done | bytes 24608 | tf_op jit(solution)/shard_map/ppermute | solution.py:373
  133.2 0.6 add_convert_fusion
  133.8 0.0 all-to-all-done.5
  133.8 0.1 copy.37
  133.9 0.0 copy-done.8
  133.9 0.8 fusion.5
  (25 shorter events, 0.2 us)
Async XLA Ops:
  0.6 23.2 %copy-start = (bf16[60,768]{1,0:T(8,128)(2,1)S(1)}, bf16[60,768]{1,0:T(8,128)(2,1)}, u32[]{:S(2)}) copy-start(bf16[60,768]{1,0:T(8,128)(2,1)} %param.11) | copy-start | bytes 276484
  1.4 23.4 %collective-permute-start = (s32[256]{0:T(256)S(1)}, s32[256]{0:T(256)S(1)}, u32[]{:S(2)}, u32[]{:S(2)}) collective-permute-start(s32[256]{0:T(256)S(1)} %get-tuple-element.32), channel_id=1, source_target_pairs={{0,4},{4,8},{8,12},{12,16},{16,20},{20,24},{24,28},{28,32},{32,36}... | collective-permute-start | bytes 3080 | tf_op jit(solution)/shard_map/ppermute | solution.py:336
  5.9 18.9 %collective-permute-start.1 = (s32[256]{0:T(256)S(1)}, s32[256]{0:T(256)S(1)}, u32[]{:S(2)}, u32[]{:S(2)}) collective-permute-start(s32[256]{0:T(256)S(1)} %get-tuple-element.33), channel_id=1, source_target_pairs={{4,0},{8,4},{12,8},{16,12},{20,16},{24,20},{28,24},{32,28},{36,32}... | collective-permute-start | bytes 3080 | tf_op jit(solution)/shard_map/ppermute | solution.py:337
  11.5 0.7 copy-start.4
  13.2 31.1 %all-to-all-start = ((bf16[128,15,96]{2,1,0:T(8,128)(2,1)}), bf16[128,15,96]{2,1,0:T(8,128)(2,1)S(1)}, u32[]{:S(2)}, u32[]{:S(2)}) async-start(bf16[128,15,96]{2,1,0:T(8,128)(2,1)} %shard_map.114), calls=%async_computation | async-start | bytes 1048576 | tf_op jit(solution)/shard_map/all_to_all | solution.py:321
  38.9 5.6 %collective-permute-start.2 = (bf16[4,40,768]{2,1,0:T(8,128)(2,1)S(1)}, bf16[4,40,768]{2,1,0:T(8,128)(2,1)S(1)}, u32[]{:S(2)}, u32[]{:S(2)}) collective-permute-start(bf16[4,40,768]{2,1,0:T(8,128)(2,1)S(1)} %bitcast.32), channel_id=1, source_target_pairs={{0,4},{4,0},{1,5},{5,1},{2,6},{6,2},{3,7},{7,3},{8,12},{12,8},{9,1... | collective-permute-start | bytes 737288 | tf_op jit(solution)/shard_map/ppermute | solution.py:347
  44.5 12.5 %copy-start.5 = (bf16[1536,192]{0,1:T(8,128)(2,1)S(1)}, bf16[1536,192]{0,1:T(8,128)(2,1)}, u32[]{:S(2)}) copy-start(bf16[1536,192]{0,1:T(8,128)(2,1)} %param.15) | copy-start | bytes 1769476
  46.0 19.1 %all-to-all-start.1 = ((bf16[32,2,384]{2,1,0:T(2,128)(2,1)}), bf16[32,2,384]{2,1,0:T(2,128)(2,1)S(1)}, u32[]{:S(2)}, u32[]{:S(2)}) async-start(bf16[32,2,384]{2,1,0:T(2,128)(2,1)} %shard_map.115), calls=%async_computation.1 | async-start | bytes 98304 | tf_op jit(solution)/shard_map/all_to_all | solution.py:321
  57.0 8.6 %copy-start.2 = (bf16[1536,128]{1,0:T(8,128)(2,1)S(1)}, bf16[1536,128]{1,0:T(8,128)(2,1)}, u32[]{:S(2)}) copy-start(bf16[1536,128]{1,0:T(8,128)(2,1)} %w_query_ref.1) | copy-start | bytes 1179652
  57.0 8.6 %copy-start.3 = (bf16[1536,128]{1,0:T(8,128)(2,1)S(1)}, bf16[1536,128]{1,0:T(8,128)(2,1)}, u32[]{:S(2)}) copy-start(bf16[1536,128]{1,0:T(8,128)(2,1)} %w_key_ref.1) | copy-start | bytes 1179652
  65.6 16.8 %copy-start.6 = (bf16[2,1536,32]{1,2,0:T(8,128)(2,1)S(1)}, bf16[2,1536,32]{1,2,0:T(8,128)(2,1)}, u32[]{:S(2)}) copy-start(bf16[2,1536,32]{1,2,0:T(8,128)(2,1)} %param.17) | copy-start | bytes 589828
  66.7 3.1 %collective-permute-start.3 = (bf16[16,128]{1,0:T(8,128)(2,1)S(1)}, bf16[16,128]{1,0:T(8,128)(2,1)S(1)}, u32[]{:S(2)}, u32[]{:S(2)}) collective-permute-start(bf16[16,128]{1,0:T(8,128)(2,1)S(1)} %get-tuple-element.14), channel_id=1, source_target_pairs={{0,4},{4,0},{1,5},{5,1},{2,6},{6,2},{3,7},{7,3},{8,12},{12,8},{9,1... | collective-permute-start | bytes 12296 | tf_op jit(solution)/shard_map/ppermute | solution.py:356
  69.8 8.4 %collective-permute-start.4 = (bf16[32,128]{1,0:T(8,128)(2,1)S(1)}, bf16[32,128]{1,0:T(8,128)(2,1)S(1)}, u32[]{:S(2)}, u32[]{:S(2)}) collective-permute-start(bf16[32,128]{1,0:T(8,128)(2,1)S(1)} %pad_maximum_fusion.3), channel_id=1, source_target_pairs={{0,8},{8,0},{1,9},{9,1},{2,10},{10,2},{3,11},{11,3},{4,12},{12,4},... | collective-permute-start | bytes 24584 | tf_op jit(solution)/shard_map/ppermute | solution.py:356
  72.0 13.6 %all-to-all-start.2 = ((bf16[16,16,384]{2,1,0:T(8,128)(2,1)}), bf16[16,16,384]{2,1,0:T(8,128)(2,1)S(1)}, u32[]{:S(2)}, u32[]{:S(2)}) async-start(bf16[16,16,384]{2,1,0:T(8,128)(2,1)} %get-tuple-element.15), calls=%async_computation.2 | async-start | bytes 393216 | tf_op jit(solution)/shard_map/all_to_all | solution.py:321
  78.1 6.1 %collective-permute-start.5 = (bf16[64,128]{1,0:T(8,128)(2,1)S(1)}, bf16[64,128]{1,0:T(8,128)(2,1)S(1)}, u32[]{:S(2)}, u32[]{:S(2)}) collective-permute-start(bf16[64,128]{1,0:T(8,128)(2,1)S(1)} %pad_maximum_fusion.2), channel_id=1, source_target_pairs={{0,16},{16,0},{1,17},{17,1},{2,18},{18,2},{3,19},{19,3},{4,20},{20... | collective-permute-start | bytes 49160 | tf_op jit(solution)/shard_map/ppermute | solution.py:356
  86.6 6.8 %copy-start.7 = (bf16[1,128,32]{1,2,0:T(8,128)(2,1)S(1)}, bf16[1,128,32]{1,2,0:T(8,128)(2,1)}, u32[]{:S(2)}) copy-start(bf16[1,128,32]{1,2,0:T(8,128)(2,1)} %param.19) | copy-start | bytes 24580
  86.6 11.9 %copy-start.1 = (bf16[192,1536]{1,0:T(8,128)(2,1)S(1)}, bf16[192,1536]{1,0:T(8,128)(2,1)}, u32[]{:S(2)}) copy-start(bf16[192,1536]{1,0:T(8,128)(2,1)} %w_out_ref.1) | copy-start | bytes 1769476
  86.6 11.9 %all-to-all-start.3 = ((f32[8,16,256]{2,1,0:T(8,128)}), f32[8,16,256]{2,1,0:T(8,128)S(1)}, u32[]{:S(2)}, u32[]{:S(2)}) async-start(f32[8,16,256]{2,1,0:T(8,128)} %shard_map.117), calls=%async_computation.3 | async-start | bytes 262144 | tf_op jit(solution)/shard_map/all_to_all | solution.py:321
  98.5 35.4 %copy-start.8 = (bf16[18,32]{1,0:T(8,128)(2,1)S(1)}, bf16[18,32]{1,0:T(8,128)(2,1)}, u32[]{:S(2)}) copy-start(bf16[18,32]{1,0:T(8,128)(2,1)} %param.18) | copy-start | bytes 3460
  99.5 10.1 %all-to-all-start.4 = ((f32[4,8,384]{2,1,0:T(8,128)}), f32[4,8,384]{2,1,0:T(8,128)S(1)}, u32[]{:S(2)}, u32[]{:S(2)}) async-start(f32[4,8,384]{2,1,0:T(8,128)} %get-tuple-element.17), calls=%async_computation.4 | async-start | bytes 98304 | tf_op jit(solution)/shard_map/all_to_all | solution.py:321
  110.5 23.4 %all-to-all-start.5 = ((f32[128,1,96]{2,1,0:T(1,128)}), f32[128,1,96]{2,1,0:T(1,128)S(1)}, u32[]{:S(2)}, u32[]{:S(2)}) async-start(f32[128,1,96]{2,1,0:T(1,128)} %bitcast.14), calls=%async_computation.5 | async-start | bytes 131072 | tf_op jit(solution)/shard_map/all_to_all | solution.py:321
  120.5 9.8 %collective-permute-start.6 = (f32[16,384]{1,0:T(8,128)S(1)}, f32[16,384]{1,0:T(8,128)S(1)}, u32[]{:S(2)}, u32[]{:S(2)}) collective-permute-start(f32[16,384]{1,0:T(8,128)S(1)} %get-tuple-element.21), channel_id=1, source_target_pairs={{0,1},{1,2},{2,3},{3,0},{4,5},{5,6},{6,7},{7,4},{8,9},{9,10},{10,1... | collective-permute-start | bytes 73736 | tf_op jit(solution)/shard_map/ppermute | solution.py:373
  122.7 8.8 %collective-permute-start.7 = (f32[16,384]{1,0:T(8,128)S(1)}, f32[16,384]{1,0:T(8,128)S(1)}, u32[]{:S(2)}, u32[]{:S(2)}) collective-permute-start(f32[16,384]{1,0:T(8,128)S(1)} %get-tuple-element.22), channel_id=1, source_target_pairs={{0,2},{1,3},{2,0},{3,1},{4,6},{5,7},{6,4},{7,5},{8,10},{9,11},{10,... | collective-permute-start | bytes 73736 | tf_op jit(solution)/shard_map/ppermute | solution.py:373
  126.8 6.4 %collective-permute-start.8 = (f32[16,384]{1,0:T(8,128)S(1)}, f32[16,384]{1,0:T(8,128)S(1)}, u32[]{:S(2)}, u32[]{:S(2)}) collective-permute-start(f32[16,384]{1,0:T(8,128)S(1)} %get-tuple-element.23), channel_id=1, source_target_pairs={{0,3},{1,0},{2,1},{3,2},{4,7},{5,4},{6,5},{7,6},{8,11},{9,8},{10,9... | collective-permute-start | bytes 73736 | tf_op jit(solution)/shard_map/ppermute | solution.py:373

commit v9 on v7

--- a/solution.py
+++ b/solution.py
@@ -16,11 +16,12 @@
 PAIR_POOL = 16
 EDGES = (1, 2, 3, 4, 6, 8, 12, 16, 24, 32, 48, 64, 96, 128, 192, 256, 384)
 
-SIZES = {"zl": 2, "y": 8, "xh": 2, "xl": 2, "core": 2, "pair": 4}
-SEQ = ("zl", "y", "xh", "xl", "core")
+SIZES = {"zl": 2, "yh": 2, "yl": 4, "xh": 2, "xl": 2, "core": 2, "pair": 4}
+SEQ = ("zl", "yh", "yl", "xh", "xl", "core")
+HALF = ("zl", "yl", "xh", "xl", "core")
 SHARE = ("zl", "xl", "core")
 SPREAD = ("xh", "xl", "core")
-LINE = ("zl", "y")
+LINE = ("zl", "yh", "yl")
 N_SEQ = math.prod(SIZES[name] for name in SEQ)
 N_SHARE = math.prod(SIZES[name] for name in SHARE)
 N_PAIR = SIZES["pair"]
@@ -78,51 +79,73 @@
         in_specs=[pl.BlockSpec(memory_space=pltpu.SMEM)] + whole(2),
         out_specs=whole(1)[0],
         compiler_params=params(),
-        cost_estimate=pl.CostEstimate(flops=40_000_000_000, bytes_accessed=200000, transcendentals=0),
+        cost_estimate=pl.CostEstimate(flops=2 * 2304 * 64 * 768, bytes_accessed=200000, transcendentals=0),
     )(place, codes, weight)
 
 
-def pack_kernel(weight_ref, out_ref, wide):
-    taps, width = weight_ref.shape
+def pack_kernel(half_ref, near_ref, far_ref, section_ref, out_ref, wide, joined):
+    taps, width = near_ref.shape
     share = width // N_SHARE
-    half = taps // 2
-    even, odd = [], []
-    for part in range(wide.shape[0]):
-        lanes = weight_ref[:, part * HQK : (part + 1) * HQK]
-        wide[part, :taps, :] = lanes.astype(jnp.float32)
-        wide[part, taps:, :] = jnp.zeros((wide.shape[1] - taps, HQK), jnp.float32)
-        even.append(wide[part, pl.ds(0, half + 1, stride=2), :])
-        odd.append(wide[part, pl.ds(1, half + 1, stride=2), :])
-    even, odd = jnp.concatenate(even, axis=1), jnp.concatenate(odd, axis=1)
-    lane = lax.broadcasted_iota(jnp.int32, (half + 1, HQK), 1)
+    rows = taps // 2
+    pairs = []
+    for ref in (near_ref, far_ref):
+        even, odd = [], []
+        for part in range(wide.shape[0]):
+            lanes = ref[:, part * HQK : (part + 1) * HQK]
+            wide[part, :taps, :] = lanes.astype(jnp.float32)
+            wide[part, taps:, :] = jnp.zeros((wide.shape[1] - taps, HQK), jnp.float32)
+            even.append(wide[part, pl.ds(0, rows + 1, stride=2), :])
+            odd.append(wide[part, pl.ds(1, rows + 1, stride=2), :])
+        pairs.append((jnp.concatenate(even, axis=1), jnp.concatenate(odd, axis=1)))
+    first = half_ref[0] == 0
+    lane = lax.broadcasted_iota(jnp.int32, (rows + 1, HQK), 1)
     blocks = []
     for index in range(N_SHARE):
-        low = pltpu.roll(even, (width - index * share) % width, 1)[:, :HQK]
-        high = pltpu.roll(odd, (width - index * share + share) % width, 1)[:, :HQK]
-        block = jnp.where(lane < share, low, high).astype(jnp.bfloat16)
-        blocks.append(block[:half, : 2 * share])
-    for place in range(N_SEQ):
+        near, far = [
+            jnp.where(
+                lane < share,
+                pltpu.roll(even, (width - index * share) % width, 1)[:, :HQK],
+                pltpu.roll(odd, (width - index * share + share) % width, 1)[:, :HQK],
+            )
+            for even, odd in pairs
+        ]
+        joined[index, : rows + 1, :] = jnp.where(first, near, far)
+        joined[index, rows : 2 * rows + 1, :] = jnp.where(first, far, near)
+        blocks.append(joined[index, :taps, : 2 * share].astype(jnp.bfloat16))
+    for place in range(out_ref.shape[0]):
         at, index, base = place, 0, 1
-        for name in reversed(SEQ):
+        for name in reversed(HALF):
             if name in SHARE:
                 index, base = index + base * (at % SIZES[name]), base * SIZES[name]
             at = at // SIZES[name]
         out_ref[place] = blocks[index]
 
 
-def pack(weight):
-    taps, width = weight.shape
+def pack(half, near, far, section):
+    taps, width = near.shape
+    count = math.prod(SIZES[name] for name in HALF)
     return pl.pallas_call(
         pack_kernel,
-        out_shape=jax.ShapeDtypeStruct((N_SEQ, taps // 2, 2 * width // N_SHARE), jnp.bfloat16),
-        in_specs=whole(1),
+        out_shape=jax.ShapeDtypeStruct((count, taps, 2 * width // N_SHARE), jnp.bfloat16),
+        in_specs=[pl.BlockSpec(memory_space=pltpu.SMEM)] + whole(2) + [pl.BlockSpec(memory_space=pl.ANY)],
         out_specs=whole(1)[0],
-        scratch_shapes=[pltpu.VMEM((width // HQK, taps + 2, HQK), jnp.float32)],
-        compiler_params=params(),
-    )(weight)
-
-
-def conv_kernel(section_ref, weight_ref, out_ref, wide, act, best):
+        scratch_shapes=[
+            pltpu.VMEM((width // HQK, taps + 2, HQK), jnp.float32),
+            pltpu.VMEM((N_SHARE, taps + 2, HQK), jnp.float32),
+        ],
+        compiler_params=params(),
+    )(half, near, far, section)
+
+
+def conv_kernel(section_ref, blocks_ref, out_ref, weights, wide, act, best):
+    count, taps, _ = blocks_ref.shape
+    rows = taps // 2
+    line = count // SIZES["zl"]
+    for source in range(count):
+        block = blocks_ref[source].astype(jnp.float32)
+        for index in range(2):
+            at = (source // line * 2 + index) * line + source % line
+            weights[at * rows : (at + 1) * rows, :] = block[index * rows : (index + 1) * rows, :]
     windows, _, channels = section_ref.shape
     half = channels // 2
     columns = out_ref.shape[2] // 8
@@ -130,7 +153,7 @@
     even, odd = None, None
     for tap in range(KS_CONV):
         rows = wide[:, tap : tap + ROWS, :].astype(jnp.bfloat16).reshape(windows * ROWS, channels)
-        weight = weight_ref[tap * half : (tap + 1) * half, :]
+        weight = weights[tap * half : (tap + 1) * half, :].astype(jnp.bfloat16)
         term = jnp.dot(rows[:, :half], weight, preferred_element_type=jnp.float32)
         even = term if even is None else even + term
         term = jnp.dot(rows[:, half:], weight, preferred_element_type=jnp.float32)
@@ -151,21 +174,22 @@
             out_ref[window * N_PAIR + index] = block
 
 
-def conv(section, weight):
+def conv(section, blocks):
     windows, _, channels = section.shape
-    columns = weight.shape[1] // 2
+    columns = blocks.shape[2] // 2
     return pl.pallas_call(
         conv_kernel,
         out_shape=jax.ShapeDtypeStruct((windows * N_PAIR, 2, 8 * columns), jnp.bfloat16),
         in_specs=whole(2),
         out_specs=whole(1)[0],
         scratch_shapes=[
+            pltpu.VMEM((blocks.shape[0] * blocks.shape[1], 2 * columns), jnp.float32),
             pltpu.VMEM((windows, EXT_PAD, channels), jnp.float32),
             pltpu.VMEM((windows * ROWS, HQK), jnp.float32),
             pltpu.VMEM((windows * ROWS // 2, HQK), jnp.float32),
         ],
         compiler_params=params(),
-    )(section, weight)
+    )(section, blocks)
 
 
 def project_kernel(trunk_ref, w_query_ref, w_key_ref, w_value_ref, query_ref, kv_ref):
@@ -194,6 +218,15 @@
         out_specs=tuple(whole(2)),
         compiler_params=params(),
     )(trunk, w_query, w_key, w_value)
+
+
+def split(x):
+    parts = []
+    for _ in range(3):
+        part = x.astype(jnp.bfloat16).astype(jnp.float32)
+        parts.append(part)
+        x = x - part
+    return parts
 
 
 def attention_kernel(place_ref, query_ref, kv_ref, out_ref):
@@ -212,7 +245,9 @@
     total = jnp.sum(expo, axis=1, keepdims=True)
     mixed = jnp.dot(expo.astype(jnp.bfloat16), kv_ref[:, HQK:], preferred_element_type=jnp.float32)
     lane = lax.broadcasted_iota(jnp.int32, mixed.shape, 1)
-    mixed = jnp.where(lane == HV, top, jnp.where(lane == HV + 1, total, mixed))
+    for index, column in enumerate(split(top) + split(total)):
+        mixed = jnp.where(lane == HV + index, column, mixed)
+    mixed = mixed.astype(jnp.bfloat16)
     groups, count, _ = out_ref.shape
     for index in range(groups):
         out_ref[place_ref[0] ^ index] = mixed[index * count : (index + 1) * count, :]
@@ -223,7 +258,7 @@
     count, width = query.shape[0] // groups, kv.shape[1] - HQK
     return pl.pallas_call(
         attention_kernel,
-        out_shape=jax.ShapeDtypeStruct((groups, count, width), jnp.float32),
+        out_shape=jax.ShapeDtypeStruct((groups, count, width), jnp.bfloat16),
         in_specs=[pl.BlockSpec(memory_space=pltpu.SMEM)] + whole(2),
         out_specs=whole(1)[0],
         compiler_params=params(),
@@ -231,10 +266,10 @@
 
 
 def combine_kernel(parts_ref, w_out_ref, out_ref):
-    parts = parts_ref[...]
-    top = parts[:, :, HV : HV + 1]
+    parts = parts_ref[...].astype(jnp.float32)
+    top = jnp.sum(parts[:, :, HV : HV + 3], axis=2, keepdims=True)
     gain = jnp.exp(top - jnp.max(top, axis=0, keepdims=True))
-    total = jnp.sum(gain * parts[:, :, HV + 1 : HV + 2], axis=0)
+    total = jnp.sum(gain * jnp.sum(parts[:, :, HV + 3 : HV + 6], axis=2, keepdims=True), axis=0)
     mixed = (jnp.sum(gain * parts, axis=0) / total)[:, :HV].astype(jnp.bfloat16)
     term = jnp.dot(mixed, w_out_ref[...], preferred_element_type=jnp.float32)
     mean = jnp.sum(term, axis=0, keepdims=True) * (1.0 / PAIR_POOL)
@@ -316,8 +351,7 @@
 
     taps, width = w_conv.shape
     share = width // N_SHARE
-    blocks = exchange(pack(w_conv), SEQ)
-    conv_weight = blocks.reshape(N_SEQ * blocks.shape[1], blocks.shape[2])
+    swapped = lax.ppermute(w_conv, "yh", [(0, 1), (1, 0)])
 
     codes = tokens + 1
     ends = N_SEQ - 1
@@ -331,9 +365,12 @@
     stem_weight = stem_weight.reshape(KS_STEM, 4, -1)[::-1].transpose(1, 0, 2)
     stem_weight = jnp.pad(stem_weight, ((0, 0), (0, 1), (0, 0))).reshape(64, -1)
     section = stem(place.astype(jnp.int32)[None], codes, stem_weight).astype(jnp.bfloat16)
+
+    half = lax.axis_index("yh").astype(jnp.int32)[None]
+    blocks = exchange(pack(half, w_conv, swapped, section), HALF)
     sections = lax.all_gather(section, SHARE, axis=0, tiled=False)
 
-    parts = exchange(conv(sections, conv_weight), SHARE + ("pair",))
+    parts = exchange(conv(sections, blocks), SHARE + ("pair",))
     count = ROWS // 2
     trunk = parts.reshape(N_SHARE, N_PAIR, count, share).transpose(2, 1, 0, 3)
     trunk = trunk.reshape(count, N_PAIR * width)

time: 132 us -> 133 us (level)
  starting transfers between devices: 64.4 us -> 66.7 us
    ppermute x0 -> x1, starting transfers between devices: none -> 3.81 us  [on_device(): swapped = lax.ppermute(w_conv, 'yh', [(0, 1), (1, 0)])]
    all_to_all x6, waiting for transfers between devices: 34.7 us -> 32.3 us  [exchange(): return lax.all_to_all(blocks, axes, split_axis=0, concat_axis=0, tiled=True)]
    ppermute x0 -> x1, waiting for transfers between devices: none -> 2.31 us  [on_device(): swapped = lax.ppermute(w_conv, 'yh', [(0, 1), (1, 0)])]
  transfers between devices with their start and end apart: 11 -> 12, of which waited for: 8 -> 9; matrix products, arithmetic and copies ran while one was open for 2% -> 2% of each run, Pallas kernels for 2% -> 1%
where the time goes in v9:
time: 133 us
  starting transfers between devices  66.7 us (50%)
  waiting for transfers between devices  37 us (28%)
  blocking collectives  15.5 us (12%)
  Pallas kernels  8.16 us (6%)
  local copies, waits for them, and re-layouts  1.9 us (1%)
  matrix products  1.33 us (1%)
    all_to_all x6, starting transfers between devices, exchange(): return lax.all_to_all(blocks, axes, split_axis=0, concat_axis=0, tiled=True)  44.2 us
    all_to_all x6, waiting for transfers between devices, exchange(): return lax.all_to_all(blocks, axes, split_axis=0, concat_axis=0, tiled=True)  32.3 us
    all_gather x1, blocking collectives, on_device(): sections = lax.all_gather(section, SHARE, axis=0, tiled=False)  15.5 us
    ppermute x3, starting transfers between devices, on_device(): other = lax.ppermute(query, name, [(0, 1), (1, 0)])  8.59 us
    ppermute x1, starting transfers between devices, on_device(): right = lax.ppermute(codes[:SIDE], SEQ, [(i + 1, i) for i in range(ends)])  5.57 us
    ppermute x1, starting transfers between devices, on_device(): left = lax.ppermute(codes[-SIDE:], SEQ, [(i, i + 1) for i in range(ends)])  4.5 us
    ppermute x1, starting transfers between devices, on_device(): swapped = lax.ppermute(w_conv, 'yh', [(0, 1), (1, 0)])  3.81 us
  transfers between devices with their start and end apart: 12, of which 9 were waited for; matrix products, arithmetic and copies ran while one was open for 2% of the time, Pallas kernels for 1%

profile of v9, /device:TPU:1, one launch (start us, length us, event | category | flops | bytes accessed | tf_op | source)
XLA Modules:
  0.0 132.6 jit_solution(3714705126061767708)
XLA Ops:
  0.6 0.0 copy-start
  0.6 0.7 broadcast_add_fusion
  1.4 4.5 %collective-permute-start = (s32[256]{0:T(256)S(1)}, s32[256]{0:T(256)S(1)}, u32[]{:S(2)}, u32[]{:S(2)}) collective-permute-start(s32[256]{0:T(256)S(1)} %get-tuple-element.16), channel_id=1, source_target_pairs={{0,4},{4,8},{8,12},{12,16},{16,20},{20,24},{24,28},{28,32},{32,36}... | collective-permute-start | bytes 3080 | tf_op jit(solution)/shard_map/ppermute | solution.py:358
  5.9 5.6 %collective-permute-start.1 = (s32[256]{0:T(256)S(1)}, s32[256]{0:T(256)S(1)}, u32[]{:S(2)}, u32[]{:S(2)}) collective-permute-start(s32[256]{0:T(256)S(1)} %get-tuple-element.17), channel_id=1, source_target_pairs={{4,0},{8,4},{12,8},{16,12},{20,16},{24,20},{28,24},{32,28},{36,32}... | collective-permute-start | bytes 3080 | tf_op jit(solution)/shard_map/ppermute | solution.py:359
  11.5 3.8 %collective-permute-start.2 = (bf16[30,384]{1,0:T(8,128)(2,1)}, bf16[30,384]{1,0:T(8,128)(2,1)S(1)}, u32[]{:S(2)}, u32[]{:S(2)}) collective-permute-start(bf16[30,384]{1,0:T(8,128)(2,1)} %near_ref.1), channel_id=1, source_target_pairs={{0,128},{128,0},{1,129},{129,1},{2,130},{130,2},{3,131},{131,3},{4... | collective-permute-start | bytes 69128 | tf_op jit(solution)/shard_map/ppermute | solution.py:354
  15.4 0.0 copy-done
  15.4 0.5 fusion.3
  15.9 0.0 copy-start.4
  16.0 0.3 rev.3
  16.3 0.0 collective-permute-done
  16.3 0.0 collective-permute-done.1
  16.4 1.7 %shard_map.113 = f32[40,768]{1,0:T(8,128)S(1)} custom-call(s32[1]{0:T(128)} %bitcast.1.place_ref, s32[1,2560]{1,0:T(1,128)S(1)} %broadcast_in_dim.24.codes_ref, bf16[64,768]{1,0:T(8,128)(2,1)S(1)} %bitcast.33), custom_call_target="tpu_custom_call" | custom-call | flops 226492416 | bytes 200000 | tf_op jit(solution)/shard_map/pallas_call | solution.py:76
  18.1 2.3 %collective-permute-done.2.far_ref = bf16[30,384]{1,0:T(8,128)(2,1)S(1)} collective-permute-done((bf16[30,384]{1,0:T(8,128)(2,1)}, bf16[30,384]{1,0:T(8,128)(2,1)S(1)}, u32[]{:S(2)}, u32[]{:S(2)}) %collective-permute-start.2) | collective-permute-done | bytes 23072 | tf_op jit(solution)/shard_map/ppermute | solution.py:354
  20.4 0.0 copy-done.4
  20.4 1.0 shard_map.114
  21.4 7.6 %all-to-all-start = ((bf16[64,30,96]{2,1,0:T(8,128)(2,1)}), bf16[64,30,96]{2,1,0:T(8,128)(2,1)S(1)}, u32[]{:S(2)}, u32[]{:S(2)}) async-start(bf16[64,30,96]{2,1,0:T(8,128)(2,1)} %shard_map.114), calls=%async_computation | async-start | bytes 1048576 | tf_op jit(solution)/shard_map/all_to_all | solution.py:345
  29.0 0.0 copy-start.5
  29.0 15.5 %all-gather = bf16[320,768]{1,0:T(8,128)(2,1)S(1)} all-gather(bf16[40,768]{1,0:T(8,128)(2,1)S(1)} %convert_element_type.143.section_ref), channel_id=2, replica_groups=mesh['zl'=2,'yh'=2,'yl'=4,'xh'=2,'xl'=2,'core'=2,'pair'=4] {'zl','xl','c..., dimensions={0}, use_global_device_ids=true | all-gather | bytes 552960 | tf_op jit(solution)/shard_map/all_gather | solution.py:371
  44.6 0.5 all-to-all-done.blocks_ref
  45.0 1.6 %shard_map.115 = bf16[32,2,384]{2,1,0:T(2,128)(2,1)} custom-call(bf16[8,40,768]{2,1,0:T(8,128)(2,1)S(1)} %bitcast.31, bf16[64,30,96]{2,1,0:T(8,128)(2,1)S(1)} %all-to-all-done.blocks_ref), custom_call_target="tpu_custom_call" | custom-call | tf_op jit(solution)/shard_map/pallas_call | solution.py:180
  46.6 11.0 %all-to-all-start.1 = ((bf16[32,2,384]{2,1,0:T(2,128)(2,1)}), bf16[32,2,384]{2,1,0:T(2,128)(2,1)S(1)}, u32[]{:S(2)}, u32[]{:S(2)}) async-start(bf16[32,2,384]{2,1,0:T(2,128)(2,1)} %shard_map.115), calls=%async_computation.1 | async-start | bytes 98304 | tf_op jit(solution)/shard_map/all_to_all | solution.py:345
  57.6 0.0 copy-done.5
  57.6 0.0 copy-start.2
  57.6 0.0 copy-start.3
  57.7 0.3 copy.23.w_value_ref
  57.9 7.9 %all-to-all-done.1 = bf16[32,2,384]{2,1,0:T(2,128)(2,1)S(1)} async-done(((bf16[32,2,384]{2,1,0:T(2,128)(2,1)}), bf16[32,2,384]{2,1,0:T(2,128)(2,1)S(1)}, u32[]{:S(2)}, u32[]{:S(2)}) %all-to-all-start.1) | async-done | bytes 49184 | tf_op jit(solution)/shard_map/all_to_all | solution.py:345
  65.8 0.2 reshape.116
  66.0 0.1 copy.32
  66.1 0.2 reshape.117.trunk_ref
  66.3 0.0 copy-done.2
  66.3 0.0 copy-done.3
  66.3 0.0 copy-start.6
  66.3 1.0 shard_map.116
  67.3 2.3 %collective-permute-start.3 = (bf16[16,128]{1,0:T(8,128)(2,1)S(1)}, bf16[16,128]{1,0:T(8,128)(2,1)S(1)}, u32[]{:S(2)}, u32[]{:S(2)}) collective-permute-start(bf16[16,128]{1,0:T(8,128)(2,1)S(1)} %get-tuple-element.7), channel_id=1, source_target_pairs={{0,4},{4,0},{1,5},{5,1},{2,6},{6,2},{3,7},{7,3},{8,12},{12,8},{9,1... | collective-permute-start | bytes 12296 | tf_op jit(solution)/shard_map/ppermute | solution.py:380
  69.6 0.8 collective-permute-done.3
  70.4 2.2 %collective-permute-start.4 = (bf16[32,128]{1,0:T(8,128)(2,1)S(1)}, bf16[32,128]{1,0:T(8,128)(2,1)S(1)}, u32[]{:S(2)}, u32[]{:S(2)}) collective-permute-start(bf16[32,128]{1,0:T(8,128)(2,1)S(1)} %pad_maximum_fusion.3), channel_id=1, source_target_pairs={{0,8},{8,0},{1,9},{9,1},{2,10},{10,2},{3,11},{11,3},{4,12},{12,4},... | collective-permute-start | bytes 24584 | tf_op jit(solution)/shard_map/ppermute | solution.py:380
  72.6 5.7 %all-to-all-start.2 = ((bf16[16,16,384]{2,1,0:T(8,128)(2,1)}), bf16[16,16,384]{2,1,0:T(8,128)(2,1)S(1)}, u32[]{:S(2)}, u32[]{:S(2)}) async-start(bf16[16,16,384]{2,1,0:T(8,128)(2,1)} %get-tuple-element.8), calls=%async_computation.2 | async-start | bytes 393216 | tf_op jit(solution)/shard_map/all_to_all | solution.py:345
  78.3 0.0 collective-permute-done.4
  78.3 4.1 %collective-permute-start.5 = (bf16[64,128]{1,0:T(8,128)(2,1)S(1)}, bf16[64,128]{1,0:T(8,128)(2,1)S(1)}, u32[]{:S(2)}, u32[]{:S(2)}) collective-permute-start(bf16[64,128]{1,0:T(8,128)(2,1)S(1)} %pad_maximum_fusion.2), channel_id=1, source_target_pairs={{0,16},{16,0},{1,17},{17,1},{2,18},{18,2},{3,19},{19,3},{4,20},{20... | collective-permute-start | bytes 49160 | tf_op jit(solution)/shard_map/ppermute | solution.py:380
  82.4 0.0 copy-done.6
  82.5 0.2 copy.30
  82.7 0.2 copy.29
  82.9 1.5 %collective-permute-done.5 = bf16[64,128]{1,0:T(8,128)(2,1)S(1)} collective-permute-done((bf16[64,128]{1,0:T(8,128)(2,1)S(1)}, bf16[64,128]{1,0:T(8,128)(2,1)S(1)}, u32[]{:S(2)}, u32[]{:S(2)}) %collective-permute-start.5) | collective-permute-done | bytes 16416 | tf_op jit(solution)/shard_map/ppermute | solution.py:380
  84.5 1.3 %all-to-all-done.2 = bf16[16,16,384]{2,1,0:T(8,128)(2,1)S(1)} async-done(((bf16[16,16,384]{2,1,0:T(8,128)(2,1)}), bf16[16,16,384]{2,1,0:T(8,128)(2,1)S(1)}, u32[]{:S(2)}, u32[]{:S(2)}) %all-to-all-start.2) | async-done | bytes 196640 | tf_op jit(solution)/shard_map/all_to_all | solution.py:345
  85.8 0.0 copy-start.7
  85.8 0.0 copy-start.1
  85.8 1.0 shard_map.117
  86.8 6.2 %all-to-all-start.3 = ((bf16[8,16,256]{2,1,0:T(8,128)(2,1)}), bf16[8,16,256]{2,1,0:T(8,128)(2,1)S(1)}, u32[]{:S(2)}, u32[]{:S(2)}) async-start(bf16[8,16,256]{2,1,0:T(8,128)(2,1)} %shard_map.117), calls=%async_computation.3 | async-start | bytes 131072 | tf_op jit(solution)/shard_map/all_to_all | solution.py:345
  93.1 0.2 pad_maximum_fusion.w_pair_ref
  93.3 0.0 copy-done.7
  93.3 0.1 copy.26.pair_ref
  93.4 4.5 %all-to-all-done.3.parts_ref = bf16[8,16,256]{2,1,0:T(8,128)(2,1)S(1)} async-done(((bf16[8,16,256]{2,1,0:T(8,128)(2,1)}), bf16[8,16,256]{2,1,0:T(8,128)(2,1)S(1)}, u32[]{:S(2)}, u32[]{:S(2)}) %all-to-all-start.3) | async-done | bytes 65568 | tf_op jit(solution)/shard_map/all_to_all | solution.py:345
  97.9 0.0 copy-done.1
  97.9 1.0 shard_map.118
  99.0 0.0 copy-start.8
  99.0 3.5 %all-to-all-start.4 = ((f32[4,24,384]{2,1,0:T(8,128)}), f32[4,24,384]{2,1,0:T(8,128)S(1)}, u32[]{:S(2)}, u32[]{:S(2)}) async-start(f32[4,24,384]{2,1,0:T(8,128)} %shard_map.118), calls=%async_computation.4 | async-start | bytes 294912 | tf_op jit(solution)/shard_map/all_to_all | solution.py:345
  102.5 7.3 %all-to-all-done.4.terms_ref = f32[4,24,384]{2,1,0:T(8,128)S(1)} async-done(((f32[4,24,384]{2,1,0:T(8,128)}), f32[4,24,384]{2,1,0:T(8,128)S(1)}, u32[]{:S(2)}, u32[]{:S(2)}) %all-to-all-start.4) | async-done | bytes 147488 | tf_op jit(solution)/shard_map/all_to_all | solution.py:345
  109.8 0.8 shard_map.119
  110.7 10.2 %all-to-all-start.5 = ((f32[128,1,96]{2,1,0:T(1,128)}), f32[128,1,96]{2,1,0:T(1,128)S(1)}, u32[]{:S(2)}, u32[]{:S(2)}) async-start(f32[128,1,96]{2,1,0:T(1,128)} %bitcast.13), calls=%async_computation.5 | async-start | bytes 131072 | tf_op jit(solution)/shard_map/all_to_all | solution.py:345
  120.9 0.1 slice_bitcast_fusion.1
  121.0 10.8 %all-to-all-done.5 = f32[128,1,96]{2,1,0:T(1,128)S(1)} async-done(((f32[128,1,96]{2,1,0:T(1,128)}), f32[128,1,96]{2,1,0:T(1,128)S(1)}, u32[]{:S(2)}, u32[]{:S(2)}) %all-to-all-start.5) | async-done | bytes 49184 | tf_op jit(solution)/shard_map/all_to_all | solution.py:345
  131.7 0.1 copy.28
  131.8 0.0 copy-done.8
  131.8 0.8 fusion.5
  (18 shorter events, 0.2 us)
Async XLA Ops:
  0.6 14.7 %copy-start = (bf16[60,768]{1,0:T(8,128)(2,1)S(1)}, bf16[60,768]{1,0:T(8,128)(2,1)}, u32[]{:S(2)}) copy-start(bf16[60,768]{1,0:T(8,128)(2,1)} %param.11) | copy-start | bytes 276484
  1.4 14.9 %collective-permute-start = (s32[256]{0:T(256)S(1)}, s32[256]{0:T(256)S(1)}, u32[]{:S(2)}, u32[]{:S(2)}) collective-permute-start(s32[256]{0:T(256)S(1)} %get-tuple-element.16), channel_id=1, source_target_pairs={{0,4},{4,8},{8,12},{12,16},{16,20},{20,24},{24,28},{28,32},{32,36}... | collective-permute-start | bytes 3080 | tf_op jit(solution)/shard_map/ppermute | solution.py:358
  5.9 10.4 %collective-permute-start.1 = (s32[256]{0:T(256)S(1)}, s32[256]{0:T(256)S(1)}, u32[]{:S(2)}, u32[]{:S(2)}) collective-permute-start(s32[256]{0:T(256)S(1)} %get-tuple-element.17), channel_id=1, source_target_pairs={{4,0},{8,4},{12,8},{16,12},{20,16},{24,20},{28,24},{32,28},{36,32}... | collective-permute-start | bytes 3080 | tf_op jit(solution)/shard_map/ppermute | solution.py:359
  11.5 9.0 %collective-permute-start.2 = (bf16[30,384]{1,0:T(8,128)(2,1)}, bf16[30,384]{1,0:T(8,128)(2,1)S(1)}, u32[]{:S(2)}, u32[]{:S(2)}) collective-permute-start(bf16[30,384]{1,0:T(8,128)(2,1)} %near_ref.1), channel_id=1, source_target_pairs={{0,128},{128,0},{1,129},{129,1},{2,130},{130,2},{3,131},{131,3},{4... | collective-permute-start | bytes 69128 | tf_op jit(solution)/shard_map/ppermute | solution.py:354
  15.9 4.5 %copy-start.4 = (bf16[30,384]{1,0:T(8,128)(2,1)S(1)}, bf16[30,384]{1,0:T(8,128)(2,1)}, u32[]{:S(2)}) copy-start(bf16[30,384]{1,0:T(8,128)(2,1)} %near_ref.1) | copy-start | bytes 69124
  21.4 23.6 %all-to-all-start = ((bf16[64,30,96]{2,1,0:T(8,128)(2,1)}), bf16[64,30,96]{2,1,0:T(8,128)(2,1)S(1)}, u32[]{:S(2)}, u32[]{:S(2)}) async-start(bf16[64,30,96]{2,1,0:T(8,128)(2,1)} %shard_map.114), calls=%async_computation | async-start | bytes 1048576 | tf_op jit(solution)/shard_map/all_to_all | solution.py:345
  29.0 28.6 %copy-start.5 = (bf16[1536,192]{0,1:T(8,128)(2,1)S(1)}, bf16[1536,192]{0,1:T(8,128)(2,1)}, u32[]{:S(2)}) copy-start(bf16[1536,192]{0,1:T(8,128)(2,1)} %param.15) | copy-start | bytes 1769476
  46.6 19.2 %all-to-all-start.1 = ((bf16[32,2,384]{2,1,0:T(2,128)(2,1)}), bf16[32,2,384]{2,1,0:T(2,128)(2,1)S(1)}, u32[]{:S(2)}, u32[]{:S(2)}) async-start(bf16[32,2,384]{2,1,0:T(2,128)(2,1)} %shard_map.115), calls=%async_computation.1 | async-start | bytes 98304 | tf_op jit(solution)/shard_map/all_to_all | solution.py:345
  57.6 8.6 %copy-start.2 = (bf16[1536,128]{1,0:T(8,128)(2,1)S(1)}, bf16[1536,128]{1,0:T(8,128)(2,1)}, u32[]{:S(2)}) copy-start(bf16[1536,128]{1,0:T(8,128)(2,1)} %w_query_ref.1) | copy-start | bytes 1179652
  57.6 8.6 %copy-start.3 = (bf16[1536,128]{1,0:T(8,128)(2,1)S(1)}, bf16[1536,128]{1,0:T(8,128)(2,1)}, u32[]{:S(2)}) copy-start(bf16[1536,128]{1,0:T(8,128)(2,1)} %w_key_ref.1) | copy-start | bytes 1179652
  66.3 16.2 %copy-start.6 = (bf16[2,1536,32]{1,2,0:T(8,128)(2,1)S(1)}, bf16[2,1536,32]{1,2,0:T(8,128)(2,1)}, u32[]{:S(2)}) copy-start(bf16[2,1536,32]{1,2,0:T(8,128)(2,1)} %param.17) | copy-start | bytes 589828
  67.3 3.1 %collective-permute-start.3 = (bf16[16,128]{1,0:T(8,128)(2,1)S(1)}, bf16[16,128]{1,0:T(8,128)(2,1)S(1)}, u32[]{:S(2)}, u32[]{:S(2)}) collective-permute-start(bf16[16,128]{1,0:T(8,128)(2,1)S(1)} %get-tuple-element.7), channel_id=1, source_target_pairs={{0,4},{4,0},{1,5},{5,1},{2,6},{6,2},{3,7},{7,3},{8,12},{12,8},{9,1... | collective-permute-start | bytes 12296 | tf_op jit(solution)/shard_map/ppermute | solution.py:380
  70.4 7.9 %collective-permute-start.4 = (bf16[32,128]{1,0:T(8,128)(2,1)S(1)}, bf16[32,128]{1,0:T(8,128)(2,1)S(1)}, u32[]{:S(2)}, u32[]{:S(2)}) collective-permute-start(bf16[32,128]{1,0:T(8,128)(2,1)S(1)} %pad_maximum_fusion.3), channel_id=1, source_target_pairs={{0,8},{8,0},{1,9},{9,1},{2,10},{10,2},{3,11},{11,3},{4,12},{12,4},... | collective-permute-start | bytes 24584 | tf_op jit(solution)/shard_map/ppermute | solution.py:380
  72.6 13.2 %all-to-all-start.2 = ((bf16[16,16,384]{2,1,0:T(8,128)(2,1)}), bf16[16,16,384]{2,1,0:T(8,128)(2,1)S(1)}, u32[]{:S(2)}, u32[]{:S(2)}) async-start(bf16[16,16,384]{2,1,0:T(8,128)(2,1)} %get-tuple-element.8), calls=%async_computation.2 | async-start | bytes 393216 | tf_op jit(solution)/shard_map/all_to_all | solution.py:345
  78.3 6.1 %collective-permute-start.5 = (bf16[64,128]{1,0:T(8,128)(2,1)S(1)}, bf16[64,128]{1,0:T(8,128)(2,1)S(1)}, u32[]{:S(2)}, u32[]{:S(2)}) collective-permute-start(bf16[64,128]{1,0:T(8,128)(2,1)S(1)} %pad_maximum_fusion.2), channel_id=1, source_target_pairs={{0,16},{16,0},{1,17},{17,1},{2,18},{18,2},{3,19},{19,3},{4,20},{20... | collective-permute-start | bytes 49160 | tf_op jit(solution)/shard_map/ppermute | solution.py:380
  85.8 7.5 %copy-start.7 = (bf16[1,128,32]{1,2,0:T(8,128)(2,1)S(1)}, bf16[1,128,32]{1,2,0:T(8,128)(2,1)}, u32[]{:S(2)}) copy-start(bf16[1,128,32]{1,2,0:T(8,128)(2,1)} %param.19) | copy-start | bytes 24580
  85.8 12.1 %copy-start.1 = (bf16[192,1536]{1,0:T(8,128)(2,1)S(1)}, bf16[192,1536]{1,0:T(8,128)(2,1)}, u32[]{:S(2)}) copy-start(bf16[192,1536]{1,0:T(8,128)(2,1)} %w_out_ref.1) | copy-start | bytes 1769476
  86.8 11.1 %all-to-all-start.3 = ((bf16[8,16,256]{2,1,0:T(8,128)(2,1)}), bf16[8,16,256]{2,1,0:T(8,128)(2,1)S(1)}, u32[]{:S(2)}, u32[]{:S(2)}) async-start(bf16[8,16,256]{2,1,0:T(8,128)(2,1)} %shard_map.117), calls=%async_computation.3 | async-start | bytes 131072 | tf_op jit(solution)/shard_map/all_to_all | solution.py:345
  99.0 32.8 %copy-start.8 = (bf16[18,32]{1,0:T(8,128)(2,1)S(1)}, bf16[18,32]{1,0:T(8,128)(2,1)}, u32[]{:S(2)}) copy-start(bf16[18,32]{1,0:T(8,128)(2,1)} %param.18) | copy-start | bytes 3460
  99.0 10.9 %all-to-all-start.4 = ((f32[4,24,384]{2,1,0:T(8,128)}), f32[4,24,384]{2,1,0:T(8,128)S(1)}, u32[]{:S(2)}, u32[]{:S(2)}) async-start(f32[4,24,384]{2,1,0:T(8,128)} %shard_map.118), calls=%async_computation.4 | async-start | bytes 294912 | tf_op jit(solution)/shard_map/all_to_all | solution.py:345
  110.7 21.1 %all-to-all-start.5 = ((f32[128,1,96]{2,1,0:T(1,128)}), f32[128,1,96]{2,1,0:T(1,128)S(1)}, u32[]{:S(2)}, u32[]{:S(2)}) async-start(f32[128,1,96]{2,1,0:T(1,128)} %bitcast.13), calls=%async_computation.5 | async-start | bytes 131072 | tf_op jit(solution)/shard_map/all_to_all | solution.py:345

commit v10 on v7

--- a/solution.py
+++ b/solution.py
@@ -27,10 +27,10 @@
 N_SPREAD = math.prod(SIZES[name] for name in SPREAD)
 N_LINE = math.prod(SIZES[name] for name in LINE)
 
-SIDE = 256
 ROWS = 32
-EXT = ROWS + 4
 EXT_PAD = 40
+EDGE = 4
+RUN = 4
 VMEM = 48 * 1024 * 1024
 
 
@@ -46,43 +46,46 @@
     return 0.5 * x * (1.0 + jnp.tanh(math.sqrt(2.0 / math.pi) * (x + 0.044715 * (x * x * x))))
 
 
-def stem_kernel(place_ref, codes_ref, weight_ref, out_ref):
-    length = codes_ref.shape[1]
-    codes = jnp.broadcast_to(codes_ref[...], (16, length))
-    first = SIDE - 2 * STEM_POOL + KS_STEM // 2
-    shifted = pltpu.roll(codes, length - first, 1, stride=1, stride_axis=0)
-    shifted = shifted[:, : EXT * STEM_POOL]
-    onehot = jnp.concatenate(
+def onehot_rows(codes, first, count):
+    length = codes.shape[1]
+    start = (length - first - KS_STEM // 2) % length
+    shifted = pltpu.roll(jnp.broadcast_to(codes, (16, length)), start, 1, stride=1, stride_axis=0)
+    shifted = shifted[:, :count]
+    return jnp.concatenate(
         [(shifted == base + 1).astype(jnp.float32) for base in range(4)], axis=0
     ).astype(jnp.bfloat16)
+
+
+def pooled_rows(onehot, weight):
+    hidden = lax.dot_general(
+        onehot, weight, (((0,), (0,)), ((), ())), preferred_element_type=jnp.float32
+    ).reshape(onehot.shape[1] // STEM_POOL, STEM_POOL, weight.shape[1])
+    high = gelu(jnp.max(hidden, axis=1))
+    low = gelu(jnp.min(hidden, axis=1))
+    return jnp.maximum(high, low)
+
+
+def stem_kernel(tokens_ref, weight_ref, out_ref):
+    onehot = onehot_rows(tokens_ref[...] + 1, 0, tokens_ref.shape[1])
     weight = weight_ref[...]
-    step = 6
-    for at in range(0, EXT, step):
+    step = 8
+    for at in range(0, ROWS, step):
         part = onehot[:, at * STEM_POOL : (at + step) * STEM_POOL]
-        hidden = lax.dot_general(
-            part, weight, (((0,), (0,)), ((), ())), preferred_element_type=jnp.float32
-        ).reshape(step, STEM_POOL, weight.shape[1])
-        high = gelu(jnp.max(hidden, axis=1))
-        low = gelu(jnp.min(hidden, axis=1))
-        rows = jnp.maximum(high, low)
-        index = place_ref[0] * ROWS - 2 + at + lax.broadcasted_iota(jnp.int32, rows.shape, 0)
-        inside = (index >= 0) & (index < N_SEQ * ROWS)
-        out_ref[at : at + step, :] = jnp.where(inside, rows, 0.0)
-    out_ref[EXT:EXT_PAD, :] = jnp.zeros((EXT_PAD - EXT, weight.shape[1]), jnp.float32)
-
-
-def stem(place, codes, weight):
+        out_ref[at : at + step, :] = pooled_rows(part, weight)
+
+
+def stem(tokens, weight):
     return pl.pallas_call(
         stem_kernel,
-        out_shape=jax.ShapeDtypeStruct((EXT_PAD, weight.shape[1]), jnp.float32),
-        in_specs=[pl.BlockSpec(memory_space=pltpu.SMEM)] + whole(2),
+        out_shape=jax.ShapeDtypeStruct((ROWS, weight.shape[1]), jnp.float32),
+        in_specs=whole(2),
         out_specs=whole(1)[0],
         compiler_params=params(),
-        cost_estimate=pl.CostEstimate(flops=40_000_000_000, bytes_accessed=200000, transcendentals=0),
-    )(place, codes, weight)
-
-
-def pack_kernel(weight_ref, out_ref, wide):
+        cost_estimate=pl.CostEstimate(flops=2 * 2048 * 64 * 768, bytes_accessed=200000, transcendentals=0),
+    )(tokens, weight)
+
+
+def pack_kernel(weight_ref, tokens_ref, out_ref, wide):
     taps, width = weight_ref.shape
     share = width // N_SHARE
     half = taps // 2
@@ -95,12 +98,19 @@
         odd.append(wide[part, pl.ds(1, half + 1, stride=2), :])
     even, odd = jnp.concatenate(even, axis=1), jnp.concatenate(odd, axis=1)
     lane = lax.broadcasted_iota(jnp.int32, (half + 1, HQK), 1)
+    row = lax.broadcasted_iota(jnp.int32, (half + 1, HQK), 0)
+    codes = (tokens_ref[...] + 1).astype(jnp.float32)
+    last = codes.shape[0] - 1
+    line = [jnp.broadcast_to(codes[at : at + 1, :], lane.shape) for at in (0, 1, last - 1, last)]
+    outer = jnp.where(lane >= HQK - 7, line[2], pltpu.roll(line[1], 96, 1))
+    for index in range(4):
+        outer = jnp.where(row == index, pltpu.roll(line[3], (96 - 32 * index) % HQK, 1), outer)
     blocks = []
     for index in range(N_SHARE):
         low = pltpu.roll(even, (width - index * share) % width, 1)[:, :HQK]
         high = pltpu.roll(odd, (width - index * share + share) % width, 1)[:, :HQK]
-        block = jnp.where(lane < share, low, high).astype(jnp.bfloat16)
-        blocks.append(block[:half, : 2 * share])
+        block = jnp.where(lane < share, low, jnp.where(lane < 2 * share, high, outer))
+        blocks.append(jnp.where(row == half, line[0], block).astype(jnp.bfloat16))
     for place in range(N_SEQ):
         at, index, base = place, 0, 1
         for name in reversed(SEQ):
@@ -110,33 +120,72 @@
         out_ref[place] = blocks[index]
 
 
-def pack(weight):
+def pack(weight, tokens):
     taps, width = weight.shape
     return pl.pallas_call(
         pack_kernel,
-        out_shape=jax.ShapeDtypeStruct((N_SEQ, taps // 2, 2 * width // N_SHARE), jnp.bfloat16),
-        in_specs=whole(1),
+        out_shape=jax.ShapeDtypeStruct((N_SEQ, taps // 2 + 1, HQK), jnp.bfloat16),
+        in_specs=whole(2),
         out_specs=whole(1)[0],
         scratch_shapes=[pltpu.VMEM((width // HQK, taps + 2, HQK), jnp.float32)],
         compiler_params=params(),
-    )(weight)
-
-
-def conv_kernel(section_ref, weight_ref, out_ref, wide, act, best):
+    )(weight, tokens)
+
+
+def border_codes(held_ref, right):
+    before = held_ref[jnp.maximum(right - 1, 0)].astype(jnp.float32)
+    after = held_ref[jnp.minimum(right, N_SEQ - 1)].astype(jnp.float32)
+    before = jnp.where(right > 0, before, 0.0)
+    after = jnp.where(right < N_SEQ, after, 0.0)
+    lane = lax.broadcasted_iota(jnp.int32, (1, HQK), 1)
+    tail = jnp.zeros((1, HQK), jnp.float32)
+    for index in range(4):
+        part = pltpu.roll(before, (32 * index + 32) % HQK, 1)[index : index + 1, :]
+        tail = jnp.where(lane // 32 == index, part, tail)
+    return jnp.concatenate(
+        [before[4:5, :], tail, after[15:16, :], pltpu.roll(after, 32, 1)[4:5, :]], axis=1
+    )
+
+
+def conv_kernel(place_ref, section_ref, held_ref, stem_ref, out_ref, weights, edges, wide, act, best):
+    count, rows, _ = held_ref.shape
+    for source in range(count):
+        block = held_ref[source].astype(jnp.float32)
+        weights[source * (rows - 1) : (source + 1) * (rows - 1), :] = block[: rows - 1, :]
+    first = ((place_ref[0] & (N_SEQ // 2 - 1)) // RUN) * RUN
+    borders = [run * (N_SEQ // 2) + first + index for run in range(2) for index in range(RUN + 1)]
+    for at in range(0, len(borders), 2):
+        onehot = jnp.concatenate(
+            [
+                onehot_rows(border_codes(held_ref, right), 128, EDGE * STEM_POOL)
+                for right in borders[at : at + 2]
+            ],
+            axis=1,
+        )
+        made = pooled_rows(onehot, stem_ref[...])
+        place = lax.broadcasted_iota(jnp.int32, made.shape, 0)
+        right = jnp.where(place < EDGE, borders[at], borders[at + 1])
+        place = right * ROWS - EDGE // 2 + place % EDGE
+        inside = (place >= 0) & (place < count * ROWS)
+        edges[at * EDGE : (at + 2) * EDGE, :] = jnp.where(inside, made, 0.0)
     windows, _, channels = section_ref.shape
     half = channels // 2
     columns = out_ref.shape[2] // 8
-    wide[...] = section_ref[...].astype(jnp.float32)
+    for window in range(windows):
+        at = (window // RUN * (RUN + 1) + window % RUN) * EDGE
+        wide[window, 3 : ROWS + 1, :] = section_ref[window].astype(jnp.float32)[1 : ROWS - 1, :]
+        wide[window, 0:3, :] = edges[at : at + 3, :]
+        wide[window, ROWS + 1 : ROWS + 4, :] = edges[at + EDGE + 1 : at + EDGE + 4, :]
     even, odd = None, None
     for tap in range(KS_CONV):
         rows = wide[:, tap : tap + ROWS, :].astype(jnp.bfloat16).reshape(windows * ROWS, channels)
-        weight = weight_ref[tap * half : (tap + 1) * half, :]
+        weight = weights[tap * half : (tap + 1) * half, :].astype(jnp.bfloat16)
         term = jnp.dot(rows[:, :half], weight, preferred_element_type=jnp.float32)
         even = term if even is None else even + term
         term = jnp.dot(rows[:, half:], weight, preferred_element_type=jnp.float32)
         odd = term if odd is None else odd + term
     act[...] = jnp.zeros(act.shape, jnp.float32)
-    act[:, :columns] = gelu(even[:, :columns] + odd[:, columns:])
+    act[:, :columns] = gelu(even[:, :columns] + odd[:, columns : 2 * columns])
     count = windows * ROWS // 2
     best[...] = jnp.maximum(act[pl.ds(0, count, stride=2), :], act[pl.ds(1, count, stride=2), :])
     flat = None
@@ -151,21 +200,23 @@
             out_ref[window * N_PAIR + index] = block
 
 
-def conv(section, weight):
+def conv(place, section, held, stem_weight, columns):
     windows, _, channels = section.shape
-    columns = weight.shape[1] // 2
+    borders = windows // RUN * (RUN + 1)
     return pl.pallas_call(
         conv_kernel,
         out_shape=jax.ShapeDtypeStruct((windows * N_PAIR, 2, 8 * columns), jnp.bfloat16),
-        in_specs=whole(2),
+        in_specs=[pl.BlockSpec(memory_space=pltpu.SMEM)] + whole(3),
         out_specs=whole(1)[0],
         scratch_shapes=[
+            pltpu.VMEM((held.shape[0] * (held.shape[1] - 1), HQK), jnp.float32),
+            pltpu.VMEM((borders * EDGE, channels), jnp.float32),
             pltpu.VMEM((windows, EXT_PAD, channels), jnp.float32),
             pltpu.VMEM((windows * ROWS, HQK), jnp.float32),
             pltpu.VMEM((windows * ROWS // 2, HQK), jnp.float32),
         ],
         compiler_params=params(),
-    )(section, weight)
+    )(place, section, held, stem_weight)
 
 
 def project_kernel(trunk_ref, w_query_ref, w_key_ref, w_value_ref, query_ref, kv_ref):
@@ -194,6 +245,15 @@
         out_specs=tuple(whole(2)),
         compiler_params=params(),
     )(trunk, w_query, w_key, w_value)
+
+
+def split(x):
+    parts = []
+    for _ in range(3):
+        part = x.astype(jnp.bfloat16).astype(jnp.float32)
+        parts.append(part)
+        x = x - part
+    return parts
 
 
 def attention_kernel(place_ref, query_ref, kv_ref, out_ref):
@@ -212,7 +272,9 @@
     total = jnp.sum(expo, axis=1, keepdims=True)
     mixed = jnp.dot(expo.astype(jnp.bfloat16), kv_ref[:, HQK:], preferred_element_type=jnp.float32)
     lane = lax.broadcasted_iota(jnp.int32, mixed.shape, 1)
-    mixed = jnp.where(lane == HV, top, jnp.where(lane == HV + 1, total, mixed))
+    for index, column in enumerate(split(top) + split(total)):
+        mixed = jnp.where(lane == HV + index, column, mixed)
+    mixed = mixed.astype(jnp.bfloat16)
     groups, count, _ = out_ref.shape
     for index in range(groups):
         out_ref[place_ref[0] ^ index] = mixed[index * count : (index + 1) * count, :]
@@ -223,7 +285,7 @@
     count, width = query.shape[0] // groups, kv.shape[1] - HQK
     return pl.pallas_call(
         attention_kernel,
-        out_shape=jax.ShapeDtypeStruct((groups, count, width), jnp.float32),
+        out_shape=jax.ShapeDtypeStruct((groups, count, width), jnp.bfloat16),
         in_specs=[pl.BlockSpec(memory_space=pltpu.SMEM)] + whole(2),
         out_specs=whole(1)[0],
         compiler_params=params(),
@@ -231,10 +293,10 @@
 
 
 def combine_kernel(parts_ref, w_out_ref, out_ref):
-    parts = parts_ref[...]
-    top = parts[:, :, HV : HV + 1]
+    parts = parts_ref[...].astype(jnp.float32)
+    top = jnp.sum(parts[:, :, HV : HV + 3], axis=2, keepdims=True)
     gain = jnp.exp(top - jnp.max(top, axis=0, keepdims=True))
-    total = jnp.sum(gain * parts[:, :, HV + 1 : HV + 2], axis=0)
+    total = jnp.sum(gain * jnp.sum(parts[:, :, HV + 3 : HV + 6], axis=2, keepdims=True), axis=0)
     mixed = (jnp.sum(gain * parts, axis=0) / total)[:, :HV].astype(jnp.bfloat16)
     term = jnp.dot(mixed, w_out_ref[...], preferred_element_type=jnp.float32)
     mean = jnp.sum(term, axis=0, keepdims=True) * (1.0 / PAIR_POOL)
@@ -316,24 +378,18 @@
 
     taps, width = w_conv.shape
     share = width // N_SHARE
-    blocks = exchange(pack(w_conv), SEQ)
-    conv_weight = blocks.reshape(N_SEQ * blocks.shape[1], blocks.shape[2])
-
-    codes = tokens + 1
-    ends = N_SEQ - 1
-    left = lax.ppermute(codes[-SIDE:], SEQ, [(i, i + 1) for i in range(ends)])
-    right = lax.ppermute(codes[:SIDE], SEQ, [(i + 1, i) for i in range(ends)])
-    codes = jnp.concatenate([left, codes, right])[None, :]
+    held = exchange(pack(w_conv, tokens.reshape(-1, HQK)), SEQ)
+
     source = jnp.arange(w_stem.shape[1]).reshape(2, -1)
     source = (2 * (source % source.shape[1]) + jnp.arange(2)[:, None]).reshape(-1)
     order = (jnp.arange(w_stem.shape[1])[:, None] == source[None, :]).astype(jnp.bfloat16)
     stem_weight = jnp.dot(w_stem, order, preferred_element_type=jnp.float32).astype(jnp.bfloat16)
     stem_weight = stem_weight.reshape(KS_STEM, 4, -1)[::-1].transpose(1, 0, 2)
     stem_weight = jnp.pad(stem_weight, ((0, 0), (0, 1), (0, 0))).reshape(64, -1)
-    section = stem(place.astype(jnp.int32)[None], codes, stem_weight).astype(jnp.bfloat16)
+    section = stem(tokens.reshape(1, -1), stem_weight).astype(jnp.bfloat16)
     sections = lax.all_gather(section, SHARE, axis=0, tiled=False)
 
-    parts = exchange(conv(sections, conv_weight), SHARE + ("pair",))
+    parts = exchange(conv(place.astype(jnp.int32)[None], sections, held, stem_weight, share), SHARE + ("pair",))
     count = ROWS // 2
     trunk = parts.reshape(N_SHARE, N_PAIR, count, share).transpose(2, 1, 0, 3)
     trunk = trunk.reshape(count, N_PAIR * width)

time: 132 us -> 125 us (0.947)
  starting transfers between devices: 64.4 us -> 55.9 us
  Pallas kernels: 8.1 us -> 10 us
  waiting for transfers between devices: 36.8 us -> 38.6 us
    ppermute x2 -> x0, starting transfers between devices: 10.1 us -> none  [the longest x1 5.57 us: on_device(): right = lax.ppermute(codes[:SIDE], SEQ, [(i + 1, i) for i in range(ends)])]
    all_to_all x6, starting transfers between devices: 45.5 us -> 47.9 us  [exchange(): return lax.all_to_all(blocks, axes, split_axis=0, concat_axis=0, tiled=True)]
    pallas_call x1, Pallas kernels: 1.5 us -> 3.69 us  [conv(): pl.pallas_call(conv_kernel, out_shape=jax.ShapeDtypeStruct((windows * N_P...]
  transfers between devices with their start and end apart: 11 -> 9, of which waited for: 8 -> 8; matrix products, arithmetic and copies ran while one was open for 2% -> 2% of each run, Pallas kernels for 2% -> 1%
where the time goes in v10:
time: 125 us
  starting transfers between devices  55.9 us (45%)
  waiting for transfers between devices  38.6 us (31%)
  blocking collectives  14.1 us (11%)
  Pallas kernels  10 us (8%)
  local copies, waits for them, and re-layouts  3.34 us (3%)
  matrix products  1.33 us (1%)
    all_to_all x6, starting transfers between devices, exchange(): return lax.all_to_all(blocks, axes, split_axis=0, concat_axis=0, tiled=True)  47.9 us
    all_to_all x6, waiting for transfers between devices, exchange(): return lax.all_to_all(blocks, axes, split_axis=0, concat_axis=0, tiled=True)  35.7 us
    all_gather x1, blocking collectives, on_device(): sections = lax.all_gather(section, SHARE, axis=0, tiled=False)  14.1 us
    ppermute x3, starting transfers between devices, on_device(): other = lax.ppermute(query, name, [(0, 1), (1, 0)])  8.05 us
    pallas_call x1, Pallas kernels, conv(): pl.pallas_call(conv_kernel, out_shape=jax.ShapeDtypeStruct((windows * N_P...  3.69 us
    ppermute x3, waiting for transfers between devices, on_device(): other = lax.ppermute(query, name, [(0, 1), (1, 0)])  2.88 us
  transfers between devices with their start and end apart: 9, of which 8 were waited for; matrix products, arithmetic and copies ran while one was open for 2% of the time, Pallas kernels for 1%

profile of v10, /device:TPU:1, one launch (start us, length us, event | category | flops | bytes accessed | tf_op | source)
XLA Modules:
  0.0 124.6 jit_solution(11172593857769349481)
XLA Ops:
  0.6 0.0 copy-start
  0.6 0.0 copy-start.4
  0.7 0.8 copy-done.4
  1.4 0.0 copy-start.5
  1.4 0.7 copy-done.5
  2.1 0.9 shard_map.114
  3.1 14.2 %all-to-all-start = ((bf16[128,16,128]{2,1,0:T(8,128)(2,1)}), bf16[128,16,128]{2,1,0:T(8,128)(2,1)S(1)}, u32[]{:S(2)}, u32[]{:S(2)}) async-start(bf16[128,16,128]{2,1,0:T(8,128)(2,1)} %shard_map.114), calls=%async_computation | async-start | bytes 1048576 | tf_op jit(solution)/shard_map/all_to_all | solution.py:372
  17.4 0.0 copy-done
  17.4 0.0 copy-start.6
  17.4 0.5 fusion.3
  18.0 0.3 rev.3
  18.3 0.0 copy-done.6
  18.3 1.5 %shard_map.113 = f32[32,768]{1,0:T(8,128)S(1)} custom-call(s32[1,2048]{1,0:T(1,128)S(1)} %bitcast.37, bf16[64,768]{1,0:T(8,128)(2,1)S(1)} %bitcast.34), custom_call_target="tpu_custom_call" | custom-call | flops 201326592 | bytes 200000 | tf_op jit(solution)/shard_map/pallas_call | solution.py:78
  19.9 0.0 copy-start.7
  19.9 14.1 %all-gather = bf16[256,768]{1,0:T(8,128)(2,1)S(1)} all-gather(bf16[32,768]{1,0:T(8,128)(2,1)S(1)} %convert_element_type.143), channel_id=2, replica_groups=mesh['zl'=2,'y'=8,'xh'=2,'xl'=2,'core'=2,'pair'=4] {'zl','xl','core'}, dimensions={0}, use_global_device_ids=true | all-gather | bytes 442368 | tf_op jit(solution)/shard_map/all_gather | solution.py:390
  34.0 3.9 %all-to-all-done.held_ref = bf16[128,16,128]{2,1,0:T(8,128)(2,1)S(1)} async-done(((bf16[128,16,128]{2,1,0:T(8,128)(2,1)}), bf16[128,16,128]{2,1,0:T(8,128)(2,1)S(1)}, u32[]{:S(2)}, u32[]{:S(2)}) %all-to-all-start) | async-done | bytes 524320 | tf_op jit(solution)/shard_map/all_to_all | solution.py:372
  37.8 3.7 %shard_map.115 = bf16[32,2,384]{2,1,0:T(2,128)(2,1)} custom-call(s32[1]{0:T(128)} %bitcast.1.place_ref, bf16[8,32,768]{2,1,0:T(8,128)(2,1)S(1)} %bitcast.32, bf16[128,16,128]{2,1,0:T(8,128)(2,1)S(1)} %all-to-all-done.held_ref, bf16[64,768]{1,0:T(8,128)(2,1)S(1)} %bitcast.35), custom_call_target="tpu_custom_call" | custom-call | tf_op jit(solution)/shard_map/pallas_call | solution.py:206
  41.5 9.9 %all-to-all-start.1 = ((bf16[32,2,384]{2,1,0:T(2,128)(2,1)}), bf16[32,2,384]{2,1,0:T(2,128)(2,1)S(1)}, u32[]{:S(2)}, u32[]{:S(2)}) async-start(bf16[32,2,384]{2,1,0:T(2,128)(2,1)} %shard_map.115), calls=%async_computation.1 | async-start | bytes 98304 | tf_op jit(solution)/shard_map/all_to_all | solution.py:372
  51.4 0.0 copy-done.7
  51.4 0.0 copy-start.2
  51.4 0.0 copy-start.3
  51.4 0.3 copy.23.w_value_ref
  51.7 7.9 %all-to-all-done.1 = bf16[32,2,384]{2,1,0:T(2,128)(2,1)S(1)} async-done(((bf16[32,2,384]{2,1,0:T(2,128)(2,1)}), bf16[32,2,384]{2,1,0:T(2,128)(2,1)S(1)}, u32[]{:S(2)}, u32[]{:S(2)}) %all-to-all-start.1) | async-done | bytes 49184 | tf_op jit(solution)/shard_map/all_to_all | solution.py:372
  59.6 0.2 reshape.124
  59.8 0.1 copy.32
  59.9 0.2 reshape.125.trunk_ref
  60.0 0.0 copy-done.2
  60.1 0.0 copy-done.3
  60.1 0.0 copy-start.8
  60.1 1.0 shard_map.116
  61.1 2.3 %collective-permute-start = (bf16[16,128]{1,0:T(8,128)(2,1)S(1)}, bf16[16,128]{1,0:T(8,128)(2,1)S(1)}, u32[]{:S(2)}, u32[]{:S(2)}) collective-permute-start(bf16[16,128]{1,0:T(8,128)(2,1)S(1)} %get-tuple-element.7), channel_id=1, source_target_pairs={{0,4},{4,0},{1,5},{5,1},{2,6},{6,2},{3,7},{7,3},{8,12},{12,8},{9,1... | collective-permute-start | bytes 12296 | tf_op jit(solution)/shard_map/ppermute | solution.py:399
  63.4 0.8 collective-permute-done
  64.2 2.2 %collective-permute-start.1 = (bf16[32,128]{1,0:T(8,128)(2,1)S(1)}, bf16[32,128]{1,0:T(8,128)(2,1)S(1)}, u32[]{:S(2)}, u32[]{:S(2)}) collective-permute-start(bf16[32,128]{1,0:T(8,128)(2,1)S(1)} %pad_maximum_fusion.3), channel_id=1, source_target_pairs={{0,8},{8,0},{1,9},{9,1},{2,10},{10,2},{3,11},{11,3},{4,12},{12,4},... | collective-permute-start | bytes 24584 | tf_op jit(solution)/shard_map/ppermute | solution.py:399
  66.4 4.4 %all-to-all-start.2 = ((bf16[16,16,384]{2,1,0:T(8,128)(2,1)}), bf16[16,16,384]{2,1,0:T(8,128)(2,1)S(1)}, u32[]{:S(2)}, u32[]{:S(2)}) async-start(bf16[16,16,384]{2,1,0:T(8,128)(2,1)} %get-tuple-element.8), calls=%async_computation.2 | async-start | bytes 393216 | tf_op jit(solution)/shard_map/all_to_all | solution.py:372
  70.8 0.0 collective-permute-done.1
  70.9 3.5 %collective-permute-start.2 = (bf16[64,128]{1,0:T(8,128)(2,1)S(1)}, bf16[64,128]{1,0:T(8,128)(2,1)S(1)}, u32[]{:S(2)}, u32[]{:S(2)}) collective-permute-start(bf16[64,128]{1,0:T(8,128)(2,1)S(1)} %pad_maximum_fusion.2), channel_id=1, source_target_pairs={{0,16},{16,0},{1,17},{17,1},{2,18},{18,2},{3,19},{19,3},{4,20},{20... | collective-permute-start | bytes 49160 | tf_op jit(solution)/shard_map/ppermute | solution.py:399
  74.4 0.0 copy-done.8
  74.4 0.2 copy.29
  74.7 0.2 copy.30
  74.9 2.1 %collective-permute-done.2 = bf16[64,128]{1,0:T(8,128)(2,1)S(1)} collective-permute-done((bf16[64,128]{1,0:T(8,128)(2,1)S(1)}, bf16[64,128]{1,0:T(8,128)(2,1)S(1)}, u32[]{:S(2)}, u32[]{:S(2)}) %collective-permute-start.2) | collective-permute-done | bytes 16416 | tf_op jit(solution)/shard_map/ppermute | solution.py:399
  77.0 1.3 %all-to-all-done.2 = bf16[16,16,384]{2,1,0:T(8,128)(2,1)S(1)} async-done(((bf16[16,16,384]{2,1,0:T(8,128)(2,1)}), bf16[16,16,384]{2,1,0:T(8,128)(2,1)S(1)}, u32[]{:S(2)}, u32[]{:S(2)}) %all-to-all-start.2) | async-done | bytes 196640 | tf_op jit(solution)/shard_map/all_to_all | solution.py:372
  78.3 0.0 copy-start.9
  78.3 0.0 copy-start.1
  78.3 1.0 shard_map.117
  79.3 5.8 %all-to-all-start.3 = ((bf16[8,16,256]{2,1,0:T(8,128)(2,1)}), bf16[8,16,256]{2,1,0:T(8,128)(2,1)S(1)}, u32[]{:S(2)}, u32[]{:S(2)}) async-start(bf16[8,16,256]{2,1,0:T(8,128)(2,1)} %shard_map.117), calls=%async_computation.3 | async-start | bytes 131072 | tf_op jit(solution)/shard_map/all_to_all | solution.py:372
  85.1 0.2 pad_maximum_fusion.w_pair_ref
  85.3 0.0 copy-done.9
  85.3 0.1 copy.26.pair_ref
  85.5 4.5 %all-to-all-done.3.parts_ref = bf16[8,16,256]{2,1,0:T(8,128)(2,1)S(1)} async-done(((bf16[8,16,256]{2,1,0:T(8,128)(2,1)}), bf16[8,16,256]{2,1,0:T(8,128)(2,1)S(1)}, u32[]{:S(2)}, u32[]{:S(2)}) %all-to-all-start.3) | async-done | bytes 65568 | tf_op jit(solution)/shard_map/all_to_all | solution.py:372
  90.0 0.0 copy-done.1
  90.0 1.0 shard_map.118
  91.0 0.0 copy-start.10
  91.0 3.5 %all-to-all-start.4 = ((f32[4,24,384]{2,1,0:T(8,128)}), f32[4,24,384]{2,1,0:T(8,128)S(1)}, u32[]{:S(2)}, u32[]{:S(2)}) async-start(f32[4,24,384]{2,1,0:T(8,128)} %shard_map.118), calls=%async_computation.4 | async-start | bytes 294912 | tf_op jit(solution)/shard_map/all_to_all | solution.py:372
  94.5 7.3 %all-to-all-done.4.terms_ref = f32[4,24,384]{2,1,0:T(8,128)S(1)} async-done(((f32[4,24,384]{2,1,0:T(8,128)}), f32[4,24,384]{2,1,0:T(8,128)S(1)}, u32[]{:S(2)}, u32[]{:S(2)}) %all-to-all-start.4) | async-done | bytes 147488 | tf_op jit(solution)/shard_map/all_to_all | solution.py:372
  101.9 0.8 shard_map.119
  102.7 10.2 %all-to-all-start.5 = ((f32[128,1,96]{2,1,0:T(1,128)}), f32[128,1,96]{2,1,0:T(1,128)S(1)}, u32[]{:S(2)}, u32[]{:S(2)}) async-start(f32[128,1,96]{2,1,0:T(1,128)} %bitcast.14), calls=%async_computation.5 | async-start | bytes 131072 | tf_op jit(solution)/shard_map/all_to_all | solution.py:372
  112.9 0.1 slice_bitcast_fusion.1
  113.0 10.7 %all-to-all-done.5 = f32[128,1,96]{2,1,0:T(1,128)S(1)} async-done(((f32[128,1,96]{2,1,0:T(1,128)}), f32[128,1,96]{2,1,0:T(1,128)S(1)}, u32[]{:S(2)}, u32[]{:S(2)}) %all-to-all-start.5) | async-done | bytes 49184 | tf_op jit(solution)/shard_map/all_to_all | solution.py:372
  123.7 0.1 copy.28
  123.8 0.0 copy-done.10
  123.8 0.8 fusion.5
  (15 shorter events, 0.2 us)
Async XLA Ops:
  0.6 16.7 %copy-start = (bf16[60,768]{1,0:T(8,128)(2,1)S(1)}, bf16[60,768]{1,0:T(8,128)(2,1)}, u32[]{:S(2)}) copy-start(bf16[60,768]{1,0:T(8,128)(2,1)} %param.11) | copy-start | bytes 276484
  0.6 0.8 copy-start.4
  1.4 0.7 copy-start.5
  3.1 34.8 %all-to-all-start = ((bf16[128,16,128]{2,1,0:T(8,128)(2,1)}), bf16[128,16,128]{2,1,0:T(8,128)(2,1)S(1)}, u32[]{:S(2)}, u32[]{:S(2)}) async-start(bf16[128,16,128]{2,1,0:T(8,128)(2,1)} %shard_map.114), calls=%async_computation | async-start | bytes 1048576 | tf_op jit(solution)/shard_map/all_to_all | solution.py:372
  17.4 0.9 copy-start.6
  19.9 31.5 %copy-start.7 = (bf16[1536,192]{0,1:T(8,128)(2,1)S(1)}, bf16[1536,192]{0,1:T(8,128)(2,1)}, u32[]{:S(2)}) copy-start(bf16[1536,192]{0,1:T(8,128)(2,1)} %param.15) | copy-start | bytes 1769476
  41.5 18.1 %all-to-all-start.1 = ((bf16[32,2,384]{2,1,0:T(2,128)(2,1)}), bf16[32,2,384]{2,1,0:T(2,128)(2,1)S(1)}, u32[]{:S(2)}, u32[]{:S(2)}) async-start(bf16[32,2,384]{2,1,0:T(2,128)(2,1)} %shard_map.115), calls=%async_computation.1 | async-start | bytes 98304 | tf_op jit(solution)/shard_map/all_to_all | solution.py:372
  51.4 8.6 %copy-start.2 = (bf16[1536,128]{1,0:T(8,128)(2,1)S(1)}, bf16[1536,128]{1,0:T(8,128)(2,1)}, u32[]{:S(2)}) copy-start(bf16[1536,128]{1,0:T(8,128)(2,1)} %w_query_ref.1) | copy-start | bytes 1179652
  51.4 8.6 %copy-start.3 = (bf16[1536,128]{1,0:T(8,128)(2,1)S(1)}, bf16[1536,128]{1,0:T(8,128)(2,1)}, u32[]{:S(2)}) copy-start(bf16[1536,128]{1,0:T(8,128)(2,1)} %w_key_ref.1) | copy-start | bytes 1179652
  60.1 14.3 %copy-start.8 = (bf16[2,1536,32]{1,2,0:T(8,128)(2,1)S(1)}, bf16[2,1536,32]{1,2,0:T(8,128)(2,1)}, u32[]{:S(2)}) copy-start(bf16[2,1536,32]{1,2,0:T(8,128)(2,1)} %param.17) | copy-start | bytes 589828
  61.1 3.1 %collective-permute-start = (bf16[16,128]{1,0:T(8,128)(2,1)S(1)}, bf16[16,128]{1,0:T(8,128)(2,1)S(1)}, u32[]{:S(2)}, u32[]{:S(2)}) collective-permute-start(bf16[16,128]{1,0:T(8,128)(2,1)S(1)} %get-tuple-element.7), channel_id=1, source_target_pairs={{0,4},{4,0},{1,5},{5,1},{2,6},{6,2},{3,7},{7,3},{8,12},{12,8},{9,1... | collective-permute-start | bytes 12296 | tf_op jit(solution)/shard_map/ppermute | solution.py:399
  64.2 6.6 %collective-permute-start.1 = (bf16[32,128]{1,0:T(8,128)(2,1)S(1)}, bf16[32,128]{1,0:T(8,128)(2,1)S(1)}, u32[]{:S(2)}, u32[]{:S(2)}) collective-permute-start(bf16[32,128]{1,0:T(8,128)(2,1)S(1)} %pad_maximum_fusion.3), channel_id=1, source_target_pairs={{0,8},{8,0},{1,9},{9,1},{2,10},{10,2},{3,11},{11,3},{4,12},{12,4},... | collective-permute-start | bytes 24584 | tf_op jit(solution)/shard_map/ppermute | solution.py:399
  66.4 11.9 %all-to-all-start.2 = ((bf16[16,16,384]{2,1,0:T(8,128)(2,1)}), bf16[16,16,384]{2,1,0:T(8,128)(2,1)S(1)}, u32[]{:S(2)}, u32[]{:S(2)}) async-start(bf16[16,16,384]{2,1,0:T(8,128)(2,1)} %get-tuple-element.8), calls=%async_computation.2 | async-start | bytes 393216 | tf_op jit(solution)/shard_map/all_to_all | solution.py:372
  70.9 6.1 %collective-permute-start.2 = (bf16[64,128]{1,0:T(8,128)(2,1)S(1)}, bf16[64,128]{1,0:T(8,128)(2,1)S(1)}, u32[]{:S(2)}, u32[]{:S(2)}) collective-permute-start(bf16[64,128]{1,0:T(8,128)(2,1)S(1)} %pad_maximum_fusion.2), channel_id=1, source_target_pairs={{0,16},{16,0},{1,17},{17,1},{2,18},{18,2},{3,19},{19,3},{4,20},{20... | collective-permute-start | bytes 49160 | tf_op jit(solution)/shard_map/ppermute | solution.py:399
  78.3 7.0 %copy-start.9 = (bf16[1,128,32]{1,2,0:T(8,128)(2,1)S(1)}, bf16[1,128,32]{1,2,0:T(8,128)(2,1)}, u32[]{:S(2)}) copy-start(bf16[1,128,32]{1,2,0:T(8,128)(2,1)} %param.19) | copy-start | bytes 24580
  78.3 11.6 %copy-start.1 = (bf16[192,1536]{1,0:T(8,128)(2,1)S(1)}, bf16[192,1536]{1,0:T(8,128)(2,1)}, u32[]{:S(2)}) copy-start(bf16[192,1536]{1,0:T(8,128)(2,1)} %w_out_ref.1) | copy-start | bytes 1769476
  79.3 10.6 %all-to-all-start.3 = ((bf16[8,16,256]{2,1,0:T(8,128)(2,1)}), bf16[8,16,256]{2,1,0:T(8,128)(2,1)S(1)}, u32[]{:S(2)}, u32[]{:S(2)}) async-start(bf16[8,16,256]{2,1,0:T(8,128)(2,1)} %shard_map.117), calls=%async_computation.3 | async-start | bytes 131072 | tf_op jit(solution)/shard_map/all_to_all | solution.py:372
  91.0 32.8 %copy-start.10 = (bf16[18,32]{1,0:T(8,128)(2,1)S(1)}, bf16[18,32]{1,0:T(8,128)(2,1)}, u32[]{:S(2)}) copy-start(bf16[18,32]{1,0:T(8,128)(2,1)} %param.18) | copy-start | bytes 3460
  91.0 10.9 %all-to-all-start.4 = ((f32[4,24,384]{2,1,0:T(8,128)}), f32[4,24,384]{2,1,0:T(8,128)S(1)}, u32[]{:S(2)}, u32[]{:S(2)}) async-start(f32[4,24,384]{2,1,0:T(8,128)} %shard_map.118), calls=%async_computation.4 | async-start | bytes 294912 | tf_op jit(solution)/shard_map/all_to_all | solution.py:372
  102.7 21.0 %all-to-all-start.5 = ((f32[128,1,96]{2,1,0:T(1,128)}), f32[128,1,96]{2,1,0:T(1,128)S(1)}, u32[]{:S(2)}, u32[]{:S(2)}) async-start(f32[128,1,96]{2,1,0:T(1,128)} %bitcast.14), calls=%async_computation.5 | async-start | bytes 131072 | tf_op jit(solution)/shard_map/all_to_all | solution.py:372

commit v11 on v10

--- a/solution.py
+++ b/solution.py
@@ -85,7 +85,22 @@
     )(tokens, weight)
 
 
-def pack_kernel(weight_ref, tokens_ref, out_ref, wide):
+def start_kernel(weight_ref, stem_ref, tokens_hbm, out_ref, made_ref, wide, tokens_ref, arrived):
+    copy = pltpu.make_async_copy(tokens_hbm, tokens_ref, arrived)
+    copy.start()
+    rows, channels = stem_ref.shape
+    row = lax.broadcasted_iota(jnp.int32, (64, rows), 0)
+    column = lax.broadcasted_iota(jnp.int32, (64, rows), 1)
+    picked = (column == (KS_STEM - 1 - row % 16) * 4 + row // 16) & (row % 16 < KS_STEM)
+    picked = picked.astype(jnp.float32).astype(jnp.bfloat16)
+    made = jnp.dot(picked, stem_ref[...], preferred_element_type=jnp.float32).astype(jnp.bfloat16)
+    half = channels // 2
+    row = lax.broadcasted_iota(jnp.int32, (channels, half), 0)
+    column = lax.broadcasted_iota(jnp.int32, (channels, half), 1)
+    for odd in range(2):
+        order = (row == 2 * column + odd).astype(jnp.float32).astype(jnp.bfloat16)
+        part = jnp.dot(made, order, preferred_element_type=jnp.float32)
+        made_ref[:, odd * half : (odd + 1) * half] = part.astype(jnp.bfloat16)
     taps, width = weight_ref.shape
     share = width // N_SHARE
     half = taps // 2
@@ -99,6 +114,7 @@
     even, odd = jnp.concatenate(even, axis=1), jnp.concatenate(odd, axis=1)
     lane = lax.broadcasted_iota(jnp.int32, (half + 1, HQK), 1)
     row = lax.broadcasted_iota(jnp.int32, (half + 1, HQK), 0)
+    copy.wait()
     codes = (tokens_ref[...] + 1).astype(jnp.float32)
     last = codes.shape[0] - 1
     line = [jnp.broadcast_to(codes[at : at + 1, :], lane.shape) for at in (0, 1, last - 1, last)]
@@ -120,16 +136,23 @@
         out_ref[place] = blocks[index]
 
 
-def pack(weight, tokens):
+def start(weight, stem_weight, tokens):
     taps, width = weight.shape
     return pl.pallas_call(
-        pack_kernel,
-        out_shape=jax.ShapeDtypeStruct((N_SEQ, taps // 2 + 1, HQK), jnp.bfloat16),
-        in_specs=whole(2),
-        out_specs=whole(1)[0],
-        scratch_shapes=[pltpu.VMEM((width // HQK, taps + 2, HQK), jnp.float32)],
-        compiler_params=params(),
-    )(weight, tokens)
+        start_kernel,
+        out_shape=(
+            jax.ShapeDtypeStruct((N_SEQ, taps // 2 + 1, HQK), jnp.bfloat16),
+            jax.ShapeDtypeStruct((64, stem_weight.shape[1]), jnp.bfloat16),
+        ),
+        in_specs=whole(2) + [pl.BlockSpec(memory_space=pl.ANY)],
+        out_specs=tuple(whole(2)),
+        scratch_shapes=[
+            pltpu.VMEM((width // HQK, taps + 2, HQK), jnp.float32),
+            pltpu.VMEM(tokens.shape, jnp.int32),
+            pltpu.SemaphoreType.DMA,
+        ],
+        compiler_params=params(),
+    )(weight, stem_weight, tokens)
 
 
 def border_codes(held_ref, right):
@@ -195,7 +218,7 @@
         part = pltpu.roll(part, index * columns, 1)
         flat = part if flat is None else flat + part
     for window in range(windows):
-        block = flat[2 * window : 2 * window + 2, :].astype(jnp.bfloat16)
+        block = flat[window // 2 * 4 : window // 2 * 4 + 4, :].astype(jnp.bfloat16)
         for index in range(N_PAIR):
             out_ref[window * N_PAIR + index] = block
 
@@ -205,7 +228,7 @@
     borders = windows // RUN * (RUN + 1)
     return pl.pallas_call(
         conv_kernel,
-        out_shape=jax.ShapeDtypeStruct((windows * N_PAIR, 2, 8 * columns), jnp.bfloat16),
+        out_shape=jax.ShapeDtypeStruct((windows * N_PAIR, 4, 8 * columns), jnp.bfloat16),
         in_specs=[pl.BlockSpec(memory_space=pltpu.SMEM)] + whole(3),
         out_specs=whole(1)[0],
         scratch_shapes=[
@@ -219,32 +242,38 @@
     )(place, section, held, stem_weight)
 
 
-def project_kernel(trunk_ref, w_query_ref, w_key_ref, w_value_ref, query_ref, kv_ref):
+def project_kernel(core_ref, trunk_ref, w_query_ref, w_key_ref, w_value_ref, query_ref, kv_ref, own_ref):
     trunk = trunk_ref[...]
-    query, key, value = [
-        jnp.dot(trunk, ref[...], preferred_element_type=jnp.float32).astype(jnp.bfloat16)
-        for ref in (w_query_ref, w_key_ref, w_value_ref)
+    first = core_ref[0] == 0
+    count = own_ref.shape[0]
+    query_ref[...] = jnp.dot(trunk, w_query_ref[...], preferred_element_type=jnp.float32).astype(jnp.bfloat16)
+    wide = trunk.astype(jnp.float32)
+    own = jnp.where(first, wide[:count], wide[count:]).astype(jnp.bfloat16)
+    own_ref[...] = own
+    key, value = [
+        jnp.dot(own, ref[...], preferred_element_type=jnp.float32).astype(jnp.bfloat16)
+        for ref in (w_key_ref, w_value_ref)
     ]
-    query_ref[...] = query
-    rest = jnp.zeros((trunk.shape[0], kv_ref.shape[2] - HQK - HV), jnp.bfloat16)
+    rest = jnp.zeros((count, kv_ref.shape[2] - HQK - HV), jnp.bfloat16)
     for index in range(N_LINE):
         kv_ref[index, :, :HQK] = key
         kv_ref[index, :, HQK : HQK + HV] = value
         kv_ref[index, :, HQK + HV :] = rest
 
 
-def project(trunk, w_query, w_key, w_value):
-    count = trunk.shape[0]
+def project(core, trunk, w_query, w_key, w_value):
+    count = trunk.shape[0] // 2
     return pl.pallas_call(
         project_kernel,
         out_shape=(
-            jax.ShapeDtypeStruct((count, HQK), jnp.bfloat16),
+            jax.ShapeDtypeStruct((2 * count, HQK), jnp.bfloat16),
             jax.ShapeDtypeStruct((N_LINE, count, 3 * HQK), jnp.bfloat16),
+            jax.ShapeDtypeStruct((count, trunk.shape[1]), jnp.bfloat16),
         ),
-        in_specs=whole(4),
-        out_specs=tuple(whole(2)),
-        compiler_params=params(),
-    )(trunk, w_query, w_key, w_value)
+        in_specs=[pl.BlockSpec(memory_space=pltpu.SMEM)] + whole(4),
+        out_specs=tuple(whole(3)),
+        compiler_params=params(),
+    )(core, trunk, w_query, w_key, w_value)
 
 
 def split(x):
@@ -277,7 +306,8 @@
     mixed = mixed.astype(jnp.bfloat16)
     groups, count, _ = out_ref.shape
     for index in range(groups):
-        out_ref[place_ref[0] ^ index] = mixed[index * count : (index + 1) * count, :]
+        place = ((place_ref[0] >> 1) ^ (index // 2)) * 2 + index % 2
+        out_ref[place] = mixed[index * count : (index + 1) * count, :]
 
 
 def attention(place, query, kv):
@@ -378,26 +408,25 @@
 
     taps, width = w_conv.shape
     share = width // N_SHARE
-    held = exchange(pack(w_conv, tokens.reshape(-1, HQK)), SEQ)
-
-    source = jnp.arange(w_stem.shape[1]).reshape(2, -1)
-    source = (2 * (source % source.shape[1]) + jnp.arange(2)[:, None]).reshape(-1)
-    order = (jnp.arange(w_stem.shape[1])[:, None] == source[None, :]).astype(jnp.bfloat16)
-    stem_weight = jnp.dot(w_stem, order, preferred_element_type=jnp.float32).astype(jnp.bfloat16)
-    stem_weight = stem_weight.reshape(KS_STEM, 4, -1)[::-1].transpose(1, 0, 2)
-    stem_weight = jnp.pad(stem_weight, ((0, 0), (0, 1), (0, 0))).reshape(64, -1)
+    blocks, stem_weight = start(w_conv, w_stem, tokens.reshape(-1, HQK))
+    held = exchange(blocks, SEQ)
+
     section = stem(tokens.reshape(1, -1), stem_weight).astype(jnp.bfloat16)
     sections = lax.all_gather(section, SHARE, axis=0, tiled=False)
 
     parts = exchange(conv(place.astype(jnp.int32)[None], sections, held, stem_weight, share), SHARE + ("pair",))
     count = ROWS // 2
-    trunk = parts.reshape(N_SHARE, N_PAIR, count, share).transpose(2, 1, 0, 3)
-    trunk = trunk.reshape(count, N_PAIR * width)
-
-    query, kv = project(trunk, w_query, w_key, w_value)
-    for name in reversed(SPREAD):
-        other = lax.ppermute(query, name, [(0, 1), (1, 0)])
-        query = jnp.concatenate([query, other], axis=0)
+    trunk = parts.reshape(N_SHARE, N_PAIR, 2 * count, share).transpose(2, 1, 0, 3)
+    trunk = trunk.reshape(2 * count, N_PAIR * width)
+
+    core = lax.axis_index("core").astype(jnp.int32)[None]
+    query, kv, trunk = project(core, trunk, w_query, w_key, w_value)
+    chips = SPREAD[:-1]
+    others = [
+        lax.ppermute(query, chips, [(i, i ^ bits) for i in range(N_SPREAD // 2)])
+        for bits in range(1, N_SPREAD // 2)
+    ]
+    query = jnp.concatenate([query] + others, axis=0)
     kv = exchange(kv, LINE).reshape(N_LINE * count, kv.shape[2])
     spread = lax.axis_index(SPREAD).astype(jnp.int32)[None]
     parts = exchange(attention(spread, query, kv), SPREAD)
@@ -413,7 +442,7 @@
     mirror = every[:, 2 * channels :]
 
     cols = jnp.arange(N_SEQ, dtype=jnp.int32)
-    bias = distance_bias(place.astype(jnp.int32), cols, pair_bias)
+    bias = lax.optimization_barrier(distance_bias(place.astype(jnp.int32), cols, pair_bias))
     cross = rows[:, :channels] * every[:, channels : 2 * channels]
     cross = cross + every[:, :channels] * rows[:, channels:]
     pair_out = (0.5 * (mine + mirror + cross) + bias).astype(jnp.bfloat16)[None]

time: 125 us -> 129 us (1.032)
  local copies, waits for them, and re-layouts: 3.34 us -> 6.1 us
  starting transfers between devices: 55.9 us -> 58.6 us
  waiting for transfers between devices: 38.6 us -> 36.5 us
    unnamed x26, local copies, waits for them, and re-layouts: 2.35 us -> 5.17 us
    ppermute x3, waiting for transfers between devices: 2.88 us -> 1.24 us  [on_device(): lax.ppermute(query, chips, [(i, i ^ bits) for i in range(N_SPREAD // 2)])]
    ppermute x3, starting transfers between devices: 8.05 us -> 9.58 us  [on_device(): lax.ppermute(query, chips, [(i, i ^ bits) for i in range(N_SPREAD // 2)])]
  transfers between devices with their start and end apart: 9 -> 9, of which waited for: 8 -> 6; matrix products, arithmetic and copies ran while one was open for 2% -> 1% of each run, Pallas kernels for 1% -> 1%
where the time goes in v11:
time: 129 us; the launch traced here: 128 us
  starting transfers between devices  58.6 us (45%)
  waiting for transfers between devices  36.5 us (28%)
  blocking collectives  14.1 us (11%)
  Pallas kernels  10.6 us (8%)
  local copies, waits for them, and re-layouts  6.1 us (5%)
    all_to_all x6, starting transfers between devices, exchange(): return lax.all_to_all(blocks, axes, split_axis=0, concat_axis=0, tiled=True)  49 us
    all_to_all x6, waiting for transfers between devices, exchange(): return lax.all_to_all(blocks, axes, split_axis=0, concat_axis=0, tiled=True)  35.3 us
    all_gather x1, blocking collectives, on_device(): sections = lax.all_gather(section, SHARE, axis=0, tiled=False)  14.1 us
    ppermute x3, starting transfers between devices, on_device(): lax.ppermute(query, chips, [(i, i ^ bits) for i in range(N_SPREAD // 2)])  9.58 us
    unnamed x26, local copies, waits for them, and re-layouts  5.17 us
    pallas_call x1, Pallas kernels, conv(): pl.pallas_call(conv_kernel, out_shape=jax.ShapeDtypeStruct((windows * N_P...  3.77 us
  transfers between devices with their start and end apart: 9, of which 6 were waited for; matrix products, arithmetic and copies ran while one was open for 1% of the time, Pallas kernels for 1%

profile of v11, /device:TPU:1, one launch (start us, length us, event | category | flops | bytes accessed | tf_op | source)
XLA Modules:
  0.0 128.0 jit_solution(2444049474836981138)
XLA Ops:
  0.6 0.0 copy-start
  0.6 0.0 copy-start.4
  0.7 0.9 copy-done.4
  1.5 0.0 copy-start.5
  1.5 0.7 copy-done.5
  2.3 0.0 copy-start.6
  2.3 0.7 copy-done.6
  3.0 1.4 %shard_map.113 = (bf16[128,16,128]{2,1,0:T(8,128)(2,1)}, bf16[64,768]{1,0:T(8,128)(2,1)S(1)}) custom-call(bf16[30,384]{1,0:T(8,128)(2,1)S(1)} %copy-done.5, bf16[60,768]{1,0:T(8,128)(2,1)S(1)} %copy-done.4, s32[16,128]{1,0:T(8,128)S(1)} %bitcast.32), custom_call_target="tpu_custom_call" | custom-call | tf_op jit(solution)/shard_map/pallas_call | solution.py:141
  4.4 14.2 %all-to-all-start = ((bf16[128,16,128]{2,1,0:T(8,128)(2,1)}), bf16[128,16,128]{2,1,0:T(8,128)(2,1)S(1)}, u32[]{:S(2)}, u32[]{:S(2)}) async-start(bf16[128,16,128]{2,1,0:T(8,128)(2,1)} %get-tuple-element.11), calls=%async_computation | async-start | bytes 1048576 | tf_op jit(solution)/shard_map/all_to_all | solution.py:402
  18.6 0.0 copy-start.7
  18.6 0.7 copy-done.7
  19.3 1.5 %shard_map.114 = f32[32,768]{1,0:T(8,128)S(1)} custom-call(s32[1,2048]{1,0:T(1,128)S(1)} %bitcast.33, bf16[64,768]{1,0:T(8,128)(2,1)S(1)} %get-tuple-element.10.weight_ref.stem_ref), custom_call_target="tpu_custom_call" | custom-call | flops 201326592 | bytes 200000 | tf_op jit(solution)/shard_map/pallas_call | solution.py:78
  20.9 14.1 %all-gather = bf16[256,768]{1,0:T(8,128)(2,1)S(1)} all-gather(bf16[32,768]{1,0:T(8,128)(2,1)S(1)} %convert_element_type.132), channel_id=2, replica_groups=mesh['zl'=2,'y'=8,'xh'=2,'xl'=2,'core'=2,'pair'=4] {'zl','xl','core'}, dimensions={0}, use_global_device_ids=true | all-gather | bytes 442368 | tf_op jit(solution)/shard_map/all_gather | solution.py:415
  35.0 4.2 %all-to-all-done.held_ref = bf16[128,16,128]{2,1,0:T(8,128)(2,1)S(1)} async-done(((bf16[128,16,128]{2,1,0:T(8,128)(2,1)}), bf16[128,16,128]{2,1,0:T(8,128)(2,1)S(1)}, u32[]{:S(2)}, u32[]{:S(2)}) %all-to-all-start) | async-done | bytes 524320 | tf_op jit(solution)/shard_map/all_to_all | solution.py:402
  39.2 0.0 copy-start.8
  39.2 3.8 %shard_map.115 = bf16[32,4,384]{2,1,0:T(4,128)(2,1)} custom-call(s32[1]{0:T(128)} %bitcast.2.place_ref, bf16[8,32,768]{2,1,0:T(8,128)(2,1)S(1)} %bitcast.30, bf16[128,16,128]{2,1,0:T(8,128)(2,1)S(1)} %all-to-all-done.held_ref, bf16[64,768]{1,0:T(8,128)(2,1)S(1)} %get-tuple-element.10.weight_ref.stem_ref), custom_call_target="tpu_custom_call" | custom-call | tf_op jit(solution)/shard_map/pallas_call | solution.py:229
  42.9 9.9 %all-to-all-start.1 = ((bf16[32,4,384]{2,1,0:T(4,128)(2,1)}), bf16[32,4,384]{2,1,0:T(4,128)(2,1)S(1)}, u32[]{:S(2)}, u32[]{:S(2)}) async-start(bf16[32,4,384]{2,1,0:T(4,128)(2,1)} %shard_map.115), calls=%async_computation.1 | async-start | bytes 196608 | tf_op jit(solution)/shard_map/all_to_all | solution.py:402
  52.8 0.0 copy-done.8
  52.8 0.3 copy.21.w_value_ref
  53.1 8.8 %all-to-all-done.1 = bf16[32,4,384]{2,1,0:T(4,128)(2,1)S(1)} async-done(((bf16[32,4,384]{2,1,0:T(4,128)(2,1)}), bf16[32,4,384]{2,1,0:T(4,128)(2,1)S(1)}, u32[]{:S(2)}, u32[]{:S(2)}) %all-to-all-start.1) | async-done | bytes 98336 | tf_op jit(solution)/shard_map/all_to_all | solution.py:402
  61.9 0.2 reshape.78
  62.2 0.0 copy-start.2
  62.2 0.0 copy-start.3
  62.2 0.2 copy.30
  62.4 0.3 reshape.79.trunk_ref
  62.7 0.5 copy-done.2
  63.2 0.1 copy-done.3
  63.3 1.0 shard_map.116
  64.3 0.0 copy-start.9
  64.3 4.3 %all-to-all-start.2 = ((bf16[16,16,384]{2,1,0:T(8,128)(2,1)}), bf16[16,16,384]{2,1,0:T(8,128)(2,1)S(1)}, u32[]{:S(2)}, u32[]{:S(2)}) async-start(bf16[16,16,384]{2,1,0:T(8,128)(2,1)} %get-tuple-element.13), calls=%async_computation.2 | async-start | bytes 393216 | tf_op jit(solution)/shard_map/all_to_all | solution.py:402
  68.7 0.0 copy-done.9
  68.7 0.2 copy.27
  68.9 0.2 copy.28
  69.2 2.2 %collective-permute-start = (bf16[32,128]{1,0:T(8,128)(2,1)S(1)}, bf16[32,128]{1,0:T(8,128)(2,1)S(1)}, u32[]{:S(2)}, u32[]{:S(2)}) collective-permute-start(bf16[32,128]{1,0:T(8,128)(2,1)S(1)} %get-tuple-element.12), channel_id=1, source_target_pairs={{0,8},{8,0},{16,24},{24,16},{1,9},{9,1},{17,25},{25,17},{2,10},{10... | collective-permute-start | bytes 24584 | tf_op jit(solution)/shard_map/ppermute | solution.py:426
  71.4 3.3 %collective-permute-start.1 = (bf16[32,128]{1,0:T(8,128)(2,1)S(1)}, bf16[32,128]{1,0:T(8,128)(2,1)S(1)}, u32[]{:S(2)}, u32[]{:S(2)}) collective-permute-start(bf16[32,128]{1,0:T(8,128)(2,1)S(1)} %get-tuple-element.12), channel_id=1, source_target_pairs={{0,16},{8,24},{16,0},{24,8},{1,17},{9,25},{17,1},{25,9},{2,18},{10... | collective-permute-start | bytes 24584 | tf_op jit(solution)/shard_map/ppermute | solution.py:426
  74.7 4.1 %collective-permute-start.2 = (bf16[32,128]{1,0:T(8,128)(2,1)S(1)}, bf16[32,128]{1,0:T(8,128)(2,1)S(1)}, u32[]{:S(2)}, u32[]{:S(2)}) collective-permute-start(bf16[32,128]{1,0:T(8,128)(2,1)S(1)} %get-tuple-element.12), channel_id=1, source_target_pairs={{0,24},{8,16},{16,8},{24,0},{1,25},{9,17},{17,9},{25,1},{2,26},{10... | collective-permute-start | bytes 24584 | tf_op jit(solution)/shard_map/ppermute | solution.py:426
  78.8 0.0 copy-start.1
  78.8 0.2 pad_maximum_fusion.w_pair_ref
  79.0 0.0 collective-permute-done
  79.0 0.0 collective-permute-done.1
  79.0 1.2 collective-permute-done.2
  80.3 0.0 all-to-all-done.2
  80.3 1.0 shard_map.117
  81.3 5.5 %all-to-all-start.3 = ((bf16[8,16,256]{2,1,0:T(8,128)(2,1)}), bf16[8,16,256]{2,1,0:T(8,128)(2,1)S(1)}, u32[]{:S(2)}, u32[]{:S(2)}) async-start(bf16[8,16,256]{2,1,0:T(8,128)(2,1)} %shard_map.117), calls=%async_computation.3 | async-start | bytes 131072 | tf_op jit(solution)/shard_map/all_to_all | solution.py:402
  86.8 4.8 %all-to-all-done.3.parts_ref = bf16[8,16,256]{2,1,0:T(8,128)(2,1)S(1)} async-done(((bf16[8,16,256]{2,1,0:T(8,128)(2,1)}), bf16[8,16,256]{2,1,0:T(8,128)(2,1)S(1)}, u32[]{:S(2)}, u32[]{:S(2)}) %all-to-all-start.3) | async-done | bytes 65568 | tf_op jit(solution)/shard_map/all_to_all | solution.py:402
  91.6 0.0 copy-done.1
  91.7 1.0 shard_map.118
  92.7 3.3 %all-to-all-start.4 = ((f32[4,24,384]{2,1,0:T(8,128)}), f32[4,24,384]{2,1,0:T(8,128)S(1)}, u32[]{:S(2)}, u32[]{:S(2)}) async-start(f32[4,24,384]{2,1,0:T(8,128)} %shard_map.118), calls=%async_computation.4 | async-start | bytes 294912 | tf_op jit(solution)/shard_map/all_to_all | solution.py:402
  96.0 0.0 copy-done
  96.0 0.2 fusion
  96.2 0.0 copy-start.10
  96.2 0.7 copy-done.10
  96.9 0.1 copy.24.pair_ref
  97.1 6.7 %all-to-all-done.4.terms_ref = f32[4,24,384]{2,1,0:T(8,128)S(1)} async-done(((f32[4,24,384]{2,1,0:T(8,128)}), f32[4,24,384]{2,1,0:T(8,128)S(1)}, u32[]{:S(2)}, u32[]{:S(2)}) %all-to-all-start.4) | async-done | bytes 147488 | tf_op jit(solution)/shard_map/all_to_all | solution.py:402
  103.8 0.8 shard_map.119
  104.6 11.8 %all-to-all-start.5 = ((f32[128,1,96]{2,1,0:T(1,128)}), f32[128,1,96]{2,1,0:T(1,128)S(1)}, u32[]{:S(2)}, u32[]{:S(2)}) async-start(f32[128,1,96]{2,1,0:T(1,128)} %bitcast.12), calls=%async_computation.5 | async-start | bytes 131072 | tf_op jit(solution)/shard_map/all_to_all | solution.py:402
  116.4 0.1 slice_bitcast_fusion.1
  116.5 10.7 %all-to-all-done.5 = f32[128,1,96]{2,1,0:T(1,128)S(1)} async-done(((f32[128,1,96]{2,1,0:T(1,128)}), f32[128,1,96]{2,1,0:T(1,128)S(1)}, u32[]{:S(2)}, u32[]{:S(2)}) %all-to-all-start.5) | async-done | bytes 49184 | tf_op jit(solution)/shard_map/all_to_all | solution.py:402
  127.2 0.1 copy.26
  127.3 0.7 fusion.7
  (5 shorter events, 0.1 us)
Async XLA Ops:
  0.6 95.4 %copy-start = (bf16[18,32]{1,0:T(8,128)(2,1)S(1)}, bf16[18,32]{1,0:T(8,128)(2,1)}, u32[]{:S(2)}) copy-start(bf16[18,32]{1,0:T(8,128)(2,1)} %param.18) | copy-start | bytes 3460
  0.6 0.9 copy-start.4
  1.5 0.7 copy-start.5
  2.3 0.7 copy-start.6
  4.4 34.8 %all-to-all-start = ((bf16[128,16,128]{2,1,0:T(8,128)(2,1)}), bf16[128,16,128]{2,1,0:T(8,128)(2,1)S(1)}, u32[]{:S(2)}, u32[]{:S(2)}) async-start(bf16[128,16,128]{2,1,0:T(8,128)(2,1)} %get-tuple-element.11), calls=%async_computation | async-start | bytes 1048576 | tf_op jit(solution)/shard_map/all_to_all | solution.py:402
  18.6 0.7 copy-start.7
  39.2 13.6 %copy-start.8 = (bf16[1536,192]{0,1:T(8,128)(2,1)S(1)}, bf16[1536,192]{0,1:T(8,128)(2,1)}, u32[]{:S(2)}) copy-start(bf16[1536,192]{0,1:T(8,128)(2,1)} %param.15) | copy-start | bytes 1769476
  42.9 19.0 %all-to-all-start.1 = ((bf16[32,4,384]{2,1,0:T(4,128)(2,1)}), bf16[32,4,384]{2,1,0:T(4,128)(2,1)S(1)}, u32[]{:S(2)}, u32[]{:S(2)}) async-start(bf16[32,4,384]{2,1,0:T(4,128)(2,1)} %shard_map.115), calls=%async_computation.1 | async-start | bytes 196608 | tf_op jit(solution)/shard_map/all_to_all | solution.py:402
  62.2 1.0 copy-start.2
  62.2 1.1 copy-start.3
  64.3 4.4 %copy-start.9 = (bf16[2,1536,32]{1,2,0:T(8,128)(2,1)S(1)}, bf16[2,1536,32]{1,2,0:T(8,128)(2,1)}, u32[]{:S(2)}) copy-start(bf16[2,1536,32]{1,2,0:T(8,128)(2,1)} %param.17) | copy-start | bytes 589828
  64.3 16.0 %all-to-all-start.2 = ((bf16[16,16,384]{2,1,0:T(8,128)(2,1)}), bf16[16,16,384]{2,1,0:T(8,128)(2,1)S(1)}, u32[]{:S(2)}, u32[]{:S(2)}) async-start(bf16[16,16,384]{2,1,0:T(8,128)(2,1)} %get-tuple-element.13), calls=%async_computation.2 | async-start | bytes 393216 | tf_op jit(solution)/shard_map/all_to_all | solution.py:402
  69.2 9.9 %collective-permute-start = (bf16[32,128]{1,0:T(8,128)(2,1)S(1)}, bf16[32,128]{1,0:T(8,128)(2,1)S(1)}, u32[]{:S(2)}, u32[]{:S(2)}) collective-permute-start(bf16[32,128]{1,0:T(8,128)(2,1)S(1)} %get-tuple-element.12), channel_id=1, source_target_pairs={{0,8},{8,0},{16,24},{24,16},{1,9},{9,1},{17,25},{25,17},{2,10},{10... | collective-permute-start | bytes 24584 | tf_op jit(solution)/shard_map/ppermute | solution.py:426
  71.4 7.6 %collective-permute-start.1 = (bf16[32,128]{1,0:T(8,128)(2,1)S(1)}, bf16[32,128]{1,0:T(8,128)(2,1)S(1)}, u32[]{:S(2)}, u32[]{:S(2)}) collective-permute-start(bf16[32,128]{1,0:T(8,128)(2,1)S(1)} %get-tuple-element.12), channel_id=1, source_target_pairs={{0,16},{8,24},{16,0},{24,8},{1,17},{9,25},{17,1},{25,9},{2,18},{10... | collective-permute-start | bytes 24584 | tf_op jit(solution)/shard_map/ppermute | solution.py:426
  74.7 5.6 %collective-permute-start.2 = (bf16[32,128]{1,0:T(8,128)(2,1)S(1)}, bf16[32,128]{1,0:T(8,128)(2,1)S(1)}, u32[]{:S(2)}, u32[]{:S(2)}) collective-permute-start(bf16[32,128]{1,0:T(8,128)(2,1)S(1)} %get-tuple-element.12), channel_id=1, source_target_pairs={{0,24},{8,16},{16,8},{24,0},{1,25},{9,17},{17,9},{25,1},{2,26},{10... | collective-permute-start | bytes 24584 | tf_op jit(solution)/shard_map/ppermute | solution.py:426
  78.8 12.9 %copy-start.1 = (bf16[192,1536]{1,0:T(8,128)(2,1)S(1)}, bf16[192,1536]{1,0:T(8,128)(2,1)}, u32[]{:S(2)}) copy-start(bf16[192,1536]{1,0:T(8,128)(2,1)} %w_out_ref.1) | copy-start | bytes 1769476
  81.3 10.3 %all-to-all-start.3 = ((bf16[8,16,256]{2,1,0:T(8,128)(2,1)}), bf16[8,16,256]{2,1,0:T(8,128)(2,1)S(1)}, u32[]{:S(2)}, u32[]{:S(2)}) async-start(bf16[8,16,256]{2,1,0:T(8,128)(2,1)} %shard_map.117), calls=%async_computation.3 | async-start | bytes 131072 | tf_op jit(solution)/shard_map/all_to_all | solution.py:402
  92.7 11.1 %all-to-all-start.4 = ((f32[4,24,384]{2,1,0:T(8,128)}), f32[4,24,384]{2,1,0:T(8,128)S(1)}, u32[]{:S(2)}, u32[]{:S(2)}) async-start(f32[4,24,384]{2,1,0:T(8,128)} %shard_map.118), calls=%async_computation.4 | async-start | bytes 294912 | tf_op jit(solution)/shard_map/all_to_all | solution.py:402
  96.2 0.7 copy-start.10
  104.6 22.6 %all-to-all-start.5 = ((f32[128,1,96]{2,1,0:T(1,128)}), f32[128,1,96]{2,1,0:T(1,128)S(1)}, u32[]{:S(2)}, u32[]{:S(2)}) async-start(f32[128,1,96]{2,1,0:T(1,128)} %bitcast.12), calls=%async_computation.5 | async-start | bytes 131072 | tf_op jit(solution)/shard_map/all_to_all | solution.py:402

commit v12 on v10

--- a/solution.py
+++ b/solution.py
@@ -29,13 +29,14 @@
 
 ROWS = 32
 EXT_PAD = 40
-EDGE = 4
 RUN = 4
+EDGES_RUN = 14
 VMEM = 48 * 1024 * 1024
-
-
-def params(**kw):
-    return pltpu.CompilerParams(vmem_limit_bytes=VMEM, **kw)
+WHOLE = 60 * 1000 * 1000
+
+
+def params(limit=VMEM):
+    return pltpu.CompilerParams(vmem_limit_bytes=limit)
 
 
 def whole(count):
@@ -49,7 +50,8 @@
 def onehot_rows(codes, first, count):
     length = codes.shape[1]
     start = (length - first - KS_STEM // 2) % length
-    shifted = pltpu.roll(jnp.broadcast_to(codes, (16, length)), start, 1, stride=1, stride_axis=0)
+    codes = jnp.broadcast_to(codes, (16, length))
+    shifted = pltpu.roll(codes, start, 1, stride=1, stride_axis=0)
     shifted = shifted[:, :count]
     return jnp.concatenate(
         [(shifted == base + 1).astype(jnp.float32) for base in range(4)], axis=0
@@ -65,27 +67,46 @@
     return jnp.maximum(high, low)
 
 
-def stem_kernel(tokens_ref, weight_ref, out_ref):
-    onehot = onehot_rows(tokens_ref[...] + 1, 0, tokens_ref.shape[1])
-    weight = weight_ref[...]
+def stem_kernel(made_ref, out_ref):
+    onehot = onehot_rows(made_ref[64:, :].astype(jnp.float32), 0, made_ref.shape[1])
+    weight = made_ref[:64, : out_ref.shape[1]]
     step = 8
     for at in range(0, ROWS, step):
         part = onehot[:, at * STEM_POOL : (at + step) * STEM_POOL]
         out_ref[at : at + step, :] = pooled_rows(part, weight)
 
 
-def stem(tokens, weight):
+def stem(made, channels):
     return pl.pallas_call(
         stem_kernel,
-        out_shape=jax.ShapeDtypeStruct((ROWS, weight.shape[1]), jnp.float32),
-        in_specs=whole(2),
+        out_shape=jax.ShapeDtypeStruct((ROWS, channels), jnp.float32),
+        in_specs=whole(1),
         out_specs=whole(1)[0],
         compiler_params=params(),
         cost_estimate=pl.CostEstimate(flops=2 * 2048 * 64 * 768, bytes_accessed=200000, transcendentals=0),
-    )(tokens, weight)
-
-
-def pack_kernel(weight_ref, tokens_ref, out_ref, wide):
+    )(made)
+
+
+def start_kernel(weight_ref, stem_ref, tokens_hbm, line_hbm, out_ref, made_ref, wide, tokens_ref, line_ref, arrived):
+    copies = [
+        pltpu.make_async_copy(tokens_hbm, tokens_ref, arrived.at[0]),
+        pltpu.make_async_copy(line_hbm, line_ref, arrived.at[1]),
+    ]
+    for copy in copies:
+        copy.start()
+    rows, channels = stem_ref.shape
+    row = lax.broadcasted_iota(jnp.int32, (64, rows), 0)
+    column = lax.broadcasted_iota(jnp.int32, (64, rows), 1)
+    picked = (column == (KS_STEM - 1 - row % 16) * 4 + row // 16) & (row % 16 < KS_STEM)
+    picked = picked.astype(jnp.float32).astype(jnp.bfloat16)
+    made = jnp.dot(picked, stem_ref[...], preferred_element_type=jnp.float32).astype(jnp.bfloat16)
+    half = channels // 2
+    row = lax.broadcasted_iota(jnp.int32, (channels, half), 0)
+    column = lax.broadcasted_iota(jnp.int32, (channels, half), 1)
+    for odd in range(2):
+        order = (row == 2 * column + odd).astype(jnp.float32).astype(jnp.bfloat16)
+        part = jnp.dot(made, order, preferred_element_type=jnp.float32)
+        made_ref[:64, odd * half : (odd + 1) * half] = part.astype(jnp.bfloat16)
     taps, width = weight_ref.shape
     share = width // N_SHARE
     half = taps // 2
@@ -99,6 +120,11 @@
     even, odd = jnp.concatenate(even, axis=1), jnp.concatenate(odd, axis=1)
     lane = lax.broadcasted_iota(jnp.int32, (half + 1, HQK), 1)
     row = lax.broadcasted_iota(jnp.int32, (half + 1, HQK), 0)
+    for copy in copies:
+        copy.wait()
+    line = (line_ref[...] + 1).astype(jnp.float32).astype(jnp.bfloat16)
+    made_ref[64:, :] = jnp.broadcast_to(line, (16, line.shape[1]))
+    made_ref[:64, channels:] = jnp.zeros((64, line.shape[1] - channels), jnp.bfloat16)
     codes = (tokens_ref[...] + 1).astype(jnp.float32)
     last = codes.shape[0] - 1
     line = [jnp.broadcast_to(codes[at : at + 1, :], lane.shape) for at in (0, 1, last - 1, last)]
@@ -120,16 +146,25 @@
         out_ref[place] = blocks[index]
 
 
-def pack(weight, tokens):
+def start(weight, stem_weight, tokens):
     taps, width = weight.shape
-    return pl.pallas_call(
-        pack_kernel,
-        out_shape=jax.ShapeDtypeStruct((N_SEQ, taps // 2 + 1, HQK), jnp.bfloat16),
-        in_specs=whole(2),
-        out_specs=whole(1)[0],
-        scratch_shapes=[pltpu.VMEM((width // HQK, taps + 2, HQK), jnp.float32)],
-        compiler_params=params(),
-    )(weight, tokens)
+    tokens, line = tokens.reshape(-1, HQK), tokens.reshape(1, -1)
+    return pl.pallas_call(
+        start_kernel,
+        out_shape=(
+            jax.ShapeDtypeStruct((N_SEQ, taps // 2 + 1, HQK), jnp.bfloat16),
+            jax.ShapeDtypeStruct((80, line.shape[1]), jnp.bfloat16),
+        ),
+        in_specs=whole(2) + [pl.BlockSpec(memory_space=pltpu.HBM)] * 2,
+        out_specs=tuple(whole(2)),
+        scratch_shapes=[
+            pltpu.VMEM((width // HQK, taps + 2, HQK), jnp.float32),
+            pltpu.VMEM(tokens.shape, jnp.int32),
+            pltpu.VMEM(line.shape, jnp.int32),
+            pltpu.SemaphoreType.DMA((2,)),
+        ],
+        compiler_params=params(WHOLE),
+    )(weight, stem_weight, tokens, line)
 
 
 def border_codes(held_ref, right):
@@ -153,29 +188,39 @@
         block = held_ref[source].astype(jnp.float32)
         weights[source * (rows - 1) : (source + 1) * (rows - 1), :] = block[: rows - 1, :]
     first = ((place_ref[0] & (N_SEQ // 2 - 1)) // RUN) * RUN
-    borders = [run * (N_SEQ // 2) + first + index for run in range(2) for index in range(RUN + 1)]
-    for at in range(0, len(borders), 2):
+    for run in range(2):
+        right = run * (N_SEQ // 2) + first
         onehot = jnp.concatenate(
             [
-                onehot_rows(border_codes(held_ref, right), 128, EDGE * STEM_POOL)
-                for right in borders[at : at + 2]
+                onehot_rows(border_codes(held_ref, right + index), 192 if inner else 128, 128 if inner else 256)
+                for index in range(RUN + 1)
+                for inner in [0 < index < RUN]
             ],
             axis=1,
         )
-        made = pooled_rows(onehot, stem_ref[...])
+        made = pooled_rows(onehot, stem_ref[:64, : section_ref.shape[2]])
         place = lax.broadcasted_iota(jnp.int32, made.shape, 0)
-        right = jnp.where(place < EDGE, borders[at], borders[at + 1])
-        place = right * ROWS - EDGE // 2 + place % EDGE
-        inside = (place >= 0) & (place < count * ROWS)
-        edges[at * EDGE : (at + 2) * EDGE, :] = jnp.where(inside, made, 0.0)
+        outside = ((place < 2) & (right == 0)) | ((place >= EDGES_RUN - 2) & (right + RUN == count))
+        edges[run * 16 : run * 16 + EDGES_RUN, :] = jnp.where(outside, 0.0, made)
     windows, _, channels = section_ref.shape
     half = channels // 2
     columns = out_ref.shape[2] // 8
     for window in range(windows):
-        at = (window // RUN * (RUN + 1) + window % RUN) * EDGE
-        wide[window, 3 : ROWS + 1, :] = section_ref[window].astype(jnp.float32)[1 : ROWS - 1, :]
-        wide[window, 0:3, :] = edges[at : at + 3, :]
-        wide[window, ROWS + 1 : ROWS + 4, :] = edges[at + EDGE + 1 : at + EDGE + 4, :]
+        run, index = window // RUN, window % RUN
+        rows = section_ref[window].astype(jnp.float32)
+        wide[window, 3 : ROWS + 1, :] = rows[1 : ROWS - 1, :]
+        at = run * 16 + 2 + 2 * index
+        if index == 0:
+            wide[window, 0:3, :] = edges[run * 16 : run * 16 + 3, :]
+        else:
+            wide[window, 1:3, :] = edges[at : at + 2, :]
+            wide[window - 1, ROWS + 3 : ROWS + 4, :] = rows[1:2, :]
+        at = at + 2
+        if index == RUN - 1:
+            wide[window, ROWS + 1 : ROWS + 4, :] = edges[at + 1 : at + 4, :]
+        else:
+            wide[window, ROWS + 1 : ROWS + 3, :] = edges[at : at + 2, :]
+            wide[window + 1, 0:1, :] = rows[ROWS - 2 : ROWS - 1, :]
     even, odd = None, None
     for tap in range(KS_CONV):
         rows = wide[:, tap : tap + ROWS, :].astype(jnp.bfloat16).reshape(windows * ROWS, channels)
@@ -202,7 +247,6 @@
 
 def conv(place, section, held, stem_weight, columns):
     windows, _, channels = section.shape
-    borders = windows // RUN * (RUN + 1)
     return pl.pallas_call(
         conv_kernel,
         out_shape=jax.ShapeDtypeStruct((windows * N_PAIR, 2, 8 * columns), jnp.bfloat16),
@@ -210,7 +254,7 @@
         out_specs=whole(1)[0],
         scratch_shapes=[
             pltpu.VMEM((held.shape[0] * (held.shape[1] - 1), HQK), jnp.float32),
-            pltpu.VMEM((borders * EDGE, channels), jnp.float32),
+            pltpu.VMEM((32, channels), jnp.float32),
             pltpu.VMEM((windows, EXT_PAD, channels), jnp.float32),
             pltpu.VMEM((windows * ROWS, HQK), jnp.float32),
             pltpu.VMEM((windows * ROWS // 2, HQK), jnp.float32),
@@ -378,18 +422,13 @@
 
     taps, width = w_conv.shape
     share = width // N_SHARE
-    held = exchange(pack(w_conv, tokens.reshape(-1, HQK)), SEQ)
-
-    source = jnp.arange(w_stem.shape[1]).reshape(2, -1)
-    source = (2 * (source % source.shape[1]) + jnp.arange(2)[:, None]).reshape(-1)
-    order = (jnp.arange(w_stem.shape[1])[:, None] == source[None, :]).astype(jnp.bfloat16)
-    stem_weight = jnp.dot(w_stem, order, preferred_element_type=jnp.float32).astype(jnp.bfloat16)
-    stem_weight = stem_weight.reshape(KS_STEM, 4, -1)[::-1].transpose(1, 0, 2)
-    stem_weight = jnp.pad(stem_weight, ((0, 0), (0, 1), (0, 0))).reshape(64, -1)
-    section = stem(tokens.reshape(1, -1), stem_weight).astype(jnp.bfloat16)
+    blocks, made = start(w_conv, w_stem, tokens)
+    held = exchange(blocks, SEQ)
+
+    section = stem(made, w_stem.shape[1]).astype(jnp.bfloat16)
     sections = lax.all_gather(section, SHARE, axis=0, tiled=False)
 
-    parts = exchange(conv(place.astype(jnp.int32)[None], sections, held, stem_weight, share), SHARE + ("pair",))
+    parts = exchange(conv(place.astype(jnp.int32)[None], sections, held, made, share), SHARE + ("pair",))
     count = ROWS // 2
     trunk = parts.reshape(N_SHARE, N_PAIR, count, share).transpose(2, 1, 0, 3)
     trunk = trunk.reshape(count, N_PAIR * width)

time: 125 us -> 124 us (level)
  Pallas kernels: 10 us -> 11.3 us
    pallas_call x2, Pallas kernels: 2.46 us -> 4.21 us  [the longest x1 2.69 us: start(): pl.pallas_call(start_kernel, out_shape=(jax.ShapeDtypeStruct((N_SEQ, taps...]
  transfers between devices with their start and end apart: 9 -> 9, of which waited for: 8 -> 8; matrix products, arithmetic and copies ran while one was open for 2% -> 1% of each run, Pallas kernels for 1% -> 1%
where the time goes in v12:
time: 124 us
  starting transfers between devices  55.3 us (45%)
  waiting for transfers between devices  38.7 us (31%)
  blocking collectives  14.2 us (11%)
  Pallas kernels  11.3 us (9%)
  local copies, waits for them, and re-layouts  2.17 us (2%)
    all_to_all x6, starting transfers between devices, exchange(): return lax.all_to_all(blocks, axes, split_axis=0, concat_axis=0, tiled=True)  47.2 us
    all_to_all x6, waiting for transfers between devices, exchange(): return lax.all_to_all(blocks, axes, split_axis=0, concat_axis=0, tiled=True)  35.8 us
    all_gather x1, blocking collectives, on_device(): sections = lax.all_gather(section, SHARE, axis=0, tiled=False)  14.2 us
    ppermute x3, starting transfers between devices, on_device(): other = lax.ppermute(query, name, [(0, 1), (1, 0)])  8.06 us
    pallas_call x1, Pallas kernels, conv(): pl.pallas_call(conv_kernel, out_shape=jax.ShapeDtypeStruct((windows * N_P...  3.22 us
    ppermute x3, waiting for transfers between devices, on_device(): other = lax.ppermute(query, name, [(0, 1), (1, 0)])  2.87 us
    pallas_call x1, Pallas kernels, start(): pl.pallas_call(start_kernel, out_shape=(jax.ShapeDtypeStruct((N_SEQ, taps...  2.69 us
  transfers between devices with their start and end apart: 9, of which 8 were waited for; matrix products, arithmetic and copies ran while one was open for 1% of the time, Pallas kernels for 1%

profile of v12, /device:TPU:1, one launch (start us, length us, event | category | flops | bytes accessed | tf_op | source)
XLA Modules:
  0.0 123.6 jit_solution(14489352274437056351)
XLA Ops:
  0.6 0.0 copy-start
  0.6 2.7 %shard_map.113 = (bf16[128,16,128]{2,1,0:T(8,128)(2,1)}, bf16[80,2048]{1,0:T(8,128)(2,1)}) custom-call(bf16[30,384]{1,0:T(8,128)(2,1)} %weight_ref.1, bf16[60,768]{1,0:T(8,128)(2,1)} %stem_ref.1, s32[16,128]{1,0:T(8,128)} %bitcast.33, s32[1,2048]{1,0:T(1,128)} %bitcast.34), custom_call_target="tpu_custom_call" | custom-call | tf_op jit(solution)/shard_map/pallas_call | solution.py:152
  3.3 0.0 copy-start.4
  3.4 14.4 %all-to-all-start = ((bf16[128,16,128]{2,1,0:T(8,128)(2,1)}), bf16[128,16,128]{2,1,0:T(8,128)(2,1)S(1)}, u32[]{:S(2)}, u32[]{:S(2)}) async-start(bf16[128,16,128]{2,1,0:T(8,128)(2,1)} %get-tuple-element.10), calls=%async_computation | async-start | bytes 1048576 | tf_op jit(solution)/shard_map/all_to_all | solution.py:416
  17.7 0.0 copy-done.4
  17.7 1.5 %shard_map.114 = f32[32,768]{1,0:T(8,128)S(1)} custom-call(bf16[80,2048]{1,0:T(8,128)(2,1)S(1)} %copy-done.4), custom_call_target="tpu_custom_call" | custom-call | flops 201326592 | bytes 200000 | tf_op jit(solution)/shard_map/pallas_call | solution.py:80
  19.3 14.2 %all-gather = bf16[256,768]{1,0:T(8,128)(2,1)S(1)} all-gather(bf16[32,768]{1,0:T(8,128)(2,1)S(1)} %convert_element_type.132), channel_id=2, replica_groups=mesh['zl'=2,'y'=8,'xh'=2,'xl'=2,'core'=2,'pair'=4] {'zl','xl','core'}, dimensions={0}, use_global_device_ids=true | all-gather | bytes 442368 | tf_op jit(solution)/shard_map/all_gather | solution.py:429
  33.5 4.8 %all-to-all-done.held_ref = bf16[128,16,128]{2,1,0:T(8,128)(2,1)S(1)} async-done(((bf16[128,16,128]{2,1,0:T(8,128)(2,1)}), bf16[128,16,128]{2,1,0:T(8,128)(2,1)S(1)}, u32[]{:S(2)}, u32[]{:S(2)}) %all-to-all-start) | async-done | bytes 524320 | tf_op jit(solution)/shard_map/all_to_all | solution.py:416
  38.3 0.0 copy-start.5
  38.3 3.2 %shard_map.115 = bf16[32,2,384]{2,1,0:T(2,128)(2,1)} custom-call(s32[1]{0:T(128)} %bitcast.1.place_ref, bf16[8,32,768]{2,1,0:T(8,128)(2,1)S(1)} %bitcast.27, bf16[128,16,128]{2,1,0:T(8,128)(2,1)S(1)} %all-to-all-done.held_ref, bf16[80,2048]{1,0:T(8,128)(2,1)S(1)} %copy-done.4), custom_call_target="tpu_custom_call" | custom-call | tf_op jit(solution)/shard_map/pallas_call | solution.py:250
  41.5 9.8 %all-to-all-start.1 = ((bf16[32,2,384]{2,1,0:T(2,128)(2,1)}), bf16[32,2,384]{2,1,0:T(2,128)(2,1)S(1)}, u32[]{:S(2)}, u32[]{:S(2)}) async-start(bf16[32,2,384]{2,1,0:T(2,128)(2,1)} %shard_map.115), calls=%async_computation.1 | async-start | bytes 98304 | tf_op jit(solution)/shard_map/all_to_all | solution.py:416
  51.3 0.0 copy-done.5
  51.4 0.0 copy-start.3
  51.4 0.3 copy.21.w_value_ref
  51.6 0.0 copy-start.2
  51.7 7.9 %all-to-all-done.1 = bf16[32,2,384]{2,1,0:T(2,128)(2,1)S(1)} async-done(((bf16[32,2,384]{2,1,0:T(2,128)(2,1)}), bf16[32,2,384]{2,1,0:T(2,128)(2,1)S(1)}, u32[]{:S(2)}, u32[]{:S(2)}) %all-to-all-start.1) | async-done | bytes 49184 | tf_op jit(solution)/shard_map/all_to_all | solution.py:416
  59.6 0.2 reshape.78
  59.7 0.1 copy.30
  59.8 0.2 reshape.79.trunk_ref
  60.0 0.0 copy-done.3
  60.0 0.0 copy-done.2
  60.0 1.0 shard_map.116
  61.0 2.3 %collective-permute-start = (bf16[16,128]{1,0:T(8,128)(2,1)S(1)}, bf16[16,128]{1,0:T(8,128)(2,1)S(1)}, u32[]{:S(2)}, u32[]{:S(2)}) collective-permute-start(bf16[16,128]{1,0:T(8,128)(2,1)S(1)} %get-tuple-element.11), channel_id=1, source_target_pairs={{0,4},{4,0},{1,5},{5,1},{2,6},{6,2},{3,7},{7,3},{8,12},{12,8},{9,1... | collective-permute-start | bytes 12296 | tf_op jit(solution)/shard_map/ppermute | solution.py:438
  63.3 0.8 collective-permute-done
  64.1 2.2 %collective-permute-start.1 = (bf16[32,128]{1,0:T(8,128)(2,1)S(1)}, bf16[32,128]{1,0:T(8,128)(2,1)S(1)}, u32[]{:S(2)}, u32[]{:S(2)}) collective-permute-start(bf16[32,128]{1,0:T(8,128)(2,1)S(1)} %pad_maximum_fusion.3), channel_id=1, source_target_pairs={{0,8},{8,0},{1,9},{9,1},{2,10},{10,2},{3,11},{11,3},{4,12},{12,4},... | collective-permute-start | bytes 24584 | tf_op jit(solution)/shard_map/ppermute | solution.py:438
  66.4 0.0 copy-start.6
  66.4 3.7 %all-to-all-start.2 = ((bf16[16,16,384]{2,1,0:T(8,128)(2,1)}), bf16[16,16,384]{2,1,0:T(8,128)(2,1)S(1)}, u32[]{:S(2)}, u32[]{:S(2)}) async-start(bf16[16,16,384]{2,1,0:T(8,128)(2,1)} %get-tuple-element.12), calls=%async_computation.2 | async-start | bytes 393216 | tf_op jit(solution)/shard_map/all_to_all | solution.py:416
  70.0 0.0 collective-permute-done.1
  70.1 3.6 %collective-permute-start.2 = (bf16[64,128]{1,0:T(8,128)(2,1)S(1)}, bf16[64,128]{1,0:T(8,128)(2,1)S(1)}, u32[]{:S(2)}, u32[]{:S(2)}) collective-permute-start(bf16[64,128]{1,0:T(8,128)(2,1)S(1)} %pad_maximum_fusion.2), channel_id=1, source_target_pairs={{0,16},{16,0},{1,17},{17,1},{2,18},{18,2},{3,19},{19,3},{4,20},{20... | collective-permute-start | bytes 49160 | tf_op jit(solution)/shard_map/ppermute | solution.py:438
  73.6 0.0 copy-done.6
  73.7 0.2 copy.27
  73.9 0.2 copy.28
  74.1 2.1 %collective-permute-done.2 = bf16[64,128]{1,0:T(8,128)(2,1)S(1)} collective-permute-done((bf16[64,128]{1,0:T(8,128)(2,1)S(1)}, bf16[64,128]{1,0:T(8,128)(2,1)S(1)}, u32[]{:S(2)}, u32[]{:S(2)}) %collective-permute-start.2) | collective-permute-done | bytes 16416 | tf_op jit(solution)/shard_map/ppermute | solution.py:438
  76.2 1.3 %all-to-all-done.2 = bf16[16,16,384]{2,1,0:T(8,128)(2,1)S(1)} async-done(((bf16[16,16,384]{2,1,0:T(8,128)(2,1)}), bf16[16,16,384]{2,1,0:T(8,128)(2,1)S(1)}, u32[]{:S(2)}, u32[]{:S(2)}) %all-to-all-start.2) | async-done | bytes 196640 | tf_op jit(solution)/shard_map/all_to_all | solution.py:416
  77.5 1.0 shard_map.117
  78.5 5.8 %all-to-all-start.3 = ((bf16[8,16,256]{2,1,0:T(8,128)(2,1)}), bf16[8,16,256]{2,1,0:T(8,128)(2,1)S(1)}, u32[]{:S(2)}, u32[]{:S(2)}) async-start(bf16[8,16,256]{2,1,0:T(8,128)(2,1)} %shard_map.117), calls=%async_computation.3 | async-start | bytes 131072 | tf_op jit(solution)/shard_map/all_to_all | solution.py:416
  84.3 0.0 copy-start.1
  84.3 0.2 pad_maximum_fusion.w_pair_ref
  84.5 0.0 copy-start.7
  84.5 0.7 copy-done.7
  85.2 0.1 copy.24.pair_ref
  85.3 3.8 %all-to-all-done.3.parts_ref = bf16[8,16,256]{2,1,0:T(8,128)(2,1)S(1)} async-done(((bf16[8,16,256]{2,1,0:T(8,128)(2,1)}), bf16[8,16,256]{2,1,0:T(8,128)(2,1)S(1)}, u32[]{:S(2)}, u32[]{:S(2)}) %all-to-all-start.3) | async-done | bytes 65568 | tf_op jit(solution)/shard_map/all_to_all | solution.py:416
  89.1 0.0 copy-done.1
  89.1 1.0 shard_map.118
  90.2 3.3 %all-to-all-start.4 = ((f32[4,24,384]{2,1,0:T(8,128)}), f32[4,24,384]{2,1,0:T(8,128)S(1)}, u32[]{:S(2)}, u32[]{:S(2)}) async-start(f32[4,24,384]{2,1,0:T(8,128)} %shard_map.118), calls=%async_computation.4 | async-start | bytes 294912 | tf_op jit(solution)/shard_map/all_to_all | solution.py:416
  93.5 7.3 %all-to-all-done.4.terms_ref = f32[4,24,384]{2,1,0:T(8,128)S(1)} async-done(((f32[4,24,384]{2,1,0:T(8,128)}), f32[4,24,384]{2,1,0:T(8,128)S(1)}, u32[]{:S(2)}, u32[]{:S(2)}) %all-to-all-start.4) | async-done | bytes 147488 | tf_op jit(solution)/shard_map/all_to_all | solution.py:416
  100.9 0.8 shard_map.119
  101.7 10.2 %all-to-all-start.5 = ((f32[128,1,96]{2,1,0:T(1,128)}), f32[128,1,96]{2,1,0:T(1,128)S(1)}, u32[]{:S(2)}, u32[]{:S(2)}) async-start(f32[128,1,96]{2,1,0:T(1,128)} %bitcast.11), calls=%async_computation.5 | async-start | bytes 131072 | tf_op jit(solution)/shard_map/all_to_all | solution.py:416
  111.9 0.1 slice_bitcast_fusion.1
  112.0 10.7 %all-to-all-done.5 = f32[128,1,96]{2,1,0:T(1,128)S(1)} async-done(((f32[128,1,96]{2,1,0:T(1,128)}), f32[128,1,96]{2,1,0:T(1,128)S(1)}, u32[]{:S(2)}, u32[]{:S(2)}) %all-to-all-start.5) | async-done | bytes 49184 | tf_op jit(solution)/shard_map/all_to_all | solution.py:416
  122.7 0.1 copy.26
  122.8 0.0 copy-done
  122.8 0.8 fusion.1
  (7 shorter events, 0.1 us)
Async XLA Ops:
  0.6 122.2 %copy-start = (bf16[18,32]{1,0:T(8,128)(2,1)S(1)}, bf16[18,32]{1,0:T(8,128)(2,1)}, u32[]{:S(2)}) copy-start(bf16[18,32]{1,0:T(8,128)(2,1)} %param.18) | copy-start | bytes 3460
  3.3 14.4 %copy-start.4 = (bf16[80,2048]{1,0:T(8,128)(2,1)S(1)}, bf16[80,2048]{1,0:T(8,128)(2,1)}, u32[]{:S(2)}) copy-start(bf16[80,2048]{1,0:T(8,128)(2,1)} %get-tuple-element.9.made_ref.stem_ref) | copy-start | bytes 983044
  3.4 34.9 %all-to-all-start = ((bf16[128,16,128]{2,1,0:T(8,128)(2,1)}), bf16[128,16,128]{2,1,0:T(8,128)(2,1)S(1)}, u32[]{:S(2)}, u32[]{:S(2)}) async-start(bf16[128,16,128]{2,1,0:T(8,128)(2,1)} %get-tuple-element.10), calls=%async_computation | async-start | bytes 1048576 | tf_op jit(solution)/shard_map/all_to_all | solution.py:416
  38.3 13.1 %copy-start.5 = (bf16[1536,192]{0,1:T(8,128)(2,1)S(1)}, bf16[1536,192]{0,1:T(8,128)(2,1)}, u32[]{:S(2)}) copy-start(bf16[1536,192]{0,1:T(8,128)(2,1)} %param.15) | copy-start | bytes 1769476
  41.5 18.1 %all-to-all-start.1 = ((bf16[32,2,384]{2,1,0:T(2,128)(2,1)}), bf16[32,2,384]{2,1,0:T(2,128)(2,1)S(1)}, u32[]{:S(2)}, u32[]{:S(2)}) async-start(bf16[32,2,384]{2,1,0:T(2,128)(2,1)} %shard_map.115), calls=%async_computation.1 | async-start | bytes 98304 | tf_op jit(solution)/shard_map/all_to_all | solution.py:416
  51.4 8.6 %copy-start.3 = (bf16[1536,128]{1,0:T(8,128)(2,1)S(1)}, bf16[1536,128]{1,0:T(8,128)(2,1)}, u32[]{:S(2)}) copy-start(bf16[1536,128]{1,0:T(8,128)(2,1)} %w_key_ref.1) | copy-start | bytes 1179652
  51.6 8.4 %copy-start.2 = (bf16[1536,128]{1,0:T(8,128)(2,1)S(1)}, bf16[1536,128]{1,0:T(8,128)(2,1)}, u32[]{:S(2)}) copy-start(bf16[1536,128]{1,0:T(8,128)(2,1)} %w_query_ref.1) | copy-start | bytes 1179652
  61.0 3.1 %collective-permute-start = (bf16[16,128]{1,0:T(8,128)(2,1)S(1)}, bf16[16,128]{1,0:T(8,128)(2,1)S(1)}, u32[]{:S(2)}, u32[]{:S(2)}) collective-permute-start(bf16[16,128]{1,0:T(8,128)(2,1)S(1)} %get-tuple-element.11), channel_id=1, source_target_pairs={{0,4},{4,0},{1,5},{5,1},{2,6},{6,2},{3,7},{7,3},{8,12},{12,8},{9,1... | collective-permute-start | bytes 12296 | tf_op jit(solution)/shard_map/ppermute | solution.py:438
  64.1 5.9 %collective-permute-start.1 = (bf16[32,128]{1,0:T(8,128)(2,1)S(1)}, bf16[32,128]{1,0:T(8,128)(2,1)S(1)}, u32[]{:S(2)}, u32[]{:S(2)}) collective-permute-start(bf16[32,128]{1,0:T(8,128)(2,1)S(1)} %pad_maximum_fusion.3), channel_id=1, source_target_pairs={{0,8},{8,0},{1,9},{9,1},{2,10},{10,2},{3,11},{11,3},{4,12},{12,4},... | collective-permute-start | bytes 24584 | tf_op jit(solution)/shard_map/ppermute | solution.py:438
  66.4 7.3 %copy-start.6 = (bf16[2,1536,32]{1,2,0:T(8,128)(2,1)S(1)}, bf16[2,1536,32]{1,2,0:T(8,128)(2,1)}, u32[]{:S(2)}) copy-start(bf16[2,1536,32]{1,2,0:T(8,128)(2,1)} %param.17) | copy-start | bytes 589828
  66.4 11.1 %all-to-all-start.2 = ((bf16[16,16,384]{2,1,0:T(8,128)(2,1)}), bf16[16,16,384]{2,1,0:T(8,128)(2,1)S(1)}, u32[]{:S(2)}, u32[]{:S(2)}) async-start(bf16[16,16,384]{2,1,0:T(8,128)(2,1)} %get-tuple-element.12), calls=%async_computation.2 | async-start | bytes 393216 | tf_op jit(solution)/shard_map/all_to_all | solution.py:416
  70.1 6.1 %collective-permute-start.2 = (bf16[64,128]{1,0:T(8,128)(2,1)S(1)}, bf16[64,128]{1,0:T(8,128)(2,1)S(1)}, u32[]{:S(2)}, u32[]{:S(2)}) collective-permute-start(bf16[64,128]{1,0:T(8,128)(2,1)S(1)} %pad_maximum_fusion.2), channel_id=1, source_target_pairs={{0,16},{16,0},{1,17},{17,1},{2,18},{18,2},{3,19},{19,3},{4,20},{20... | collective-permute-start | bytes 49160 | tf_op jit(solution)/shard_map/ppermute | solution.py:438
  78.5 10.6 %all-to-all-start.3 = ((bf16[8,16,256]{2,1,0:T(8,128)(2,1)}), bf16[8,16,256]{2,1,0:T(8,128)(2,1)S(1)}, u32[]{:S(2)}, u32[]{:S(2)}) async-start(bf16[8,16,256]{2,1,0:T(8,128)(2,1)} %shard_map.117), calls=%async_computation.3 | async-start | bytes 131072 | tf_op jit(solution)/shard_map/all_to_all | solution.py:416
  84.3 4.9 %copy-start.1 = (bf16[192,1536]{1,0:T(8,128)(2,1)S(1)}, bf16[192,1536]{1,0:T(8,128)(2,1)}, u32[]{:S(2)}) copy-start(bf16[192,1536]{1,0:T(8,128)(2,1)} %w_out_ref.1) | copy-start | bytes 1769476
  84.5 0.7 copy-start.7
  90.2 10.7 %all-to-all-start.4 = ((f32[4,24,384]{2,1,0:T(8,128)}), f32[4,24,384]{2,1,0:T(8,128)S(1)}, u32[]{:S(2)}, u32[]{:S(2)}) async-start(f32[4,24,384]{2,1,0:T(8,128)} %shard_map.118), calls=%async_computation.4 | async-start | bytes 294912 | tf_op jit(solution)/shard_map/all_to_all | solution.py:416
  101.7 21.0 %all-to-all-start.5 = ((f32[128,1,96]{2,1,0:T(1,128)}), f32[128,1,96]{2,1,0:T(1,128)S(1)}, u32[]{:S(2)}, u32[]{:S(2)}) async-start(f32[128,1,96]{2,1,0:T(1,128)} %bitcast.11), calls=%async_computation.5 | async-start | bytes 131072 | tf_op jit(solution)/shard_map/all_to_all | solution.py:416

commit v13 on v12

--- a/solution.py
+++ b/solution.py
@@ -240,7 +240,7 @@
         part = pltpu.roll(part, index * columns, 1)
         flat = part if flat is None else flat + part
     for window in range(windows):
-        block = flat[2 * window : 2 * window + 2, :].astype(jnp.bfloat16)
+        block = flat[window // 2 * 4 : window // 2 * 4 + 4, :].astype(jnp.bfloat16)
         for index in range(N_PAIR):
             out_ref[window * N_PAIR + index] = block
 
@@ -249,7 +249,7 @@
     windows, _, channels = section.shape
     return pl.pallas_call(
         conv_kernel,
-        out_shape=jax.ShapeDtypeStruct((windows * N_PAIR, 2, 8 * columns), jnp.bfloat16),
+        out_shape=jax.ShapeDtypeStruct((windows * N_PAIR, 4, 8 * columns), jnp.bfloat16),
         in_specs=[pl.BlockSpec(memory_space=pltpu.SMEM)] + whole(3),
         out_specs=whole(1)[0],
         scratch_shapes=[
@@ -263,32 +263,39 @@
     )(place, section, held, stem_weight)
 
 
-def project_kernel(trunk_ref, w_query_ref, w_key_ref, w_value_ref, query_ref, kv_ref):
+def project_kernel(core_ref, trunk_ref, w_query_ref, w_key_ref, w_value_ref, query_ref, kv_ref, own_ref):
     trunk = trunk_ref[...]
-    query, key, value = [
-        jnp.dot(trunk, ref[...], preferred_element_type=jnp.float32).astype(jnp.bfloat16)
-        for ref in (w_query_ref, w_key_ref, w_value_ref)
-    ]
-    query_ref[...] = query
-    rest = jnp.zeros((trunk.shape[0], kv_ref.shape[2] - HQK - HV), jnp.bfloat16)
+    first = core_ref[0] == 0
+    count = own_ref.shape[0]
+    half = count // 2
+    query_ref[...] = jnp.dot(trunk, w_query_ref[...], preferred_element_type=jnp.float32).astype(jnp.bfloat16)
+    wide = trunk.astype(jnp.float32)
+    own = jnp.where(first, wide[:count], wide[count:]).astype(jnp.bfloat16)
+    own_ref[...] = own
+    key = jnp.dot(own, w_key_ref[...], preferred_element_type=jnp.float32).astype(jnp.bfloat16)
+    value = jnp.dot(own, w_value_ref[...], preferred_element_type=jnp.float32)
+    rest = jnp.pad(value[:, HQK:], ((0, 0), (0, 2 * HQK - HV)))
+    rest = (rest[:half] + pltpu.roll(rest[half:], HV - HQK, 1)).astype(jnp.bfloat16)
+    value = value[:, :HQK].astype(jnp.bfloat16)
     for index in range(N_LINE):
-        kv_ref[index, :, :HQK] = key
-        kv_ref[index, :, HQK : HQK + HV] = value
-        kv_ref[index, :, HQK + HV :] = rest
-
-
-def project(trunk, w_query, w_key, w_value):
-    count = trunk.shape[0]
+        kv_ref[index, :count, :] = key
+        kv_ref[index, count : 2 * count, :] = value
+        kv_ref[index, 2 * count :, :] = rest
+
+
+def project(core, trunk, w_query, w_key, w_value):
+    count = trunk.shape[0] // 2
     return pl.pallas_call(
         project_kernel,
         out_shape=(
-            jax.ShapeDtypeStruct((count, HQK), jnp.bfloat16),
-            jax.ShapeDtypeStruct((N_LINE, count, 3 * HQK), jnp.bfloat16),
+            jax.ShapeDtypeStruct((2 * count, HQK), jnp.bfloat16),
+            jax.ShapeDtypeStruct((N_LINE, 2 * count + count // 2, HQK), jnp.bfloat16),
+            jax.ShapeDtypeStruct((count, trunk.shape[1]), jnp.bfloat16),
         ),
-        in_specs=whole(4),
-        out_specs=tuple(whole(2)),
-        compiler_params=params(),
-    )(trunk, w_query, w_key, w_value)
+        in_specs=[pl.BlockSpec(memory_space=pltpu.SMEM)] + whole(4),
+        out_specs=tuple(whole(3)),
+        compiler_params=params(),
+    )(core, trunk, w_query, w_key, w_value)
 
 
 def split(x):
@@ -302,31 +309,39 @@
 
 def attention_kernel(place_ref, query_ref, kv_ref, out_ref):
     scale = 1.0 / math.sqrt(HQK)
+    line, rows, _ = kv_ref.shape
+    count = out_ref.shape[1]
+    keys = kv_ref[:, :count, :].reshape(line * count, HQK)
+    values = kv_ref[:, count : 2 * count, :].reshape(line * count, HQK)
+    rest = kv_ref[:, 2 * count :, :].astype(jnp.float32)
+    rest = jnp.stack([rest, pltpu.roll(rest, HQK - (HV - HQK), 2)], axis=1)
+    rest = rest.reshape(line * count, HQK).astype(jnp.bfloat16)
     scores = (
         lax.dot_general(
-            query_ref[...],
-            kv_ref[:, :HQK],
-            (((1,), (1,)), ((), ())),
-            preferred_element_type=jnp.float32,
+            query_ref[...], keys, (((1,), (1,)), ((), ())), preferred_element_type=jnp.float32
         )
         * scale
     )
     top = jnp.max(scores, axis=1, keepdims=True)
     expo = jnp.exp(scores - top)
     total = jnp.sum(expo, axis=1, keepdims=True)
-    mixed = jnp.dot(expo.astype(jnp.bfloat16), kv_ref[:, HQK:], preferred_element_type=jnp.float32)
+    expo = expo.astype(jnp.bfloat16)
+    mixed = jnp.concatenate(
+        [jnp.dot(expo, part, preferred_element_type=jnp.float32) for part in (values, rest)], axis=1
+    )
     lane = lax.broadcasted_iota(jnp.int32, mixed.shape, 1)
     for index, column in enumerate(split(top) + split(total)):
         mixed = jnp.where(lane == HV + index, column, mixed)
     mixed = mixed.astype(jnp.bfloat16)
     groups, count, _ = out_ref.shape
     for index in range(groups):
-        out_ref[place_ref[0] ^ index] = mixed[index * count : (index + 1) * count, :]
+        place = ((place_ref[0] >> 1) ^ (index // 2)) * 2 + index % 2
+        out_ref[place] = mixed[index * count : (index + 1) * count, :]
 
 
 def attention(place, query, kv):
     groups = N_SPREAD
-    count, width = query.shape[0] // groups, kv.shape[1] - HQK
+    count, width = query.shape[0] // groups, 2 * HQK
     return pl.pallas_call(
         attention_kernel,
         out_shape=jax.ShapeDtypeStruct((groups, count, width), jnp.bfloat16),
@@ -430,14 +445,15 @@
 
     parts = exchange(conv(place.astype(jnp.int32)[None], sections, held, made, share), SHARE + ("pair",))
     count = ROWS // 2
-    trunk = parts.reshape(N_SHARE, N_PAIR, count, share).transpose(2, 1, 0, 3)
-    trunk = trunk.reshape(count, N_PAIR * width)
-
-    query, kv = project(trunk, w_query, w_key, w_value)
-    for name in reversed(SPREAD):
+    trunk = parts.reshape(N_SHARE, N_PAIR, 2 * count, share).transpose(2, 1, 0, 3)
+    trunk = trunk.reshape(2 * count, N_PAIR * width)
+
+    core = lax.axis_index("core").astype(jnp.int32)[None]
+    query, kv, trunk = project(core, trunk, w_query, w_key, w_value)
+    for name in reversed(SPREAD[:-1]):
         other = lax.ppermute(query, name, [(0, 1), (1, 0)])
         query = jnp.concatenate([query, other], axis=0)
-    kv = exchange(kv, LINE).reshape(N_LINE * count, kv.shape[2])
+    kv = exchange(kv, LINE)
     spread = lax.axis_index(SPREAD).astype(jnp.int32)[None]
     parts = exchange(attention(spread, query, kv), SPREAD)
     terms = exchange(combine(parts, w_out), ("pair",))

time: 124 us -> 123 us (level)
  starting transfers between devices: 55.3 us -> 53.2 us
    ppermute x3 -> x2, starting transfers between devices: 8.06 us -> 5.97 us  [on_device(): other = lax.ppermute(query, name, [(0, 1), (1, 0)])]
    ppermute x3 -> x2, waiting for transfers between devices: 2.87 us -> 1.99 us  [on_device(): other = lax.ppermute(query, name, [(0, 1), (1, 0)])]
  transfers between devices with their start and end apart: 9 -> 8, of which waited for: 8 -> 7; matrix products, arithmetic and copies ran while one was open for 1% -> 1% of each run, Pallas kernels for 1% -> 1%
where the time goes in v13:
time: 123 us; the launch traced here: 122 us
  starting transfers between devices  53.2 us (43%)
  waiting for transfers between devices  38.6 us (31%)
  blocking collectives  14.2 us (12%)
  Pallas kernels  11.4 us (9%)
  local copies, waits for them, and re-layouts  3.07 us (2%)
    all_to_all x6, starting transfers between devices, exchange(): return lax.all_to_all(blocks, axes, split_axis=0, concat_axis=0, tiled=True)  47.2 us
    all_to_all x6, waiting for transfers between devices, exchange(): return lax.all_to_all(blocks, axes, split_axis=0, concat_axis=0, tiled=True)  36.6 us
    all_gather x1, blocking collectives, on_device(): sections = lax.all_gather(section, SHARE, axis=0, tiled=False)  14.2 us
    ppermute x2, starting transfers between devices, on_device(): other = lax.ppermute(query, name, [(0, 1), (1, 0)])  5.97 us
    pallas_call x1, Pallas kernels, conv(): pl.pallas_call(conv_kernel, out_shape=jax.ShapeDtypeStruct((windows * N_P...  3.23 us
    pallas_call x1, Pallas kernels, start(): pl.pallas_call(start_kernel, out_shape=(jax.ShapeDtypeStruct((N_SEQ, taps...  2.66 us
  transfers between devices with their start and end apart: 8, of which 7 were waited for; matrix products, arithmetic and copies ran while one was open for 1% of the time, Pallas kernels for 1%

profile of v13, /device:TPU:1, one launch (start us, length us, event | category | flops | bytes accessed | tf_op | source)
XLA Modules:
  0.0 122.4 jit_solution(3432559464224154290)
XLA Ops:
  0.6 0.0 copy-start
  0.6 2.7 %shard_map.113 = (bf16[128,16,128]{2,1,0:T(8,128)(2,1)}, bf16[80,2048]{1,0:T(8,128)(2,1)}) custom-call(bf16[30,384]{1,0:T(8,128)(2,1)} %weight_ref.1, bf16[60,768]{1,0:T(8,128)(2,1)} %stem_ref.1, s32[16,128]{1,0:T(8,128)} %bitcast.32, s32[1,2048]{1,0:T(1,128)} %bitcast.33), custom_call_target="tpu_custom_call" | custom-call | tf_op jit(solution)/shard_map/pallas_call | solution.py:152
  3.3 0.0 copy-start.4
  3.3 14.4 %all-to-all-start = ((bf16[128,16,128]{2,1,0:T(8,128)(2,1)}), bf16[128,16,128]{2,1,0:T(8,128)(2,1)S(1)}, u32[]{:S(2)}, u32[]{:S(2)}) async-start(bf16[128,16,128]{2,1,0:T(8,128)(2,1)} %get-tuple-element.11), calls=%async_computation | async-start | bytes 1048576 | tf_op jit(solution)/shard_map/all_to_all | solution.py:431
  17.7 0.0 copy-done.4
  17.7 1.5 %shard_map.114 = f32[32,768]{1,0:T(8,128)S(1)} custom-call(bf16[80,2048]{1,0:T(8,128)(2,1)S(1)} %copy-done.4), custom_call_target="tpu_custom_call" | custom-call | flops 201326592 | bytes 200000 | tf_op jit(solution)/shard_map/pallas_call | solution.py:80
  19.3 14.2 %all-gather = bf16[256,768]{1,0:T(8,128)(2,1)S(1)} all-gather(bf16[32,768]{1,0:T(8,128)(2,1)S(1)} %convert_element_type.132), channel_id=2, replica_groups=mesh['zl'=2,'y'=8,'xh'=2,'xl'=2,'core'=2,'pair'=4] {'zl','xl','core'}, dimensions={0}, use_global_device_ids=true | all-gather | bytes 442368 | tf_op jit(solution)/shard_map/all_gather | solution.py:444
  33.5 4.8 %all-to-all-done.held_ref = bf16[128,16,128]{2,1,0:T(8,128)(2,1)S(1)} async-done(((bf16[128,16,128]{2,1,0:T(8,128)(2,1)}), bf16[128,16,128]{2,1,0:T(8,128)(2,1)S(1)}, u32[]{:S(2)}, u32[]{:S(2)}) %all-to-all-start) | async-done | bytes 524320 | tf_op jit(solution)/shard_map/all_to_all | solution.py:431
  38.2 0.0 copy-start.5
  38.2 3.2 %shard_map.115 = bf16[32,4,384]{2,1,0:T(4,128)(2,1)} custom-call(s32[1]{0:T(128)} %bitcast.2.place_ref, bf16[8,32,768]{2,1,0:T(8,128)(2,1)S(1)} %bitcast.27, bf16[128,16,128]{2,1,0:T(8,128)(2,1)S(1)} %all-to-all-done.held_ref, bf16[80,2048]{1,0:T(8,128)(2,1)S(1)} %copy-done.4), custom_call_target="tpu_custom_call" | custom-call | tf_op jit(solution)/shard_map/pallas_call | solution.py:250
  41.5 9.9 %all-to-all-start.1 = ((bf16[32,4,384]{2,1,0:T(4,128)(2,1)}), bf16[32,4,384]{2,1,0:T(4,128)(2,1)S(1)}, u32[]{:S(2)}, u32[]{:S(2)}) async-start(bf16[32,4,384]{2,1,0:T(4,128)(2,1)} %shard_map.115), calls=%async_computation.1 | async-start | bytes 196608 | tf_op jit(solution)/shard_map/all_to_all | solution.py:431
  51.3 0.0 copy-done.5
  51.4 0.3 copy.21.w_value_ref
  51.6 8.8 %all-to-all-done.1 = bf16[32,4,384]{2,1,0:T(4,128)(2,1)S(1)} async-done(((bf16[32,4,384]{2,1,0:T(4,128)(2,1)}), bf16[32,4,384]{2,1,0:T(4,128)(2,1)S(1)}, u32[]{:S(2)}, u32[]{:S(2)}) %all-to-all-start.1) | async-done | bytes 98336 | tf_op jit(solution)/shard_map/all_to_all | solution.py:431
  60.5 0.2 reshape.75
  60.7 0.0 copy-start.2
  60.7 0.0 copy-start.3
  60.7 0.2 copy.30
  60.9 0.3 reshape.76.trunk_ref
  61.2 0.5 copy-done.2
  61.7 0.1 copy-done.3
  61.8 1.1 shard_map.116
  62.9 0.0 copy-start.6
  62.9 2.2 %collective-permute-start = (bf16[32,128]{1,0:T(8,128)(2,1)S(1)}, bf16[32,128]{1,0:T(8,128)(2,1)S(1)}, u32[]{:S(2)}, u32[]{:S(2)}) collective-permute-start(bf16[32,128]{1,0:T(8,128)(2,1)S(1)} %get-tuple-element.12), channel_id=1, source_target_pairs={{0,8},{8,0},{1,9},{9,1},{2,10},{10,2},{3,11},{11,3},{4,12},{12,4},... | collective-permute-start | bytes 24584 | tf_op jit(solution)/shard_map/ppermute | solution.py:454
  65.1 3.5 %all-to-all-start.2 = ((bf16[16,40,128]{2,1,0:T(8,128)(2,1)}), bf16[16,40,128]{2,1,0:T(8,128)(2,1)S(1)}, u32[]{:S(2)}, u32[]{:S(2)}) async-start(bf16[16,40,128]{2,1,0:T(8,128)(2,1)} %get-tuple-element.13), calls=%async_computation.2 | async-start | bytes 327680 | tf_op jit(solution)/shard_map/all_to_all | solution.py:431
  68.6 0.0 collective-permute-done
  68.7 3.8 %collective-permute-start.1 = (bf16[64,128]{1,0:T(8,128)(2,1)S(1)}, bf16[64,128]{1,0:T(8,128)(2,1)S(1)}, u32[]{:S(2)}, u32[]{:S(2)}) collective-permute-start(bf16[64,128]{1,0:T(8,128)(2,1)S(1)} %pad_maximum_fusion.2), channel_id=1, source_target_pairs={{0,16},{16,0},{1,17},{17,1},{2,18},{18,2},{3,19},{19,3},{4,20},{20... | collective-permute-start | bytes 49160 | tf_op jit(solution)/shard_map/ppermute | solution.py:454
  72.5 0.0 copy-done.6
  72.5 0.2 copy.27
  72.7 0.2 copy.28
  73.0 2.0 %collective-permute-done.1 = bf16[64,128]{1,0:T(8,128)(2,1)S(1)} collective-permute-done((bf16[64,128]{1,0:T(8,128)(2,1)S(1)}, bf16[64,128]{1,0:T(8,128)(2,1)S(1)}, u32[]{:S(2)}, u32[]{:S(2)}) %collective-permute-start.1) | collective-permute-done | bytes 16416 | tf_op jit(solution)/shard_map/ppermute | solution.py:454
  74.9 1.1 all-to-all-done.2.kv_ref
  76.0 1.1 shard_map.117
  77.1 5.6 %all-to-all-start.3 = ((bf16[8,16,256]{2,1,0:T(8,128)(2,1)}), bf16[8,16,256]{2,1,0:T(8,128)(2,1)S(1)}, u32[]{:S(2)}, u32[]{:S(2)}) async-start(bf16[8,16,256]{2,1,0:T(8,128)(2,1)} %shard_map.117), calls=%async_computation.3 | async-start | bytes 131072 | tf_op jit(solution)/shard_map/all_to_all | solution.py:431
  82.8 0.0 copy-start.1
  82.8 0.2 pad_maximum_fusion.w_pair_ref
  83.0 0.0 copy-start.7
  83.0 0.7 copy-done.7
  83.7 0.1 copy.24.pair_ref
  83.8 3.8 %all-to-all-done.3.parts_ref = bf16[8,16,256]{2,1,0:T(8,128)(2,1)S(1)} async-done(((bf16[8,16,256]{2,1,0:T(8,128)(2,1)}), bf16[8,16,256]{2,1,0:T(8,128)(2,1)S(1)}, u32[]{:S(2)}, u32[]{:S(2)}) %all-to-all-start.3) | async-done | bytes 65568 | tf_op jit(solution)/shard_map/all_to_all | solution.py:431
  87.7 0.0 copy-done.1
  87.7 1.0 shard_map.118
  88.7 3.3 %all-to-all-start.4 = ((f32[4,24,384]{2,1,0:T(8,128)}), f32[4,24,384]{2,1,0:T(8,128)S(1)}, u32[]{:S(2)}, u32[]{:S(2)}) async-start(f32[4,24,384]{2,1,0:T(8,128)} %shard_map.118), calls=%async_computation.4 | async-start | bytes 294912 | tf_op jit(solution)/shard_map/all_to_all | solution.py:431
  92.1 7.3 %all-to-all-done.4.terms_ref = f32[4,24,384]{2,1,0:T(8,128)S(1)} async-done(((f32[4,24,384]{2,1,0:T(8,128)}), f32[4,24,384]{2,1,0:T(8,128)S(1)}, u32[]{:S(2)}, u32[]{:S(2)}) %all-to-all-start.4) | async-done | bytes 147488 | tf_op jit(solution)/shard_map/all_to_all | solution.py:431
  99.4 0.8 shard_map.119
  100.2 10.5 %all-to-all-start.5 = ((f32[128,1,96]{2,1,0:T(1,128)}), f32[128,1,96]{2,1,0:T(1,128)S(1)}, u32[]{:S(2)}, u32[]{:S(2)}) async-start(f32[128,1,96]{2,1,0:T(1,128)} %bitcast.11), calls=%async_computation.5 | async-start | bytes 131072 | tf_op jit(solution)/shard_map/all_to_all | solution.py:431
  110.7 0.1 slice_bitcast_fusion.1
  110.8 10.7 %all-to-all-done.5 = f32[128,1,96]{2,1,0:T(1,128)S(1)} async-done(((f32[128,1,96]{2,1,0:T(1,128)}), f32[128,1,96]{2,1,0:T(1,128)S(1)}, u32[]{:S(2)}, u32[]{:S(2)}) %all-to-all-start.5) | async-done | bytes 49184 | tf_op jit(solution)/shard_map/all_to_all | solution.py:431
  121.5 0.1 copy.26
  121.6 0.0 copy-done
  121.6 0.8 fusion.1
  (6 shorter events, 0.1 us)
Async XLA Ops:
  0.6 121.0 %copy-start = (bf16[18,32]{1,0:T(8,128)(2,1)S(1)}, bf16[18,32]{1,0:T(8,128)(2,1)}, u32[]{:S(2)}) copy-start(bf16[18,32]{1,0:T(8,128)(2,1)} %param.18) | copy-start | bytes 3460
  3.3 14.4 %copy-start.4 = (bf16[80,2048]{1,0:T(8,128)(2,1)S(1)}, bf16[80,2048]{1,0:T(8,128)(2,1)}, u32[]{:S(2)}) copy-start(bf16[80,2048]{1,0:T(8,128)(2,1)} %get-tuple-element.10.made_ref.stem_ref) | copy-start | bytes 983044
  3.3 34.9 %all-to-all-start = ((bf16[128,16,128]{2,1,0:T(8,128)(2,1)}), bf16[128,16,128]{2,1,0:T(8,128)(2,1)S(1)}, u32[]{:S(2)}, u32[]{:S(2)}) async-start(bf16[128,16,128]{2,1,0:T(8,128)(2,1)} %get-tuple-element.11), calls=%async_computation | async-start | bytes 1048576 | tf_op jit(solution)/shard_map/all_to_all | solution.py:431
  38.2 13.1 %copy-start.5 = (bf16[1536,192]{0,1:T(8,128)(2,1)S(1)}, bf16[1536,192]{0,1:T(8,128)(2,1)}, u32[]{:S(2)}) copy-start(bf16[1536,192]{0,1:T(8,128)(2,1)} %param.15) | copy-start | bytes 1769476
  41.5 19.0 %all-to-all-start.1 = ((bf16[32,4,384]{2,1,0:T(4,128)(2,1)}), bf16[32,4,384]{2,1,0:T(4,128)(2,1)S(1)}, u32[]{:S(2)}, u32[]{:S(2)}) async-start(bf16[32,4,384]{2,1,0:T(4,128)(2,1)} %shard_map.115), calls=%async_computation.1 | async-start | bytes 196608 | tf_op jit(solution)/shard_map/all_to_all | solution.py:431
  60.7 1.0 copy-start.2
  60.7 1.1 copy-start.3
  62.9 9.5 %copy-start.6 = (bf16[2,1536,32]{1,2,0:T(8,128)(2,1)S(1)}, bf16[2,1536,32]{1,2,0:T(8,128)(2,1)}, u32[]{:S(2)}) copy-start(bf16[2,1536,32]{1,2,0:T(8,128)(2,1)} %param.17) | copy-start | bytes 589828
  62.9 5.7 %collective-permute-start = (bf16[32,128]{1,0:T(8,128)(2,1)S(1)}, bf16[32,128]{1,0:T(8,128)(2,1)S(1)}, u32[]{:S(2)}, u32[]{:S(2)}) collective-permute-start(bf16[32,128]{1,0:T(8,128)(2,1)S(1)} %get-tuple-element.12), channel_id=1, source_target_pairs={{0,8},{8,0},{1,9},{9,1},{2,10},{10,2},{3,11},{11,3},{4,12},{12,4},... | collective-permute-start | bytes 24584 | tf_op jit(solution)/shard_map/ppermute | solution.py:454
  65.1 10.9 %all-to-all-start.2 = ((bf16[16,40,128]{2,1,0:T(8,128)(2,1)}), bf16[16,40,128]{2,1,0:T(8,128)(2,1)S(1)}, u32[]{:S(2)}, u32[]{:S(2)}) async-start(bf16[16,40,128]{2,1,0:T(8,128)(2,1)} %get-tuple-element.13), calls=%async_computation.2 | async-start | bytes 327680 | tf_op jit(solution)/shard_map/all_to_all | solution.py:431
  68.7 6.3 %collective-permute-start.1 = (bf16[64,128]{1,0:T(8,128)(2,1)S(1)}, bf16[64,128]{1,0:T(8,128)(2,1)S(1)}, u32[]{:S(2)}, u32[]{:S(2)}) collective-permute-start(bf16[64,128]{1,0:T(8,128)(2,1)S(1)} %pad_maximum_fusion.2), channel_id=1, source_target_pairs={{0,16},{16,0},{1,17},{17,1},{2,18},{18,2},{3,19},{19,3},{4,20},{20... | collective-permute-start | bytes 49160 | tf_op jit(solution)/shard_map/ppermute | solution.py:454
  77.1 10.5 %all-to-all-start.3 = ((bf16[8,16,256]{2,1,0:T(8,128)(2,1)}), bf16[8,16,256]{2,1,0:T(8,128)(2,1)S(1)}, u32[]{:S(2)}, u32[]{:S(2)}) async-start(bf16[8,16,256]{2,1,0:T(8,128)(2,1)} %shard_map.117), calls=%async_computation.3 | async-start | bytes 131072 | tf_op jit(solution)/shard_map/all_to_all | solution.py:431
  82.8 4.9 %copy-start.1 = (bf16[192,1536]{1,0:T(8,128)(2,1)S(1)}, bf16[192,1536]{1,0:T(8,128)(2,1)}, u32[]{:S(2)}) copy-start(bf16[192,1536]{1,0:T(8,128)(2,1)} %w_out_ref.1) | copy-start | bytes 1769476
  83.0 0.7 copy-start.7
  88.7 10.7 %all-to-all-start.4 = ((f32[4,24,384]{2,1,0:T(8,128)}), f32[4,24,384]{2,1,0:T(8,128)S(1)}, u32[]{:S(2)}, u32[]{:S(2)}) async-start(f32[4,24,384]{2,1,0:T(8,128)} %shard_map.118), calls=%async_computation.4 | async-start | bytes 294912 | tf_op jit(solution)/shard_map/all_to_all | solution.py:431
  100.2 21.3 %all-to-all-start.5 = ((f32[128,1,96]{2,1,0:T(1,128)}), f32[128,1,96]{2,1,0:T(1,128)S(1)}, u32[]{:S(2)}, u32[]{:S(2)}) async-start(f32[128,1,96]{2,1,0:T(1,128)} %bitcast.11), calls=%async_computation.5 | async-start | bytes 131072 | tf_op jit(solution)/shard_map/all_to_all | solution.py:431

commit v14 on v13

--- a/solution.py
+++ b/solution.py
@@ -21,6 +21,10 @@
 SHARE = ("zl", "xl", "core")
 SPREAD = ("xh", "xl", "core")
 LINE = ("zl", "y")
+MIDDLE_SEQ = 32
+MIDDLE_LINE = 4
+MIDDLE_SPREAD = 2
+MIDDLE_PAIR = 1
 N_SEQ = math.prod(SIZES[name] for name in SEQ)
 N_SHARE = math.prod(SIZES[name] for name in SHARE)
 N_PAIR = SIZES["pair"]
@@ -168,8 +172,8 @@
 
 
 def border_codes(held_ref, right):
-    before = held_ref[jnp.maximum(right - 1, 0)].astype(jnp.float32)
-    after = held_ref[jnp.minimum(right, N_SEQ - 1)].astype(jnp.float32)
+    before = held_ref[jnp.maximum(right - 1, 0) ^ MIDDLE_SEQ].astype(jnp.float32)
+    after = held_ref[jnp.minimum(right, N_SEQ - 1) ^ MIDDLE_SEQ].astype(jnp.float32)
     before = jnp.where(right > 0, before, 0.0)
     after = jnp.where(right < N_SEQ, after, 0.0)
     lane = lax.broadcasted_iota(jnp.int32, (1, HQK), 1)
@@ -185,7 +189,7 @@
 def conv_kernel(place_ref, section_ref, held_ref, stem_ref, out_ref, weights, edges, wide, act, best):
     count, rows, _ = held_ref.shape
     for source in range(count):
-        block = held_ref[source].astype(jnp.float32)
+        block = held_ref[source ^ MIDDLE_SEQ].astype(jnp.float32)
         weights[source * (rows - 1) : (source + 1) * (rows - 1), :] = block[: rows - 1, :]
     first = ((place_ref[0] & (N_SEQ // 2 - 1)) // RUN) * RUN
     for run in range(2):
@@ -336,7 +340,7 @@
     groups, count, _ = out_ref.shape
     for index in range(groups):
         place = ((place_ref[0] >> 1) ^ (index // 2)) * 2 + index % 2
-        out_ref[place] = mixed[index * count : (index + 1) * count, :]
+        out_ref[place ^ MIDDLE_SPREAD] = mixed[index * count : (index + 1) * count, :]
 
 
 def attention(place, query, kv):
@@ -367,8 +371,8 @@
         axis=0,
     )
     for c in range(N_PAIR):
-        out_ref[c, :count, :] = term[:, c * width : (c + 1) * width]
-        out_ref[c, count:, :] = tail
+        out_ref[c ^ MIDDLE_PAIR, :count, :] = term[:, c * width : (c + 1) * width]
+        out_ref[c ^ MIDDLE_PAIR, count:, :] = tail
 
 
 def combine(parts, w_out):
@@ -400,7 +404,10 @@
     rows_ref[...] = rows
     mine = pair_ref[0].astype(jnp.float32)
     factors = jnp.broadcast_to(rows[:1], (mine.shape[0], rows.shape[1]))
-    every_ref[...] = jnp.concatenate([factors, mine], axis=1)
+    every = jnp.concatenate([factors, mine], axis=1)
+    for at in range(0, every.shape[0], MIDDLE_SEQ):
+        to = at ^ MIDDLE_SEQ
+        every_ref[to : to + MIDDLE_SEQ, :] = every[at : at + MIDDLE_SEQ, :]
 
 
 def close(terms, own, trunk, w_pair, pair_in):
@@ -427,8 +434,11 @@
     return jnp.dot(onehot, pair_bias, preferred_element_type=jnp.float32)
 
 
-def exchange(blocks, axes):
-    return lax.all_to_all(blocks, axes, split_axis=0, concat_axis=0, tiled=True)
+def exchange(blocks, axes, middle=0):
+    order = [index ^ middle for index in range(blocks.shape[0])]
+    return lax.all_to_all(
+        blocks, axes, split_axis=0, concat_axis=0, tiled=True, axis_index_groups=[order] if middle else None
+    )
 
 
 def on_device(tokens, w_stem, w_conv, w_query, w_key, w_value, w_out, w_pair, pair_bias, pair_in):
@@ -438,7 +448,7 @@
     taps, width = w_conv.shape
     share = width // N_SHARE
     blocks, made = start(w_conv, w_stem, tokens)
-    held = exchange(blocks, SEQ)
+    held = exchange(blocks, SEQ, MIDDLE_SEQ)
 
     section = stem(made, w_stem.shape[1]).astype(jnp.bfloat16)
     sections = lax.all_gather(section, SHARE, axis=0, tiled=False)
@@ -453,10 +463,10 @@
     for name in reversed(SPREAD[:-1]):
         other = lax.ppermute(query, name, [(0, 1), (1, 0)])
         query = jnp.concatenate([query, other], axis=0)
-    kv = exchange(kv, LINE)
+    kv = exchange(kv, LINE, MIDDLE_LINE)
     spread = lax.axis_index(SPREAD).astype(jnp.int32)[None]
-    parts = exchange(attention(spread, query, kv), SPREAD)
-    terms = exchange(combine(parts, w_out), ("pair",))
+    parts = exchange(attention(spread, query, kv), SPREAD, MIDDLE_SPREAD)
+    terms = exchange(combine(parts, w_out), ("pair",), MIDDLE_PAIR)
 
     own = lax.dynamic_slice_in_dim(trunk, pair_place * width, width, 1)
     factors = jnp.concatenate([w_pair[0], w_pair[1]], axis=1)
@@ -464,7 +474,8 @@
     channels = pair_in.shape[2]
     mine = pair_in[0].astype(jnp.float32)
     rows = rows[:1]
-    every = exchange(every[:, None], SEQ)[:, 0]
+    every = exchange(every[:, None], SEQ, MIDDLE_SEQ)[:, 0]
+    every = every.reshape(-1, 2, MIDDLE_SEQ, every.shape[1])[:, ::-1].reshape(every.shape)
     mirror = every[:, 2 * channels :]
 
     cols = jnp.arange(N_SEQ, dtype=jnp.int32)

time: 123 us -> 119 us (0.967)
  waiting for transfers between devices: 38.6 us -> 26.1 us
  starting transfers between devices: 53.2 us -> 61.4 us
    all_to_all x6, waiting for transfers between devices: 36.6 us -> 24.5 us  [exchange(): lax.all_to_all(blocks, axes, split_axis=0, concat_axis=0, tiled=True, axi...]
    all_to_all x6, starting transfers between devices: 47.2 us -> 55.3 us  [exchange(): lax.all_to_all(blocks, axes, split_axis=0, concat_axis=0, tiled=True, axi...]
  transfers between devices with their start and end apart: 8 -> 8, of which waited for: 7 -> 5; matrix products, arithmetic and copies ran while one was open for 1% -> 1% of each run, Pallas kernels for 1% -> 1%
where the time goes in v14:
time: 119 us; the launch traced here: 118 us
  starting transfers between devices  61.4 us (52%)
  waiting for transfers between devices  26.1 us (22%)
  blocking collectives  13.9 us (12%)
  Pallas kernels  11.5 us (10%)
  local copies, waits for them, and re-layouts  3.29 us (3%)
    all_to_all x6, starting transfers between devices, exchange(): lax.all_to_all(blocks, axes, split_axis=0, concat_axis=0, tiled=True, axi...  55.3 us
    all_to_all x6, waiting for transfers between devices, exchange(): lax.all_to_all(blocks, axes, split_axis=0, concat_axis=0, tiled=True, axi...  24.5 us
    all_gather x1, blocking collectives, on_device(): sections = lax.all_gather(section, SHARE, axis=0, tiled=False)  13.9 us
    ppermute x2, starting transfers between devices, on_device(): other = lax.ppermute(query, name, [(0, 1), (1, 0)])  6.07 us
    pallas_call x1, Pallas kernels, conv(): pl.pallas_call(conv_kernel, out_shape=jax.ShapeDtypeStruct((windows * N_P...  3.25 us
    pallas_call x1, Pallas kernels, start(): pl.pallas_call(start_kernel, out_shape=(jax.ShapeDtypeStruct((N_SEQ, taps...  2.69 us
  transfers between devices with their start and end apart: 8, of which 5 were waited for; matrix products, arithmetic and copies ran while one was open for 1% of the time, Pallas kernels for 1%

profile of v14, /device:TPU:1, one launch (start us, length us, event | category | flops | bytes accessed | tf_op | source)
XLA Modules:
  0.0 118.2 jit_solution(1494293456564264977)
XLA Ops:
  0.6 0.0 copy-start
  0.6 2.7 %shard_map.113 = (bf16[128,16,128]{2,1,0:T(8,128)(2,1)}, bf16[80,2048]{1,0:T(8,128)(2,1)}) custom-call(bf16[30,384]{1,0:T(8,128)(2,1)} %weight_ref.1, bf16[60,768]{1,0:T(8,128)(2,1)} %stem_ref.1, s32[16,128]{1,0:T(8,128)} %bitcast.34, s32[1,2048]{1,0:T(1,128)} %bitcast.35), custom_call_target="tpu_custom_call" | custom-call | tf_op jit(solution)/shard_map/pallas_call | solution.py:156
  3.3 0.0 copy-start.4
  3.4 15.3 %all-to-all-start = ((bf16[128,16,128]{2,1,0:T(8,128)(2,1)}), bf16[128,16,128]{2,1,0:T(8,128)(2,1)S(1)}, u32[]{:S(2)}, u32[]{:S(2)}) async-start(bf16[128,16,128]{2,1,0:T(8,128)(2,1)} %get-tuple-element.11), calls=%async_computation | async-start | bytes 1048576 | tf_op jit(solution)/shard_map/all_to_all | solution.py:439
  18.7 0.0 copy-done.4
  18.7 1.5 %shard_map.114 = f32[32,768]{1,0:T(8,128)S(1)} custom-call(bf16[80,2048]{1,0:T(8,128)(2,1)S(1)} %copy-done.4), custom_call_target="tpu_custom_call" | custom-call | flops 201326592 | bytes 200000 | tf_op jit(solution)/shard_map/pallas_call | solution.py:84
  20.3 13.9 %all-gather = bf16[256,768]{1,0:T(8,128)(2,1)S(1)} all-gather(bf16[32,768]{1,0:T(8,128)(2,1)S(1)} %convert_element_type.132), channel_id=2, replica_groups=mesh['zl'=2,'y'=8,'xh'=2,'xl'=2,'core'=2,'pair'=4] {'zl','xl','core'}, dimensions={0}, use_global_device_ids=true | all-gather | bytes 442368 | tf_op jit(solution)/shard_map/all_gather | solution.py:454
  34.2 0.0 all-to-all-done.held_ref
  34.2 0.0 copy-start.5
  34.2 3.2 %shard_map.115 = bf16[32,4,384]{2,1,0:T(4,128)(2,1)} custom-call(s32[1]{0:T(128)} %bitcast.2.place_ref, bf16[8,32,768]{2,1,0:T(8,128)(2,1)S(1)} %bitcast.28, bf16[128,16,128]{2,1,0:T(8,128)(2,1)S(1)} %all-to-all-done.held_ref, bf16[80,2048]{1,0:T(8,128)(2,1)S(1)} %copy-done.4), custom_call_target="tpu_custom_call" | custom-call | tf_op jit(solution)/shard_map/pallas_call | solution.py:254
  37.4 11.0 %all-to-all-start.1 = ((bf16[32,4,384]{2,1,0:T(4,128)(2,1)}), bf16[32,4,384]{2,1,0:T(4,128)(2,1)S(1)}, u32[]{:S(2)}, u32[]{:S(2)}) async-start(bf16[32,4,384]{2,1,0:T(4,128)(2,1)} %shard_map.115), calls=%async_computation.1 | async-start | bytes 196608 | tf_op jit(solution)/shard_map/all_to_all | solution.py:439
  48.4 0.0 copy-done.5
  48.4 0.3 copy.27.w_value_ref
  48.7 8.8 %all-to-all-done.1 = bf16[32,4,384]{2,1,0:T(4,128)(2,1)S(1)} async-done(((bf16[32,4,384]{2,1,0:T(4,128)(2,1)}), bf16[32,4,384]{2,1,0:T(4,128)(2,1)S(1)}, u32[]{:S(2)}, u32[]{:S(2)}) %all-to-all-start.1) | async-done | bytes 98336 | tf_op jit(solution)/shard_map/all_to_all | solution.py:439
  57.5 0.2 reshape.78
  57.7 0.0 copy-start.2
  57.8 0.0 copy-start.3
  57.8 0.2 copy.41
  58.0 0.3 reshape.79.trunk_ref
  58.3 0.5 copy-done.2
  58.7 0.1 copy-done.3
  58.9 1.1 shard_map.116
  59.9 0.0 copy-start.6
  60.0 2.2 %collective-permute-start = (bf16[32,128]{1,0:T(8,128)(2,1)S(1)}, bf16[32,128]{1,0:T(8,128)(2,1)S(1)}, u32[]{:S(2)}, u32[]{:S(2)}) collective-permute-start(bf16[32,128]{1,0:T(8,128)(2,1)S(1)} %get-tuple-element.12), channel_id=1, source_target_pairs={{0,8},{8,0},{1,9},{9,1},{2,10},{10,2},{3,11},{11,3},{4,12},{12,4},... | collective-permute-start | bytes 24584 | tf_op jit(solution)/shard_map/ppermute | solution.py:464
  62.1 7.0 %all-to-all-start.2 = ((bf16[16,40,128]{2,1,0:T(8,128)(2,1)}), bf16[16,40,128]{2,1,0:T(8,128)(2,1)S(1)}, u32[]{:S(2)}, u32[]{:S(2)}) async-start(bf16[16,40,128]{2,1,0:T(8,128)(2,1)} %get-tuple-element.13), calls=%async_computation.2 | async-start | bytes 327680 | tf_op jit(solution)/shard_map/all_to_all | solution.py:439
  69.1 0.0 collective-permute-done
  69.1 3.9 %collective-permute-start.1 = (bf16[64,128]{1,0:T(8,128)(2,1)S(1)}, bf16[64,128]{1,0:T(8,128)(2,1)S(1)}, u32[]{:S(2)}, u32[]{:S(2)}) collective-permute-start(bf16[64,128]{1,0:T(8,128)(2,1)S(1)} %pad_maximum_fusion.2), channel_id=1, source_target_pairs={{0,16},{16,0},{1,17},{17,1},{2,18},{18,2},{3,19},{19,3},{4,20},{20... | collective-permute-start | bytes 49160 | tf_op jit(solution)/shard_map/ppermute | solution.py:464
  73.0 0.0 copy-done.6
  73.1 0.2 copy.35
  73.3 0.2 copy.36
  73.5 1.6 %collective-permute-done.1 = bf16[64,128]{1,0:T(8,128)(2,1)S(1)} collective-permute-done((bf16[64,128]{1,0:T(8,128)(2,1)S(1)}, bf16[64,128]{1,0:T(8,128)(2,1)S(1)}, u32[]{:S(2)}, u32[]{:S(2)}) %collective-permute-start.1) | collective-permute-done | bytes 16416 | tf_op jit(solution)/shard_map/ppermute | solution.py:464
  75.1 0.0 all-to-all-done.2.kv_ref
  75.1 1.1 shard_map.117
  76.2 6.1 %all-to-all-start.3 = ((bf16[8,16,256]{2,1,0:T(8,128)(2,1)}), bf16[8,16,256]{2,1,0:T(8,128)(2,1)S(1)}, u32[]{:S(2)}, u32[]{:S(2)}) async-start(bf16[8,16,256]{2,1,0:T(8,128)(2,1)} %shard_map.117), calls=%async_computation.3 | async-start | bytes 131072 | tf_op jit(solution)/shard_map/all_to_all | solution.py:439
  82.3 0.0 copy-start.1
  82.3 0.2 pad_maximum_fusion.w_pair_ref
  82.5 0.0 copy-start.7
  82.5 0.7 copy-done.7
  83.2 0.1 copy.30.pair_ref
  83.3 3.1 %all-to-all-done.3.parts_ref = bf16[8,16,256]{2,1,0:T(8,128)(2,1)S(1)} async-done(((bf16[8,16,256]{2,1,0:T(8,128)(2,1)}), bf16[8,16,256]{2,1,0:T(8,128)(2,1)S(1)}, u32[]{:S(2)}, u32[]{:S(2)}) %all-to-all-start.3) | async-done | bytes 65568 | tf_op jit(solution)/shard_map/all_to_all | solution.py:439
  86.5 0.0 copy-done.1
  86.5 1.0 shard_map.118
  87.5 4.6 %all-to-all-start.4 = ((f32[4,24,384]{2,1,0:T(8,128)}), f32[4,24,384]{2,1,0:T(8,128)S(1)}, u32[]{:S(2)}, u32[]{:S(2)}) async-start(f32[4,24,384]{2,1,0:T(8,128)} %shard_map.118), calls=%async_computation.4 | async-start | bytes 294912 | tf_op jit(solution)/shard_map/all_to_all | solution.py:439
  92.1 6.9 %all-to-all-done.4.terms_ref = f32[4,24,384]{2,1,0:T(8,128)S(1)} async-done(((f32[4,24,384]{2,1,0:T(8,128)}), f32[4,24,384]{2,1,0:T(8,128)S(1)}, u32[]{:S(2)}, u32[]{:S(2)}) %all-to-all-start.4) | async-done | bytes 147488 | tf_op jit(solution)/shard_map/all_to_all | solution.py:439
  99.0 0.8 shard_map.119
  99.8 11.4 %all-to-all-start.5 = ((f32[128,1,96]{2,1,0:T(1,128)}), f32[128,1,96]{2,1,0:T(1,128)S(1)}, u32[]{:S(2)}, u32[]{:S(2)}) async-start(f32[128,1,96]{2,1,0:T(1,128)} %bitcast.11), calls=%async_computation.5 | async-start | bytes 131072 | tf_op jit(solution)/shard_map/all_to_all | solution.py:439
  111.3 0.1 slice_bitcast_fusion.1
  111.3 5.7 %all-to-all-done.5 = f32[128,1,96]{2,1,0:T(1,128)S(1)} async-done(((f32[128,1,96]{2,1,0:T(1,128)}), f32[128,1,96]{2,1,0:T(1,128)S(1)}, u32[]{:S(2)}, u32[]{:S(2)}) %all-to-all-start.5) | async-done | bytes 49184 | tf_op jit(solution)/shard_map/all_to_all | solution.py:439
  117.0 0.1 fusion.22
  117.1 0.1 copy.37
  117.2 0.1 copy.38
  117.2 0.1 copy.39
  117.3 0.0 copy-done
  117.3 0.8 fusion.1
  (7 shorter events, 0.1 us)
Async XLA Ops:
  0.6 116.7 %copy-start = (bf16[18,32]{1,0:T(8,128)(2,1)S(1)}, bf16[18,32]{1,0:T(8,128)(2,1)}, u32[]{:S(2)}) copy-start(bf16[18,32]{1,0:T(8,128)(2,1)} %param.18) | copy-start | bytes 3460
  3.3 15.3 %copy-start.4 = (bf16[80,2048]{1,0:T(8,128)(2,1)S(1)}, bf16[80,2048]{1,0:T(8,128)(2,1)}, u32[]{:S(2)}) copy-start(bf16[80,2048]{1,0:T(8,128)(2,1)} %get-tuple-element.10.made_ref.stem_ref) | copy-start | bytes 983044
  3.4 30.8 %all-to-all-start = ((bf16[128,16,128]{2,1,0:T(8,128)(2,1)}), bf16[128,16,128]{2,1,0:T(8,128)(2,1)S(1)}, u32[]{:S(2)}, u32[]{:S(2)}) async-start(bf16[128,16,128]{2,1,0:T(8,128)(2,1)} %get-tuple-element.11), calls=%async_computation | async-start | bytes 1048576 | tf_op jit(solution)/shard_map/all_to_all | solution.py:439
  34.2 14.2 %copy-start.5 = (bf16[1536,192]{0,1:T(8,128)(2,1)S(1)}, bf16[1536,192]{0,1:T(8,128)(2,1)}, u32[]{:S(2)}) copy-start(bf16[1536,192]{0,1:T(8,128)(2,1)} %param.15) | copy-start | bytes 1769476
  37.4 20.1 %all-to-all-start.1 = ((bf16[32,4,384]{2,1,0:T(4,128)(2,1)}), bf16[32,4,384]{2,1,0:T(4,128)(2,1)S(1)}, u32[]{:S(2)}, u32[]{:S(2)}) async-start(bf16[32,4,384]{2,1,0:T(4,128)(2,1)} %shard_map.115), calls=%async_computation.1 | async-start | bytes 196608 | tf_op jit(solution)/shard_map/all_to_all | solution.py:439
  57.7 1.0 copy-start.2
  57.8 1.1 copy-start.3
  59.9 13.1 %copy-start.6 = (bf16[2,1536,32]{1,2,0:T(8,128)(2,1)S(1)}, bf16[2,1536,32]{1,2,0:T(8,128)(2,1)}, u32[]{:S(2)}) copy-start(bf16[2,1536,32]{1,2,0:T(8,128)(2,1)} %param.17) | copy-start | bytes 589828
  60.0 9.2 %collective-permute-start = (bf16[32,128]{1,0:T(8,128)(2,1)S(1)}, bf16[32,128]{1,0:T(8,128)(2,1)S(1)}, u32[]{:S(2)}, u32[]{:S(2)}) collective-permute-start(bf16[32,128]{1,0:T(8,128)(2,1)S(1)} %get-tuple-element.12), channel_id=1, source_target_pairs={{0,8},{8,0},{1,9},{9,1},{2,10},{10,2},{3,11},{11,3},{4,12},{12,4},... | collective-permute-start | bytes 24584 | tf_op jit(solution)/shard_map/ppermute | solution.py:464
  62.1 13.0 %all-to-all-start.2 = ((bf16[16,40,128]{2,1,0:T(8,128)(2,1)}), bf16[16,40,128]{2,1,0:T(8,128)(2,1)S(1)}, u32[]{:S(2)}, u32[]{:S(2)}) async-start(bf16[16,40,128]{2,1,0:T(8,128)(2,1)} %get-tuple-element.13), calls=%async_computation.2 | async-start | bytes 327680 | tf_op jit(solution)/shard_map/all_to_all | solution.py:439
  69.1 6.0 %collective-permute-start.1 = (bf16[64,128]{1,0:T(8,128)(2,1)S(1)}, bf16[64,128]{1,0:T(8,128)(2,1)S(1)}, u32[]{:S(2)}, u32[]{:S(2)}) collective-permute-start(bf16[64,128]{1,0:T(8,128)(2,1)S(1)} %pad_maximum_fusion.2), channel_id=1, source_target_pairs={{0,16},{16,0},{1,17},{17,1},{2,18},{18,2},{3,19},{19,3},{4,20},{20... | collective-permute-start | bytes 49160 | tf_op jit(solution)/shard_map/ppermute | solution.py:464
  76.2 10.3 %all-to-all-start.3 = ((bf16[8,16,256]{2,1,0:T(8,128)(2,1)}), bf16[8,16,256]{2,1,0:T(8,128)(2,1)S(1)}, u32[]{:S(2)}, u32[]{:S(2)}) async-start(bf16[8,16,256]{2,1,0:T(8,128)(2,1)} %shard_map.117), calls=%async_computation.3 | async-start | bytes 131072 | tf_op jit(solution)/shard_map/all_to_all | solution.py:439
  82.3 4.2 %copy-start.1 = (bf16[192,1536]{1,0:T(8,128)(2,1)S(1)}, bf16[192,1536]{1,0:T(8,128)(2,1)}, u32[]{:S(2)}) copy-start(bf16[192,1536]{1,0:T(8,128)(2,1)} %w_out_ref.1) | copy-start | bytes 1769476
  82.5 0.7 copy-start.7
  87.5 11.5 %all-to-all-start.4 = ((f32[4,24,384]{2,1,0:T(8,128)}), f32[4,24,384]{2,1,0:T(8,128)S(1)}, u32[]{:S(2)}, u32[]{:S(2)}) async-start(f32[4,24,384]{2,1,0:T(8,128)} %shard_map.118), calls=%async_computation.4 | async-start | bytes 294912 | tf_op jit(solution)/shard_map/all_to_all | solution.py:439
  99.8 17.2 %all-to-all-start.5 = ((f32[128,1,96]{2,1,0:T(1,128)}), f32[128,1,96]{2,1,0:T(1,128)S(1)}, u32[]{:S(2)}, u32[]{:S(2)}) async-start(f32[128,1,96]{2,1,0:T(1,128)} %bitcast.11), calls=%async_computation.5 | async-start | bytes 131072 | tf_op jit(solution)/shard_map/all_to_all | solution.py:439

commit v15 on v14

--- a/solution.py
+++ b/solution.py
@@ -21,7 +21,8 @@
 SHARE = ("zl", "xl", "core")
 SPREAD = ("xh", "xl", "core")
 LINE = ("zl", "y")
-MIDDLE_SEQ = 32
+MIDDLE_SEQ = 32 + 2
+MIDDLE_SHARE = 16 + 1
 MIDDLE_LINE = 4
 MIDDLE_SPREAD = 2
 MIDDLE_PAIR = 1
@@ -147,7 +148,7 @@
             if name in SHARE:
                 index, base = index + base * (at % SIZES[name]), base * SIZES[name]
             at = at // SIZES[name]
-        out_ref[place] = blocks[index]
+        out_ref[place ^ MIDDLE_SEQ] = blocks[index]
 
 
 def start(weight, stem_weight, tokens):
@@ -246,7 +247,7 @@
     for window in range(windows):
         block = flat[window // 2 * 4 : window // 2 * 4 + 4, :].astype(jnp.bfloat16)
         for index in range(N_PAIR):
-            out_ref[window * N_PAIR + index] = block
+            out_ref[(window * N_PAIR + index) ^ MIDDLE_SHARE] = block
 
 
 def conv(place, section, held, stem_weight, columns):
@@ -404,10 +405,7 @@
     rows_ref[...] = rows
     mine = pair_ref[0].astype(jnp.float32)
     factors = jnp.broadcast_to(rows[:1], (mine.shape[0], rows.shape[1]))
-    every = jnp.concatenate([factors, mine], axis=1)
-    for at in range(0, every.shape[0], MIDDLE_SEQ):
-        to = at ^ MIDDLE_SEQ
-        every_ref[to : to + MIDDLE_SEQ, :] = every[at : at + MIDDLE_SEQ, :]
+    every_ref[...] = jnp.concatenate([factors, mine], axis=1)
 
 
 def close(terms, own, trunk, w_pair, pair_in):
@@ -441,6 +439,10 @@
     )
 
 
+def from_middle(rows):
+    return rows.reshape(2, 2, 8, 2, 2, -1)[:, ::-1, :, ::-1].reshape(rows.shape)
+
+
 def on_device(tokens, w_stem, w_conv, w_query, w_key, w_value, w_out, w_pair, pair_bias, pair_in):
     place = lax.axis_index(SEQ)
     pair_place = lax.axis_index("pair")
@@ -453,8 +455,11 @@
     section = stem(made, w_stem.shape[1]).astype(jnp.bfloat16)
     sections = lax.all_gather(section, SHARE, axis=0, tiled=False)
 
-    parts = exchange(conv(place.astype(jnp.int32)[None], sections, held, made, share), SHARE + ("pair",))
+    parts = exchange(
+        conv(place.astype(jnp.int32)[None], sections, held, made, share), SHARE + ("pair",), MIDDLE_SHARE
+    )
     count = ROWS // 2
+    parts = parts.reshape(2, N_SHARE // 2, 2, 2, 2 * count, share)[::-1, :, :, ::-1]
     trunk = parts.reshape(N_SHARE, N_PAIR, 2 * count, share).transpose(2, 1, 0, 3)
     trunk = trunk.reshape(2 * count, N_PAIR * width)
 
@@ -470,12 +475,12 @@
 
     own = lax.dynamic_slice_in_dim(trunk, pair_place * width, width, 1)
     factors = jnp.concatenate([w_pair[0], w_pair[1]], axis=1)
-    seq_out, rows, every = close(terms, own, trunk, factors, pair_in)
+    seq_out, rows, every = close(terms, own, trunk, factors, from_middle(pair_in[0])[None])
     channels = pair_in.shape[2]
     mine = pair_in[0].astype(jnp.float32)
     rows = rows[:1]
     every = exchange(every[:, None], SEQ, MIDDLE_SEQ)[:, 0]
-    every = every.reshape(-1, 2, MIDDLE_SEQ, every.shape[1])[:, ::-1].reshape(every.shape)
+    every = from_middle(every)
     mirror = every[:, 2 * channels :]
 
     cols = jnp.arange(N_SEQ, dtype=jnp.int32)

time: 119 us -> 120 us (level)
  starting transfers between devices: 61.4 us -> 65.5 us
  waiting for transfers between devices: 26.1 us -> 22.1 us
    all_to_all x6, waiting for transfers between devices: 24.5 us -> 21.5 us  [exchange(): lax.all_to_all(blocks, axes, split_axis=0, concat_axis=0, tiled=True, axi...]
    ppermute x2, starting transfers between devices: 6.07 us -> 8.38 us  [on_device(): other = lax.ppermute(query, name, [(0, 1), (1, 0)])]
    all_to_all x6, starting transfers between devices: 55.3 us -> 57.2 us  [exchange(): lax.all_to_all(blocks, axes, split_axis=0, concat_axis=0, tiled=True, axi...]
where the time goes in v15:
time: 120 us; the launch traced here: 119 us
  starting transfers between devices  65.5 us (55%)
  waiting for transfers between devices  22.1 us (18%)
  blocking collectives  14.6 us (12%)
  Pallas kernels  11.5 us (10%)
  local copies, waits for them, and re-layouts  3.35 us (3%)
    all_to_all x6, starting transfers between devices, exchange(): lax.all_to_all(blocks, axes, split_axis=0, concat_axis=0, tiled=True, axi...  57.2 us
    all_to_all x6, waiting for transfers between devices, exchange(): lax.all_to_all(blocks, axes, split_axis=0, concat_axis=0, tiled=True, axi...  21.5 us
    all_gather x1, blocking collectives, on_device(): sections = lax.all_gather(section, SHARE, axis=0, tiled=False)  14.6 us
    ppermute x2, starting transfers between devices, on_device(): other = lax.ppermute(query, name, [(0, 1), (1, 0)])  8.38 us
    pallas_call x1, Pallas kernels, conv(): pl.pallas_call(conv_kernel, out_shape=jax.ShapeDtypeStruct((windows * N_P...  3.24 us
    pallas_call x1, Pallas kernels, start(): pl.pallas_call(start_kernel, out_shape=(jax.ShapeDtypeStruct((N_SEQ, taps...  2.69 us
  transfers between devices with their start and end apart: 8, of which 5 were waited for; matrix products, arithmetic and copies ran while one was open for 1% of the time, Pallas kernels for 1%

profile of v15, /device:TPU:1, one launch (start us, length us, event | category | flops | bytes accessed | tf_op | source)
XLA Modules:
  0.0 119.0 jit_solution(8793634449927839856)
XLA Ops:
  0.6 0.0 copy-start
  0.6 2.7 %shard_map.113 = (bf16[128,16,128]{2,1,0:T(8,128)(2,1)}, bf16[80,2048]{1,0:T(8,128)(2,1)}) custom-call(bf16[30,384]{1,0:T(8,128)(2,1)} %weight_ref.1, bf16[60,768]{1,0:T(8,128)(2,1)} %stem_ref.1, s32[16,128]{1,0:T(8,128)} %bitcast.38, s32[1,2048]{1,0:T(1,128)} %bitcast.39), custom_call_target="tpu_custom_call" | custom-call | tf_op jit(solution)/shard_map/pallas_call | solution.py:157
  3.3 0.0 copy-start.4
  3.4 16.2 %all-to-all-start = ((bf16[128,16,128]{2,1,0:T(8,128)(2,1)}), bf16[128,16,128]{2,1,0:T(8,128)(2,1)S(1)}, u32[]{:S(2)}, u32[]{:S(2)}) async-start(bf16[128,16,128]{2,1,0:T(8,128)(2,1)} %get-tuple-element.11), calls=%async_computation | async-start | bytes 1048576 | tf_op jit(solution)/shard_map/all_to_all | solution.py:437
  19.6 0.0 copy-done.4
  19.6 1.5 %shard_map.114 = f32[32,768]{1,0:T(8,128)S(1)} custom-call(bf16[80,2048]{1,0:T(8,128)(2,1)S(1)} %copy-done.4), custom_call_target="tpu_custom_call" | custom-call | flops 201326592 | bytes 200000 | tf_op jit(solution)/shard_map/pallas_call | solution.py:85
  21.2 14.6 %all-gather = bf16[256,768]{1,0:T(8,128)(2,1)S(1)} all-gather(bf16[32,768]{1,0:T(8,128)(2,1)S(1)} %convert_element_type.132), channel_id=2, replica_groups=mesh['zl'=2,'y'=8,'xh'=2,'xl'=2,'core'=2,'pair'=4] {'zl','xl','core'}, dimensions={0}, use_global_device_ids=true | all-gather | bytes 442368 | tf_op jit(solution)/shard_map/all_gather | solution.py:456
  35.7 0.0 all-to-all-done.held_ref
  35.7 0.0 copy-start.5
  35.7 3.2 %shard_map.115 = bf16[32,4,384]{2,1,0:T(4,128)(2,1)} custom-call(s32[1]{0:T(128)} %bitcast.2.place_ref, bf16[8,32,768]{2,1,0:T(8,128)(2,1)S(1)} %bitcast.30, bf16[128,16,128]{2,1,0:T(8,128)(2,1)S(1)} %all-to-all-done.held_ref, bf16[80,2048]{1,0:T(8,128)(2,1)S(1)} %copy-done.4), custom_call_target="tpu_custom_call" | custom-call | tf_op jit(solution)/shard_map/pallas_call | solution.py:255
  39.0 11.0 %all-to-all-start.1 = ((bf16[32,4,384]{2,1,0:T(4,128)(2,1)}), bf16[32,4,384]{2,1,0:T(4,128)(2,1)S(1)}, u32[]{:S(2)}, u32[]{:S(2)}) async-start(bf16[32,4,384]{2,1,0:T(4,128)(2,1)} %shard_map.115), calls=%async_computation.1 | async-start | bytes 196608 | tf_op jit(solution)/shard_map/all_to_all | solution.py:437
  50.0 0.0 copy-done.5
  50.0 0.3 copy.27.w_value_ref
  50.3 6.1 %all-to-all-done.1 = bf16[32,4,384]{2,1,0:T(4,128)(2,1)S(1)} async-done(((bf16[32,4,384]{2,1,0:T(4,128)(2,1)}), bf16[32,4,384]{2,1,0:T(4,128)(2,1)S(1)}, u32[]{:S(2)}, u32[]{:S(2)}) %all-to-all-start.1) | async-done | bytes 98336 | tf_op jit(solution)/shard_map/all_to_all | solution.py:437
  56.4 0.2 reshape.81
  56.7 0.0 copy-start.2
  56.7 0.0 copy-start.3
  56.7 0.2 copy.26
  56.9 0.3 reshape.83.trunk_ref
  57.2 0.4 copy-done.2
  57.7 0.1 copy-done.3
  57.8 1.1 shard_map.116
  58.9 0.0 copy-start.6
  58.9 2.5 %collective-permute-start = (bf16[32,128]{1,0:T(8,128)(2,1)S(1)}, bf16[32,128]{1,0:T(8,128)(2,1)S(1)}, u32[]{:S(2)}, u32[]{:S(2)}) collective-permute-start(bf16[32,128]{1,0:T(8,128)(2,1)S(1)} %get-tuple-element.12), channel_id=1, source_target_pairs={{0,8},{8,0},{1,9},{9,1},{2,10},{10,2},{3,11},{11,3},{4,12},{12,4},... | collective-permute-start | bytes 24584 | tf_op jit(solution)/shard_map/ppermute | solution.py:469
  61.4 7.6 %all-to-all-start.2 = ((bf16[16,40,128]{2,1,0:T(8,128)(2,1)}), bf16[16,40,128]{2,1,0:T(8,128)(2,1)S(1)}, u32[]{:S(2)}, u32[]{:S(2)}) async-start(bf16[16,40,128]{2,1,0:T(8,128)(2,1)} %get-tuple-element.13), calls=%async_computation.2 | async-start | bytes 327680 | tf_op jit(solution)/shard_map/all_to_all | solution.py:437
  69.0 0.0 collective-permute-done
  69.0 5.9 %collective-permute-start.1 = (bf16[64,128]{1,0:T(8,128)(2,1)S(1)}, bf16[64,128]{1,0:T(8,128)(2,1)S(1)}, u32[]{:S(2)}, u32[]{:S(2)}) collective-permute-start(bf16[64,128]{1,0:T(8,128)(2,1)S(1)} %pad_maximum_fusion.2), channel_id=1, source_target_pairs={{0,16},{16,0},{1,17},{17,1},{2,18},{18,2},{3,19},{19,3},{4,20},{20... | collective-permute-start | bytes 49160 | tf_op jit(solution)/shard_map/ppermute | solution.py:469
  74.9 0.0 copy-done.6
  74.9 0.2 copy.35
  75.2 0.2 copy.36
  75.4 0.6 collective-permute-done.1
  76.0 0.0 all-to-all-done.2.kv_ref
  76.0 1.1 shard_map.117
  77.1 7.2 %all-to-all-start.3 = ((bf16[8,16,256]{2,1,0:T(8,128)(2,1)}), bf16[8,16,256]{2,1,0:T(8,128)(2,1)S(1)}, u32[]{:S(2)}, u32[]{:S(2)}) async-start(bf16[8,16,256]{2,1,0:T(8,128)(2,1)} %shard_map.117), calls=%async_computation.3 | async-start | bytes 131072 | tf_op jit(solution)/shard_map/all_to_all | solution.py:437
  84.3 0.0 copy-start.1
  84.3 0.2 pad_maximum_fusion.w_pair_ref
  84.5 0.0 copy-start.7
  84.6 0.7 copy-done.7
  85.2 0.1 copy.30
  85.4 3.1 %all-to-all-done.3.parts_ref = bf16[8,16,256]{2,1,0:T(8,128)(2,1)S(1)} async-done(((bf16[8,16,256]{2,1,0:T(8,128)(2,1)}), bf16[8,16,256]{2,1,0:T(8,128)(2,1)S(1)}, u32[]{:S(2)}, u32[]{:S(2)}) %all-to-all-start.3) | async-done | bytes 65568 | tf_op jit(solution)/shard_map/all_to_all | solution.py:437
  88.5 0.0 copy-done.1
  88.5 1.0 shard_map.118
  89.5 4.6 %all-to-all-start.4 = ((f32[4,24,384]{2,1,0:T(8,128)}), f32[4,24,384]{2,1,0:T(8,128)S(1)}, u32[]{:S(2)}, u32[]{:S(2)}) async-start(f32[4,24,384]{2,1,0:T(8,128)} %shard_map.118), calls=%async_computation.4 | async-start | bytes 294912 | tf_op jit(solution)/shard_map/all_to_all | solution.py:437
  94.2 7.0 %all-to-all-done.4.terms_ref = f32[4,24,384]{2,1,0:T(8,128)S(1)} async-done(((f32[4,24,384]{2,1,0:T(8,128)}), f32[4,24,384]{2,1,0:T(8,128)S(1)}, u32[]{:S(2)}, u32[]{:S(2)}) %all-to-all-start.4) | async-done | bytes 147488 | tf_op jit(solution)/shard_map/all_to_all | solution.py:437
  101.2 0.8 shard_map.119
  102.0 10.5 %all-to-all-start.5 = ((f32[128,1,96]{2,1,0:T(1,128)}), f32[128,1,96]{2,1,0:T(1,128)S(1)}, u32[]{:S(2)}, u32[]{:S(2)}) async-start(f32[128,1,96]{2,1,0:T(1,128)} %bitcast.14), calls=%async_computation.5 | async-start | bytes 131072 | tf_op jit(solution)/shard_map/all_to_all | solution.py:437
  112.5 0.1 slice_bitcast_fusion.1
  112.5 5.3 %all-to-all-done.5 = f32[128,1,96]{2,1,0:T(1,128)S(1)} async-done(((f32[128,1,96]{2,1,0:T(1,128)}), f32[128,1,96]{2,1,0:T(1,128)S(1)}, u32[]{:S(2)}, u32[]{:S(2)}) %all-to-all-start.5) | async-done | bytes 49184 | tf_op jit(solution)/shard_map/all_to_all | solution.py:437
  117.8 0.1 fusion.22
  117.9 0.1 copy.37
  118.0 0.1 copy.38
  118.1 0.1 copy.39
  118.1 0.0 copy-done
  118.2 0.8 fusion.1
  (9 shorter events, 0.1 us)
Async XLA Ops:
  0.6 117.5 %copy-start = (bf16[18,32]{1,0:T(8,128)(2,1)S(1)}, bf16[18,32]{1,0:T(8,128)(2,1)}, u32[]{:S(2)}) copy-start(bf16[18,32]{1,0:T(8,128)(2,1)} %param.18) | copy-start | bytes 3460
  3.3 16.3 %copy-start.4 = (bf16[80,2048]{1,0:T(8,128)(2,1)S(1)}, bf16[80,2048]{1,0:T(8,128)(2,1)}, u32[]{:S(2)}) copy-start(bf16[80,2048]{1,0:T(8,128)(2,1)} %get-tuple-element.10.made_ref.stem_ref) | copy-start | bytes 983044
  3.4 32.4 %all-to-all-start = ((bf16[128,16,128]{2,1,0:T(8,128)(2,1)}), bf16[128,16,128]{2,1,0:T(8,128)(2,1)S(1)}, u32[]{:S(2)}, u32[]{:S(2)}) async-start(bf16[128,16,128]{2,1,0:T(8,128)(2,1)} %get-tuple-element.11), calls=%async_computation | async-start | bytes 1048576 | tf_op jit(solution)/shard_map/all_to_all | solution.py:437
  35.7 14.3 %copy-start.5 = (bf16[1536,192]{0,1:T(8,128)(2,1)S(1)}, bf16[1536,192]{0,1:T(8,128)(2,1)}, u32[]{:S(2)}) copy-start(bf16[1536,192]{0,1:T(8,128)(2,1)} %param.15) | copy-start | bytes 1769476
  39.0 17.4 %all-to-all-start.1 = ((bf16[32,4,384]{2,1,0:T(4,128)(2,1)}), bf16[32,4,384]{2,1,0:T(4,128)(2,1)S(1)}, u32[]{:S(2)}, u32[]{:S(2)}) async-start(bf16[32,4,384]{2,1,0:T(4,128)(2,1)} %shard_map.115), calls=%async_computation.1 | async-start | bytes 196608 | tf_op jit(solution)/shard_map/all_to_all | solution.py:437
  56.7 1.0 copy-start.2
  56.7 1.1 copy-start.3
  58.9 16.0 %copy-start.6 = (bf16[2,1536,32]{1,2,0:T(8,128)(2,1)S(1)}, bf16[2,1536,32]{1,2,0:T(8,128)(2,1)}, u32[]{:S(2)}) copy-start(bf16[2,1536,32]{1,2,0:T(8,128)(2,1)} %param.17) | copy-start | bytes 589828
  58.9 10.1 %collective-permute-start = (bf16[32,128]{1,0:T(8,128)(2,1)S(1)}, bf16[32,128]{1,0:T(8,128)(2,1)S(1)}, u32[]{:S(2)}, u32[]{:S(2)}) collective-permute-start(bf16[32,128]{1,0:T(8,128)(2,1)S(1)} %get-tuple-element.12), channel_id=1, source_target_pairs={{0,8},{8,0},{1,9},{9,1},{2,10},{10,2},{3,11},{11,3},{4,12},{12,4},... | collective-permute-start | bytes 24584 | tf_op jit(solution)/shard_map/ppermute | solution.py:469
  61.4 14.6 %all-to-all-start.2 = ((bf16[16,40,128]{2,1,0:T(8,128)(2,1)}), bf16[16,40,128]{2,1,0:T(8,128)(2,1)S(1)}, u32[]{:S(2)}, u32[]{:S(2)}) async-start(bf16[16,40,128]{2,1,0:T(8,128)(2,1)} %get-tuple-element.13), calls=%async_computation.2 | async-start | bytes 327680 | tf_op jit(solution)/shard_map/all_to_all | solution.py:437
  69.0 7.0 %collective-permute-start.1 = (bf16[64,128]{1,0:T(8,128)(2,1)S(1)}, bf16[64,128]{1,0:T(8,128)(2,1)S(1)}, u32[]{:S(2)}, u32[]{:S(2)}) collective-permute-start(bf16[64,128]{1,0:T(8,128)(2,1)S(1)} %pad_maximum_fusion.2), channel_id=1, source_target_pairs={{0,16},{16,0},{1,17},{17,1},{2,18},{18,2},{3,19},{19,3},{4,20},{20... | collective-permute-start | bytes 49160 | tf_op jit(solution)/shard_map/ppermute | solution.py:469
  77.1 11.4 %all-to-all-start.3 = ((bf16[8,16,256]{2,1,0:T(8,128)(2,1)}), bf16[8,16,256]{2,1,0:T(8,128)(2,1)S(1)}, u32[]{:S(2)}, u32[]{:S(2)}) async-start(bf16[8,16,256]{2,1,0:T(8,128)(2,1)} %shard_map.117), calls=%async_computation.3 | async-start | bytes 131072 | tf_op jit(solution)/shard_map/all_to_all | solution.py:437
  84.3 4.2 %copy-start.1 = (bf16[192,1536]{1,0:T(8,128)(2,1)S(1)}, bf16[192,1536]{1,0:T(8,128)(2,1)}, u32[]{:S(2)}) copy-start(bf16[192,1536]{1,0:T(8,128)(2,1)} %w_out_ref.1) | copy-start | bytes 1769476
  84.5 0.7 copy-start.7
  89.5 11.6 %all-to-all-start.4 = ((f32[4,24,384]{2,1,0:T(8,128)}), f32[4,24,384]{2,1,0:T(8,128)S(1)}, u32[]{:S(2)}, u32[]{:S(2)}) async-start(f32[4,24,384]{2,1,0:T(8,128)} %shard_map.118), calls=%async_computation.4 | async-start | bytes 294912 | tf_op jit(solution)/shard_map/all_to_all | solution.py:437
  102.0 15.8 %all-to-all-start.5 = ((f32[128,1,96]{2,1,0:T(1,128)}), f32[128,1,96]{2,1,0:T(1,128)S(1)}, u32[]{:S(2)}, u32[]{:S(2)}) async-start(f32[128,1,96]{2,1,0:T(1,128)} %bitcast.14), calls=%async_computation.5 | async-start | bytes 131072 | tf_op jit(solution)/shard_map/all_to_all | solution.py:437

commit v16 on v14

--- a/solution.py
+++ b/solution.py
@@ -22,6 +22,7 @@
 SPREAD = ("xh", "xl", "core")
 LINE = ("zl", "y")
 MIDDLE_SEQ = 32
+MIDDLE_SHARE = 16 + 1
 MIDDLE_LINE = 4
 MIDDLE_SPREAD = 2
 MIDDLE_PAIR = 1
@@ -246,7 +247,7 @@
     for window in range(windows):
         block = flat[window // 2 * 4 : window // 2 * 4 + 4, :].astype(jnp.bfloat16)
         for index in range(N_PAIR):
-            out_ref[window * N_PAIR + index] = block
+            out_ref[(window * N_PAIR + index) ^ MIDDLE_SHARE] = block
 
 
 def conv(place, section, held, stem_weight, columns):
@@ -453,8 +454,11 @@
     section = stem(made, w_stem.shape[1]).astype(jnp.bfloat16)
     sections = lax.all_gather(section, SHARE, axis=0, tiled=False)
 
-    parts = exchange(conv(place.astype(jnp.int32)[None], sections, held, made, share), SHARE + ("pair",))
+    parts = exchange(
+        conv(place.astype(jnp.int32)[None], sections, held, made, share), SHARE + ("pair",), MIDDLE_SHARE
+    )
     count = ROWS // 2
+    parts = parts.reshape(2, N_SHARE // 2, 2, 2, 2 * count, share)[::-1, :, :, ::-1]
     trunk = parts.reshape(N_SHARE, N_PAIR, 2 * count, share).transpose(2, 1, 0, 3)
     trunk = trunk.reshape(2 * count, N_PAIR * width)
 

time: 119 us -> 119 us (level)
  starting transfers between devices: 61.4 us -> 64.5 us
  waiting for transfers between devices: 26.1 us -> 23.5 us
    all_to_all x6, starting transfers between devices: 55.3 us -> 58 us  [exchange(): lax.all_to_all(blocks, axes, split_axis=0, concat_axis=0, tiled=True, axi...]
    all_to_all x6, waiting for transfers between devices: 24.5 us -> 21.9 us  [exchange(): lax.all_to_all(blocks, axes, split_axis=0, concat_axis=0, tiled=True, axi...]
where the time goes in v16:
time: 119 us
  starting transfers between devices  64.5 us (54%)
  waiting for transfers between devices  23.5 us (20%)
  blocking collectives  13.9 us (12%)
  Pallas kernels  11.5 us (10%)
  local copies, waits for them, and re-layouts  3.31 us (3%)
    all_to_all x6, starting transfers between devices, exchange(): lax.all_to_all(blocks, axes, split_axis=0, concat_axis=0, tiled=True, axi...  58 us
    all_to_all x6, waiting for transfers between devices, exchange(): lax.all_to_all(blocks, axes, split_axis=0, concat_axis=0, tiled=True, axi...  21.9 us
    all_gather x1, blocking collectives, on_device(): sections = lax.all_gather(section, SHARE, axis=0, tiled=False)  13.9 us
    ppermute x2, starting transfers between devices, on_device(): other = lax.ppermute(query, name, [(0, 1), (1, 0)])  6.44 us
    pallas_call x1, Pallas kernels, conv(): pl.pallas_call(conv_kernel, out_shape=jax.ShapeDtypeStruct((windows * N_P...  3.25 us
    pallas_call x1, Pallas kernels, start(): pl.pallas_call(start_kernel, out_shape=(jax.ShapeDtypeStruct((N_SEQ, taps...  2.69 us
  transfers between devices with their start and end apart: 8, of which 5 were waited for; matrix products, arithmetic and copies ran while one was open for 1% of the time, Pallas kernels for 1%

profile of v16, /device:TPU:1, one launch (start us, length us, event | category | flops | bytes accessed | tf_op | source)
XLA Modules:
  0.0 118.6 jit_solution(15083573138179876542)
XLA Ops:
  0.6 0.0 copy-start
  0.6 2.7 %shard_map.113 = (bf16[128,16,128]{2,1,0:T(8,128)(2,1)}, bf16[80,2048]{1,0:T(8,128)(2,1)}) custom-call(bf16[30,384]{1,0:T(8,128)(2,1)} %weight_ref.1, bf16[60,768]{1,0:T(8,128)(2,1)} %stem_ref.1, s32[16,128]{1,0:T(8,128)} %bitcast.34, s32[1,2048]{1,0:T(1,128)} %bitcast.35), custom_call_target="tpu_custom_call" | custom-call | tf_op jit(solution)/shard_map/pallas_call | solution.py:157
  3.3 0.0 copy-start.4
  3.4 15.3 %all-to-all-start = ((bf16[128,16,128]{2,1,0:T(8,128)(2,1)}), bf16[128,16,128]{2,1,0:T(8,128)(2,1)S(1)}, u32[]{:S(2)}, u32[]{:S(2)}) async-start(bf16[128,16,128]{2,1,0:T(8,128)(2,1)} %get-tuple-element.11), calls=%async_computation | async-start | bytes 1048576 | tf_op jit(solution)/shard_map/all_to_all | solution.py:440
  18.7 0.0 copy-done.4
  18.7 1.5 %shard_map.114 = f32[32,768]{1,0:T(8,128)S(1)} custom-call(bf16[80,2048]{1,0:T(8,128)(2,1)S(1)} %copy-done.4), custom_call_target="tpu_custom_call" | custom-call | flops 201326592 | bytes 200000 | tf_op jit(solution)/shard_map/pallas_call | solution.py:85
  20.3 13.9 %all-gather = bf16[256,768]{1,0:T(8,128)(2,1)S(1)} all-gather(bf16[32,768]{1,0:T(8,128)(2,1)S(1)} %convert_element_type.132), channel_id=2, replica_groups=mesh['zl'=2,'y'=8,'xh'=2,'xl'=2,'core'=2,'pair'=4] {'zl','xl','core'}, dimensions={0}, use_global_device_ids=true | all-gather | bytes 442368 | tf_op jit(solution)/shard_map/all_gather | solution.py:455
  34.2 0.0 all-to-all-done.held_ref
  34.2 0.0 copy-start.5
  34.2 3.2 %shard_map.115 = bf16[32,4,384]{2,1,0:T(4,128)(2,1)} custom-call(s32[1]{0:T(128)} %bitcast.2.place_ref, bf16[8,32,768]{2,1,0:T(8,128)(2,1)S(1)} %bitcast.28, bf16[128,16,128]{2,1,0:T(8,128)(2,1)S(1)} %all-to-all-done.held_ref, bf16[80,2048]{1,0:T(8,128)(2,1)S(1)} %copy-done.4), custom_call_target="tpu_custom_call" | custom-call | tf_op jit(solution)/shard_map/pallas_call | solution.py:255
  37.4 13.5 %all-to-all-start.1 = ((bf16[32,4,384]{2,1,0:T(4,128)(2,1)}), bf16[32,4,384]{2,1,0:T(4,128)(2,1)S(1)}, u32[]{:S(2)}, u32[]{:S(2)}) async-start(bf16[32,4,384]{2,1,0:T(4,128)(2,1)} %shard_map.115), calls=%async_computation.1 | async-start | bytes 196608 | tf_op jit(solution)/shard_map/all_to_all | solution.py:440
  50.9 0.0 copy-done.5
  50.9 0.3 copy.27.w_value_ref
  51.2 6.1 %all-to-all-done.1 = bf16[32,4,384]{2,1,0:T(4,128)(2,1)S(1)} async-done(((bf16[32,4,384]{2,1,0:T(4,128)(2,1)}), bf16[32,4,384]{2,1,0:T(4,128)(2,1)S(1)}, u32[]{:S(2)}, u32[]{:S(2)}) %all-to-all-start.1) | async-done | bytes 98336 | tf_op jit(solution)/shard_map/all_to_all | solution.py:440
  57.3 0.2 reshape.81
  57.5 0.0 copy-start.2
  57.6 0.0 copy-start.3
  57.6 0.2 copy.26
  57.8 0.3 reshape.83.trunk_ref
  58.1 0.4 copy-done.2
  58.5 0.1 copy-done.3
  58.7 1.1 shard_map.116
  59.7 0.0 copy-start.6
  59.7 2.5 %collective-permute-start = (bf16[32,128]{1,0:T(8,128)(2,1)S(1)}, bf16[32,128]{1,0:T(8,128)(2,1)S(1)}, u32[]{:S(2)}, u32[]{:S(2)}) collective-permute-start(bf16[32,128]{1,0:T(8,128)(2,1)S(1)} %get-tuple-element.12), channel_id=1, source_target_pairs={{0,8},{8,0},{1,9},{9,1},{2,10},{10,2},{3,11},{11,3},{4,12},{12,4},... | collective-permute-start | bytes 24584 | tf_op jit(solution)/shard_map/ppermute | solution.py:468
  62.3 7.6 %all-to-all-start.2 = ((bf16[16,40,128]{2,1,0:T(8,128)(2,1)}), bf16[16,40,128]{2,1,0:T(8,128)(2,1)S(1)}, u32[]{:S(2)}, u32[]{:S(2)}) async-start(bf16[16,40,128]{2,1,0:T(8,128)(2,1)} %get-tuple-element.13), calls=%async_computation.2 | async-start | bytes 327680 | tf_op jit(solution)/shard_map/all_to_all | solution.py:440
  69.9 0.0 collective-permute-done
  69.9 3.9 %collective-permute-start.1 = (bf16[64,128]{1,0:T(8,128)(2,1)S(1)}, bf16[64,128]{1,0:T(8,128)(2,1)S(1)}, u32[]{:S(2)}, u32[]{:S(2)}) collective-permute-start(bf16[64,128]{1,0:T(8,128)(2,1)S(1)} %pad_maximum_fusion.2), channel_id=1, source_target_pairs={{0,16},{16,0},{1,17},{17,1},{2,18},{18,2},{3,19},{19,3},{4,20},{20... | collective-permute-start | bytes 49160 | tf_op jit(solution)/shard_map/ppermute | solution.py:468
  73.8 0.0 copy-done.6
  73.9 0.2 copy.35
  74.1 0.2 copy.36
  74.3 1.6 %collective-permute-done.1 = bf16[64,128]{1,0:T(8,128)(2,1)S(1)} collective-permute-done((bf16[64,128]{1,0:T(8,128)(2,1)S(1)}, bf16[64,128]{1,0:T(8,128)(2,1)S(1)}, u32[]{:S(2)}, u32[]{:S(2)}) %collective-permute-start.1) | collective-permute-done | bytes 16416 | tf_op jit(solution)/shard_map/ppermute | solution.py:468
  75.9 0.0 all-to-all-done.2.kv_ref
  75.9 1.1 shard_map.117
  77.0 6.6 %all-to-all-start.3 = ((bf16[8,16,256]{2,1,0:T(8,128)(2,1)}), bf16[8,16,256]{2,1,0:T(8,128)(2,1)S(1)}, u32[]{:S(2)}, u32[]{:S(2)}) async-start(bf16[8,16,256]{2,1,0:T(8,128)(2,1)} %shard_map.117), calls=%async_computation.3 | async-start | bytes 131072 | tf_op jit(solution)/shard_map/all_to_all | solution.py:440
  83.6 0.0 copy-start.1
  83.6 0.2 pad_maximum_fusion.w_pair_ref
  83.8 0.0 copy-start.7
  83.8 0.7 copy-done.7
  84.5 0.1 copy.30.pair_ref
  84.6 3.1 %all-to-all-done.3.parts_ref = bf16[8,16,256]{2,1,0:T(8,128)(2,1)S(1)} async-done(((bf16[8,16,256]{2,1,0:T(8,128)(2,1)}), bf16[8,16,256]{2,1,0:T(8,128)(2,1)S(1)}, u32[]{:S(2)}, u32[]{:S(2)}) %all-to-all-start.3) | async-done | bytes 65568 | tf_op jit(solution)/shard_map/all_to_all | solution.py:440
  87.7 0.0 copy-done.1
  87.8 1.0 shard_map.118
  88.8 4.6 %all-to-all-start.4 = ((f32[4,24,384]{2,1,0:T(8,128)}), f32[4,24,384]{2,1,0:T(8,128)S(1)}, u32[]{:S(2)}, u32[]{:S(2)}) async-start(f32[4,24,384]{2,1,0:T(8,128)} %shard_map.118), calls=%async_computation.4 | async-start | bytes 294912 | tf_op jit(solution)/shard_map/all_to_all | solution.py:440
  93.4 7.0 %all-to-all-done.4.terms_ref = f32[4,24,384]{2,1,0:T(8,128)S(1)} async-done(((f32[4,24,384]{2,1,0:T(8,128)}), f32[4,24,384]{2,1,0:T(8,128)S(1)}, u32[]{:S(2)}, u32[]{:S(2)}) %all-to-all-start.4) | async-done | bytes 147488 | tf_op jit(solution)/shard_map/all_to_all | solution.py:440
  100.4 0.8 shard_map.119
  101.2 10.5 %all-to-all-start.5 = ((f32[128,1,96]{2,1,0:T(1,128)}), f32[128,1,96]{2,1,0:T(1,128)S(1)}, u32[]{:S(2)}, u32[]{:S(2)}) async-start(f32[128,1,96]{2,1,0:T(1,128)} %bitcast.12), calls=%async_computation.5 | async-start | bytes 131072 | tf_op jit(solution)/shard_map/all_to_all | solution.py:440
  111.7 0.1 slice_bitcast_fusion.1
  111.8 5.7 %all-to-all-done.5 = f32[128,1,96]{2,1,0:T(1,128)S(1)} async-done(((f32[128,1,96]{2,1,0:T(1,128)}), f32[128,1,96]{2,1,0:T(1,128)S(1)}, u32[]{:S(2)}, u32[]{:S(2)}) %all-to-all-start.5) | async-done | bytes 49184 | tf_op jit(solution)/shard_map/all_to_all | solution.py:440
  117.4 0.1 fusion.22
  117.5 0.1 copy.37
  117.6 0.1 copy.38
  117.7 0.1 copy.39
  117.8 0.0 copy-done
  117.8 0.8 fusion.1
  (8 shorter events, 0.1 us)
Async XLA Ops:
  0.6 117.1 %copy-start = (bf16[18,32]{1,0:T(8,128)(2,1)S(1)}, bf16[18,32]{1,0:T(8,128)(2,1)}, u32[]{:S(2)}) copy-start(bf16[18,32]{1,0:T(8,128)(2,1)} %param.18) | copy-start | bytes 3460
  3.3 15.3 %copy-start.4 = (bf16[80,2048]{1,0:T(8,128)(2,1)S(1)}, bf16[80,2048]{1,0:T(8,128)(2,1)}, u32[]{:S(2)}) copy-start(bf16[80,2048]{1,0:T(8,128)(2,1)} %get-tuple-element.10.made_ref.stem_ref) | copy-start | bytes 983044
  3.4 30.8 %all-to-all-start = ((bf16[128,16,128]{2,1,0:T(8,128)(2,1)}), bf16[128,16,128]{2,1,0:T(8,128)(2,1)S(1)}, u32[]{:S(2)}, u32[]{:S(2)}) async-start(bf16[128,16,128]{2,1,0:T(8,128)(2,1)} %get-tuple-element.11), calls=%async_computation | async-start | bytes 1048576 | tf_op jit(solution)/shard_map/all_to_all | solution.py:440
  34.2 16.7 %copy-start.5 = (bf16[1536,192]{0,1:T(8,128)(2,1)S(1)}, bf16[1536,192]{0,1:T(8,128)(2,1)}, u32[]{:S(2)}) copy-start(bf16[1536,192]{0,1:T(8,128)(2,1)} %param.15) | copy-start | bytes 1769476
  37.4 19.9 %all-to-all-start.1 = ((bf16[32,4,384]{2,1,0:T(4,128)(2,1)}), bf16[32,4,384]{2,1,0:T(4,128)(2,1)S(1)}, u32[]{:S(2)}, u32[]{:S(2)}) async-start(bf16[32,4,384]{2,1,0:T(4,128)(2,1)} %shard_map.115), calls=%async_computation.1 | async-start | bytes 196608 | tf_op jit(solution)/shard_map/all_to_all | solution.py:440
  57.5 1.0 copy-start.2
  57.6 1.1 copy-start.3
  59.7 14.1 %copy-start.6 = (bf16[2,1536,32]{1,2,0:T(8,128)(2,1)S(1)}, bf16[2,1536,32]{1,2,0:T(8,128)(2,1)}, u32[]{:S(2)}) copy-start(bf16[2,1536,32]{1,2,0:T(8,128)(2,1)} %param.17) | copy-start | bytes 589828
  59.7 10.1 %collective-permute-start = (bf16[32,128]{1,0:T(8,128)(2,1)S(1)}, bf16[32,128]{1,0:T(8,128)(2,1)S(1)}, u32[]{:S(2)}, u32[]{:S(2)}) collective-permute-start(bf16[32,128]{1,0:T(8,128)(2,1)S(1)} %get-tuple-element.12), channel_id=1, source_target_pairs={{0,8},{8,0},{1,9},{9,1},{2,10},{10,2},{3,11},{11,3},{4,12},{12,4},... | collective-permute-start | bytes 24584 | tf_op jit(solution)/shard_map/ppermute | solution.py:468
  62.3 13.6 %all-to-all-start.2 = ((bf16[16,40,128]{2,1,0:T(8,128)(2,1)}), bf16[16,40,128]{2,1,0:T(8,128)(2,1)S(1)}, u32[]{:S(2)}, u32[]{:S(2)}) async-start(bf16[16,40,128]{2,1,0:T(8,128)(2,1)} %get-tuple-element.13), calls=%async_computation.2 | async-start | bytes 327680 | tf_op jit(solution)/shard_map/all_to_all | solution.py:440
  69.9 6.0 %collective-permute-start.1 = (bf16[64,128]{1,0:T(8,128)(2,1)S(1)}, bf16[64,128]{1,0:T(8,128)(2,1)S(1)}, u32[]{:S(2)}, u32[]{:S(2)}) collective-permute-start(bf16[64,128]{1,0:T(8,128)(2,1)S(1)} %pad_maximum_fusion.2), channel_id=1, source_target_pairs={{0,16},{16,0},{1,17},{17,1},{2,18},{18,2},{3,19},{19,3},{4,20},{20... | collective-permute-start | bytes 49160 | tf_op jit(solution)/shard_map/ppermute | solution.py:468
  77.0 10.8 %all-to-all-start.3 = ((bf16[8,16,256]{2,1,0:T(8,128)(2,1)}), bf16[8,16,256]{2,1,0:T(8,128)(2,1)S(1)}, u32[]{:S(2)}, u32[]{:S(2)}) async-start(bf16[8,16,256]{2,1,0:T(8,128)(2,1)} %shard_map.117), calls=%async_computation.3 | async-start | bytes 131072 | tf_op jit(solution)/shard_map/all_to_all | solution.py:440
  83.6 4.2 %copy-start.1 = (bf16[192,1536]{1,0:T(8,128)(2,1)S(1)}, bf16[192,1536]{1,0:T(8,128)(2,1)}, u32[]{:S(2)}) copy-start(bf16[192,1536]{1,0:T(8,128)(2,1)} %w_out_ref.1) | copy-start | bytes 1769476
  83.8 0.7 copy-start.7
  88.8 11.6 %all-to-all-start.4 = ((f32[4,24,384]{2,1,0:T(8,128)}), f32[4,24,384]{2,1,0:T(8,128)S(1)}, u32[]{:S(2)}, u32[]{:S(2)}) async-start(f32[4,24,384]{2,1,0:T(8,128)} %shard_map.118), calls=%async_computation.4 | async-start | bytes 294912 | tf_op jit(solution)/shard_map/all_to_all | solution.py:440
  101.2 16.2 %all-to-all-start.5 = ((f32[128,1,96]{2,1,0:T(1,128)}), f32[128,1,96]{2,1,0:T(1,128)S(1)}, u32[]{:S(2)}, u32[]{:S(2)}) async-start(f32[128,1,96]{2,1,0:T(1,128)} %bitcast.12), calls=%async_computation.5 | async-start | bytes 131072 | tf_op jit(solution)/shard_map/all_to_all | solution.py:440

commit v17 on v14

--- a/solution.py
+++ b/solution.py
@@ -337,9 +337,10 @@
     for index, column in enumerate(split(top) + split(total)):
         mixed = jnp.where(lane == HV + index, column, mixed)
     mixed = mixed.astype(jnp.bfloat16)
+    flips = (0, 2, 1, 3)
     groups, count, _ = out_ref.shape
     for index in range(groups):
-        place = ((place_ref[0] >> 1) ^ (index // 2)) * 2 + index % 2
+        place = ((place_ref[0] >> 1) ^ flips[index // 2]) * 2 + index % 2
         out_ref[place ^ MIDDLE_SPREAD] = mixed[index * count : (index + 1) * count, :]
 
 
@@ -460,7 +461,7 @@
 
     core = lax.axis_index("core").astype(jnp.int32)[None]
     query, kv, trunk = project(core, trunk, w_query, w_key, w_value)
-    for name in reversed(SPREAD[:-1]):
+    for name in SPREAD[:-1]:
         other = lax.ppermute(query, name, [(0, 1), (1, 0)])
         query = jnp.concatenate([query, other], axis=0)
     kv = exchange(kv, LINE, MIDDLE_LINE)
@@ -479,7 +480,7 @@
     mirror = every[:, 2 * channels :]
 
     cols = jnp.arange(N_SEQ, dtype=jnp.int32)
-    bias = distance_bias(place.astype(jnp.int32), cols, pair_bias)
+    bias = lax.optimization_barrier(distance_bias(place.astype(jnp.int32), cols, pair_bias))
     cross = rows[:, :channels] * every[:, channels : 2 * channels]
     cross = cross + every[:, :channels] * rows[:, channels:]
     pair_out = (0.5 * (mine + mirror + cross) + bias).astype(jnp.bfloat16)[None]

time: 119 us -> 118 us (level)
  starting transfers between devices: 61.4 us -> 59.3 us
    all_to_all x6, starting transfers between devices: 55.3 us -> 53.5 us  [exchange(): lax.all_to_all(blocks, axes, split_axis=0, concat_axis=0, tiled=True, axi...]
  transfers between devices with their start and end apart: 8 -> 8, of which waited for: 5 -> 6; matrix products, arithmetic and copies ran while one was open for 1% -> 1% of each run, Pallas kernels for 1% -> 1%
where the time goes in v17:
time: 118 us; the launch traced here: 117 us
  starting transfers between devices  59.3 us (50%)
  waiting for transfers between devices  27.2 us (23%)
  blocking collectives  13.9 us (12%)
  Pallas kernels  11.5 us (10%)
  local copies, waits for them, and re-layouts  3.32 us (3%)
    all_to_all x6, starting transfers between devices, exchange(): lax.all_to_all(blocks, axes, split_axis=0, concat_axis=0, tiled=True, axi...  53.5 us
    all_to_all x6, waiting for transfers between devices, exchange(): lax.all_to_all(blocks, axes, split_axis=0, concat_axis=0, tiled=True, axi...  24.6 us
    all_gather x1, blocking collectives, on_device(): sections = lax.all_gather(section, SHARE, axis=0, tiled=False)  13.9 us
    ppermute x2, starting transfers between devices, on_device(): other = lax.ppermute(query, name, [(0, 1), (1, 0)])  5.81 us
    pallas_call x1, Pallas kernels, conv(): pl.pallas_call(conv_kernel, out_shape=jax.ShapeDtypeStruct((windows * N_P...  3.24 us
    pallas_call x1, Pallas kernels, start(): pl.pallas_call(start_kernel, out_shape=(jax.ShapeDtypeStruct((N_SEQ, taps...  2.69 us
    ppermute x2, waiting for transfers between devices, on_device(): other = lax.ppermute(query, name, [(0, 1), (1, 0)])  2.61 us
    unnamed x23, local copies, waits for them, and re-layouts  2.37 us
  transfers between devices with their start and end apart: 8, of which 6 were waited for; matrix products, arithmetic and copies ran while one was open for 1% of the time, Pallas kernels for 1%

profile of v17, /device:TPU:1, one launch (start us, length us, event | category | flops | bytes accessed | tf_op | source)
XLA Modules:
  0.0 117.2 jit_solution(17567181940484356005)
XLA Ops:
  0.6 0.0 copy-start
  0.6 2.7 %shard_map.113 = (bf16[128,16,128]{2,1,0:T(8,128)(2,1)}, bf16[80,2048]{1,0:T(8,128)(2,1)}) custom-call(bf16[30,384]{1,0:T(8,128)(2,1)} %weight_ref.1, bf16[60,768]{1,0:T(8,128)(2,1)} %stem_ref.1, s32[16,128]{1,0:T(8,128)} %bitcast.34, s32[1,2048]{1,0:T(1,128)} %bitcast.35), custom_call_target="tpu_custom_call" | custom-call | tf_op jit(solution)/shard_map/pallas_call | solution.py:156
  3.3 0.0 copy-start.4
  3.4 15.3 %all-to-all-start = ((bf16[128,16,128]{2,1,0:T(8,128)(2,1)}), bf16[128,16,128]{2,1,0:T(8,128)(2,1)S(1)}, u32[]{:S(2)}, u32[]{:S(2)}) async-start(bf16[128,16,128]{2,1,0:T(8,128)(2,1)} %get-tuple-element.11), calls=%async_computation | async-start | bytes 1048576 | tf_op jit(solution)/shard_map/all_to_all | solution.py:440
  18.7 0.0 copy-done.4
  18.7 1.5 %shard_map.114 = f32[32,768]{1,0:T(8,128)S(1)} custom-call(bf16[80,2048]{1,0:T(8,128)(2,1)S(1)} %copy-done.4), custom_call_target="tpu_custom_call" | custom-call | flops 201326592 | bytes 200000 | tf_op jit(solution)/shard_map/pallas_call | solution.py:84
  20.3 13.9 %all-gather = bf16[256,768]{1,0:T(8,128)(2,1)S(1)} all-gather(bf16[32,768]{1,0:T(8,128)(2,1)S(1)} %convert_element_type.132), channel_id=2, replica_groups=mesh['zl'=2,'y'=8,'xh'=2,'xl'=2,'core'=2,'pair'=4] {'zl','xl','core'}, dimensions={0}, use_global_device_ids=true | all-gather | bytes 442368 | tf_op jit(solution)/shard_map/all_gather | solution.py:455
  34.2 0.0 all-to-all-done.held_ref
  34.2 0.0 copy-start.5
  34.2 3.2 %shard_map.115 = bf16[32,4,384]{2,1,0:T(4,128)(2,1)} custom-call(s32[1]{0:T(128)} %bitcast.2.place_ref, bf16[8,32,768]{2,1,0:T(8,128)(2,1)S(1)} %bitcast.28, bf16[128,16,128]{2,1,0:T(8,128)(2,1)S(1)} %all-to-all-done.held_ref, bf16[80,2048]{1,0:T(8,128)(2,1)S(1)} %copy-done.4), custom_call_target="tpu_custom_call" | custom-call | tf_op jit(solution)/shard_map/pallas_call | solution.py:254
  37.4 11.0 %all-to-all-start.1 = ((bf16[32,4,384]{2,1,0:T(4,128)(2,1)}), bf16[32,4,384]{2,1,0:T(4,128)(2,1)S(1)}, u32[]{:S(2)}, u32[]{:S(2)}) async-start(bf16[32,4,384]{2,1,0:T(4,128)(2,1)} %shard_map.115), calls=%async_computation.1 | async-start | bytes 196608 | tf_op jit(solution)/shard_map/all_to_all | solution.py:440
  48.4 0.0 copy-done.5
  48.4 0.3 copy.27.w_value_ref
  48.7 8.8 %all-to-all-done.1 = bf16[32,4,384]{2,1,0:T(4,128)(2,1)S(1)} async-done(((bf16[32,4,384]{2,1,0:T(4,128)(2,1)}), bf16[32,4,384]{2,1,0:T(4,128)(2,1)S(1)}, u32[]{:S(2)}, u32[]{:S(2)}) %all-to-all-start.1) | async-done | bytes 98336 | tf_op jit(solution)/shard_map/all_to_all | solution.py:440
  57.5 0.2 reshape.78
  57.7 0.0 copy-start.2
  57.8 0.0 copy-start.3
  57.8 0.2 copy.41
  58.0 0.3 reshape.79.trunk_ref
  58.3 0.5 copy-done.2
  58.7 0.1 copy-done.3
  58.9 0.0 copy-start.6
  58.9 1.1 shard_map.116
  60.0 3.9 %collective-permute-start = (bf16[32,128]{1,0:T(8,128)(2,1)S(1)}, bf16[32,128]{1,0:T(8,128)(2,1)S(1)}, u32[]{:S(2)}, u32[]{:S(2)}) collective-permute-start(bf16[32,128]{1,0:T(8,128)(2,1)S(1)} %get-tuple-element.12), channel_id=1, source_target_pairs={{0,16},{16,0},{1,17},{17,1},{2,18},{18,2},{3,19},{19,3},{4,20},{20... | collective-permute-start | bytes 24584 | tf_op jit(solution)/shard_map/ppermute | solution.py:465
  63.8 0.0 copy-done.6
  63.9 0.2 copy.35
  64.1 0.2 copy.36
  64.3 6.8 %all-to-all-start.2 = ((bf16[16,40,128]{2,1,0:T(8,128)(2,1)}), bf16[16,40,128]{2,1,0:T(8,128)(2,1)S(1)}, u32[]{:S(2)}, u32[]{:S(2)}) async-start(bf16[16,40,128]{2,1,0:T(8,128)(2,1)} %get-tuple-element.13), calls=%async_computation.2 | async-start | bytes 327680 | tf_op jit(solution)/shard_map/all_to_all | solution.py:440
  71.1 0.0 collective-permute-done
  71.2 1.9 %collective-permute-start.1 = (bf16[64,128]{1,0:T(8,128)(2,1)S(1)}, bf16[64,128]{1,0:T(8,128)(2,1)S(1)}, u32[]{:S(2)}, u32[]{:S(2)}) collective-permute-start(bf16[64,128]{1,0:T(8,128)(2,1)S(1)} %pad_maximum_fusion.2), channel_id=1, source_target_pairs={{0,8},{8,0},{1,9},{9,1},{2,10},{10,2},{3,11},{11,3},{4,12},{12,4},... | collective-permute-start | bytes 49160 | tf_op jit(solution)/shard_map/ppermute | solution.py:465
  73.1 0.0 copy-start.1
  73.1 0.2 pad_maximum_fusion.w_pair_ref
  73.3 2.6 %collective-permute-done.1 = bf16[64,128]{1,0:T(8,128)(2,1)S(1)} collective-permute-done((bf16[64,128]{1,0:T(8,128)(2,1)S(1)}, bf16[64,128]{1,0:T(8,128)(2,1)S(1)}, u32[]{:S(2)}, u32[]{:S(2)}) %collective-permute-start.1) | collective-permute-done | bytes 16416 | tf_op jit(solution)/shard_map/ppermute | solution.py:465
  75.9 0.1 all-to-all-done.2.kv_ref
  76.0 1.1 shard_map.117
  77.1 4.8 %all-to-all-start.3 = ((bf16[8,16,256]{2,1,0:T(8,128)(2,1)}), bf16[8,16,256]{2,1,0:T(8,128)(2,1)S(1)}, u32[]{:S(2)}, u32[]{:S(2)}) async-start(bf16[8,16,256]{2,1,0:T(8,128)(2,1)} %shard_map.117), calls=%async_computation.3 | async-start | bytes 131072 | tf_op jit(solution)/shard_map/all_to_all | solution.py:440
  81.9 4.2 %all-to-all-done.3.parts_ref = bf16[8,16,256]{2,1,0:T(8,128)(2,1)S(1)} async-done(((bf16[8,16,256]{2,1,0:T(8,128)(2,1)}), bf16[8,16,256]{2,1,0:T(8,128)(2,1)S(1)}, u32[]{:S(2)}, u32[]{:S(2)}) %all-to-all-start.3) | async-done | bytes 65568 | tf_op jit(solution)/shard_map/all_to_all | solution.py:440
  86.0 0.0 copy-done.1
  86.0 1.0 shard_map.118
  87.1 4.3 %all-to-all-start.4 = ((f32[4,24,384]{2,1,0:T(8,128)}), f32[4,24,384]{2,1,0:T(8,128)S(1)}, u32[]{:S(2)}, u32[]{:S(2)}) async-start(f32[4,24,384]{2,1,0:T(8,128)} %shard_map.118), calls=%async_computation.4 | async-start | bytes 294912 | tf_op jit(solution)/shard_map/all_to_all | solution.py:440
  91.4 0.0 copy-done
  91.4 0.2 fusion
  91.6 0.0 copy-start.7
  91.6 0.7 copy-done.7
  92.3 0.1 copy.30.pair_ref
  92.4 5.9 %all-to-all-done.4.terms_ref = f32[4,24,384]{2,1,0:T(8,128)S(1)} async-done(((f32[4,24,384]{2,1,0:T(8,128)}), f32[4,24,384]{2,1,0:T(8,128)S(1)}, u32[]{:S(2)}, u32[]{:S(2)}) %all-to-all-start.4) | async-done | bytes 147488 | tf_op jit(solution)/shard_map/all_to_all | solution.py:440
  98.3 0.8 shard_map.119
  99.1 11.4 %all-to-all-start.5 = ((f32[128,1,96]{2,1,0:T(1,128)}), f32[128,1,96]{2,1,0:T(1,128)S(1)}, u32[]{:S(2)}, u32[]{:S(2)}) async-start(f32[128,1,96]{2,1,0:T(1,128)} %bitcast.11), calls=%async_computation.5 | async-start | bytes 131072 | tf_op jit(solution)/shard_map/all_to_all | solution.py:440
  110.5 0.1 slice_bitcast_fusion.1
  110.6 5.7 %all-to-all-done.5 = f32[128,1,96]{2,1,0:T(1,128)S(1)} async-done(((f32[128,1,96]{2,1,0:T(1,128)}), f32[128,1,96]{2,1,0:T(1,128)S(1)}, u32[]{:S(2)}, u32[]{:S(2)}) %all-to-all-start.5) | async-done | bytes 49184 | tf_op jit(solution)/shard_map/all_to_all | solution.py:440
  116.2 0.1 fusion.24
  116.3 0.1 copy.37
  116.4 0.1 copy.38
  116.5 0.1 copy.39
  116.5 0.7 fusion.6
  (7 shorter events, 0.1 us)
Async XLA Ops:
  0.6 90.7 %copy-start = (bf16[18,32]{1,0:T(8,128)(2,1)S(1)}, bf16[18,32]{1,0:T(8,128)(2,1)}, u32[]{:S(2)}) copy-start(bf16[18,32]{1,0:T(8,128)(2,1)} %param.18) | copy-start | bytes 3460
  3.3 15.3 %copy-start.4 = (bf16[80,2048]{1,0:T(8,128)(2,1)S(1)}, bf16[80,2048]{1,0:T(8,128)(2,1)}, u32[]{:S(2)}) copy-start(bf16[80,2048]{1,0:T(8,128)(2,1)} %get-tuple-element.10.made_ref.stem_ref) | copy-start | bytes 983044
  3.4 30.8 %all-to-all-start = ((bf16[128,16,128]{2,1,0:T(8,128)(2,1)}), bf16[128,16,128]{2,1,0:T(8,128)(2,1)S(1)}, u32[]{:S(2)}, u32[]{:S(2)}) async-start(bf16[128,16,128]{2,1,0:T(8,128)(2,1)} %get-tuple-element.11), calls=%async_computation | async-start | bytes 1048576 | tf_op jit(solution)/shard_map/all_to_all | solution.py:440
  34.2 14.2 %copy-start.5 = (bf16[1536,192]{0,1:T(8,128)(2,1)S(1)}, bf16[1536,192]{0,1:T(8,128)(2,1)}, u32[]{:S(2)}) copy-start(bf16[1536,192]{0,1:T(8,128)(2,1)} %param.15) | copy-start | bytes 1769476
  37.4 20.1 %all-to-all-start.1 = ((bf16[32,4,384]{2,1,0:T(4,128)(2,1)}), bf16[32,4,384]{2,1,0:T(4,128)(2,1)S(1)}, u32[]{:S(2)}, u32[]{:S(2)}) async-start(bf16[32,4,384]{2,1,0:T(4,128)(2,1)} %shard_map.115), calls=%async_computation.1 | async-start | bytes 196608 | tf_op jit(solution)/shard_map/all_to_all | solution.py:440
  57.7 1.0 copy-start.2
  57.8 1.1 copy-start.3
  58.9 5.0 %copy-start.6 = (bf16[2,1536,32]{1,2,0:T(8,128)(2,1)S(1)}, bf16[2,1536,32]{1,2,0:T(8,128)(2,1)}, u32[]{:S(2)}) copy-start(bf16[2,1536,32]{1,2,0:T(8,128)(2,1)} %param.17) | copy-start | bytes 589828
  60.0 11.2 %collective-permute-start = (bf16[32,128]{1,0:T(8,128)(2,1)S(1)}, bf16[32,128]{1,0:T(8,128)(2,1)S(1)}, u32[]{:S(2)}, u32[]{:S(2)}) collective-permute-start(bf16[32,128]{1,0:T(8,128)(2,1)S(1)} %get-tuple-element.12), channel_id=1, source_target_pairs={{0,16},{16,0},{1,17},{17,1},{2,18},{18,2},{3,19},{19,3},{4,20},{20... | collective-permute-start | bytes 24584 | tf_op jit(solution)/shard_map/ppermute | solution.py:465
  64.3 11.7 %all-to-all-start.2 = ((bf16[16,40,128]{2,1,0:T(8,128)(2,1)}), bf16[16,40,128]{2,1,0:T(8,128)(2,1)S(1)}, u32[]{:S(2)}, u32[]{:S(2)}) async-start(bf16[16,40,128]{2,1,0:T(8,128)(2,1)} %get-tuple-element.13), calls=%async_computation.2 | async-start | bytes 327680 | tf_op jit(solution)/shard_map/all_to_all | solution.py:440
  71.2 4.8 %collective-permute-start.1 = (bf16[64,128]{1,0:T(8,128)(2,1)S(1)}, bf16[64,128]{1,0:T(8,128)(2,1)S(1)}, u32[]{:S(2)}, u32[]{:S(2)}) collective-permute-start(bf16[64,128]{1,0:T(8,128)(2,1)S(1)} %pad_maximum_fusion.2), channel_id=1, source_target_pairs={{0,8},{8,0},{1,9},{9,1},{2,10},{10,2},{3,11},{11,3},{4,12},{12,4},... | collective-permute-start | bytes 49160 | tf_op jit(solution)/shard_map/ppermute | solution.py:465
  73.1 12.9 %copy-start.1 = (bf16[192,1536]{1,0:T(8,128)(2,1)S(1)}, bf16[192,1536]{1,0:T(8,128)(2,1)}, u32[]{:S(2)}) copy-start(bf16[192,1536]{1,0:T(8,128)(2,1)} %w_out_ref.1) | copy-start | bytes 1769476
  77.1 8.9 %all-to-all-start.3 = ((bf16[8,16,256]{2,1,0:T(8,128)(2,1)}), bf16[8,16,256]{2,1,0:T(8,128)(2,1)S(1)}, u32[]{:S(2)}, u32[]{:S(2)}) async-start(bf16[8,16,256]{2,1,0:T(8,128)(2,1)} %shard_map.117), calls=%async_computation.3 | async-start | bytes 131072 | tf_op jit(solution)/shard_map/all_to_all | solution.py:440
  87.1 11.2 %all-to-all-start.4 = ((f32[4,24,384]{2,1,0:T(8,128)}), f32[4,24,384]{2,1,0:T(8,128)S(1)}, u32[]{:S(2)}, u32[]{:S(2)}) async-start(f32[4,24,384]{2,1,0:T(8,128)} %shard_map.118), calls=%async_computation.4 | async-start | bytes 294912 | tf_op jit(solution)/shard_map/all_to_all | solution.py:440
  91.6 0.7 copy-start.7
  99.1 17.1 %all-to-all-start.5 = ((f32[128,1,96]{2,1,0:T(1,128)}), f32[128,1,96]{2,1,0:T(1,128)S(1)}, u32[]{:S(2)}, u32[]{:S(2)}) async-start(f32[128,1,96]{2,1,0:T(1,128)} %bitcast.11), calls=%async_computation.5 | async-start | bytes 131072 | tf_op jit(solution)/shard_map/all_to_all | solution.py:440

commit v18 on v17

--- a/solution.py
+++ b/solution.py
@@ -267,17 +267,19 @@
     )(place, section, held, stem_weight)
 
 
-def project_kernel(core_ref, trunk_ref, w_query_ref, w_key_ref, w_value_ref, query_ref, kv_ref, own_ref):
+def project_kernel(core_ref, trunk_ref, weight_ref, query_ref, kv_ref, own_ref):
     trunk = trunk_ref[...]
     first = core_ref[0] == 0
     count = own_ref.shape[0]
     half = count // 2
-    query_ref[...] = jnp.dot(trunk, w_query_ref[...], preferred_element_type=jnp.float32).astype(jnp.bfloat16)
+    query = jnp.dot(trunk, weight_ref[:, :HQK], preferred_element_type=jnp.float32)
+    query_ref[...] = query.astype(jnp.bfloat16)
     wide = trunk.astype(jnp.float32)
     own = jnp.where(first, wide[:count], wide[count:]).astype(jnp.bfloat16)
     own_ref[...] = own
-    key = jnp.dot(own, w_key_ref[...], preferred_element_type=jnp.float32).astype(jnp.bfloat16)
-    value = jnp.dot(own, w_value_ref[...], preferred_element_type=jnp.float32)
+    key = jnp.dot(own, weight_ref[:, HQK : 2 * HQK], preferred_element_type=jnp.float32)
+    key = key.astype(jnp.bfloat16)
+    value = jnp.dot(own, weight_ref[:, 2 * HQK :], preferred_element_type=jnp.float32)
     rest = jnp.pad(value[:, HQK:], ((0, 0), (0, 2 * HQK - HV)))
     rest = (rest[:half] + pltpu.roll(rest[half:], HV - HQK, 1)).astype(jnp.bfloat16)
     value = value[:, :HQK].astype(jnp.bfloat16)
@@ -287,7 +289,7 @@
         kv_ref[index, 2 * count :, :] = rest
 
 
-def project(core, trunk, w_query, w_key, w_value):
+def project(core, trunk, weight):
     count = trunk.shape[0] // 2
     return pl.pallas_call(
         project_kernel,
@@ -296,10 +298,10 @@
             jax.ShapeDtypeStruct((N_LINE, 2 * count + count // 2, HQK), jnp.bfloat16),
             jax.ShapeDtypeStruct((count, trunk.shape[1]), jnp.bfloat16),
         ),
-        in_specs=[pl.BlockSpec(memory_space=pltpu.SMEM)] + whole(4),
+        in_specs=[pl.BlockSpec(memory_space=pltpu.SMEM)] + whole(2),
         out_specs=tuple(whole(3)),
         compiler_params=params(),
-    )(core, trunk, w_query, w_key, w_value)
+    )(core, trunk, weight)
 
 
 def split(x):
@@ -460,7 +462,7 @@
     trunk = trunk.reshape(2 * count, N_PAIR * width)
 
     core = lax.axis_index("core").astype(jnp.int32)[None]
-    query, kv, trunk = project(core, trunk, w_query, w_key, w_value)
+    query, kv, trunk = project(core, trunk, jnp.concatenate([w_query, w_key, w_value], axis=1))
     for name in SPREAD[:-1]:
         other = lax.ppermute(query, name, [(0, 1), (1, 0)])
         query = jnp.concatenate([query, other], axis=0)

time: 118 us -> 119 us (level)
  no operation moved by 1% of the time
where the time goes in v18:
time: 119 us; the launch traced here: 118 us
  starting transfers between devices  59.4 us (50%)
  waiting for transfers between devices  27.9 us (23%)
  blocking collectives  14 us (12%)
  Pallas kernels  11.5 us (10%)
  local copies, waits for them, and re-layouts  3.02 us (3%)
    all_to_all x6, starting transfers between devices, exchange(): lax.all_to_all(blocks, axes, split_axis=0, concat_axis=0, tiled=True, axi...  53.9 us
    all_to_all x6, waiting for transfers between devices, exchange(): lax.all_to_all(blocks, axes, split_axis=0, concat_axis=0, tiled=True, axi...  25.3 us
    all_gather x1, blocking collectives, on_device(): sections = lax.all_gather(section, SHARE, axis=0, tiled=False)  14 us
    ppermute x2, starting transfers between devices, on_device(): other = lax.ppermute(query, name, [(0, 1), (1, 0)])  5.49 us
    pallas_call x1, Pallas kernels, conv(): pl.pallas_call(conv_kernel, out_shape=jax.ShapeDtypeStruct((windows * N_P...  3.26 us
    pallas_call x1, Pallas kernels, start(): pl.pallas_call(start_kernel, out_shape=(jax.ShapeDtypeStruct((N_SEQ, taps...  2.74 us
    ppermute x2, waiting for transfers between devices, on_device(): other = lax.ppermute(query, name, [(0, 1), (1, 0)])  2.62 us
  transfers between devices with their start and end apart: 8, of which 6 were waited for; matrix products, arithmetic and copies ran while one was open for 1% of the time, Pallas kernels for 1%

profile of v18, /device:TPU:1, one launch (start us, length us, event | category | flops | bytes accessed | tf_op | source)
XLA Modules:
  0.0 118.1 jit_solution(13778215326072307405)
XLA Ops:
  0.6 0.0 copy-start
  0.6 0.0 copy-start.4
  0.7 2.7 %shard_map.113 = (bf16[128,16,128]{2,1,0:T(8,128)(2,1)}, bf16[80,2048]{1,0:T(8,128)(2,1)}) custom-call(bf16[30,384]{1,0:T(8,128)(2,1)} %weight_ref.1, bf16[60,768]{1,0:T(8,128)(2,1)} %stem_ref.1, s32[16,128]{1,0:T(8,128)} %bitcast.34, s32[1,2048]{1,0:T(1,128)} %bitcast.35), custom_call_target="tpu_custom_call" | custom-call | tf_op jit(solution)/shard_map/pallas_call | solution.py:156
  3.4 0.0 copy-start.3
  3.4 15.3 %all-to-all-start = ((bf16[128,16,128]{2,1,0:T(8,128)(2,1)}), bf16[128,16,128]{2,1,0:T(8,128)(2,1)S(1)}, u32[]{:S(2)}, u32[]{:S(2)}) async-start(bf16[128,16,128]{2,1,0:T(8,128)(2,1)} %get-tuple-element.11), calls=%async_computation | async-start | bytes 1048576 | tf_op jit(solution)/shard_map/all_to_all | solution.py:442
  18.7 0.0 copy-start.2
  18.8 1.0 copy-done.2
  19.7 1.5 %shard_map.114 = f32[32,768]{1,0:T(8,128)S(1)} custom-call(bf16[80,2048]{1,0:T(8,128)(2,1)S(1)} %copy-done.2), custom_call_target="tpu_custom_call" | custom-call | flops 201326592 | bytes 200000 | tf_op jit(solution)/shard_map/pallas_call | solution.py:84
  21.3 0.0 copy-done.4
  21.3 0.0 copy-start.5
  21.3 0.3 copy.27
  21.6 0.0 copy-start.6
  21.6 14.0 %all-gather = bf16[256,768]{1,0:T(8,128)(2,1)S(1)} all-gather(bf16[32,768]{1,0:T(8,128)(2,1)S(1)} %convert_element_type.132), channel_id=2, replica_groups=mesh['zl'=2,'y'=8,'xh'=2,'xl'=2,'core'=2,'pair'=4] {'zl','xl','core'}, dimensions={0}, use_global_device_ids=true | all-gather | bytes 442368 | tf_op jit(solution)/shard_map/all_gather | solution.py:457
  35.6 0.0 all-to-all-done.held_ref
  35.6 0.0 copy-done.3
  35.6 3.3 %shard_map.115 = bf16[32,4,384]{2,1,0:T(4,128)(2,1)} custom-call(s32[1]{0:T(128)} %bitcast.2.place_ref, bf16[8,32,768]{2,1,0:T(8,128)(2,1)S(1)} %bitcast.28, bf16[128,16,128]{2,1,0:T(8,128)(2,1)S(1)} %all-to-all-done.held_ref, bf16[80,2048]{1,0:T(8,128)(2,1)S(1)} %copy-done.3), custom_call_target="tpu_custom_call" | custom-call | tf_op jit(solution)/shard_map/pallas_call | solution.py:254
  38.8 11.1 %all-to-all-start.1 = ((bf16[32,4,384]{2,1,0:T(4,128)(2,1)}), bf16[32,4,384]{2,1,0:T(4,128)(2,1)S(1)}, u32[]{:S(2)}, u32[]{:S(2)}) async-start(bf16[32,4,384]{2,1,0:T(4,128)(2,1)} %shard_map.115), calls=%async_computation.1 | async-start | bytes 196608 | tf_op jit(solution)/shard_map/all_to_all | solution.py:442
  50.0 0.0 copy-done.5
  50.0 0.0 copy-done.6
  50.0 0.2 pad_maximum_fusion.weight_ref
  50.2 0.0 copy-start.7
  50.2 8.9 %all-to-all-done.1 = bf16[32,4,384]{2,1,0:T(4,128)(2,1)S(1)} async-done(((bf16[32,4,384]{2,1,0:T(4,128)(2,1)}), bf16[32,4,384]{2,1,0:T(4,128)(2,1)S(1)}, u32[]{:S(2)}, u32[]{:S(2)}) %all-to-all-start.1) | async-done | bytes 98336 | tf_op jit(solution)/shard_map/all_to_all | solution.py:442
  59.1 0.2 reshape.78
  59.3 0.2 copy.41
  59.5 0.3 reshape.79.trunk_ref
  59.8 1.1 shard_map.116
  60.9 3.6 %collective-permute-start = (bf16[32,128]{1,0:T(8,128)(2,1)S(1)}, bf16[32,128]{1,0:T(8,128)(2,1)S(1)}, u32[]{:S(2)}, u32[]{:S(2)}) collective-permute-start(bf16[32,128]{1,0:T(8,128)(2,1)S(1)} %get-tuple-element.12), channel_id=1, source_target_pairs={{0,16},{16,0},{1,17},{17,1},{2,18},{18,2},{3,19},{19,3},{4,20},{20... | collective-permute-start | bytes 24584 | tf_op jit(solution)/shard_map/ppermute | solution.py:467
  64.5 0.0 copy-done.7
  64.5 0.0 copy-start.1
  64.5 0.2 copy.35
  64.8 0.2 copy.36
  65.0 0.0 copy-start.8
  65.0 6.8 %all-to-all-start.2 = ((bf16[16,40,128]{2,1,0:T(8,128)(2,1)}), bf16[16,40,128]{2,1,0:T(8,128)(2,1)S(1)}, u32[]{:S(2)}, u32[]{:S(2)}) async-start(bf16[16,40,128]{2,1,0:T(8,128)(2,1)} %get-tuple-element.13), calls=%async_computation.2 | async-start | bytes 327680 | tf_op jit(solution)/shard_map/all_to_all | solution.py:442
  71.8 0.0 collective-permute-done
  71.8 1.9 %collective-permute-start.1 = (bf16[64,128]{1,0:T(8,128)(2,1)S(1)}, bf16[64,128]{1,0:T(8,128)(2,1)S(1)}, u32[]{:S(2)}, u32[]{:S(2)}) collective-permute-start(bf16[64,128]{1,0:T(8,128)(2,1)S(1)} %pad_maximum_fusion.3), channel_id=1, source_target_pairs={{0,8},{8,0},{1,9},{9,1},{2,10},{10,2},{3,11},{11,3},{4,12},{12,4},... | collective-permute-start | bytes 49160 | tf_op jit(solution)/shard_map/ppermute | solution.py:467
  73.8 0.2 pad_maximum_fusion.1.w_pair_ref
  74.0 2.6 %collective-permute-done.1 = bf16[64,128]{1,0:T(8,128)(2,1)S(1)} collective-permute-done((bf16[64,128]{1,0:T(8,128)(2,1)S(1)}, bf16[64,128]{1,0:T(8,128)(2,1)S(1)}, u32[]{:S(2)}, u32[]{:S(2)}) %collective-permute-start.1) | collective-permute-done | bytes 16416 | tf_op jit(solution)/shard_map/ppermute | solution.py:467
  76.6 0.1 all-to-all-done.2.kv_ref
  76.7 1.1 shard_map.117
  77.8 5.0 %all-to-all-start.3 = ((bf16[8,16,256]{2,1,0:T(8,128)(2,1)}), bf16[8,16,256]{2,1,0:T(8,128)(2,1)S(1)}, u32[]{:S(2)}, u32[]{:S(2)}) async-start(bf16[8,16,256]{2,1,0:T(8,128)(2,1)} %shard_map.117), calls=%async_computation.3 | async-start | bytes 131072 | tf_op jit(solution)/shard_map/all_to_all | solution.py:442
  82.7 4.2 %all-to-all-done.3.parts_ref = bf16[8,16,256]{2,1,0:T(8,128)(2,1)S(1)} async-done(((bf16[8,16,256]{2,1,0:T(8,128)(2,1)}), bf16[8,16,256]{2,1,0:T(8,128)(2,1)S(1)}, u32[]{:S(2)}, u32[]{:S(2)}) %all-to-all-start.3) | async-done | bytes 65568 | tf_op jit(solution)/shard_map/all_to_all | solution.py:442
  86.9 0.0 copy-done.1
  86.9 1.0 shard_map.118
  87.9 4.3 %all-to-all-start.4 = ((f32[4,24,384]{2,1,0:T(8,128)}), f32[4,24,384]{2,1,0:T(8,128)S(1)}, u32[]{:S(2)}, u32[]{:S(2)}) async-start(f32[4,24,384]{2,1,0:T(8,128)} %shard_map.118), calls=%async_computation.4 | async-start | bytes 294912 | tf_op jit(solution)/shard_map/all_to_all | solution.py:442
  92.2 0.0 copy-done
  92.2 0.2 fusion
  92.4 0.0 copy-done.8
  92.4 0.1 copy.30.pair_ref
  92.6 6.6 %all-to-all-done.4.terms_ref = f32[4,24,384]{2,1,0:T(8,128)S(1)} async-done(((f32[4,24,384]{2,1,0:T(8,128)}), f32[4,24,384]{2,1,0:T(8,128)S(1)}, u32[]{:S(2)}, u32[]{:S(2)}) %all-to-all-start.4) | async-done | bytes 147488 | tf_op jit(solution)/shard_map/all_to_all | solution.py:442
  99.2 0.8 shard_map.119
  100.0 11.4 %all-to-all-start.5 = ((f32[128,1,96]{2,1,0:T(1,128)}), f32[128,1,96]{2,1,0:T(1,128)S(1)}, u32[]{:S(2)}, u32[]{:S(2)}) async-start(f32[128,1,96]{2,1,0:T(1,128)} %bitcast.11), calls=%async_computation.5 | async-start | bytes 131072 | tf_op jit(solution)/shard_map/all_to_all | solution.py:442
  111.4 0.1 slice_bitcast_fusion.1
  111.4 5.7 %all-to-all-done.5 = f32[128,1,96]{2,1,0:T(1,128)S(1)} async-done(((f32[128,1,96]{2,1,0:T(1,128)}), f32[128,1,96]{2,1,0:T(1,128)S(1)}, u32[]{:S(2)}, u32[]{:S(2)}) %all-to-all-start.5) | async-done | bytes 49184 | tf_op jit(solution)/shard_map/all_to_all | solution.py:442
  117.1 0.1 fusion.24
  117.2 0.1 copy.37
  117.3 0.1 copy.38
  117.4 0.1 copy.39
  117.4 0.7 fusion.6
  (7 shorter events, 0.1 us)
Async XLA Ops:
  0.6 91.6 %copy-start = (bf16[18,32]{1,0:T(8,128)(2,1)S(1)}, bf16[18,32]{1,0:T(8,128)(2,1)}, u32[]{:S(2)}) copy-start(bf16[18,32]{1,0:T(8,128)(2,1)} %param.18) | copy-start | bytes 3460
  0.6 20.6 %copy-start.4 = (bf16[1536,192]{0,1:T(8,128)(2,1)S(1)}, bf16[1536,192]{0,1:T(8,128)(2,1)}, u32[]{:S(2)}) copy-start(bf16[1536,192]{0,1:T(8,128)(2,1)} %param.15) | copy-start | bytes 1769476
  3.4 32.1 %copy-start.3 = (bf16[80,2048]{1,0:T(8,128)(2,1)S(1)}, bf16[80,2048]{1,0:T(8,128)(2,1)}, u32[]{:S(2)}) copy-start(bf16[80,2048]{1,0:T(8,128)(2,1)} %get-tuple-element.10.made_ref.stem_ref) | copy-start | bytes 983044
  3.4 32.1 %all-to-all-start = ((bf16[128,16,128]{2,1,0:T(8,128)(2,1)}), bf16[128,16,128]{2,1,0:T(8,128)(2,1)S(1)}, u32[]{:S(2)}, u32[]{:S(2)}) async-start(bf16[128,16,128]{2,1,0:T(8,128)(2,1)} %get-tuple-element.11), calls=%async_computation | async-start | bytes 1048576 | tf_op jit(solution)/shard_map/all_to_all | solution.py:442
  18.7 1.0 copy-start.2
  21.3 28.7 %copy-start.5 = (bf16[1536,128]{1,0:T(8,128)(2,1)S(1)}, bf16[1536,128]{1,0:T(8,128)(2,1)}, u32[]{:S(2)}) copy-start(bf16[1536,128]{1,0:T(8,128)(2,1)} %param.14) | copy-start | bytes 1179652
  21.6 28.4 %copy-start.6 = (bf16[1536,128]{1,0:T(8,128)(2,1)S(1)}, bf16[1536,128]{1,0:T(8,128)(2,1)}, u32[]{:S(2)}) copy-start(bf16[1536,128]{1,0:T(8,128)(2,1)} %param.13) | copy-start | bytes 1179652
  38.8 20.3 %all-to-all-start.1 = ((bf16[32,4,384]{2,1,0:T(4,128)(2,1)}), bf16[32,4,384]{2,1,0:T(4,128)(2,1)S(1)}, u32[]{:S(2)}, u32[]{:S(2)}) async-start(bf16[32,4,384]{2,1,0:T(4,128)(2,1)} %shard_map.115), calls=%async_computation.1 | async-start | bytes 196608 | tf_op jit(solution)/shard_map/all_to_all | solution.py:442
  50.2 14.3 %copy-start.7 = (bf16[2,1536,32]{1,2,0:T(8,128)(2,1)S(1)}, bf16[2,1536,32]{1,2,0:T(8,128)(2,1)}, u32[]{:S(2)}) copy-start(bf16[2,1536,32]{1,2,0:T(8,128)(2,1)} %param.17) | copy-start | bytes 589828
  60.9 10.9 %collective-permute-start = (bf16[32,128]{1,0:T(8,128)(2,1)S(1)}, bf16[32,128]{1,0:T(8,128)(2,1)S(1)}, u32[]{:S(2)}, u32[]{:S(2)}) collective-permute-start(bf16[32,128]{1,0:T(8,128)(2,1)S(1)} %get-tuple-element.12), channel_id=1, source_target_pairs={{0,16},{16,0},{1,17},{17,1},{2,18},{18,2},{3,19},{19,3},{4,20},{20... | collective-permute-start | bytes 24584 | tf_op jit(solution)/shard_map/ppermute | solution.py:467
  64.5 22.4 %copy-start.1 = (bf16[192,1536]{1,0:T(8,128)(2,1)S(1)}, bf16[192,1536]{1,0:T(8,128)(2,1)}, u32[]{:S(2)}) copy-start(bf16[192,1536]{1,0:T(8,128)(2,1)} %w_out_ref.1) | copy-start | bytes 1769476
  65.0 27.4 %copy-start.8 = (bf16[1,128,32]{1,2,0:T(8,128)(2,1)S(1)}, bf16[1,128,32]{1,2,0:T(8,128)(2,1)}, u32[]{:S(2)}) copy-start(bf16[1,128,32]{1,2,0:T(8,128)(2,1)} %param.19) | copy-start | bytes 24580
  65.0 11.7 %all-to-all-start.2 = ((bf16[16,40,128]{2,1,0:T(8,128)(2,1)}), bf16[16,40,128]{2,1,0:T(8,128)(2,1)S(1)}, u32[]{:S(2)}, u32[]{:S(2)}) async-start(bf16[16,40,128]{2,1,0:T(8,128)(2,1)} %get-tuple-element.13), calls=%async_computation.2 | async-start | bytes 327680 | tf_op jit(solution)/shard_map/all_to_all | solution.py:442
  71.8 4.8 %collective-permute-start.1 = (bf16[64,128]{1,0:T(8,128)(2,1)S(1)}, bf16[64,128]{1,0:T(8,128)(2,1)S(1)}, u32[]{:S(2)}, u32[]{:S(2)}) collective-permute-start(bf16[64,128]{1,0:T(8,128)(2,1)S(1)} %pad_maximum_fusion.3), channel_id=1, source_target_pairs={{0,8},{8,0},{1,9},{9,1},{2,10},{10,2},{3,11},{11,3},{4,12},{12,4},... | collective-permute-start | bytes 49160 | tf_op jit(solution)/shard_map/ppermute | solution.py:467
  77.8 9.1 %all-to-all-start.3 = ((bf16[8,16,256]{2,1,0:T(8,128)(2,1)}), bf16[8,16,256]{2,1,0:T(8,128)(2,1)S(1)}, u32[]{:S(2)}, u32[]{:S(2)}) async-start(bf16[8,16,256]{2,1,0:T(8,128)(2,1)} %shard_map.117), calls=%async_computation.3 | async-start | bytes 131072 | tf_op jit(solution)/shard_map/all_to_all | solution.py:442
  87.9 11.2 %all-to-all-start.4 = ((f32[4,24,384]{2,1,0:T(8,128)}), f32[4,24,384]{2,1,0:T(8,128)S(1)}, u32[]{:S(2)}, u32[]{:S(2)}) async-start(f32[4,24,384]{2,1,0:T(8,128)} %shard_map.118), calls=%async_computation.4 | async-start | bytes 294912 | tf_op jit(solution)/shard_map/all_to_all | solution.py:442
  100.0 17.1 %all-to-all-start.5 = ((f32[128,1,96]{2,1,0:T(1,128)}), f32[128,1,96]{2,1,0:T(1,128)S(1)}, u32[]{:S(2)}, u32[]{:S(2)}) async-start(f32[128,1,96]{2,1,0:T(1,128)} %bitcast.11), calls=%async_computation.5 | async-start | bytes 131072 | tf_op jit(solution)/shard_map/all_to_all | solution.py:442

commit v19 on v17

--- a/solution.py
+++ b/solution.py
@@ -22,6 +22,7 @@
 SPREAD = ("xh", "xl", "core")
 LINE = ("zl", "y")
 MIDDLE_SEQ = 32
+LATE_SHARE = 3
 MIDDLE_LINE = 4
 MIDDLE_SPREAD = 2
 MIDDLE_PAIR = 1
@@ -246,7 +247,7 @@
     for window in range(windows):
         block = flat[window // 2 * 4 : window // 2 * 4 + 4, :].astype(jnp.bfloat16)
         for index in range(N_PAIR):
-            out_ref[window * N_PAIR + index] = block
+            out_ref[(window * N_PAIR + index) ^ LATE_SHARE] = block
 
 
 def conv(place, section, held, stem_weight, columns):
@@ -454,9 +455,12 @@
     section = stem(made, w_stem.shape[1]).astype(jnp.bfloat16)
     sections = lax.all_gather(section, SHARE, axis=0, tiled=False)
 
-    parts = exchange(conv(place.astype(jnp.int32)[None], sections, held, made, share), SHARE + ("pair",))
+    parts = exchange(
+        conv(place.astype(jnp.int32)[None], sections, held, made, share), SHARE + ("pair",), LATE_SHARE
+    )
     count = ROWS // 2
-    trunk = parts.reshape(N_SHARE, N_PAIR, 2 * count, share).transpose(2, 1, 0, 3)
+    parts = parts.reshape(N_SHARE, N_PAIR, 2 * count, share)[:, ::-1]
+    trunk = parts.transpose(2, 1, 0, 3)
     trunk = trunk.reshape(2 * count, N_PAIR * width)
 
     core = lax.axis_index("core").astype(jnp.int32)[None]

time: 118 us -> 119 us (level)
  starting transfers between devices: 59.3 us -> 62.9 us
  waiting for transfers between devices: 27.2 us -> 23.9 us
    all_to_all x6, waiting for transfers between devices: 24.6 us -> 21.3 us  [exchange(): lax.all_to_all(blocks, axes, split_axis=0, concat_axis=0, tiled=True, axi...]
    all_to_all x6, starting transfers between devices: 53.5 us -> 56.8 us  [exchange(): lax.all_to_all(blocks, axes, split_axis=0, concat_axis=0, tiled=True, axi...]
  transfers between devices with their start and end apart: 8 -> 8, of which waited for: 6 -> 5; matrix products, arithmetic and copies ran while one was open for 1% -> 1% of each run, Pallas kernels for 1% -> 1%
where the time goes in v19:
time: 119 us; the launch traced here: 118 us
  starting transfers between devices  62.9 us (53%)
  waiting for transfers between devices  23.9 us (20%)
  blocking collectives  13.9 us (12%)
  Pallas kernels  11.5 us (10%)
  local copies, waits for them, and re-layouts  3.49 us (3%)
    all_to_all x6, starting transfers between devices, exchange(): lax.all_to_all(blocks, axes, split_axis=0, concat_axis=0, tiled=True, axi...  56.8 us
    all_to_all x6, waiting for transfers between devices, exchange(): lax.all_to_all(blocks, axes, split_axis=0, concat_axis=0, tiled=True, axi...  21.3 us
    all_gather x1, blocking collectives, on_device(): sections = lax.all_gather(section, SHARE, axis=0, tiled=False)  13.9 us
    ppermute x2, starting transfers between devices, on_device(): other = lax.ppermute(query, name, [(0, 1), (1, 0)])  6.16 us
    pallas_call x1, Pallas kernels, conv(): pl.pallas_call(conv_kernel, out_shape=jax.ShapeDtypeStruct((windows * N_P...  3.24 us
    pallas_call x1, Pallas kernels, start(): pl.pallas_call(start_kernel, out_shape=(jax.ShapeDtypeStruct((N_SEQ, taps...  2.69 us
    ppermute x2, waiting for transfers between devices, on_device(): other = lax.ppermute(query, name, [(0, 1), (1, 0)])  2.61 us
    unnamed x23, local copies, waits for them, and re-layouts  2.5 us
  transfers between devices with their start and end apart: 8, of which 5 were waited for; matrix products, arithmetic and copies ran while one was open for 1% of the time, Pallas kernels for 1%

profile of v19, /device:TPU:1, one launch (start us, length us, event | category | flops | bytes accessed | tf_op | source)
XLA Modules:
  0.0 117.7 jit_solution(5615328866832017101)
XLA Ops:
  0.6 0.0 copy-start
  0.6 2.7 %shard_map.113 = (bf16[128,16,128]{2,1,0:T(8,128)(2,1)}, bf16[80,2048]{1,0:T(8,128)(2,1)}) custom-call(bf16[30,384]{1,0:T(8,128)(2,1)} %weight_ref.1, bf16[60,768]{1,0:T(8,128)(2,1)} %stem_ref.1, s32[16,128]{1,0:T(8,128)} %bitcast.32, s32[1,2048]{1,0:T(1,128)} %bitcast.33), custom_call_target="tpu_custom_call" | custom-call | tf_op jit(solution)/shard_map/pallas_call | solution.py:157
  3.3 0.0 copy-start.4
  3.4 15.3 %all-to-all-start = ((bf16[128,16,128]{2,1,0:T(8,128)(2,1)}), bf16[128,16,128]{2,1,0:T(8,128)(2,1)S(1)}, u32[]{:S(2)}, u32[]{:S(2)}) async-start(bf16[128,16,128]{2,1,0:T(8,128)(2,1)} %get-tuple-element.11), calls=%async_computation | async-start | bytes 1048576 | tf_op jit(solution)/shard_map/all_to_all | solution.py:441
  18.7 0.0 copy-done.4
  18.7 1.5 %shard_map.114 = f32[32,768]{1,0:T(8,128)S(1)} custom-call(bf16[80,2048]{1,0:T(8,128)(2,1)S(1)} %copy-done.4), custom_call_target="tpu_custom_call" | custom-call | flops 201326592 | bytes 200000 | tf_op jit(solution)/shard_map/pallas_call | solution.py:85
  20.3 13.9 %all-gather = bf16[256,768]{1,0:T(8,128)(2,1)S(1)} all-gather(bf16[32,768]{1,0:T(8,128)(2,1)S(1)} %convert_element_type.132), channel_id=2, replica_groups=mesh['zl'=2,'y'=8,'xh'=2,'xl'=2,'core'=2,'pair'=4] {'zl','xl','core'}, dimensions={0}, use_global_device_ids=true | all-gather | bytes 442368 | tf_op jit(solution)/shard_map/all_gather | solution.py:456
  34.2 0.0 all-to-all-done.held_ref
  34.2 0.0 copy-start.5
  34.2 3.2 %shard_map.115 = bf16[32,4,384]{2,1,0:T(4,128)(2,1)} custom-call(s32[1]{0:T(128)} %bitcast.2.place_ref, bf16[8,32,768]{2,1,0:T(8,128)(2,1)S(1)} %bitcast.27, bf16[128,16,128]{2,1,0:T(8,128)(2,1)S(1)} %all-to-all-done.held_ref, bf16[80,2048]{1,0:T(8,128)(2,1)S(1)} %copy-done.4), custom_call_target="tpu_custom_call" | custom-call | tf_op jit(solution)/shard_map/pallas_call | solution.py:255
  37.4 11.7 %all-to-all-start.1 = ((bf16[32,4,384]{2,1,0:T(4,128)(2,1)}), bf16[32,4,384]{2,1,0:T(4,128)(2,1)S(1)}, u32[]{:S(2)}, u32[]{:S(2)}) async-start(bf16[32,4,384]{2,1,0:T(4,128)(2,1)} %shard_map.115), calls=%async_computation.1 | async-start | bytes 196608 | tf_op jit(solution)/shard_map/all_to_all | solution.py:441
  49.1 0.0 copy-done.5
  49.1 0.3 copy.27.w_value_ref
  49.4 5.6 %all-to-all-done.1 = bf16[32,4,384]{2,1,0:T(4,128)(2,1)S(1)} async-done(((bf16[32,4,384]{2,1,0:T(4,128)(2,1)}), bf16[32,4,384]{2,1,0:T(4,128)(2,1)S(1)}, u32[]{:S(2)}, u32[]{:S(2)}) %all-to-all-start.1) | async-done | bytes 98336 | tf_op jit(solution)/shard_map/all_to_all | solution.py:441
  54.9 0.2 reshape.78
  55.2 0.2 copy.26
  55.4 0.0 copy-start.2
  55.4 0.0 copy-start.3
  55.4 0.3 reshape.79.trunk_ref
  55.8 0.6 copy-done.2
  56.4 0.1 copy-done.3
  56.5 0.0 copy-start.6
  56.5 1.1 shard_map.116
  57.6 4.2 %collective-permute-start = (bf16[32,128]{1,0:T(8,128)(2,1)S(1)}, bf16[32,128]{1,0:T(8,128)(2,1)S(1)}, u32[]{:S(2)}, u32[]{:S(2)}) collective-permute-start(bf16[32,128]{1,0:T(8,128)(2,1)S(1)} %get-tuple-element.12), channel_id=1, source_target_pairs={{0,16},{16,0},{1,17},{17,1},{2,18},{18,2},{3,19},{19,3},{4,20},{20... | collective-permute-start | bytes 24584 | tf_op jit(solution)/shard_map/ppermute | solution.py:469
  61.8 0.0 copy-done.6
  61.8 0.2 copy.35
  62.1 0.2 copy.36
  62.3 7.0 %all-to-all-start.2 = ((bf16[16,40,128]{2,1,0:T(8,128)(2,1)}), bf16[16,40,128]{2,1,0:T(8,128)(2,1)S(1)}, u32[]{:S(2)}, u32[]{:S(2)}) async-start(bf16[16,40,128]{2,1,0:T(8,128)(2,1)} %get-tuple-element.13), calls=%async_computation.2 | async-start | bytes 327680 | tf_op jit(solution)/shard_map/all_to_all | solution.py:441
  69.3 0.0 collective-permute-done
  69.4 1.9 %collective-permute-start.1 = (bf16[64,128]{1,0:T(8,128)(2,1)S(1)}, bf16[64,128]{1,0:T(8,128)(2,1)S(1)}, u32[]{:S(2)}, u32[]{:S(2)}) collective-permute-start(bf16[64,128]{1,0:T(8,128)(2,1)S(1)} %pad_maximum_fusion.2), channel_id=1, source_target_pairs={{0,8},{8,0},{1,9},{9,1},{2,10},{10,2},{3,11},{11,3},{4,12},{12,4},... | collective-permute-start | bytes 49160 | tf_op jit(solution)/shard_map/ppermute | solution.py:469
  71.3 0.0 copy-start.1
  71.3 0.2 pad_maximum_fusion.w_pair_ref
  71.5 2.6 %collective-permute-done.1 = bf16[64,128]{1,0:T(8,128)(2,1)S(1)} collective-permute-done((bf16[64,128]{1,0:T(8,128)(2,1)S(1)}, bf16[64,128]{1,0:T(8,128)(2,1)S(1)}, u32[]{:S(2)}, u32[]{:S(2)}) %collective-permute-start.1) | collective-permute-done | bytes 16416 | tf_op jit(solution)/shard_map/ppermute | solution.py:469
  74.1 0.0 all-to-all-done.2.kv_ref
  74.1 1.1 shard_map.117
  75.2 5.3 %all-to-all-start.3 = ((bf16[8,16,256]{2,1,0:T(8,128)(2,1)}), bf16[8,16,256]{2,1,0:T(8,128)(2,1)S(1)}, u32[]{:S(2)}, u32[]{:S(2)}) async-start(bf16[8,16,256]{2,1,0:T(8,128)(2,1)} %shard_map.117), calls=%async_computation.3 | async-start | bytes 131072 | tf_op jit(solution)/shard_map/all_to_all | solution.py:441
  80.5 4.2 %all-to-all-done.3.parts_ref = bf16[8,16,256]{2,1,0:T(8,128)(2,1)S(1)} async-done(((bf16[8,16,256]{2,1,0:T(8,128)(2,1)}), bf16[8,16,256]{2,1,0:T(8,128)(2,1)S(1)}, u32[]{:S(2)}, u32[]{:S(2)}) %all-to-all-start.3) | async-done | bytes 65568 | tf_op jit(solution)/shard_map/all_to_all | solution.py:441
  84.7 0.0 copy-done.1
  84.7 1.0 shard_map.118
  85.7 6.0 %all-to-all-start.4 = ((f32[4,24,384]{2,1,0:T(8,128)}), f32[4,24,384]{2,1,0:T(8,128)S(1)}, u32[]{:S(2)}, u32[]{:S(2)}) async-start(f32[4,24,384]{2,1,0:T(8,128)} %shard_map.118), calls=%async_computation.4 | async-start | bytes 294912 | tf_op jit(solution)/shard_map/all_to_all | solution.py:441
  91.8 0.0 copy-done
  91.8 0.2 fusion
  92.0 0.0 copy-start.7
  92.0 0.7 copy-done.7
  92.7 0.1 copy.30.pair_ref
  92.8 5.9 %all-to-all-done.4.terms_ref = f32[4,24,384]{2,1,0:T(8,128)S(1)} async-done(((f32[4,24,384]{2,1,0:T(8,128)}), f32[4,24,384]{2,1,0:T(8,128)S(1)}, u32[]{:S(2)}, u32[]{:S(2)}) %all-to-all-start.4) | async-done | bytes 147488 | tf_op jit(solution)/shard_map/all_to_all | solution.py:441
  98.7 0.8 shard_map.119
  99.5 11.4 %all-to-all-start.5 = ((f32[128,1,96]{2,1,0:T(1,128)}), f32[128,1,96]{2,1,0:T(1,128)S(1)}, u32[]{:S(2)}, u32[]{:S(2)}) async-start(f32[128,1,96]{2,1,0:T(1,128)} %bitcast.11), calls=%async_computation.5 | async-start | bytes 131072 | tf_op jit(solution)/shard_map/all_to_all | solution.py:441
  111.0 0.1 slice_bitcast_fusion.1
  111.1 5.7 %all-to-all-done.5 = f32[128,1,96]{2,1,0:T(1,128)S(1)} async-done(((f32[128,1,96]{2,1,0:T(1,128)}), f32[128,1,96]{2,1,0:T(1,128)S(1)}, u32[]{:S(2)}, u32[]{:S(2)}) %all-to-all-start.5) | async-done | bytes 49184 | tf_op jit(solution)/shard_map/all_to_all | solution.py:441
  116.7 0.1 fusion.24
  116.8 0.1 copy.37
  116.9 0.1 copy.38
  117.0 0.1 copy.39
  117.0 0.7 fusion.6
  (8 shorter events, 0.1 us)
Async XLA Ops:
  0.6 91.2 %copy-start = (bf16[18,32]{1,0:T(8,128)(2,1)S(1)}, bf16[18,32]{1,0:T(8,128)(2,1)}, u32[]{:S(2)}) copy-start(bf16[18,32]{1,0:T(8,128)(2,1)} %param.18) | copy-start | bytes 3460
  3.3 15.3 %copy-start.4 = (bf16[80,2048]{1,0:T(8,128)(2,1)S(1)}, bf16[80,2048]{1,0:T(8,128)(2,1)}, u32[]{:S(2)}) copy-start(bf16[80,2048]{1,0:T(8,128)(2,1)} %get-tuple-element.10.made_ref.stem_ref) | copy-start | bytes 983044
  3.4 30.8 %all-to-all-start = ((bf16[128,16,128]{2,1,0:T(8,128)(2,1)}), bf16[128,16,128]{2,1,0:T(8,128)(2,1)S(1)}, u32[]{:S(2)}, u32[]{:S(2)}) async-start(bf16[128,16,128]{2,1,0:T(8,128)(2,1)} %get-tuple-element.11), calls=%async_computation | async-start | bytes 1048576 | tf_op jit(solution)/shard_map/all_to_all | solution.py:441
  34.2 14.9 %copy-start.5 = (bf16[1536,192]{0,1:T(8,128)(2,1)S(1)}, bf16[1536,192]{0,1:T(8,128)(2,1)}, u32[]{:S(2)}) copy-start(bf16[1536,192]{0,1:T(8,128)(2,1)} %param.15) | copy-start | bytes 1769476
  37.4 17.5 %all-to-all-start.1 = ((bf16[32,4,384]{2,1,0:T(4,128)(2,1)}), bf16[32,4,384]{2,1,0:T(4,128)(2,1)S(1)}, u32[]{:S(2)}, u32[]{:S(2)}) async-start(bf16[32,4,384]{2,1,0:T(4,128)(2,1)} %shard_map.115), calls=%async_computation.1 | async-start | bytes 196608 | tf_op jit(solution)/shard_map/all_to_all | solution.py:441
  55.4 1.0 copy-start.2
  55.4 1.1 copy-start.3
  56.5 5.3 %copy-start.6 = (bf16[2,1536,32]{1,2,0:T(8,128)(2,1)S(1)}, bf16[2,1536,32]{1,2,0:T(8,128)(2,1)}, u32[]{:S(2)}) copy-start(bf16[2,1536,32]{1,2,0:T(8,128)(2,1)} %param.17) | copy-start | bytes 589828
  57.6 11.8 %collective-permute-start = (bf16[32,128]{1,0:T(8,128)(2,1)S(1)}, bf16[32,128]{1,0:T(8,128)(2,1)S(1)}, u32[]{:S(2)}, u32[]{:S(2)}) collective-permute-start(bf16[32,128]{1,0:T(8,128)(2,1)S(1)} %get-tuple-element.12), channel_id=1, source_target_pairs={{0,16},{16,0},{1,17},{17,1},{2,18},{18,2},{3,19},{19,3},{4,20},{20... | collective-permute-start | bytes 24584 | tf_op jit(solution)/shard_map/ppermute | solution.py:469
  62.3 11.8 %all-to-all-start.2 = ((bf16[16,40,128]{2,1,0:T(8,128)(2,1)}), bf16[16,40,128]{2,1,0:T(8,128)(2,1)S(1)}, u32[]{:S(2)}, u32[]{:S(2)}) async-start(bf16[16,40,128]{2,1,0:T(8,128)(2,1)} %get-tuple-element.13), calls=%async_computation.2 | async-start | bytes 327680 | tf_op jit(solution)/shard_map/all_to_all | solution.py:441
  69.4 4.8 %collective-permute-start.1 = (bf16[64,128]{1,0:T(8,128)(2,1)S(1)}, bf16[64,128]{1,0:T(8,128)(2,1)S(1)}, u32[]{:S(2)}, u32[]{:S(2)}) collective-permute-start(bf16[64,128]{1,0:T(8,128)(2,1)S(1)} %pad_maximum_fusion.2), channel_id=1, source_target_pairs={{0,8},{8,0},{1,9},{9,1},{2,10},{10,2},{3,11},{11,3},{4,12},{12,4},... | collective-permute-start | bytes 49160 | tf_op jit(solution)/shard_map/ppermute | solution.py:469
  71.3 13.4 %copy-start.1 = (bf16[192,1536]{1,0:T(8,128)(2,1)S(1)}, bf16[192,1536]{1,0:T(8,128)(2,1)}, u32[]{:S(2)}) copy-start(bf16[192,1536]{1,0:T(8,128)(2,1)} %w_out_ref.1) | copy-start | bytes 1769476
  75.2 9.5 %all-to-all-start.3 = ((bf16[8,16,256]{2,1,0:T(8,128)(2,1)}), bf16[8,16,256]{2,1,0:T(8,128)(2,1)S(1)}, u32[]{:S(2)}, u32[]{:S(2)}) async-start(bf16[8,16,256]{2,1,0:T(8,128)(2,1)} %shard_map.117), calls=%async_computation.3 | async-start | bytes 131072 | tf_op jit(solution)/shard_map/all_to_all | solution.py:441
  85.7 13.0 %all-to-all-start.4 = ((f32[4,24,384]{2,1,0:T(8,128)}), f32[4,24,384]{2,1,0:T(8,128)S(1)}, u32[]{:S(2)}, u32[]{:S(2)}) async-start(f32[4,24,384]{2,1,0:T(8,128)} %shard_map.118), calls=%async_computation.4 | async-start | bytes 294912 | tf_op jit(solution)/shard_map/all_to_all | solution.py:441
  92.0 0.7 copy-start.7
  99.5 17.2 %all-to-all-start.5 = ((f32[128,1,96]{2,1,0:T(1,128)}), f32[128,1,96]{2,1,0:T(1,128)S(1)}, u32[]{:S(2)}, u32[]{:S(2)}) async-start(f32[128,1,96]{2,1,0:T(1,128)} %bitcast.11), calls=%async_computation.5 | async-start | bytes 131072 | tf_op jit(solution)/shard_map/all_to_all | solution.py:441

commit v20 on v17

--- a/solution.py
+++ b/solution.py
@@ -24,7 +24,7 @@
 MIDDLE_SEQ = 32
 MIDDLE_LINE = 4
 MIDDLE_SPREAD = 2
-MIDDLE_PAIR = 1
+MIDDLE_PAIR = 2
 N_SEQ = math.prod(SIZES[name] for name in SEQ)
 N_SHARE = math.prod(SIZES[name] for name in SHARE)
 N_PAIR = SIZES["pair"]

time: 118 us -> 117 us (level)
  waiting for transfers between devices: 27.2 us -> 23.2 us
  starting transfers between devices: 59.3 us -> 62.7 us
    all_to_all x6, waiting for transfers between devices: 24.6 us -> 20.5 us  [exchange(): lax.all_to_all(blocks, axes, split_axis=0, concat_axis=0, tiled=True, axi...]
    all_to_all x6, starting transfers between devices: 53.5 us -> 56.9 us  [exchange(): lax.all_to_all(blocks, axes, split_axis=0, concat_axis=0, tiled=True, axi...]
where the time goes in v20:
time: 117 us
  starting transfers between devices  62.7 us (54%)
  waiting for transfers between devices  23.2 us (20%)
  blocking collectives  13.9 us (12%)
  Pallas kernels  11.5 us (10%)
  local copies, waits for them, and re-layouts  3.32 us (3%)
    all_to_all x6, starting transfers between devices, exchange(): lax.all_to_all(blocks, axes, split_axis=0, concat_axis=0, tiled=True, axi...  56.9 us
    all_to_all x6, waiting for transfers between devices, exchange(): lax.all_to_all(blocks, axes, split_axis=0, concat_axis=0, tiled=True, axi...  20.5 us
    all_gather x1, blocking collectives, on_device(): sections = lax.all_gather(section, SHARE, axis=0, tiled=False)  13.9 us
    ppermute x2, starting transfers between devices, on_device(): other = lax.ppermute(query, name, [(0, 1), (1, 0)])  5.81 us
    pallas_call x1, Pallas kernels, conv(): pl.pallas_call(conv_kernel, out_shape=jax.ShapeDtypeStruct((windows * N_P...  3.24 us
    pallas_call x1, Pallas kernels, start(): pl.pallas_call(start_kernel, out_shape=(jax.ShapeDtypeStruct((N_SEQ, taps...  2.69 us
    ppermute x2, waiting for transfers between devices, on_device(): other = lax.ppermute(query, name, [(0, 1), (1, 0)])  2.61 us
    unnamed x23, local copies, waits for them, and re-layouts  2.37 us
  transfers between devices with their start and end apart: 8, of which 6 were waited for; matrix products, arithmetic and copies ran while one was open for 1% of the time, Pallas kernels for 1%

profile of v20, /device:TPU:1, one launch (start us, length us, event | category | flops | bytes accessed | tf_op | source)
XLA Modules:
  0.0 116.7 jit_solution(14267168718393343957)
XLA Ops:
  0.6 0.0 copy-start
  0.6 2.7 %shard_map.113 = (bf16[128,16,128]{2,1,0:T(8,128)(2,1)}, bf16[80,2048]{1,0:T(8,128)(2,1)}) custom-call(bf16[30,384]{1,0:T(8,128)(2,1)} %weight_ref.1, bf16[60,768]{1,0:T(8,128)(2,1)} %stem_ref.1, s32[16,128]{1,0:T(8,128)} %bitcast.34, s32[1,2048]{1,0:T(1,128)} %bitcast.35), custom_call_target="tpu_custom_call" | custom-call | tf_op jit(solution)/shard_map/pallas_call | solution.py:156
  3.3 0.0 copy-start.4
  3.4 15.3 %all-to-all-start = ((bf16[128,16,128]{2,1,0:T(8,128)(2,1)}), bf16[128,16,128]{2,1,0:T(8,128)(2,1)S(1)}, u32[]{:S(2)}, u32[]{:S(2)}) async-start(bf16[128,16,128]{2,1,0:T(8,128)(2,1)} %get-tuple-element.11), calls=%async_computation | async-start | bytes 1048576 | tf_op jit(solution)/shard_map/all_to_all | solution.py:440
  18.7 0.0 copy-done.4
  18.7 1.5 %shard_map.114 = f32[32,768]{1,0:T(8,128)S(1)} custom-call(bf16[80,2048]{1,0:T(8,128)(2,1)S(1)} %copy-done.4), custom_call_target="tpu_custom_call" | custom-call | flops 201326592 | bytes 200000 | tf_op jit(solution)/shard_map/pallas_call | solution.py:84
  20.3 13.9 %all-gather = bf16[256,768]{1,0:T(8,128)(2,1)S(1)} all-gather(bf16[32,768]{1,0:T(8,128)(2,1)S(1)} %convert_element_type.132), channel_id=2, replica_groups=mesh['zl'=2,'y'=8,'xh'=2,'xl'=2,'core'=2,'pair'=4] {'zl','xl','core'}, dimensions={0}, use_global_device_ids=true | all-gather | bytes 442368 | tf_op jit(solution)/shard_map/all_gather | solution.py:455
  34.2 0.0 all-to-all-done.held_ref
  34.2 0.0 copy-start.5
  34.2 3.2 %shard_map.115 = bf16[32,4,384]{2,1,0:T(4,128)(2,1)} custom-call(s32[1]{0:T(128)} %bitcast.2.place_ref, bf16[8,32,768]{2,1,0:T(8,128)(2,1)S(1)} %bitcast.28, bf16[128,16,128]{2,1,0:T(8,128)(2,1)S(1)} %all-to-all-done.held_ref, bf16[80,2048]{1,0:T(8,128)(2,1)S(1)} %copy-done.4), custom_call_target="tpu_custom_call" | custom-call | tf_op jit(solution)/shard_map/pallas_call | solution.py:254
  37.4 11.0 %all-to-all-start.1 = ((bf16[32,4,384]{2,1,0:T(4,128)(2,1)}), bf16[32,4,384]{2,1,0:T(4,128)(2,1)S(1)}, u32[]{:S(2)}, u32[]{:S(2)}) async-start(bf16[32,4,384]{2,1,0:T(4,128)(2,1)} %shard_map.115), calls=%async_computation.1 | async-start | bytes 196608 | tf_op jit(solution)/shard_map/all_to_all | solution.py:440
  48.4 0.0 copy-done.5
  48.4 0.3 copy.27.w_value_ref
  48.7 8.8 %all-to-all-done.1 = bf16[32,4,384]{2,1,0:T(4,128)(2,1)S(1)} async-done(((bf16[32,4,384]{2,1,0:T(4,128)(2,1)}), bf16[32,4,384]{2,1,0:T(4,128)(2,1)S(1)}, u32[]{:S(2)}, u32[]{:S(2)}) %all-to-all-start.1) | async-done | bytes 98336 | tf_op jit(solution)/shard_map/all_to_all | solution.py:440
  57.5 0.2 reshape.78
  57.7 0.0 copy-start.2
  57.8 0.0 copy-start.3
  57.8 0.2 copy.41
  58.0 0.3 reshape.79.trunk_ref
  58.3 0.5 copy-done.2
  58.7 0.1 copy-done.3
  58.9 0.0 copy-start.6
  58.9 1.1 shard_map.116
  60.0 3.9 %collective-permute-start = (bf16[32,128]{1,0:T(8,128)(2,1)S(1)}, bf16[32,128]{1,0:T(8,128)(2,1)S(1)}, u32[]{:S(2)}, u32[]{:S(2)}) collective-permute-start(bf16[32,128]{1,0:T(8,128)(2,1)S(1)} %get-tuple-element.12), channel_id=1, source_target_pairs={{0,16},{16,0},{1,17},{17,1},{2,18},{18,2},{3,19},{19,3},{4,20},{20... | collective-permute-start | bytes 24584 | tf_op jit(solution)/shard_map/ppermute | solution.py:465
  63.8 0.0 copy-done.6
  63.9 0.2 copy.35
  64.1 0.2 copy.36
  64.3 6.8 %all-to-all-start.2 = ((bf16[16,40,128]{2,1,0:T(8,128)(2,1)}), bf16[16,40,128]{2,1,0:T(8,128)(2,1)S(1)}, u32[]{:S(2)}, u32[]{:S(2)}) async-start(bf16[16,40,128]{2,1,0:T(8,128)(2,1)} %get-tuple-element.13), calls=%async_computation.2 | async-start | bytes 327680 | tf_op jit(solution)/shard_map/all_to_all | solution.py:440
  71.1 0.0 collective-permute-done
  71.2 1.9 %collective-permute-start.1 = (bf16[64,128]{1,0:T(8,128)(2,1)S(1)}, bf16[64,128]{1,0:T(8,128)(2,1)S(1)}, u32[]{:S(2)}, u32[]{:S(2)}) collective-permute-start(bf16[64,128]{1,0:T(8,128)(2,1)S(1)} %pad_maximum_fusion.2), channel_id=1, source_target_pairs={{0,8},{8,0},{1,9},{9,1},{2,10},{10,2},{3,11},{11,3},{4,12},{12,4},... | collective-permute-start | bytes 49160 | tf_op jit(solution)/shard_map/ppermute | solution.py:465
  73.1 0.0 copy-start.1
  73.1 0.2 pad_maximum_fusion.w_pair_ref
  73.3 2.6 %collective-permute-done.1 = bf16[64,128]{1,0:T(8,128)(2,1)S(1)} collective-permute-done((bf16[64,128]{1,0:T(8,128)(2,1)S(1)}, bf16[64,128]{1,0:T(8,128)(2,1)S(1)}, u32[]{:S(2)}, u32[]{:S(2)}) %collective-permute-start.1) | collective-permute-done | bytes 16416 | tf_op jit(solution)/shard_map/ppermute | solution.py:465
  75.9 0.1 all-to-all-done.2.kv_ref
  76.0 1.1 shard_map.117
  77.1 4.8 %all-to-all-start.3 = ((bf16[8,16,256]{2,1,0:T(8,128)(2,1)}), bf16[8,16,256]{2,1,0:T(8,128)(2,1)S(1)}, u32[]{:S(2)}, u32[]{:S(2)}) async-start(bf16[8,16,256]{2,1,0:T(8,128)(2,1)} %shard_map.117), calls=%async_computation.3 | async-start | bytes 131072 | tf_op jit(solution)/shard_map/all_to_all | solution.py:440
  81.9 4.2 %all-to-all-done.3.parts_ref = bf16[8,16,256]{2,1,0:T(8,128)(2,1)S(1)} async-done(((bf16[8,16,256]{2,1,0:T(8,128)(2,1)}), bf16[8,16,256]{2,1,0:T(8,128)(2,1)S(1)}, u32[]{:S(2)}, u32[]{:S(2)}) %all-to-all-start.3) | async-done | bytes 65568 | tf_op jit(solution)/shard_map/all_to_all | solution.py:440
  86.0 0.0 copy-done.1
  86.0 1.0 shard_map.118
  87.1 6.6 %all-to-all-start.4 = ((f32[4,24,384]{2,1,0:T(8,128)}), f32[4,24,384]{2,1,0:T(8,128)S(1)}, u32[]{:S(2)}, u32[]{:S(2)}) async-start(f32[4,24,384]{2,1,0:T(8,128)} %shard_map.118), calls=%async_computation.4 | async-start | bytes 294912 | tf_op jit(solution)/shard_map/all_to_all | solution.py:440
  93.7 0.0 copy-done
  93.7 0.2 fusion
  93.9 0.0 copy-start.7
  93.9 0.7 copy-done.7
  94.6 0.1 copy.30.pair_ref
  94.8 1.8 %all-to-all-done.4.terms_ref = f32[4,24,384]{2,1,0:T(8,128)S(1)} async-done(((f32[4,24,384]{2,1,0:T(8,128)}), f32[4,24,384]{2,1,0:T(8,128)S(1)}, u32[]{:S(2)}, u32[]{:S(2)}) %all-to-all-start.4) | async-done | bytes 147488 | tf_op jit(solution)/shard_map/all_to_all | solution.py:440
  96.6 0.8 shard_map.119
  97.4 12.5 %all-to-all-start.5 = ((f32[128,1,96]{2,1,0:T(1,128)}), f32[128,1,96]{2,1,0:T(1,128)S(1)}, u32[]{:S(2)}, u32[]{:S(2)}) async-start(f32[128,1,96]{2,1,0:T(1,128)} %bitcast.11), calls=%async_computation.5 | async-start | bytes 131072 | tf_op jit(solution)/shard_map/all_to_all | solution.py:440
  109.9 0.1 slice_bitcast_fusion.1
  110.0 5.7 %all-to-all-done.5 = f32[128,1,96]{2,1,0:T(1,128)S(1)} async-done(((f32[128,1,96]{2,1,0:T(1,128)}), f32[128,1,96]{2,1,0:T(1,128)S(1)}, u32[]{:S(2)}, u32[]{:S(2)}) %all-to-all-start.5) | async-done | bytes 49184 | tf_op jit(solution)/shard_map/all_to_all | solution.py:440
  115.6 0.1 fusion.24
  115.7 0.1 copy.37
  115.8 0.1 copy.38
  115.9 0.1 copy.39
  115.9 0.7 fusion.6
  (7 shorter events, 0.1 us)
Async XLA Ops:
  0.6 93.1 %copy-start = (bf16[18,32]{1,0:T(8,128)(2,1)S(1)}, bf16[18,32]{1,0:T(8,128)(2,1)}, u32[]{:S(2)}) copy-start(bf16[18,32]{1,0:T(8,128)(2,1)} %param.18) | copy-start | bytes 3460
  3.3 15.3 %copy-start.4 = (bf16[80,2048]{1,0:T(8,128)(2,1)S(1)}, bf16[80,2048]{1,0:T(8,128)(2,1)}, u32[]{:S(2)}) copy-start(bf16[80,2048]{1,0:T(8,128)(2,1)} %get-tuple-element.10.made_ref.stem_ref) | copy-start | bytes 983044
  3.4 30.8 %all-to-all-start = ((bf16[128,16,128]{2,1,0:T(8,128)(2,1)}), bf16[128,16,128]{2,1,0:T(8,128)(2,1)S(1)}, u32[]{:S(2)}, u32[]{:S(2)}) async-start(bf16[128,16,128]{2,1,0:T(8,128)(2,1)} %get-tuple-element.11), calls=%async_computation | async-start | bytes 1048576 | tf_op jit(solution)/shard_map/all_to_all | solution.py:440
  34.2 14.2 %copy-start.5 = (bf16[1536,192]{0,1:T(8,128)(2,1)S(1)}, bf16[1536,192]{0,1:T(8,128)(2,1)}, u32[]{:S(2)}) copy-start(bf16[1536,192]{0,1:T(8,128)(2,1)} %param.15) | copy-start | bytes 1769476
  37.4 20.1 %all-to-all-start.1 = ((bf16[32,4,384]{2,1,0:T(4,128)(2,1)}), bf16[32,4,384]{2,1,0:T(4,128)(2,1)S(1)}, u32[]{:S(2)}, u32[]{:S(2)}) async-start(bf16[32,4,384]{2,1,0:T(4,128)(2,1)} %shard_map.115), calls=%async_computation.1 | async-start | bytes 196608 | tf_op jit(solution)/shard_map/all_to_all | solution.py:440
  57.7 1.0 copy-start.2
  57.8 1.1 copy-start.3
  58.9 5.0 %copy-start.6 = (bf16[2,1536,32]{1,2,0:T(8,128)(2,1)S(1)}, bf16[2,1536,32]{1,2,0:T(8,128)(2,1)}, u32[]{:S(2)}) copy-start(bf16[2,1536,32]{1,2,0:T(8,128)(2,1)} %param.17) | copy-start | bytes 589828
  60.0 11.2 %collective-permute-start = (bf16[32,128]{1,0:T(8,128)(2,1)S(1)}, bf16[32,128]{1,0:T(8,128)(2,1)S(1)}, u32[]{:S(2)}, u32[]{:S(2)}) collective-permute-start(bf16[32,128]{1,0:T(8,128)(2,1)S(1)} %get-tuple-element.12), channel_id=1, source_target_pairs={{0,16},{16,0},{1,17},{17,1},{2,18},{18,2},{3,19},{19,3},{4,20},{20... | collective-permute-start | bytes 24584 | tf_op jit(solution)/shard_map/ppermute | solution.py:465
  64.3 11.7 %all-to-all-start.2 = ((bf16[16,40,128]{2,1,0:T(8,128)(2,1)}), bf16[16,40,128]{2,1,0:T(8,128)(2,1)S(1)}, u32[]{:S(2)}, u32[]{:S(2)}) async-start(bf16[16,40,128]{2,1,0:T(8,128)(2,1)} %get-tuple-element.13), calls=%async_computation.2 | async-start | bytes 327680 | tf_op jit(solution)/shard_map/all_to_all | solution.py:440
  71.2 4.8 %collective-permute-start.1 = (bf16[64,128]{1,0:T(8,128)(2,1)S(1)}, bf16[64,128]{1,0:T(8,128)(2,1)S(1)}, u32[]{:S(2)}, u32[]{:S(2)}) collective-permute-start(bf16[64,128]{1,0:T(8,128)(2,1)S(1)} %pad_maximum_fusion.2), channel_id=1, source_target_pairs={{0,8},{8,0},{1,9},{9,1},{2,10},{10,2},{3,11},{11,3},{4,12},{12,4},... | collective-permute-start | bytes 49160 | tf_op jit(solution)/shard_map/ppermute | solution.py:465
  73.1 12.9 %copy-start.1 = (bf16[192,1536]{1,0:T(8,128)(2,1)S(1)}, bf16[192,1536]{1,0:T(8,128)(2,1)}, u32[]{:S(2)}) copy-start(bf16[192,1536]{1,0:T(8,128)(2,1)} %w_out_ref.1) | copy-start | bytes 1769476
  77.1 8.9 %all-to-all-start.3 = ((bf16[8,16,256]{2,1,0:T(8,128)(2,1)}), bf16[8,16,256]{2,1,0:T(8,128)(2,1)S(1)}, u32[]{:S(2)}, u32[]{:S(2)}) async-start(bf16[8,16,256]{2,1,0:T(8,128)(2,1)} %shard_map.117), calls=%async_computation.3 | async-start | bytes 131072 | tf_op jit(solution)/shard_map/all_to_all | solution.py:440
  87.1 9.5 %all-to-all-start.4 = ((f32[4,24,384]{2,1,0:T(8,128)}), f32[4,24,384]{2,1,0:T(8,128)S(1)}, u32[]{:S(2)}, u32[]{:S(2)}) async-start(f32[4,24,384]{2,1,0:T(8,128)} %shard_map.118), calls=%async_computation.4 | async-start | bytes 294912 | tf_op jit(solution)/shard_map/all_to_all | solution.py:440
  93.9 0.7 copy-start.7
  97.4 18.2 %all-to-all-start.5 = ((f32[128,1,96]{2,1,0:T(1,128)}), f32[128,1,96]{2,1,0:T(1,128)S(1)}, u32[]{:S(2)}, u32[]{:S(2)}) async-start(f32[128,1,96]{2,1,0:T(1,128)} %bitcast.11), calls=%async_computation.5 | async-start | bytes 131072 | tf_op jit(solution)/shard_map/all_to_all | solution.py:440
